TPU v7x, 32 devices: a whole 2x2x4 slice. The times are simulated.
32 devices in a mesh: seq: 4 (over y, x), exp: 8 (over z, core).
Axes of the slice: x: 2, y: 2, z: 4, core: 2. Of those that a mesh axis runs over, the one named last changes fastest.
Arguments:
- query: bfloat16 [512, 1024], P('seq', 'exp'), may hold values from -6 to 6
- key_in: bfloat16 [512, 1024], P('seq', 'exp'), may hold values from -6 to 6
- value: bfloat16 [512, 1024], P('seq', 'exp'), may hold values from -6 to 6
- decay_log: float32 [512, 8], P('seq', 'exp'), may hold values from -1 to 0
- norm_gain: bfloat16 [1024], P('exp'), may hold values from 0.099609375 to 1.8984375
- w_out: bfloat16 [1024, 4096], P('exp'), may hold values from -0.1875 to 0.1875
- router: bfloat16 [4096, 4], replicated, may hold values from -0.09375 to 0.09375
- routes: int32 [512, 2], P('seq'), may hold values from 0 to 3, all different within a row; in each aligned block of 128 rows (0 to 127, 128 to 255, ...) at most 96 rows name the same one
- w_gate: bfloat16 [8, 4096, 288], P('exp'), may hold values from -0.09375 to 0.09375
- w_up: bfloat16 [8, 4096, 288], P('exp'), may hold values from -0.09375 to 0.09375
- w_down: bfloat16 [8, 288, 4096], P('exp'), may hold values from -0.25 to 0.25
Outputs:
- output: bfloat16 [512, 4096], P(('seq', 'exp'))
Inputs may be any that keep to these rules, and one draw needn't show every extreme that they name: `routes`: among the positions of one block of 128 positions no expert is named more than 96 times, a bound that some block reaches; a position names 2 different experts.
All inputs are finite; a program needn't handle non-finite values.
Results may differ from a plain program's by a relative error of at most 0.015.
Values may be sent and summed in bfloat16 or wider, within the bound.
No kernel may reach another device: no remote copies, remote signals or barrier semaphores. Data moves between devices by JAX's collectives and lax.ppermute only.
A program may use at most 64 MiB of HBM per device.

v0:
```python
import functools

import jax
import jax.numpy as jnp
from jax import lax
from jax.experimental import pallas as pl
from jax.experimental.pallas import tpu as pltpu
from jax.sharding import PartitionSpec as P

F32 = jnp.float32
BF16 = jnp.bfloat16
TILE_ROWS = 16
COLUMNS = 1024
PARTS = 2
VMEM_LIMIT = 16 * 1024 * 1024


def plain_plan(query, key_in, value, decay_log, norm_gain, w_out, router, routes, w_gate, w_up, w_down):
    tok_count = query.shape[0]
    head_count = decay_log.shape[1]
    head_size = query.shape[1] // head_count
    top_count = routes.shape[1]
    expert_count = router.shape[1]
    capacity = max(2, 3 * tok_count * top_count // (2 * expert_count))
    exp_count = lax.axis_size("exp")
    slice_count = exp_count // expert_count
    queries = query.reshape(tok_count, head_count, head_size)
    keys_local = key_in.reshape(tok_count, head_count, head_size)
    values_local = value.reshape(tok_count, head_count, head_size)
    cumulative = jnp.cumsum(decay_log, axis=0)
    scores = jnp.einsum("thd,shd->hts", queries, keys_local, preferred_element_type=jnp.float32)
    spread = cumulative.T[:, :, None] - cumulative.T[:, None, :]
    causal = jnp.arange(tok_count)[:, None] >= jnp.arange(tok_count)[None, :]
    weights = jnp.where(causal, jnp.exp(jnp.where(causal, spread, 0.0)), 0.0)
    attend = (scores * weights / head_size).astype(jnp.bfloat16)
    intra_part = jnp.einsum(
        "hts,she->the", attend, values_local, preferred_element_type=jnp.float32
    )
    totals = cumulative[-1]
    tail_decay = jnp.exp(totals[None, :] - cumulative)
    state_delta = jnp.einsum(
        "shd,she->hde",
        keys_local.astype(jnp.float32) * tail_decay[:, :, None],
        values_local.astype(jnp.float32),
        precision=lax.Precision.HIGHEST,
    )
    decay_rows = lax.all_gather(totals[None, :], "seq", axis=0, tiled=True)
    my_rank = lax.axis_index("seq")
    seq_ranks = jnp.arange(decay_rows.shape[0])
    state_piece = lax.all_gather(
        state_delta[None].astype(jnp.bfloat16), "seq", axis=0, tiled=True
    ).astype(jnp.float32)
    piece_rank = jnp.arange(state_piece.shape[0])
    between = (seq_ranks[None, :] > piece_rank[:, None]) & (seq_ranks[None, :] < my_rank)
    logsum = jnp.dot(between.astype(jnp.float32), decay_rows, precision=lax.Precision.HIGHEST)
    factor = jnp.where((piece_rank < my_rank)[:, None], jnp.exp(logsum), 0.0)
    incoming = jnp.zeros_like(state_delta) + jnp.einsum(
        "ih,ihde->hde", factor, state_piece, precision=lax.Precision.HIGHEST
    )
    inter_part = (
        jnp.exp(cumulative)[:, :, None]
        * jnp.einsum(
            "thd,hde->the", queries.astype(jnp.float32), incoming, precision=lax.Precision.HIGHEST
        )
        / head_size
    )
    attended = intra_part + inter_part
    inverse_rms = lax.rsqrt(jnp.mean(attended * attended, axis=-1, keepdims=True) + 1e-06)
    gain_f32 = norm_gain.astype(jnp.float32).reshape(head_count, head_size)
    normed = (
        (attended * inverse_rms * gain_f32)
        .astype(jnp.bfloat16)
        .reshape(tok_count, head_count * head_size)
    )
    own_mixed = lax.psum_scatter(
        jnp.dot(normed, w_out, preferred_element_type=jnp.float32),
        "exp",
        scatter_dimension=0,
        tiled=True,
    ).astype(jnp.bfloat16)
    mixed = lax.all_gather(own_mixed, "exp", axis=0, tiled=True)
    logits = jnp.dot(mixed, router, preferred_element_type=jnp.float32)
    member = routes[:, :, None] == jnp.arange(expert_count)[None, None, :]
    picked = jnp.sum(jnp.where(member, logits[:, None, :], 0.0), axis=-1)
    raised = jnp.exp(picked)
    gate_probs = raised / jnp.sum(raised, axis=-1, keepdims=True)
    my_expert = lax.axis_index("exp") // slice_count
    flat_hit = (routes.reshape(-1) == my_expert).astype(jnp.int32)
    slot_flat = jnp.cumsum(flat_hit) - flat_hit
    slot_match = (slot_flat[:, None] == jnp.arange(capacity)[None, :]) & (flat_hit[:, None] > 0)
    token_select = jnp.sum(
        slot_match.reshape(tok_count, top_count, capacity).astype(jnp.float32), axis=1
    )
    token_gate = jnp.sum(jnp.where(routes == my_expert, gate_probs, 0.0), axis=1)
    slot_rows = jnp.dot(
        token_select.astype(jnp.bfloat16).T, mixed, preferred_element_type=jnp.float32
    ).astype(jnp.bfloat16)
    gate_part = jnp.dot(slot_rows, w_gate[0], preferred_element_type=jnp.float32)
    up_part = jnp.dot(slot_rows, w_up[0], preferred_element_type=jnp.float32)
    hidden = (jax.nn.silu(gate_part) * up_part).astype(jnp.bfloat16)
    slice_out = jnp.dot(hidden, w_down[0], preferred_element_type=jnp.float32)
    spread_out = jnp.dot(token_select, slice_out, precision=lax.Precision.HIGHEST)
    summed = lax.psum_scatter(
        token_gate[:, None] * spread_out, "exp", scatter_dimension=0, tiled=True
    )
    return (own_mixed.astype(jnp.float32) + summed).astype(jnp.bfloat16)


def iota2(shape, axis):
    return lax.broadcasted_iota(jnp.int32, shape, axis)


def cumulate(decay_row):
    t = decay_row.shape[1]
    row, col = iota2((t, t), 0), iota2((t, t), 1)
    spread = jnp.broadcast_to(decay_row, (t, t))
    column = jnp.sum(jnp.where(col <= row, spread, 0.0), axis=1, keepdims=True)
    own = jnp.sum(jnp.where(col == row, spread, 0.0), axis=1, keepdims=True)
    line = jnp.sum(jnp.where(row <= col, own, 0.0), axis=0, keepdims=True)
    return column, line


def dot_f32(a, b, dims):
    return lax.dot_general(a, b, (dims, ((), ())), preferred_element_type=F32)


def split_dot(a_f32, b, dims):
    high = a_f32.astype(BF16)
    low = (a_f32 - high.astype(F32)).astype(BF16)
    return dot_f32(high, b, dims) + dot_f32(low, b, dims)


def dma_in(sems, pairs):
    copies = [pltpu.make_async_copy(a, b, sems.at[i]) for i, (a, b) in enumerate(pairs)]
    for copy in copies:
        copy.start()
    return copies


def put_state(out_ref, state, total):
    d = state.shape[1]
    out_ref[0:d, :] = state.astype(BF16)
    wide = jnp.broadcast_to(total, (TILE_ROWS, d))
    part0 = wide.astype(BF16).astype(F32)
    part1 = (wide - part0).astype(BF16).astype(F32)
    part2 = wide - part0 - part1
    row = iota2((TILE_ROWS, d), 0)
    parts = jnp.where(row == 0, part0, jnp.where(row == 1, part1, jnp.where(row == 2, part2, 0.0)))
    out_ref[d:, :] = parts.astype(BF16)


def get_state(ref):
    d = ref.shape[1]
    return ref[0:d, :].astype(F32), jnp.sum(ref[d:, :].astype(F32), axis=0, keepdims=True)


def state_kernel(key_hbm, value_hbm, decay_hbm, out_ref, key_ref, value_ref, decay_ref, sems):
    t, d = key_ref.shape
    copies = dma_in(sems, [(decay_hbm, decay_ref), (key_hbm, key_ref), (value_hbm, value_ref)])
    for copy in copies:
        copy.wait()
    column, _ = cumulate(decay_ref[...])
    total = column[t - 1 :, :]
    keyed = key_ref[...].astype(F32) * jnp.exp(total - column)
    put_state(out_ref, split_dot(keyed, value_ref[...], ((0,), (0,))), jnp.broadcast_to(total, (1, d)))


def within_kernel(
    query_hbm, key_hbm, value_hbm, decay_hbm, gain_hbm, w_out_hbm, _,
    intra_ref, grown_ref, query_ref, gain_ref, w_out_ref,
    key_ref, value_ref, decay_ref, gain_in_ref, sems,
):
    t, d = query_ref.shape
    copies = dma_in(
        sems,
        [
            (decay_hbm, decay_ref),
            (query_hbm, query_ref),
            (key_hbm, key_ref),
            (value_hbm, value_ref),
            (gain_hbm, gain_in_ref),
            (w_out_hbm, w_out_ref),
        ],
    )
    for copy in copies[:5]:
        copy.wait()
    column, line = cumulate(decay_ref[...])
    query, key, value = query_ref[...], key_ref[...], value_ref[...]
    scores = dot_f32(query, key, ((1,), (1,)))
    causal = iota2((t, t), 0) >= iota2((t, t), 1)
    weights = jnp.where(causal, jnp.exp(jnp.where(causal, column - line, 0.0)), 0.0)
    attend = (scores * weights * (1.0 / d)).astype(BF16)
    intra_ref[...] = dot_f32(attend, value, ((1,), (0,)))
    grown_ref[...] = jnp.broadcast_to(jnp.exp(column) * (1.0 / d), (t, d))
    gain_ref[...] = jnp.broadcast_to(gain_in_ref[...].astype(F32), gain_ref.shape)
    copies[5].wait()


def place_matrix(rows, n_pair, pair, core):
    size = 2 * n_pair * rows
    i, j = iota2((size, size), 0), iota2((size, size), 1)
    half, inner = i // (n_pair * rows), i % (n_pair * rows)
    who = (inner // rows + pair) % n_pair
    source = (2 * who + (core + half) % 2) * rows + inner % rows
    return jnp.where(source == j, 1.0, 0.0).astype(BF16)


def fetch_kernel(
    n_pair, router_hbm, routes_hbm, gate_hbm, up_hbm, down_hbm, _,
    in_ref, down_ref, member_ref, router_ref, routes_ref, sems,
):
    hid = gate_hbm.shape[0]
    copies = dma_in(
        sems,
        [
            (router_hbm, router_ref),
            (routes_hbm, routes_ref),
            (gate_hbm, in_ref.at[0:hid]),
            (up_hbm, in_ref.at[hid : 2 * hid]),
            (down_hbm, down_ref),
        ],
    )
    for copy in copies[:2]:
        copy.wait()
    experts, t = router_ref.shape[0], routes_ref.shape[1]
    rows = t // (2 * n_pair)
    in_ref[2 * hid :, :] = jnp.zeros((TILE_ROWS, in_ref.shape[1]), BF16)
    in_ref[2 * hid : 2 * hid + experts, :] = router_ref[...]
    padded = member_ref.shape[0]
    hits = jnp.zeros((padded, t), F32)
    for k in range(routes_ref.shape[0]):
        hits = hits + jnp.where(routes_ref[k : k + 1, :] == iota2((padded, t), 0), 1.0, 0.0)
    exp_index = lax.axis_index("exp")
    place = place_matrix(rows, n_pair, exp_index // 2, exp_index % 2)
    member_ref[...] = dot_f32(hits.astype(BF16), place, ((1,), (1,)))
    for copy in copies[2:]:
        copy.wait()


def normed_kernel(n_pair, moves, *refs):
    states = refs[: len(moves)]
    intra_ref, grown_ref, query_ref, gain_ref, out_ref = refs[len(moves) :]
    t, d = query_ref.shape
    me = lax.axis_index("seq")
    ranks = [move(me) for move in moves]
    parts = [get_state(ref) for ref in states]
    incoming = jnp.zeros((d, d), F32)
    for rank, (state, _) in zip(ranks, parts):
        logsum = jnp.zeros((1, d), F32)
        for other, (_, total) in zip(ranks, parts):
            logsum = logsum + jnp.where(jnp.logical_and(rank < other, other < me), total, 0.0)
        incoming = incoming + jnp.where(rank < me, jnp.exp(logsum), 0.0) * state
    high = incoming.astype(BF16)
    low = (incoming - high.astype(F32)).astype(BF16)
    query = query_ref[...]
    read = dot_f32(query, high, ((1,), (0,))) + dot_f32(query, low, ((1,), (0,)))
    attended = intra_ref[...] + grown_ref[...] * read
    inverse = lax.rsqrt(jnp.mean(attended * attended, axis=1, keepdims=True) + 1e-06)
    normed = (attended * inverse * gain_ref[0:1, :]).astype(BF16)
    exp_index = lax.axis_index("exp")
    place = place_matrix(t // (2 * n_pair), n_pair, exp_index // 2, exp_index % 2)
    out_ref[...] = dot_f32(place, normed, ((1,), (0,))).astype(BF16)


def product_kernel(at, x_ref, w_ref, mine_ref, theirs_ref):
    half = mine_ref.shape[0]
    for i in range(at.start, at.stop, COLUMNS):
        part = dot_f32(x_ref[...], w_ref[:, i : i + COLUMNS], ((1,), (0,))).astype(BF16)
        mine_ref[:, i - at.start : i - at.start + COLUMNS] = part[:half]
        theirs_ref[:, i - at.start : i - at.start + COLUMNS] = part[half:]


def add_kernel(groups, a_ref, b_ref, *refs):
    outs = refs[-len(groups) :]
    rows = outs[0].shape[0] // len(groups[0])
    for group, ref in zip(groups, outs):
        for i, block in enumerate(group):
            at = slice(block * rows, (block + 1) * rows)
            total = a_ref[at, :].astype(F32) + b_ref[at, :].astype(F32)
            ref[i * rows : (i + 1) * rows, :] = total.astype(ref.dtype)


def sum_kernel(count, *refs):
    total = refs[0][...].astype(F32)
    for ref in refs[1:count]:
        total = total + ref[...].astype(F32)
    refs[-1][...] = total.astype(BF16)


def join_kernel(*refs):
    start = 0
    for ref in refs[:-1]:
        refs[-1][start : start + ref.shape[0], :] = ref[...]
        start += ref.shape[0]


def enter_part(at, in_ref, own_ref, other_ref):
    x = jnp.concatenate([own_ref[...], other_ref[...]], axis=0)
    return dot_f32(in_ref[:, at], x, ((1,), (1,)))


def enter_kernel(at, in_ref, own_ref, other_ref, out_ref):
    out_ref[...] = enter_part(at, in_ref, own_ref, other_ref)


def hidden_kernel(at, slices, experts, in_ref, own_ref, other_ref, before_ref, member_ref, out_ref):
    total = before_ref[...] + enter_part(at, in_ref, own_ref, other_ref)
    t, hid = out_ref.shape
    gate, up, logits = total[0:hid], total[hid : 2 * hid], total[2 * hid : 2 * hid + experts]
    raised = jnp.where(member_ref[0:experts, :] > 0.5, jnp.exp(logits), 0.0)
    mine = iota2((experts, t), 0) == lax.axis_index("exp") // slices
    prob = jnp.sum(jnp.where(mine, raised, 0.0), axis=0, keepdims=True) / jnp.sum(raised, axis=0, keepdims=True)
    out_ref[...] = (gate / (1.0 + jnp.exp(-gate)) * up * prob).T.astype(BF16)


def result_kernel(count, *refs):
    out_ref = refs[-1]
    width = refs[0].shape[1]
    for i in range(len(refs) // count):
        total = refs[i * count][...].astype(F32)
        for ref in refs[i * count + 1 : (i + 1) * count]:
            total = total + ref[...].astype(F32)
        out_ref[:, i * width : (i + 1) * width] = total.astype(BF16)


def call(kernel, outs, args, scratch=(), far=0):
    whole = pl.BlockSpec(memory_space=pltpu.VMEM)
    if far:
        args = [pltpu.with_memory_space_constraint(a, pltpu.HBM) for a in args[:far]] + list(args[far:])
    return pl.pallas_call(
        kernel,
        out_shape=outs,
        in_specs=[pl.BlockSpec(memory_space=pl.ANY) if far else whole] * len(args),
        out_specs=[whole] * len(outs),
        scratch_shapes=list(scratch),
        compiler_params=pltpu.CompilerParams(vmem_limit_bytes=VMEM_LIMIT),
        cost_estimate=pl.CostEstimate(flops=0, bytes_accessed=0, transcendentals=0),
    )(*args)


def local(query, key_in, value, decay_log, norm_gain, w_out, router, routes, w_gate, w_up, w_down):
    t, d = query.shape
    width = w_out.shape[1]
    exp_count, seq_count = lax.axis_size("exp"), lax.axis_size("seq")
    n_pair = exp_count // 2
    rows = t // exp_count
    experts = router.shape[1]
    slices = exp_count // experts
    hid = w_gate.shape[2]
    out = jax.ShapeDtypeStruct
    dma = pltpu.SemaphoreType.DMA

    def shift(x, r):
        return lax.ppermute(x, "exp", [(e, (e + 2 * r) % exp_count) for e in range(exp_count)])

    def across(x):
        return lax.ppermute(x, "exp", [(e, e ^ 1) for e in range(exp_count)])

    size = width // PARTS
    ranges = [slice(i * size, (i + 1) * size) for i in range(PARTS)]

    def rows_of(count):
        return out((count * rows, size), BF16)

    def reduce(products):
        others = [across(theirs) for _, theirs in products]
        terms = [
            call(functools.partial(add_kernel, [[r] for r in range(n_pair)]), [rows_of(1)] * n_pair, (mine, other))
            for (mine, _), other in zip(products, others)
        ]
        return [[term[0]] + [shift(term[r], r) for r in range(1, n_pair)] for term in terms], terms[-1][-1]

    def products_of(x, w):
        return [call(functools.partial(product_kernel, at), [rows_of(n_pair)] * 2, (x, w)) for at in ranges]

    decay_row = decay_log.T
    block = pltpu.VMEM((t, d), BF16)
    decay_block = pltpu.VMEM((1, t), F32)
    (state,) = call(
        state_kernel,
        [out((d + TILE_ROWS, d), BF16)],
        (key_in, value, decay_row),
        [block, block, decay_block, dma((3,))],
        far=3,
    )
    moves = [lambda i, k=k: i ^ k for k in range(1, seq_count)]
    states = [lax.ppermute(state, "seq", [(move(i), i) for i in range(seq_count)]) for move in moves]
    intra, grown, query_near, gain, w_out_near = call(
        within_kernel,
        [out((t, d), F32), out((t, d), F32), out((t, d), BF16), out((8, d), F32), out(w_out.shape, BF16)],
        (query, key_in, value, decay_row, norm_gain[None, :], w_out, state),
        [block, block, decay_block, pltpu.VMEM((1, d), BF16), dma((6,))],
        far=6,
    )
    (normed,) = call(
        functools.partial(normed_kernel, n_pair, moves),
        [out((t, d), BF16)],
        (*states, intra, grown, query_near, gain),
    )
    terms, last = reduce(products_of(normed, w_out_near))
    w_in, w_down_near, member = call(
        functools.partial(fetch_kernel, n_pair),
        [
            out((2 * hid + TILE_ROWS, width), BF16),
            out((hid, width), BF16),
            out((-(-experts // 8) * 8, t), F32),
        ],
        (router.T, routes.T, w_gate[0].T, w_up[0].T, w_down[0], last),
        [pltpu.VMEM((experts, width), BF16), pltpu.VMEM((routes.shape[1], t), jnp.int32), dma((5,))],
        far=5,
    )
    mixed = [call(functools.partial(sum_kernel, n_pair), [rows_of(1)], (*term, member))[0] for term in terms]
    gathered = [[shift(m, -r) if r else m for r in range(n_pair)] for m in mixed]
    own = [call(join_kernel, [rows_of(n_pair)], blocks)[0] for blocks in gathered]
    total = ()
    for at, x in zip(ranges, own):
        if at.stop < width:
            kernel, shape = functools.partial(enter_kernel, at), out((w_in.shape[0], t), F32)
        else:
            kernel, shape = functools.partial(hidden_kernel, at, slices, experts), out((t, hid), BF16)
            total = (*total, member)
        total = call(kernel, [shape], (w_in, x, across(x), *total))
    sums, _ = reduce(products_of(total[0], w_down_near))
    args = [x for some, m in zip(sums, mixed) for x in (*some, m)]
    return call(functools.partial(result_kernel, n_pair + 1), [out((rows, width), BF16)], args)[0]


def solution(mesh):
    placed = (
        P("seq", "exp"),
        P("seq", "exp"),
        P("seq", "exp"),
        P("seq", "exp"),
        P("exp"),
        P("exp", None),
        P(),
        P("seq", None),
        P("exp", None, None),
        P("exp", None, None),
        P("exp", None, None),
    )

    def pick(query, key_in, value, decay_log, *rest):
        rows = query.shape[0] // lax.axis_size("exp")
        exp_count = lax.axis_size("exp")
        tiled = rows % TILE_ROWS == 0 and decay_log.shape[1] == 1
        for count in (exp_count, lax.axis_size("seq")):
            tiled = tiled and count >= 4 and count & (count - 1) == 0
        plan = local if tiled else plain_plan
        return plan(query, key_in, value, decay_log, *rest)

    return jax.shard_map(
        pick, mesh=mesh, in_specs=placed, out_specs=P(("seq", "exp"), None), check_vma=False
    )
```

profile of v0, /device:TPU:0, one launch (start us, length us, event | category | flops | bytes accessed | tf_op | source)
XLA Modules:
  0.0 59.5 jit_solution(13740089164415353879)
XLA Ops:
  0.0 1.1 %shard_map.109._ = bf16[144,128]{1,0:T(8,128)(2,1)S(1)} custom-call(bf16[128,128]{1,0:T(8,128)(2,1)} %key_hbm.3, bf16[128,128]{1,0:T(8,128)(2,1)} %value_hbm.3, f32[1,128]{1,0:T(1,128)} %bitcast.15), custom_call_target="tpu_custom_call" | custom-call | tf_op jit(solution)/shard_map/pallas_call | solution.py:330
  1.1 4.0 %collective-permute-start.2 = (bf16[144,128]{1,0:T(8,128)(2,1)S(1)}, bf16[144,128]{1,0:T(8,128)(2,1)S(1)}, u32[]{:S(2)}, u32[]{:S(2)}) collective-permute-start(bf16[144,128]{1,0:T(8,128)(2,1)S(1)} %shard_map.109._), channel_id=1, source_target_pairs={{24,0},{16,8},{8,16},{0,24},{25,1},{17,9},{9,17},{1,25},{26,2},{18... | collective-permute-start | bytes 110600 | tf_op jit(solution)/shard_map/ppermute | solution.py:387
  5.1 0.5 collective-permute-start.1
  5.6 0.1 collective-permute-start
  5.7 1.4 %shard_map.110 = (f32[128,128]{1,0:T(8,128)S(1)}, f32[128,128]{1,0:T(8,128)S(1)}, bf16[128,128]{1,0:T(8,128)(2,1)S(1)}, f32[8,128]{1,0:T(8,128)S(1)}, bf16[128,4096]{1,0:T(8,128)(2,1)S(1)}) custom-call(bf16[128,128]{1,0:T(8,128)(2,1)} %query_hbm.1, bf16[128,128]{1,0:T(8,128)(2,1)} %key_hbm.3, bf16[128,128]{1,0:T(8,128)(2,1)} %value_hbm.3, ...), custom_call_target="tpu_custom_call" | custom-call | tf_op jit(solution)/shard_map/pallas_call | solution.py:330
  7.1 1.9 %collective-permute-done.1.refs_1_ = bf16[144,128]{1,0:T(8,128)(2,1)S(1)} collective-permute-done((bf16[144,128]{1,0:T(8,128)(2,1)S(1)}, bf16[144,128]{1,0:T(8,128)(2,1)S(1)}, u32[]{:S(2)}, u32[]{:S(2)}) %collective-permute-start.1) | collective-permute-done | bytes 36896 | tf_op jit(solution)/shard_map/ppermute | solution.py:387
  9.0 0.5 collective-permute-done.refs_0_
  9.5 0.4 shard_map.111.x_ref
  10.0 0.3 shard_map.117
  10.3 0.1 collective-permute-start.11
  10.3 0.3 shard_map.112
  10.6 0.6 collective-permute-start.3
  11.2 0.7 %collective-permute-done.11.b_ref = bf16[64,2048]{1,0:T(8,128)(2,1)S(1)} collective-permute-done((bf16[64,2048]{1,0:T(8,128)(2,1)S(1)}, bf16[64,2048]{1,0:T(8,128)(2,1)S(1)}, u32[]{:S(2)}, u32[]{:S(2)}) %collective-permute-start.11) | collective-permute-done | bytes 262176 | tf_op jit(solution)/shard_map/ppermute | solution.py:357
  11.9 1.6 %collective-permute-start.12 = (bf16[16,2048]{1,0:T(8,128)(2,1)S(1)}, bf16[16,2048]{1,0:T(8,128)(2,1)S(1)}, u32[]{:S(2)}, u32[]{:S(2)}) collective-permute-start(bf16[16,2048]{1,0:T(8,128)(2,1)S(1)} %get-tuple-element.53), channel_id=1, source_target_pairs={{0,2},{1,3},{2,4},{3,5},{4,6},{5,7},{6,0},{7,1},{8,10},{9,11},{10,... | collective-permute-start | bytes 196616 | tf_op jit(solution)/shard_map/ppermute | solution.py:354
  13.5 2.6 %collective-permute-start.13 = (bf16[16,2048]{1,0:T(8,128)(2,1)S(1)}, bf16[16,2048]{1,0:T(8,128)(2,1)S(1)}, u32[]{:S(2)}, u32[]{:S(2)}) collective-permute-start(bf16[16,2048]{1,0:T(8,128)(2,1)S(1)} %get-tuple-element.54), channel_id=1, source_target_pairs={{0,4},{1,5},{2,6},{3,7},{4,0},{5,1},{6,2},{7,3},{8,12},{9,13},{10,... | collective-permute-start | bytes 196616 | tf_op jit(solution)/shard_map/ppermute | solution.py:354
  16.1 1.3 %collective-permute-start.14 = (bf16[16,2048]{1,0:T(8,128)(2,1)S(1)}, bf16[16,2048]{1,0:T(8,128)(2,1)S(1)}, u32[]{:S(2)}, u32[]{:S(2)}) collective-permute-start(bf16[16,2048]{1,0:T(8,128)(2,1)S(1)} %get-tuple-element.55), channel_id=1, source_target_pairs={{0,6},{1,7},{2,0},{3,1},{4,2},{5,3},{6,4},{7,5},{8,14},{9,15},{10,... | collective-permute-start | bytes 196616 | tf_op jit(solution)/shard_map/ppermute | solution.py:354
  17.6 0.7 %collective-permute-start.4 = (bf16[16,2048]{1,0:T(8,128)(2,1)S(1)}, bf16[16,2048]{1,0:T(8,128)(2,1)S(1)}, u32[]{:S(2)}, u32[]{:S(2)}) collective-permute-start(bf16[16,2048]{1,0:T(8,128)(2,1)S(1)} %get-tuple-element.47), channel_id=1, source_target_pairs={{0,2},{1,3},{2,4},{3,5},{4,6},{5,7},{6,0},{7,1},{8,10},{9,11},{10,... | collective-permute-start | bytes 196616 | tf_op jit(solution)/shard_map/ppermute | solution.py:354
  18.3 3.1 %collective-permute-start.6 = (bf16[16,2048]{1,0:T(8,128)(2,1)S(1)}, bf16[16,2048]{1,0:T(8,128)(2,1)S(1)}, u32[]{:S(2)}, u32[]{:S(2)}) collective-permute-start(bf16[16,2048]{1,0:T(8,128)(2,1)S(1)} %get-tuple-element.44._), channel_id=1, source_target_pairs={{0,6},{1,7},{2,0},{3,1},{4,2},{5,3},{6,4},{7,5},{8,14},{9,15},{10,... | collective-permute-start | bytes 196616 | tf_op jit(solution)/shard_map/ppermute | solution.py:354
  21.4 3.2 %shard_map.114 = (bf16[592,4096]{1,0:T(8,128)(2,1)S(1)}, bf16[288,4096]{1,0:T(8,128)(2,1)S(1)}, f32[8,128]{1,0:T(8,128)S(1)}) custom-call(bf16[4,4096]{1,0:T(4,128)(2,1)} %bitcast.14, s32[2,128]{1,0:T(2,128)} %bitcast.17, bf16[288,4096]{1,0:T(8,128)(2,1)} %bitcast.11, bf16[288,4096]{1,0:T(8,128)(2,1)} %bitcast.12, bf16[288,4096]{1,0:T(8,128)(2,1)} %bitcast.13, ...), custom_call_target="tpu_custom_call" | custom-call | tf_op jit(solution)/shard_map/pallas_call | solution.py:330
  24.6 0.1 collective-permute-start.5
  24.8 0.6 collective-permute-start.17
  25.3 2.4 %collective-permute-start.16 = (bf16[16,2048]{1,0:T(8,128)(2,1)S(1)}, bf16[16,2048]{1,0:T(8,128)(2,1)S(1)}, u32[]{:S(2)}, u32[]{:S(2)}) collective-permute-start(bf16[16,2048]{1,0:T(8,128)(2,1)S(1)} %shard_map.119.refs_0_.refs_4_), channel_id=1, source_target_pairs={{0,4},{1,5},{2,6},{3,7},{4,0},{5,1},{6,2},{7,3},{8,12},{9,13},{10,... | collective-permute-start | bytes 196616 | tf_op jit(solution)/shard_map/ppermute | solution.py:354
  27.8 2.8 %collective-permute-start.15 = (bf16[16,2048]{1,0:T(8,128)(2,1)S(1)}, bf16[16,2048]{1,0:T(8,128)(2,1)S(1)}, u32[]{:S(2)}, u32[]{:S(2)}) collective-permute-start(bf16[16,2048]{1,0:T(8,128)(2,1)S(1)} %shard_map.119.refs_0_.refs_4_), channel_id=1, source_target_pairs={{0,6},{1,7},{2,0},{3,1},{4,2},{5,3},{6,4},{7,5},{8,14},{9,15},{10,... | collective-permute-start | bytes 196616 | tf_op jit(solution)/shard_map/ppermute | solution.py:354
  30.6 1.4 %collective-permute-done.5.refs_2_ = bf16[16,2048]{1,0:T(8,128)(2,1)S(1)} collective-permute-done((bf16[16,2048]{1,0:T(8,128)(2,1)S(1)}, bf16[16,2048]{1,0:T(8,128)(2,1)S(1)}, u32[]{:S(2)}, u32[]{:S(2)}) %collective-permute-start.5) | collective-permute-done | bytes 65568 | tf_op jit(solution)/shard_map/ppermute | solution.py:354
  32.1 0.1 collective-permute-start.8
  32.2 3.7 %collective-permute-start.7 = (bf16[16,2048]{1,0:T(8,128)(2,1)S(1)}, bf16[16,2048]{1,0:T(8,128)(2,1)S(1)}, u32[]{:S(2)}, u32[]{:S(2)}) collective-permute-start(bf16[16,2048]{1,0:T(8,128)(2,1)S(1)} %shard_map.115.refs_0_.refs_9_), channel_id=1, source_target_pairs={{0,6},{1,7},{2,0},{3,1},{4,2},{5,3},{6,4},{7,5},{8,14},{9,15},{10,... | collective-permute-start | bytes 196616 | tf_op jit(solution)/shard_map/ppermute | solution.py:354
  36.0 0.1 collective-permute-start.18
  36.0 2.2 %collective-permute-done.9.refs_3_ = bf16[16,2048]{1,0:T(8,128)(2,1)S(1)} collective-permute-done((bf16[16,2048]{1,0:T(8,128)(2,1)S(1)}, bf16[16,2048]{1,0:T(8,128)(2,1)S(1)}, u32[]{:S(2)}, u32[]{:S(2)}) %collective-permute-start.9) | collective-permute-done | bytes 65568 | tf_op jit(solution)/shard_map/ppermute | solution.py:354
  38.3 1.2 %collective-permute-done.8.refs_2_ = bf16[16,2048]{1,0:T(8,128)(2,1)S(1)} collective-permute-done((bf16[16,2048]{1,0:T(8,128)(2,1)S(1)}, bf16[16,2048]{1,0:T(8,128)(2,1)S(1)}, u32[]{:S(2)}, u32[]{:S(2)}) %collective-permute-start.8) | collective-permute-done | bytes 65568 | tf_op jit(solution)/shard_map/ppermute | solution.py:354
  39.7 0.8 %shard_map.121.before_ref = f32[592,128]{1,0:T(8,128)S(1)} custom-call(bf16[592,4096]{1,0:T(8,128)(2,1)S(1)} %get-tuple-element.45.in_ref, bf16[64,2048]{1,0:T(8,128)(2,1)S(1)} %shard_map.120.own_ref, bf16[64,2048]{1,0:T(8,128)(2,1)S(1)} %collective-permute-done.18.other_ref), custom_call_target="tpu_custom_call" | custom-call | tf_op jit(solution)/shard_map/pallas_call | solution.py:330
  40.5 0.7 %collective-permute-done.10.other_ref = bf16[64,2048]{1,0:T(8,128)(2,1)S(1)} collective-permute-done((bf16[64,2048]{1,0:T(8,128)(2,1)S(1)}, bf16[64,2048]{1,0:T(8,128)(2,1)S(1)}, u32[]{:S(2)}, u32[]{:S(2)}) %collective-permute-start.10) | collective-permute-done | bytes 262176 | tf_op jit(solution)/shard_map/ppermute | solution.py:357
  41.2 0.9 %shard_map.122.x_ref = bf16[128,288]{1,0:T(8,128)(2,1)S(1)} custom-call(bf16[592,4096]{1,0:T(8,128)(2,1)S(1)} %get-tuple-element.45.in_ref, bf16[64,2048]{1,0:T(8,128)(2,1)S(1)} %shard_map.116.own_ref, bf16[64,2048]{1,0:T(8,128)(2,1)S(1)} %collective-permute-done.10.other_ref, f32[592,128]{1,0:T(8,128)S(1)} %shard_map.121.before_ref, ...), custom_call_target="tpu_custom_call" | custom-call | tf_op jit(solution)/shard_map/pallas_call | solution.py:330
  42.1 0.4 shard_map.125
  42.6 0.2 collective-permute-start.23
  42.8 0.4 shard_map.123
  43.2 0.4 collective-permute-start.19
  43.6 0.5 collective-permute-done.23.b_ref
  44.2 1.3 %collective-permute-start.24 = (bf16[16,2048]{1,0:T(8,128)(2,1)S(1)}, bf16[16,2048]{1,0:T(8,128)(2,1)S(1)}, u32[]{:S(2)}, u32[]{:S(2)}) collective-permute-start(bf16[16,2048]{1,0:T(8,128)(2,1)S(1)} %get-tuple-element.66), channel_id=1, source_target_pairs={{0,2},{1,3},{2,4},{3,5},{4,6},{5,7},{6,0},{7,1},{8,10},{9,11},{10,... | collective-permute-start | bytes 196616 | tf_op jit(solution)/shard_map/ppermute | solution.py:354
  45.5 1.8 %collective-permute-start.25 = (bf16[16,2048]{1,0:T(8,128)(2,1)S(1)}, bf16[16,2048]{1,0:T(8,128)(2,1)S(1)}, u32[]{:S(2)}, u32[]{:S(2)}) collective-permute-start(bf16[16,2048]{1,0:T(8,128)(2,1)S(1)} %get-tuple-element.67), channel_id=1, source_target_pairs={{0,4},{1,5},{2,6},{3,7},{4,0},{5,1},{6,2},{7,3},{8,12},{9,13},{10,... | collective-permute-start | bytes 196616 | tf_op jit(solution)/shard_map/ppermute | solution.py:354
  47.3 0.8 %collective-permute-start.26 = (bf16[16,2048]{1,0:T(8,128)(2,1)S(1)}, bf16[16,2048]{1,0:T(8,128)(2,1)S(1)}, u32[]{:S(2)}, u32[]{:S(2)}) collective-permute-start(bf16[16,2048]{1,0:T(8,128)(2,1)S(1)} %get-tuple-element.68), channel_id=1, source_target_pairs={{0,6},{1,7},{2,0},{3,1},{4,2},{5,3},{6,4},{7,5},{8,14},{9,15},{10,... | collective-permute-start | bytes 196616 | tf_op jit(solution)/shard_map/ppermute | solution.py:354
  48.2 1.3 %collective-permute-start.20 = (bf16[16,2048]{1,0:T(8,128)(2,1)S(1)}, bf16[16,2048]{1,0:T(8,128)(2,1)S(1)}, u32[]{:S(2)}, u32[]{:S(2)}) collective-permute-start(bf16[16,2048]{1,0:T(8,128)(2,1)S(1)} %get-tuple-element.60), channel_id=1, source_target_pairs={{0,2},{1,3},{2,4},{3,5},{4,6},{5,7},{6,0},{7,1},{8,10},{9,11},{10,... | collective-permute-start | bytes 196616 | tf_op jit(solution)/shard_map/ppermute | solution.py:354
  49.4 1.2 %collective-permute-start.21 = (bf16[16,2048]{1,0:T(8,128)(2,1)S(1)}, bf16[16,2048]{1,0:T(8,128)(2,1)S(1)}, u32[]{:S(2)}, u32[]{:S(2)}) collective-permute-start(bf16[16,2048]{1,0:T(8,128)(2,1)S(1)} %get-tuple-element.61), channel_id=1, source_target_pairs={{0,4},{1,5},{2,6},{3,7},{4,0},{5,1},{6,2},{7,3},{8,12},{9,13},{10,... | collective-permute-start | bytes 196616 | tf_op jit(solution)/shard_map/ppermute | solution.py:354
  50.6 0.5 collective-permute-done.24.refs_6_
  51.1 2.1 %collective-permute-start.22 = (bf16[16,2048]{1,0:T(8,128)(2,1)S(1)}, bf16[16,2048]{1,0:T(8,128)(2,1)S(1)}, u32[]{:S(2)}, u32[]{:S(2)}) collective-permute-start(bf16[16,2048]{1,0:T(8,128)(2,1)S(1)} %get-tuple-element.62), channel_id=1, source_target_pairs={{0,6},{1,7},{2,0},{3,1},{4,2},{5,3},{6,4},{7,5},{8,14},{9,15},{10,... | collective-permute-start | bytes 196616 | tf_op jit(solution)/shard_map/ppermute | solution.py:354
  53.2 2.0 %collective-permute-done.25.refs_7_ = bf16[16,2048]{1,0:T(8,128)(2,1)S(1)} collective-permute-done((bf16[16,2048]{1,0:T(8,128)(2,1)S(1)}, bf16[16,2048]{1,0:T(8,128)(2,1)S(1)}, u32[]{:S(2)}, u32[]{:S(2)}) %collective-permute-start.25) | collective-permute-done | bytes 65568 | tf_op jit(solution)/shard_map/ppermute | solution.py:354
  55.2 0.1 collective-permute-done.20.refs_1_
  55.3 3.5 %collective-permute-done.21.refs_2_ = bf16[16,2048]{1,0:T(8,128)(2,1)S(1)} collective-permute-done((bf16[16,2048]{1,0:T(8,128)(2,1)S(1)}, bf16[16,2048]{1,0:T(8,128)(2,1)S(1)}, u32[]{:S(2)}, u32[]{:S(2)}) %collective-permute-start.21) | collective-permute-done | bytes 65568 | tf_op jit(solution)/shard_map/ppermute | solution.py:354
  58.7 0.7 %shard_map.127 = bf16[16,4096]{1,0:T(8,128)(2,1)} custom-call(bf16[16,2048]{1,0:T(8,128)(2,1)S(1)} %get-tuple-element.59.refs_0_, bf16[16,2048]{1,0:T(8,128)(2,1)S(1)} %collective-permute-done.20.refs_1_, bf16[16,2048]{1,0:T(8,128)(2,1)S(1)} %collective-permute-done.21.refs_2_, bf16[16,2048]{1,0:T(8,128)(2,1)S(1)} %collective-permute-done.22.refs_3_, ...), custom_call_target="tpu_custom_call" | custom-call | tf_op jit(solution)/shard_map/pallas_call | solution.py:330
  (25 shorter events, 0.5 us)
Async XLA Ops:
  1.1 6.0 %collective-permute-start.2 = (bf16[144,128]{1,0:T(8,128)(2,1)S(1)}, bf16[144,128]{1,0:T(8,128)(2,1)S(1)}, u32[]{:S(2)}, u32[]{:S(2)}) collective-permute-start(bf16[144,128]{1,0:T(8,128)(2,1)S(1)} %shard_map.109._), channel_id=1, source_target_pairs={{24,0},{16,8},{8,16},{0,24},{25,1},{17,9},{9,17},{1,25},{26,2},{18... | collective-permute-start | bytes 110600 | tf_op jit(solution)/shard_map/ppermute | solution.py:387
  5.1 4.0 %collective-permute-start.1 = (bf16[144,128]{1,0:T(8,128)(2,1)S(1)}, bf16[144,128]{1,0:T(8,128)(2,1)S(1)}, u32[]{:S(2)}, u32[]{:S(2)}) collective-permute-start(bf16[144,128]{1,0:T(8,128)(2,1)S(1)} %shard_map.109._), channel_id=1, source_target_pairs={{16,0},{24,8},{0,16},{8,24},{17,1},{25,9},{1,17},{9,25},{18,2},{26... | collective-permute-start | bytes 110600 | tf_op jit(solution)/shard_map/ppermute | solution.py:387
  5.6 4.0 %collective-permute-start = (bf16[144,128]{1,0:T(8,128)(2,1)S(1)}, bf16[144,128]{1,0:T(8,128)(2,1)S(1)}, u32[]{:S(2)}, u32[]{:S(2)}) collective-permute-start(bf16[144,128]{1,0:T(8,128)(2,1)S(1)} %shard_map.109._), channel_id=1, source_target_pairs={{8,0},{0,8},{24,16},{16,24},{9,1},{1,9},{25,17},{17,25},{10,2},{2,... | collective-permute-start | bytes 110600 | tf_op jit(solution)/shard_map/ppermute | solution.py:387
  10.3 1.6 %collective-permute-start.11 = (bf16[64,2048]{1,0:T(8,128)(2,1)S(1)}, bf16[64,2048]{1,0:T(8,128)(2,1)S(1)}, u32[]{:S(2)}, u32[]{:S(2)}) collective-permute-start(bf16[64,2048]{1,0:T(8,128)(2,1)S(1)} %get-tuple-element.51), channel_id=1, source_target_pairs={{0,1},{1,0},{2,3},{3,2},{4,5},{5,4},{6,7},{7,6},{8,9},{9,8},{10,11... | collective-permute-start | bytes 786440 | tf_op jit(solution)/shard_map/ppermute | solution.py:357
  10.6 6.9 %collective-permute-start.3 = (bf16[64,2048]{1,0:T(8,128)(2,1)S(1)}, bf16[64,2048]{1,0:T(8,128)(2,1)S(1)}, u32[]{:S(2)}, u32[]{:S(2)}) collective-permute-start(bf16[64,2048]{1,0:T(8,128)(2,1)S(1)} %get-tuple-element.43), channel_id=1, source_target_pairs={{0,1},{1,0},{2,3},{3,2},{4,5},{5,4},{6,7},{7,6},{8,9},{9,8},{10,11... | collective-permute-start | bytes 786440 | tf_op jit(solution)/shard_map/ppermute | solution.py:357
  11.9 12.7 %collective-permute-start.12 = (bf16[16,2048]{1,0:T(8,128)(2,1)S(1)}, bf16[16,2048]{1,0:T(8,128)(2,1)S(1)}, u32[]{:S(2)}, u32[]{:S(2)}) collective-permute-start(bf16[16,2048]{1,0:T(8,128)(2,1)S(1)} %get-tuple-element.53), channel_id=1, source_target_pairs={{0,2},{1,3},{2,4},{3,5},{4,6},{5,7},{6,0},{7,1},{8,10},{9,11},{10,... | collective-permute-start | bytes 196616 | tf_op jit(solution)/shard_map/ppermute | solution.py:354
  13.5 11.1 %collective-permute-start.13 = (bf16[16,2048]{1,0:T(8,128)(2,1)S(1)}, bf16[16,2048]{1,0:T(8,128)(2,1)S(1)}, u32[]{:S(2)}, u32[]{:S(2)}) collective-permute-start(bf16[16,2048]{1,0:T(8,128)(2,1)S(1)} %get-tuple-element.54), channel_id=1, source_target_pairs={{0,4},{1,5},{2,6},{3,7},{4,0},{5,1},{6,2},{7,3},{8,12},{9,13},{10,... | collective-permute-start | bytes 196616 | tf_op jit(solution)/shard_map/ppermute | solution.py:354
  16.1 8.6 %collective-permute-start.14 = (bf16[16,2048]{1,0:T(8,128)(2,1)S(1)}, bf16[16,2048]{1,0:T(8,128)(2,1)S(1)}, u32[]{:S(2)}, u32[]{:S(2)}) collective-permute-start(bf16[16,2048]{1,0:T(8,128)(2,1)S(1)} %get-tuple-element.55), channel_id=1, source_target_pairs={{0,6},{1,7},{2,0},{3,1},{4,2},{5,3},{6,4},{7,5},{8,14},{9,15},{10,... | collective-permute-start | bytes 196616 | tf_op jit(solution)/shard_map/ppermute | solution.py:354
  17.6 10.2 %collective-permute-start.4 = (bf16[16,2048]{1,0:T(8,128)(2,1)S(1)}, bf16[16,2048]{1,0:T(8,128)(2,1)S(1)}, u32[]{:S(2)}, u32[]{:S(2)}) collective-permute-start(bf16[16,2048]{1,0:T(8,128)(2,1)S(1)} %get-tuple-element.47), channel_id=1, source_target_pairs={{0,2},{1,3},{2,4},{3,5},{4,6},{5,7},{6,0},{7,1},{8,10},{9,11},{10,... | collective-permute-start | bytes 196616 | tf_op jit(solution)/shard_map/ppermute | solution.py:354
  18.3 13.7 %collective-permute-start.6 = (bf16[16,2048]{1,0:T(8,128)(2,1)S(1)}, bf16[16,2048]{1,0:T(8,128)(2,1)S(1)}, u32[]{:S(2)}, u32[]{:S(2)}) collective-permute-start(bf16[16,2048]{1,0:T(8,128)(2,1)S(1)} %get-tuple-element.44._), channel_id=1, source_target_pairs={{0,6},{1,7},{2,0},{3,1},{4,2},{5,3},{6,4},{7,5},{8,14},{9,15},{10,... | collective-permute-start | bytes 196616 | tf_op jit(solution)/shard_map/ppermute | solution.py:354
  24.6 7.4 %collective-permute-start.5 = (bf16[16,2048]{1,0:T(8,128)(2,1)S(1)}, bf16[16,2048]{1,0:T(8,128)(2,1)S(1)}, u32[]{:S(2)}, u32[]{:S(2)}) collective-permute-start(bf16[16,2048]{1,0:T(8,128)(2,1)S(1)} %get-tuple-element.48), channel_id=1, source_target_pairs={{0,4},{1,5},{2,6},{3,7},{4,0},{5,1},{6,2},{7,3},{8,12},{9,13},{10,... | collective-permute-start | bytes 196616 | tf_op jit(solution)/shard_map/ppermute | solution.py:354
  24.8 7.4 %collective-permute-start.17 = (bf16[16,2048]{1,0:T(8,128)(2,1)S(1)}, bf16[16,2048]{1,0:T(8,128)(2,1)S(1)}, u32[]{:S(2)}, u32[]{:S(2)}) collective-permute-start(bf16[16,2048]{1,0:T(8,128)(2,1)S(1)} %shard_map.119.refs_0_.refs_4_), channel_id=1, source_target_pairs={{0,2},{1,3},{2,4},{3,5},{4,6},{5,7},{6,0},{7,1},{8,10},{9,11},{10,... | collective-permute-start | bytes 196616 | tf_op jit(solution)/shard_map/ppermute | solution.py:354
  25.3 10.6 %collective-permute-start.16 = (bf16[16,2048]{1,0:T(8,128)(2,1)S(1)}, bf16[16,2048]{1,0:T(8,128)(2,1)S(1)}, u32[]{:S(2)}, u32[]{:S(2)}) collective-permute-start(bf16[16,2048]{1,0:T(8,128)(2,1)S(1)} %shard_map.119.refs_0_.refs_4_), channel_id=1, source_target_pairs={{0,4},{1,5},{2,6},{3,7},{4,0},{5,1},{6,2},{7,3},{8,12},{9,13},{10,... | collective-permute-start | bytes 196616 | tf_op jit(solution)/shard_map/ppermute | solution.py:354
  27.8 8.2 %collective-permute-start.15 = (bf16[16,2048]{1,0:T(8,128)(2,1)S(1)}, bf16[16,2048]{1,0:T(8,128)(2,1)S(1)}, u32[]{:S(2)}, u32[]{:S(2)}) collective-permute-start(bf16[16,2048]{1,0:T(8,128)(2,1)S(1)} %shard_map.119.refs_0_.refs_4_), channel_id=1, source_target_pairs={{0,6},{1,7},{2,0},{3,1},{4,2},{5,3},{6,4},{7,5},{8,14},{9,15},{10,... | collective-permute-start | bytes 196616 | tf_op jit(solution)/shard_map/ppermute | solution.py:354
  32.1 6.2 %collective-permute-start.9 = (bf16[16,2048]{1,0:T(8,128)(2,1)S(1)}, bf16[16,2048]{1,0:T(8,128)(2,1)S(1)}, u32[]{:S(2)}, u32[]{:S(2)}) collective-permute-start(bf16[16,2048]{1,0:T(8,128)(2,1)S(1)} %shard_map.115.refs_0_.refs_9_), channel_id=1, source_target_pairs={{0,2},{1,3},{2,4},{3,5},{4,6},{5,7},{6,0},{7,1},{8,10},{9,11},{10,... | collective-permute-start | bytes 196616 | tf_op jit(solution)/shard_map/ppermute | solution.py:354
  32.1 7.4 %collective-permute-start.8 = (bf16[16,2048]{1,0:T(8,128)(2,1)S(1)}, bf16[16,2048]{1,0:T(8,128)(2,1)S(1)}, u32[]{:S(2)}, u32[]{:S(2)}) collective-permute-start(bf16[16,2048]{1,0:T(8,128)(2,1)S(1)} %shard_map.115.refs_0_.refs_9_), channel_id=1, source_target_pairs={{0,4},{1,5},{2,6},{3,7},{4,0},{5,1},{6,2},{7,3},{8,12},{9,13},{10,... | collective-permute-start | bytes 196616 | tf_op jit(solution)/shard_map/ppermute | solution.py:354
  32.2 7.3 %collective-permute-start.7 = (bf16[16,2048]{1,0:T(8,128)(2,1)S(1)}, bf16[16,2048]{1,0:T(8,128)(2,1)S(1)}, u32[]{:S(2)}, u32[]{:S(2)}) collective-permute-start(bf16[16,2048]{1,0:T(8,128)(2,1)S(1)} %shard_map.115.refs_0_.refs_9_), channel_id=1, source_target_pairs={{0,6},{1,7},{2,0},{3,1},{4,2},{5,3},{6,4},{7,5},{8,14},{9,15},{10,... | collective-permute-start | bytes 196616 | tf_op jit(solution)/shard_map/ppermute | solution.py:354
  36.0 3.7 %collective-permute-start.18 = (bf16[64,2048]{1,0:T(8,128)(2,1)S(1)}, bf16[64,2048]{1,0:T(8,128)(2,1)S(1)}, u32[]{:S(2)}, u32[]{:S(2)}) collective-permute-start(bf16[64,2048]{1,0:T(8,128)(2,1)S(1)} %shard_map.120.own_ref), channel_id=1, source_target_pairs={{0,1},{1,0},{2,3},{3,2},{4,5},{5,4},{6,7},{7,6},{8,9},{9,8},{10,11... | collective-permute-start | bytes 786440 | tf_op jit(solution)/shard_map/ppermute | solution.py:357
  39.6 1.6 %collective-permute-start.10 = (bf16[64,2048]{1,0:T(8,128)(2,1)S(1)}, bf16[64,2048]{1,0:T(8,128)(2,1)S(1)}, u32[]{:S(2)}, u32[]{:S(2)}) collective-permute-start(bf16[64,2048]{1,0:T(8,128)(2,1)S(1)} %shard_map.116.own_ref), channel_id=1, source_target_pairs={{0,1},{1,0},{2,3},{3,2},{4,5},{5,4},{6,7},{7,6},{8,9},{9,8},{10,11... | collective-permute-start | bytes 786440 | tf_op jit(solution)/shard_map/ppermute | solution.py:357
  42.6 1.6 %collective-permute-start.23 = (bf16[64,2048]{1,0:T(8,128)(2,1)S(1)}, bf16[64,2048]{1,0:T(8,128)(2,1)S(1)}, u32[]{:S(2)}, u32[]{:S(2)}) collective-permute-start(bf16[64,2048]{1,0:T(8,128)(2,1)S(1)} %get-tuple-element.64), channel_id=1, source_target_pairs={{0,1},{1,0},{2,3},{3,2},{4,5},{5,4},{6,7},{7,6},{8,9},{9,8},{10,11... | collective-permute-start | bytes 786440 | tf_op jit(solution)/shard_map/ppermute | solution.py:357
  43.2 4.9 %collective-permute-start.19 = (bf16[64,2048]{1,0:T(8,128)(2,1)S(1)}, bf16[64,2048]{1,0:T(8,128)(2,1)S(1)}, u32[]{:S(2)}, u32[]{:S(2)}) collective-permute-start(bf16[64,2048]{1,0:T(8,128)(2,1)S(1)} %get-tuple-element.58), channel_id=1, source_target_pairs={{0,1},{1,0},{2,3},{3,2},{4,5},{5,4},{6,7},{7,6},{8,9},{9,8},{10,11... | collective-permute-start | bytes 786440 | tf_op jit(solution)/shard_map/ppermute | solution.py:357
  44.2 6.8 %collective-permute-start.24 = (bf16[16,2048]{1,0:T(8,128)(2,1)S(1)}, bf16[16,2048]{1,0:T(8,128)(2,1)S(1)}, u32[]{:S(2)}, u32[]{:S(2)}) collective-permute-start(bf16[16,2048]{1,0:T(8,128)(2,1)S(1)} %get-tuple-element.66), channel_id=1, source_target_pairs={{0,2},{1,3},{2,4},{3,5},{4,6},{5,7},{6,0},{7,1},{8,10},{9,11},{10,... | collective-permute-start | bytes 196616 | tf_op jit(solution)/shard_map/ppermute | solution.py:354
  45.5 9.6 %collective-permute-start.25 = (bf16[16,2048]{1,0:T(8,128)(2,1)S(1)}, bf16[16,2048]{1,0:T(8,128)(2,1)S(1)}, u32[]{:S(2)}, u32[]{:S(2)}) collective-permute-start(bf16[16,2048]{1,0:T(8,128)(2,1)S(1)} %get-tuple-element.67), channel_id=1, source_target_pairs={{0,4},{1,5},{2,6},{3,7},{4,0},{5,1},{6,2},{7,3},{8,12},{9,13},{10,... | collective-permute-start | bytes 196616 | tf_op jit(solution)/shard_map/ppermute | solution.py:354
  47.3 7.9 %collective-permute-start.26 = (bf16[16,2048]{1,0:T(8,128)(2,1)S(1)}, bf16[16,2048]{1,0:T(8,128)(2,1)S(1)}, u32[]{:S(2)}, u32[]{:S(2)}) collective-permute-start(bf16[16,2048]{1,0:T(8,128)(2,1)S(1)} %get-tuple-element.68), channel_id=1, source_target_pairs={{0,6},{1,7},{2,0},{3,1},{4,2},{5,3},{6,4},{7,5},{8,14},{9,15},{10,... | collective-permute-start | bytes 196616 | tf_op jit(solution)/shard_map/ppermute | solution.py:354
  48.2 7.1 %collective-permute-start.20 = (bf16[16,2048]{1,0:T(8,128)(2,1)S(1)}, bf16[16,2048]{1,0:T(8,128)(2,1)S(1)}, u32[]{:S(2)}, u32[]{:S(2)}) collective-permute-start(bf16[16,2048]{1,0:T(8,128)(2,1)S(1)} %get-tuple-element.60), channel_id=1, source_target_pairs={{0,2},{1,3},{2,4},{3,5},{4,6},{5,7},{6,0},{7,1},{8,10},{9,11},{10,... | collective-permute-start | bytes 196616 | tf_op jit(solution)/shard_map/ppermute | solution.py:354
  49.4 9.3 %collective-permute-start.21 = (bf16[16,2048]{1,0:T(8,128)(2,1)S(1)}, bf16[16,2048]{1,0:T(8,128)(2,1)S(1)}, u32[]{:S(2)}, u32[]{:S(2)}) collective-permute-start(bf16[16,2048]{1,0:T(8,128)(2,1)S(1)} %get-tuple-element.61), channel_id=1, source_target_pairs={{0,4},{1,5},{2,6},{3,7},{4,0},{5,1},{6,2},{7,3},{8,12},{9,13},{10,... | collective-permute-start | bytes 196616 | tf_op jit(solution)/shard_map/ppermute | solution.py:354
  51.1 7.7 %collective-permute-start.22 = (bf16[16,2048]{1,0:T(8,128)(2,1)S(1)}, bf16[16,2048]{1,0:T(8,128)(2,1)S(1)}, u32[]{:S(2)}, u32[]{:S(2)}) collective-permute-start(bf16[16,2048]{1,0:T(8,128)(2,1)S(1)} %get-tuple-element.62), channel_id=1, source_target_pairs={{0,6},{1,7},{2,0},{3,1},{4,2},{5,3},{6,4},{7,5},{8,14},{9,15},{10,... | collective-permute-start | bytes 196616 | tf_op jit(solution)/shard_map/ppermute | solution.py:354
where the time goes:
time: 59.7 us; the launch traced here: 59.5 us
  starting transfers between devices  33.7 us (56%)
  waiting for transfers between devices  15.2 us (25%)
  Pallas kernels  10.3 us (17%)
    ppermute x18, starting transfers between devices, shift(): lax.ppermute(x, 'exp', [(e, (e + 2 * r) % exp_count) for e in range(exp_c...  27.7 us
    ppermute x18, waiting for transfers between devices, shift(): lax.ppermute(x, 'exp', [(e, (e + 2 * r) % exp_count) for e in range(exp_c...  10.9 us
    pallas_call x19, Pallas kernels, call(): pl.pallas_call(kernel, out_shape=outs, in_specs=[pl.BlockSpec(memory_spac...  10.3 us
    ppermute x3, starting transfers between devices, local(): lax.ppermute(state, 'seq', [(move(i), i) for i in range(seq_count)])  4.6 us
    ppermute x3, waiting for transfers between devices, local(): lax.ppermute(state, 'seq', [(move(i), i) for i in range(seq_count)])  2.44 us
    ppermute x6, waiting for transfers between devices, across(): return lax.ppermute(x, 'exp', [(e, e ^ 1) for e in range(exp_count)])  1.9 us
    ppermute x6, starting transfers between devices, across(): return lax.ppermute(x, 'exp', [(e, e ^ 1) for e in range(exp_count)])  1.42 us
  transfers between devices with their start and end apart: 27, of which 12 were waited for; matrix products, arithmetic and copies ran while one was open for 0% of the time, Pallas kernels for 11%

commit v1 on v0

--- a/solution.py
+++ b/solution.py
@@ -166,11 +166,12 @@
 
 
 def within_kernel(
-    query_hbm, key_hbm, value_hbm, decay_hbm, gain_hbm, w_out_hbm, _,
-    intra_ref, grown_ref, query_ref, gain_ref, w_out_ref,
-    key_ref, value_ref, decay_ref, gain_in_ref, sems,
+    n_pair, query_hbm, key_hbm, value_hbm, decay_hbm, gain_hbm, router_hbm, routes_hbm, w_out_hbm, gate_hbm, up_hbm, _,
+    intra_ref, grown_ref, query_ref, gain_ref, w_out_ref, in_ref, member_ref,
+    key_ref, value_ref, decay_ref, gain_in_ref, router_ref, routes_ref, sems,
 ):
     t, d = query_ref.shape
+    hid = gate_hbm.shape[0]
     copies = dma_in(
         sems,
         [
@@ -179,10 +180,14 @@
             (key_hbm, key_ref),
             (value_hbm, value_ref),
             (gain_hbm, gain_in_ref),
+            (router_hbm, router_ref),
+            (routes_hbm, routes_ref),
             (w_out_hbm, w_out_ref),
+            (gate_hbm, in_ref.at[0:hid]),
+            (up_hbm, in_ref.at[hid : 2 * hid]),
         ],
     )
-    for copy in copies[:5]:
+    for copy in copies[:7]:
         copy.wait()
     column, line = cumulate(decay_ref[...])
     query, key, value = query_ref[...], key_ref[...], value_ref[...]
@@ -193,7 +198,18 @@
     intra_ref[...] = dot_f32(attend, value, ((1,), (0,)))
     grown_ref[...] = jnp.broadcast_to(jnp.exp(column) * (1.0 / d), (t, d))
     gain_ref[...] = jnp.broadcast_to(gain_in_ref[...].astype(F32), gain_ref.shape)
-    copies[5].wait()
+    experts = router_ref.shape[0]
+    in_ref[2 * hid :, :] = jnp.zeros((TILE_ROWS, in_ref.shape[1]), BF16)
+    in_ref[2 * hid : 2 * hid + experts, :] = router_ref[...]
+    padded = member_ref.shape[0]
+    hits = jnp.zeros((padded, t), F32)
+    for k in range(routes_ref.shape[0]):
+        hits = hits + jnp.where(routes_ref[k : k + 1, :] == iota2((padded, t), 0), 1.0, 0.0)
+    exp_index = lax.axis_index("exp")
+    place = place_matrix(t // (2 * n_pair), n_pair, exp_index // 2, exp_index % 2)
+    member_ref[...] = dot_f32(hits.astype(BF16), place, ((1,), (1,)))
+    for copy in copies[7:]:
+        copy.wait()
 
 
 def place_matrix(rows, n_pair, pair, core):
@@ -205,36 +221,11 @@
     return jnp.where(source == j, 1.0, 0.0).astype(BF16)
 
 
-def fetch_kernel(
-    n_pair, router_hbm, routes_hbm, gate_hbm, up_hbm, down_hbm, _,
-    in_ref, down_ref, member_ref, router_ref, routes_ref, sems,
-):
-    hid = gate_hbm.shape[0]
-    copies = dma_in(
-        sems,
-        [
-            (router_hbm, router_ref),
-            (routes_hbm, routes_ref),
-            (gate_hbm, in_ref.at[0:hid]),
-            (up_hbm, in_ref.at[hid : 2 * hid]),
-            (down_hbm, down_ref),
-        ],
-    )
-    for copy in copies[:2]:
-        copy.wait()
-    experts, t = router_ref.shape[0], routes_ref.shape[1]
-    rows = t // (2 * n_pair)
-    in_ref[2 * hid :, :] = jnp.zeros((TILE_ROWS, in_ref.shape[1]), BF16)
-    in_ref[2 * hid : 2 * hid + experts, :] = router_ref[...]
-    padded = member_ref.shape[0]
-    hits = jnp.zeros((padded, t), F32)
-    for k in range(routes_ref.shape[0]):
-        hits = hits + jnp.where(routes_ref[k : k + 1, :] == iota2((padded, t), 0), 1.0, 0.0)
-    exp_index = lax.axis_index("exp")
-    place = place_matrix(rows, n_pair, exp_index // 2, exp_index % 2)
-    member_ref[...] = dot_f32(hits.astype(BF16), place, ((1,), (1,)))
-    for copy in copies[2:]:
-        copy.wait()
+def fetch_down_kernel(down_hbm, _, down_ref, token_ref, sem):
+    copy = pltpu.make_async_copy(down_hbm, down_ref, sem)
+    copy.start()
+    token_ref[...] = jnp.zeros(token_ref.shape, F32)
+    copy.wait()
 
 
 def normed_kernel(n_pair, moves, *refs):
@@ -287,9 +278,9 @@
     refs[-1][...] = total.astype(BF16)
 
 
-def join_kernel(*refs):
+def join_kernel(count, *refs):
     start = 0
-    for ref in refs[:-1]:
+    for ref in refs[:count]:
         refs[-1][start : start + ref.shape[0], :] = ref[...]
         start += ref.shape[0]
 
@@ -368,7 +359,7 @@
             call(functools.partial(add_kernel, [[r] for r in range(n_pair)]), [rows_of(1)] * n_pair, (mine, other))
             for (mine, _), other in zip(products, others)
         ]
-        return [[term[0]] + [shift(term[r], r) for r in range(1, n_pair)] for term in terms], terms[-1][-1]
+        return [[term[0]] + [shift(term[r], r) for r in range(1, n_pair)] for term in terms]
 
     def products_of(x, w):
         return [call(functools.partial(product_kernel, at), [rows_of(n_pair)] * 2, (x, w)) for at in ranges]
@@ -385,33 +376,45 @@
     )
     moves = [lambda i, k=k: i ^ k for k in range(1, seq_count)]
     states = [lax.ppermute(state, "seq", [(move(i), i) for i in range(seq_count)]) for move in moves]
-    intra, grown, query_near, gain, w_out_near = call(
-        within_kernel,
-        [out((t, d), F32), out((t, d), F32), out((t, d), BF16), out((8, d), F32), out(w_out.shape, BF16)],
-        (query, key_in, value, decay_row, norm_gain[None, :], w_out, state),
-        [block, block, decay_block, pltpu.VMEM((1, d), BF16), dma((6,))],
-        far=6,
+    intra, grown, query_near, gain, w_out_near, w_in, member = call(
+        functools.partial(within_kernel, n_pair),
+        [
+            out((t, d), F32),
+            out((t, d), F32),
+            out((t, d), BF16),
+            out((8, d), F32),
+            out(w_out.shape, BF16),
+            out((2 * hid + TILE_ROWS, width), BF16),
+            out((-(-experts // 8) * 8, t), F32),
+        ],
+        (query, key_in, value, decay_row, norm_gain[None, :], router.T, routes.T, w_out, w_gate[0].T, w_up[0].T, state),
+        [
+            block,
+            block,
+            decay_block,
+            pltpu.VMEM((1, d), BF16),
+            pltpu.VMEM((experts, width), BF16),
+            pltpu.VMEM((routes.shape[1], t), jnp.int32),
+            dma((10,)),
+        ],
+        far=10,
     )
     (normed,) = call(
         functools.partial(normed_kernel, n_pair, moves),
         [out((t, d), BF16)],
         (*states, intra, grown, query_near, gain),
     )
-    terms, last = reduce(products_of(normed, w_out_near))
-    w_in, w_down_near, member = call(
-        functools.partial(fetch_kernel, n_pair),
-        [
-            out((2 * hid + TILE_ROWS, width), BF16),
-            out((hid, width), BF16),
-            out((-(-experts // 8) * 8, t), F32),
-        ],
-        (router.T, routes.T, w_gate[0].T, w_up[0].T, w_down[0], last),
-        [pltpu.VMEM((experts, width), BF16), pltpu.VMEM((routes.shape[1], t), jnp.int32), dma((5,))],
-        far=5,
-    )
-    mixed = [call(functools.partial(sum_kernel, n_pair), [rows_of(1)], (*term, member))[0] for term in terms]
+    terms = reduce(products_of(normed, w_out_near))
+    mixed = [call(functools.partial(sum_kernel, n_pair), [rows_of(1)], term)[0] for term in terms]
     gathered = [[shift(m, -r) if r else m for r in range(n_pair)] for m in mixed]
-    own = [call(join_kernel, [rows_of(n_pair)], blocks)[0] for blocks in gathered]
+    own, after = [], ()
+    for blocks in gathered:
+        own += call(functools.partial(join_kernel, n_pair), [rows_of(n_pair)], (*blocks, *after))
+        if not after:
+            w_down_near, token = call(
+                fetch_down_kernel, [out((hid, width), BF16), out((8, 128), F32)], (w_down[0], own[0]), [dma], far=1
+            )
+            after = (token,)
     total = ()
     for at, x in zip(ranges, own):
         if at.stop < width:
@@ -420,7 +423,7 @@
             kernel, shape = functools.partial(hidden_kernel, at, slices, experts), out((t, hid), BF16)
             total = (*total, member)
         total = call(kernel, [shape], (w_in, x, across(x), *total))
-    sums, _ = reduce(products_of(total[0], w_down_near))
+    sums = reduce(products_of(total[0], w_down_near))
     args = [x for some, m in zip(sums, mixed) for x in (*some, m)]
     return call(functools.partial(result_kernel, n_pair + 1), [out((rows, width), BF16)], args)[0]
 

time: 59.7 us -> 57.9 us (0.970)
  waiting for transfers between devices: 15.2 us -> 10.9 us
  starting transfers between devices: 33.7 us -> 36.2 us
    ppermute x18, waiting for transfers between devices: 10.9 us -> 8.13 us  [shift(): lax.ppermute(x, 'exp', [(e, (e + 2 * r) % exp_count) for e in range(exp_c...]
    ppermute x18, starting transfers between devices: 27.7 us -> 30.2 us  [shift(): lax.ppermute(x, 'exp', [(e, (e + 2 * r) % exp_count) for e in range(exp_c...]
    ppermute x3, waiting for transfers between devices: 2.44 us -> 0.9 us  [local(): lax.ppermute(state, 'seq', [(move(i), i) for i in range(seq_count)])]
  transfers between devices with their start and end apart: 27 -> 27, of which waited for: 12 -> 9; matrix products, arithmetic and copies ran while one was open for 0% -> 0% of each run, Pallas kernels for 11% -> 11%
where the time goes in v1:
time: 57.9 us; the launch traced here: 57.7 us
  starting transfers between devices  36.2 us (63%)
  waiting for transfers between devices  10.9 us (19%)
  Pallas kernels  10.4 us (18%)
    ppermute x18, starting transfers between devices, shift(): lax.ppermute(x, 'exp', [(e, (e + 2 * r) % exp_count) for e in range(exp_c...  30.2 us
    pallas_call x19, Pallas kernels, call(): pl.pallas_call(kernel, out_shape=outs, in_specs=[pl.BlockSpec(memory_spac...  10.4 us
    ppermute x18, waiting for transfers between devices, shift(): lax.ppermute(x, 'exp', [(e, (e + 2 * r) % exp_count) for e in range(exp_c...  8.13 us
    ppermute x3, starting transfers between devices, local(): lax.ppermute(state, 'seq', [(move(i), i) for i in range(seq_count)])  4.6 us
    ppermute x6, waiting for transfers between devices, across(): return lax.ppermute(x, 'exp', [(e, e ^ 1) for e in range(exp_count)])  1.9 us
    ppermute x6, starting transfers between devices, across(): return lax.ppermute(x, 'exp', [(e, e ^ 1) for e in range(exp_count)])  1.42 us
  transfers between devices with their start and end apart: 27, of which 9 were waited for; matrix products, arithmetic and copies ran while one was open for 0% of the time, Pallas kernels for 11%

profile of v1, /device:TPU:0, one launch (start us, length us, event | category | flops | bytes accessed | tf_op | source)
XLA Modules:
  0.0 57.7 jit_solution(8188326623489693517)
XLA Ops:
  0.0 1.1 %shard_map.109._ = bf16[144,128]{1,0:T(8,128)(2,1)S(1)} custom-call(bf16[128,128]{1,0:T(8,128)(2,1)} %key_hbm.3, bf16[128,128]{1,0:T(8,128)(2,1)} %value_hbm.3, f32[1,128]{1,0:T(1,128)} %bitcast.15), custom_call_target="tpu_custom_call" | custom-call | tf_op jit(solution)/shard_map/pallas_call | solution.py:321
  1.1 4.0 %collective-permute-start.2 = (bf16[144,128]{1,0:T(8,128)(2,1)S(1)}, bf16[144,128]{1,0:T(8,128)(2,1)S(1)}, u32[]{:S(2)}, u32[]{:S(2)}) collective-permute-start(bf16[144,128]{1,0:T(8,128)(2,1)S(1)} %shard_map.109._), channel_id=1, source_target_pairs={{24,0},{16,8},{8,16},{0,24},{25,1},{17,9},{9,17},{1,25},{26,2},{18... | collective-permute-start | bytes 110600 | tf_op jit(solution)/shard_map/ppermute | solution.py:378
  5.1 0.5 collective-permute-start.1
  5.6 0.1 collective-permute-start
  5.7 2.9 %shard_map.110 = (f32[128,128]{1,0:T(8,128)S(1)}, f32[128,128]{1,0:T(8,128)S(1)}, bf16[128,128]{1,0:T(8,128)(2,1)S(1)}, f32[8,128]{1,0:T(8,128)S(1)}, bf16[128,4...) custom-call(bf16[128,128]{1,0:T(8,128)(2,1)} %query_hbm.1, bf16[128,128]{1,0:T(8,128)(2,1)} %key_hbm.3, ...), custom_call_target="tpu_custom_call" | custom-call | tf_op jit(solution)/shard_map/pallas_call | solution.py:321
  8.6 0.4 collective-permute-done.1.refs_1_
  9.0 0.5 collective-permute-done.refs_0_
  9.5 0.4 shard_map.111.x_ref
  10.0 0.3 shard_map.115
  10.3 0.1 collective-permute-start.10
  10.3 0.3 shard_map.112
  10.6 0.6 collective-permute-start.3
  11.2 0.7 %collective-permute-done.10.b_ref = bf16[64,2048]{1,0:T(8,128)(2,1)S(1)} collective-permute-done((bf16[64,2048]{1,0:T(8,128)(2,1)S(1)}, bf16[64,2048]{1,0:T(8,128)(2,1)S(1)}, u32[]{:S(2)}, u32[]{:S(2)}) %collective-permute-start.10) | collective-permute-done | bytes 262176 | tf_op jit(solution)/shard_map/ppermute | solution.py:348
  11.9 0.1 shard_map.116
  11.9 1.6 %collective-permute-start.11 = (bf16[16,2048]{1,0:T(8,128)(2,1)S(1)}, bf16[16,2048]{1,0:T(8,128)(2,1)S(1)}, u32[]{:S(2)}, u32[]{:S(2)}) collective-permute-start(bf16[16,2048]{1,0:T(8,128)(2,1)S(1)} %get-tuple-element.53), channel_id=1, source_target_pairs={{0,2},{1,3},{2,4},{3,5},{4,6},{5,7},{6,0},{7,1},{8,10},{9,11},{10,... | collective-permute-start | bytes 196616 | tf_op jit(solution)/shard_map/ppermute | solution.py:345
  13.5 2.6 %collective-permute-start.12 = (bf16[16,2048]{1,0:T(8,128)(2,1)S(1)}, bf16[16,2048]{1,0:T(8,128)(2,1)S(1)}, u32[]{:S(2)}, u32[]{:S(2)}) collective-permute-start(bf16[16,2048]{1,0:T(8,128)(2,1)S(1)} %get-tuple-element.54), channel_id=1, source_target_pairs={{0,4},{1,5},{2,6},{3,7},{4,0},{5,1},{6,2},{7,3},{8,12},{9,13},{10,... | collective-permute-start | bytes 196616 | tf_op jit(solution)/shard_map/ppermute | solution.py:345
  16.1 1.3 %collective-permute-start.13 = (bf16[16,2048]{1,0:T(8,128)(2,1)S(1)}, bf16[16,2048]{1,0:T(8,128)(2,1)S(1)}, u32[]{:S(2)}, u32[]{:S(2)}) collective-permute-start(bf16[16,2048]{1,0:T(8,128)(2,1)S(1)} %get-tuple-element.55), channel_id=1, source_target_pairs={{0,6},{1,7},{2,0},{3,1},{4,2},{5,3},{6,4},{7,5},{8,14},{9,15},{10,... | collective-permute-start | bytes 196616 | tf_op jit(solution)/shard_map/ppermute | solution.py:345
  17.5 0.1 shard_map.113
  17.6 0.7 %collective-permute-start.4 = (bf16[16,2048]{1,0:T(8,128)(2,1)S(1)}, bf16[16,2048]{1,0:T(8,128)(2,1)S(1)}, u32[]{:S(2)}, u32[]{:S(2)}) collective-permute-start(bf16[16,2048]{1,0:T(8,128)(2,1)S(1)} %get-tuple-element.47), channel_id=1, source_target_pairs={{0,2},{1,3},{2,4},{3,5},{4,6},{5,7},{6,0},{7,1},{8,10},{9,11},{10,... | collective-permute-start | bytes 196616 | tf_op jit(solution)/shard_map/ppermute | solution.py:345
  18.3 0.3 collective-permute-start.5
  18.6 2.8 %collective-permute-start.6 = (bf16[16,2048]{1,0:T(8,128)(2,1)S(1)}, bf16[16,2048]{1,0:T(8,128)(2,1)S(1)}, u32[]{:S(2)}, u32[]{:S(2)}) collective-permute-start(bf16[16,2048]{1,0:T(8,128)(2,1)S(1)} %get-tuple-element.49), channel_id=1, source_target_pairs={{0,6},{1,7},{2,0},{3,1},{4,2},{5,3},{6,4},{7,5},{8,14},{9,15},{10,... | collective-permute-start | bytes 196616 | tf_op jit(solution)/shard_map/ppermute | solution.py:345
  21.5 4.3 %collective-permute-start.16 = (bf16[16,2048]{1,0:T(8,128)(2,1)S(1)}, bf16[16,2048]{1,0:T(8,128)(2,1)S(1)}, u32[]{:S(2)}, u32[]{:S(2)}) collective-permute-start(bf16[16,2048]{1,0:T(8,128)(2,1)S(1)} %shard_map.117.refs_0_.refs_4_), channel_id=1, source_target_pairs={{0,2},{1,3},{2,4},{3,5},{4,6},{5,7},{6,0},{7,1},{8,10},{9,11},{10,... | collective-permute-start | bytes 196616 | tf_op jit(solution)/shard_map/ppermute | solution.py:345
  25.7 2.4 %collective-permute-start.14 = (bf16[16,2048]{1,0:T(8,128)(2,1)S(1)}, bf16[16,2048]{1,0:T(8,128)(2,1)S(1)}, u32[]{:S(2)}, u32[]{:S(2)}) collective-permute-start(bf16[16,2048]{1,0:T(8,128)(2,1)S(1)} %shard_map.117.refs_0_.refs_4_), channel_id=1, source_target_pairs={{0,6},{1,7},{2,0},{3,1},{4,2},{5,3},{6,4},{7,5},{8,14},{9,15},{10,... | collective-permute-start | bytes 196616 | tf_op jit(solution)/shard_map/ppermute | solution.py:345
  28.2 2.7 %collective-permute-start.9 = (bf16[16,2048]{1,0:T(8,128)(2,1)S(1)}, bf16[16,2048]{1,0:T(8,128)(2,1)S(1)}, u32[]{:S(2)}, u32[]{:S(2)}) collective-permute-start(bf16[16,2048]{1,0:T(8,128)(2,1)S(1)} %shard_map.114.refs_0_.refs_9_), channel_id=1, source_target_pairs={{0,2},{1,3},{2,4},{3,5},{4,6},{5,7},{6,0},{7,1},{8,10},{9,11},{10,... | collective-permute-start | bytes 196616 | tf_op jit(solution)/shard_map/ppermute | solution.py:345
  30.9 2.4 %collective-permute-start.7 = (bf16[16,2048]{1,0:T(8,128)(2,1)S(1)}, bf16[16,2048]{1,0:T(8,128)(2,1)S(1)}, u32[]{:S(2)}, u32[]{:S(2)}) collective-permute-start(bf16[16,2048]{1,0:T(8,128)(2,1)S(1)} %shard_map.114.refs_0_.refs_9_), channel_id=1, source_target_pairs={{0,6},{1,7},{2,0},{3,1},{4,2},{5,3},{6,4},{7,5},{8,14},{9,15},{10,... | collective-permute-start | bytes 196616 | tf_op jit(solution)/shard_map/ppermute | solution.py:345
  33.4 0.1 collective-permute-start.18
  33.5 1.7 %shard_map.119 = (bf16[288,4096]{1,0:T(8,128)(2,1)S(1)}, f32[8,128]{1,0:T(8,128)S(1)}) custom-call(bf16[288,4096]{1,0:T(8,128)(2,1)} %bitcast.13, bf16[64,2048]{1,0:T(8,128)(2,1)S(1)} %shard_map.118._.own_ref), custom_call_target="tpu_custom_call" | custom-call | tf_op jit(solution)/shard_map/pallas_call | solution.py:321
  35.2 2.5 %collective-permute-done.8.refs_2_ = bf16[16,2048]{1,0:T(8,128)(2,1)S(1)} collective-permute-done((bf16[16,2048]{1,0:T(8,128)(2,1)S(1)}, bf16[16,2048]{1,0:T(8,128)(2,1)S(1)}, u32[]{:S(2)}, u32[]{:S(2)}) %collective-permute-start.8) | collective-permute-done | bytes 65568 | tf_op jit(solution)/shard_map/ppermute | solution.py:345
  37.7 0.1 collective-permute-start.17
  37.8 0.8 %shard_map.121.before_ref = f32[592,128]{1,0:T(8,128)S(1)} custom-call(bf16[592,4096]{1,0:T(8,128)(2,1)S(1)} %get-tuple-element.38.in_ref, bf16[64,2048]{1,0:T(8,128)(2,1)S(1)} %shard_map.118._.own_ref, bf16[64,2048]{1,0:T(8,128)(2,1)S(1)} %collective-permute-done.18.other_ref), custom_call_target="tpu_custom_call" | custom-call | tf_op jit(solution)/shard_map/pallas_call | solution.py:321
  38.6 0.7 %collective-permute-done.17.other_ref = bf16[64,2048]{1,0:T(8,128)(2,1)S(1)} collective-permute-done((bf16[64,2048]{1,0:T(8,128)(2,1)S(1)}, bf16[64,2048]{1,0:T(8,128)(2,1)S(1)}, u32[]{:S(2)}, u32[]{:S(2)}) %collective-permute-start.17) | collective-permute-done | bytes 262176 | tf_op jit(solution)/shard_map/ppermute | solution.py:348
  39.3 0.9 %shard_map.122.x_ref = bf16[128,288]{1,0:T(8,128)(2,1)S(1)} custom-call(bf16[592,4096]{1,0:T(8,128)(2,1)S(1)} %get-tuple-element.38.in_ref, bf16[64,2048]{1,0:T(8,128)(2,1)S(1)} %shard_map.120.own_ref, bf16[64,2048]{1,0:T(8,128)(2,1)S(1)} %collective-permute-done.17.other_ref, f32[592,128]{1,0:T(8,128)S(1)} %shard_map.121.before_ref, ...), custom_call_target="tpu_custom_call" | custom-call | tf_op jit(solution)/shard_map/pallas_call | solution.py:321
  40.3 0.4 shard_map.125
  40.7 0.2 collective-permute-start.23
  40.9 0.4 shard_map.123
  41.4 0.4 collective-permute-start.19
  41.8 0.5 collective-permute-done.23.b_ref
  42.3 0.1 shard_map.126
  42.4 1.9 %collective-permute-start.24 = (bf16[16,2048]{1,0:T(8,128)(2,1)S(1)}, bf16[16,2048]{1,0:T(8,128)(2,1)S(1)}, u32[]{:S(2)}, u32[]{:S(2)}) collective-permute-start(bf16[16,2048]{1,0:T(8,128)(2,1)S(1)} %get-tuple-element.68), channel_id=1, source_target_pairs={{0,2},{1,3},{2,4},{3,5},{4,6},{5,7},{6,0},{7,1},{8,10},{9,11},{10,... | collective-permute-start | bytes 196616 | tf_op jit(solution)/shard_map/ppermute | solution.py:345
  44.3 1.8 %collective-permute-start.25 = (bf16[16,2048]{1,0:T(8,128)(2,1)S(1)}, bf16[16,2048]{1,0:T(8,128)(2,1)S(1)}, u32[]{:S(2)}, u32[]{:S(2)}) collective-permute-start(bf16[16,2048]{1,0:T(8,128)(2,1)S(1)} %get-tuple-element.69), channel_id=1, source_target_pairs={{0,4},{1,5},{2,6},{3,7},{4,0},{5,1},{6,2},{7,3},{8,12},{9,13},{10,... | collective-permute-start | bytes 196616 | tf_op jit(solution)/shard_map/ppermute | solution.py:345
  46.1 0.7 %collective-permute-start.26 = (bf16[16,2048]{1,0:T(8,128)(2,1)S(1)}, bf16[16,2048]{1,0:T(8,128)(2,1)S(1)}, u32[]{:S(2)}, u32[]{:S(2)}) collective-permute-start(bf16[16,2048]{1,0:T(8,128)(2,1)S(1)} %get-tuple-element.70), channel_id=1, source_target_pairs={{0,6},{1,7},{2,0},{3,1},{4,2},{5,3},{6,4},{7,5},{8,14},{9,15},{10,... | collective-permute-start | bytes 196616 | tf_op jit(solution)/shard_map/ppermute | solution.py:345
  46.8 1.4 %collective-permute-start.20 = (bf16[16,2048]{1,0:T(8,128)(2,1)S(1)}, bf16[16,2048]{1,0:T(8,128)(2,1)S(1)}, u32[]{:S(2)}, u32[]{:S(2)}) collective-permute-start(bf16[16,2048]{1,0:T(8,128)(2,1)S(1)} %get-tuple-element.62), channel_id=1, source_target_pairs={{0,2},{1,3},{2,4},{3,5},{4,6},{5,7},{6,0},{7,1},{8,10},{9,11},{10,... | collective-permute-start | bytes 196616 | tf_op jit(solution)/shard_map/ppermute | solution.py:345
  48.2 1.2 %collective-permute-start.21 = (bf16[16,2048]{1,0:T(8,128)(2,1)S(1)}, bf16[16,2048]{1,0:T(8,128)(2,1)S(1)}, u32[]{:S(2)}, u32[]{:S(2)}) collective-permute-start(bf16[16,2048]{1,0:T(8,128)(2,1)S(1)} %get-tuple-element.63), channel_id=1, source_target_pairs={{0,4},{1,5},{2,6},{3,7},{4,0},{5,1},{6,2},{7,3},{8,12},{9,13},{10,... | collective-permute-start | bytes 196616 | tf_op jit(solution)/shard_map/ppermute | solution.py:345
  49.4 2.0 %collective-permute-start.22 = (bf16[16,2048]{1,0:T(8,128)(2,1)S(1)}, bf16[16,2048]{1,0:T(8,128)(2,1)S(1)}, u32[]{:S(2)}, u32[]{:S(2)}) collective-permute-start(bf16[16,2048]{1,0:T(8,128)(2,1)S(1)} %get-tuple-element.64), channel_id=1, source_target_pairs={{0,6},{1,7},{2,0},{3,1},{4,2},{5,3},{6,4},{7,5},{8,14},{9,15},{10,... | collective-permute-start | bytes 196616 | tf_op jit(solution)/shard_map/ppermute | solution.py:345
  51.4 1.7 %collective-permute-done.25.refs_7_ = bf16[16,2048]{1,0:T(8,128)(2,1)S(1)} collective-permute-done((bf16[16,2048]{1,0:T(8,128)(2,1)S(1)}, bf16[16,2048]{1,0:T(8,128)(2,1)S(1)}, u32[]{:S(2)}, u32[]{:S(2)}) %collective-permute-start.25) | collective-permute-done | bytes 65568 | tf_op jit(solution)/shard_map/ppermute | solution.py:345
  53.1 0.6 %collective-permute-done.20.refs_1_ = bf16[16,2048]{1,0:T(8,128)(2,1)S(1)} collective-permute-done((bf16[16,2048]{1,0:T(8,128)(2,1)S(1)}, bf16[16,2048]{1,0:T(8,128)(2,1)S(1)}, u32[]{:S(2)}, u32[]{:S(2)}) %collective-permute-start.20) | collective-permute-done | bytes 65568 | tf_op jit(solution)/shard_map/ppermute | solution.py:345
  53.7 3.2 %collective-permute-done.21.refs_2_ = bf16[16,2048]{1,0:T(8,128)(2,1)S(1)} collective-permute-done((bf16[16,2048]{1,0:T(8,128)(2,1)S(1)}, bf16[16,2048]{1,0:T(8,128)(2,1)S(1)}, u32[]{:S(2)}, u32[]{:S(2)}) %collective-permute-start.21) | collective-permute-done | bytes 65568 | tf_op jit(solution)/shard_map/ppermute | solution.py:345
  56.9 0.7 %shard_map.127 = bf16[16,4096]{1,0:T(8,128)(2,1)} custom-call(bf16[16,2048]{1,0:T(8,128)(2,1)S(1)} %get-tuple-element.61.refs_0_, bf16[16,2048]{1,0:T(8,128)(2,1)S(1)} %collective-permute-done.20.refs_1_, bf16[16,2048]{1,0:T(8,128)(2,1)S(1)} %collective-permute-done.21.refs_2_, bf16[16,2048]{1,0:T(8,128)(2,1)S(1)} %collective-permute-done.22.refs_3_, ...), custom_call_target="tpu_custom_call" | custom-call | tf_op jit(solution)/shard_map/pallas_call | solution.py:321
  (25 shorter events, 0.2 us)
Async XLA Ops:
  1.1 7.5 %collective-permute-start.2 = (bf16[144,128]{1,0:T(8,128)(2,1)S(1)}, bf16[144,128]{1,0:T(8,128)(2,1)S(1)}, u32[]{:S(2)}, u32[]{:S(2)}) collective-permute-start(bf16[144,128]{1,0:T(8,128)(2,1)S(1)} %shard_map.109._), channel_id=1, source_target_pairs={{24,0},{16,8},{8,16},{0,24},{25,1},{17,9},{9,17},{1,25},{26,2},{18... | collective-permute-start | bytes 110600 | tf_op jit(solution)/shard_map/ppermute | solution.py:378
  5.1 4.0 %collective-permute-start.1 = (bf16[144,128]{1,0:T(8,128)(2,1)S(1)}, bf16[144,128]{1,0:T(8,128)(2,1)S(1)}, u32[]{:S(2)}, u32[]{:S(2)}) collective-permute-start(bf16[144,128]{1,0:T(8,128)(2,1)S(1)} %shard_map.109._), channel_id=1, source_target_pairs={{16,0},{24,8},{0,16},{8,24},{17,1},{25,9},{1,17},{9,25},{18,2},{26... | collective-permute-start | bytes 110600 | tf_op jit(solution)/shard_map/ppermute | solution.py:378
  5.6 4.0 %collective-permute-start = (bf16[144,128]{1,0:T(8,128)(2,1)S(1)}, bf16[144,128]{1,0:T(8,128)(2,1)S(1)}, u32[]{:S(2)}, u32[]{:S(2)}) collective-permute-start(bf16[144,128]{1,0:T(8,128)(2,1)S(1)} %shard_map.109._), channel_id=1, source_target_pairs={{8,0},{0,8},{24,16},{16,24},{9,1},{1,9},{25,17},{17,25},{10,2},{2,... | collective-permute-start | bytes 110600 | tf_op jit(solution)/shard_map/ppermute | solution.py:378
  10.3 1.6 %collective-permute-start.10 = (bf16[64,2048]{1,0:T(8,128)(2,1)S(1)}, bf16[64,2048]{1,0:T(8,128)(2,1)S(1)}, u32[]{:S(2)}, u32[]{:S(2)}) collective-permute-start(bf16[64,2048]{1,0:T(8,128)(2,1)S(1)} %get-tuple-element.51), channel_id=1, source_target_pairs={{0,1},{1,0},{2,3},{3,2},{4,5},{5,4},{6,7},{7,6},{8,9},{9,8},{10,11... | collective-permute-start | bytes 786440 | tf_op jit(solution)/shard_map/ppermute | solution.py:348
  10.6 6.9 %collective-permute-start.3 = (bf16[64,2048]{1,0:T(8,128)(2,1)S(1)}, bf16[64,2048]{1,0:T(8,128)(2,1)S(1)}, u32[]{:S(2)}, u32[]{:S(2)}) collective-permute-start(bf16[64,2048]{1,0:T(8,128)(2,1)S(1)} %get-tuple-element.45), channel_id=1, source_target_pairs={{0,1},{1,0},{2,3},{3,2},{4,5},{5,4},{6,7},{7,6},{8,9},{9,8},{10,11... | collective-permute-start | bytes 786440 | tf_op jit(solution)/shard_map/ppermute | solution.py:348
  11.9 6.7 %collective-permute-start.11 = (bf16[16,2048]{1,0:T(8,128)(2,1)S(1)}, bf16[16,2048]{1,0:T(8,128)(2,1)S(1)}, u32[]{:S(2)}, u32[]{:S(2)}) collective-permute-start(bf16[16,2048]{1,0:T(8,128)(2,1)S(1)} %get-tuple-element.53), channel_id=1, source_target_pairs={{0,2},{1,3},{2,4},{3,5},{4,6},{5,7},{6,0},{7,1},{8,10},{9,11},{10,... | collective-permute-start | bytes 196616 | tf_op jit(solution)/shard_map/ppermute | solution.py:345
  13.5 7.9 %collective-permute-start.12 = (bf16[16,2048]{1,0:T(8,128)(2,1)S(1)}, bf16[16,2048]{1,0:T(8,128)(2,1)S(1)}, u32[]{:S(2)}, u32[]{:S(2)}) collective-permute-start(bf16[16,2048]{1,0:T(8,128)(2,1)S(1)} %get-tuple-element.54), channel_id=1, source_target_pairs={{0,4},{1,5},{2,6},{3,7},{4,0},{5,1},{6,2},{7,3},{8,12},{9,13},{10,... | collective-permute-start | bytes 196616 | tf_op jit(solution)/shard_map/ppermute | solution.py:345
  16.1 5.3 %collective-permute-start.13 = (bf16[16,2048]{1,0:T(8,128)(2,1)S(1)}, bf16[16,2048]{1,0:T(8,128)(2,1)S(1)}, u32[]{:S(2)}, u32[]{:S(2)}) collective-permute-start(bf16[16,2048]{1,0:T(8,128)(2,1)S(1)} %get-tuple-element.55), channel_id=1, source_target_pairs={{0,6},{1,7},{2,0},{3,1},{4,2},{5,3},{6,4},{7,5},{8,14},{9,15},{10,... | collective-permute-start | bytes 196616 | tf_op jit(solution)/shard_map/ppermute | solution.py:345
  17.6 8.2 %collective-permute-start.4 = (bf16[16,2048]{1,0:T(8,128)(2,1)S(1)}, bf16[16,2048]{1,0:T(8,128)(2,1)S(1)}, u32[]{:S(2)}, u32[]{:S(2)}) collective-permute-start(bf16[16,2048]{1,0:T(8,128)(2,1)S(1)} %get-tuple-element.47), channel_id=1, source_target_pairs={{0,2},{1,3},{2,4},{3,5},{4,6},{5,7},{6,0},{7,1},{8,10},{9,11},{10,... | collective-permute-start | bytes 196616 | tf_op jit(solution)/shard_map/ppermute | solution.py:345
  18.3 9.9 %collective-permute-start.5 = (bf16[16,2048]{1,0:T(8,128)(2,1)S(1)}, bf16[16,2048]{1,0:T(8,128)(2,1)S(1)}, u32[]{:S(2)}, u32[]{:S(2)}) collective-permute-start(bf16[16,2048]{1,0:T(8,128)(2,1)S(1)} %get-tuple-element.48), channel_id=1, source_target_pairs={{0,4},{1,5},{2,6},{3,7},{4,0},{5,1},{6,2},{7,3},{8,12},{9,13},{10,... | collective-permute-start | bytes 196616 | tf_op jit(solution)/shard_map/ppermute | solution.py:345
  18.6 9.6 %collective-permute-start.6 = (bf16[16,2048]{1,0:T(8,128)(2,1)S(1)}, bf16[16,2048]{1,0:T(8,128)(2,1)S(1)}, u32[]{:S(2)}, u32[]{:S(2)}) collective-permute-start(bf16[16,2048]{1,0:T(8,128)(2,1)S(1)} %get-tuple-element.49), channel_id=1, source_target_pairs={{0,6},{1,7},{2,0},{3,1},{4,2},{5,3},{6,4},{7,5},{8,14},{9,15},{10,... | collective-permute-start | bytes 196616 | tf_op jit(solution)/shard_map/ppermute | solution.py:345
  21.5 9.4 %collective-permute-start.16 = (bf16[16,2048]{1,0:T(8,128)(2,1)S(1)}, bf16[16,2048]{1,0:T(8,128)(2,1)S(1)}, u32[]{:S(2)}, u32[]{:S(2)}) collective-permute-start(bf16[16,2048]{1,0:T(8,128)(2,1)S(1)} %shard_map.117.refs_0_.refs_4_), channel_id=1, source_target_pairs={{0,2},{1,3},{2,4},{3,5},{4,6},{5,7},{6,0},{7,1},{8,10},{9,11},{10,... | collective-permute-start | bytes 196616 | tf_op jit(solution)/shard_map/ppermute | solution.py:345
  25.7 7.6 %collective-permute-start.15 = (bf16[16,2048]{1,0:T(8,128)(2,1)S(1)}, bf16[16,2048]{1,0:T(8,128)(2,1)S(1)}, u32[]{:S(2)}, u32[]{:S(2)}) collective-permute-start(bf16[16,2048]{1,0:T(8,128)(2,1)S(1)} %shard_map.117.refs_0_.refs_4_), channel_id=1, source_target_pairs={{0,4},{1,5},{2,6},{3,7},{4,0},{5,1},{6,2},{7,3},{8,12},{9,13},{10,... | collective-permute-start | bytes 196616 | tf_op jit(solution)/shard_map/ppermute | solution.py:345
  25.7 7.6 %collective-permute-start.14 = (bf16[16,2048]{1,0:T(8,128)(2,1)S(1)}, bf16[16,2048]{1,0:T(8,128)(2,1)S(1)}, u32[]{:S(2)}, u32[]{:S(2)}) collective-permute-start(bf16[16,2048]{1,0:T(8,128)(2,1)S(1)} %shard_map.117.refs_0_.refs_4_), channel_id=1, source_target_pairs={{0,6},{1,7},{2,0},{3,1},{4,2},{5,3},{6,4},{7,5},{8,14},{9,15},{10,... | collective-permute-start | bytes 196616 | tf_op jit(solution)/shard_map/ppermute | solution.py:345
  28.2 6.9 %collective-permute-start.9 = (bf16[16,2048]{1,0:T(8,128)(2,1)S(1)}, bf16[16,2048]{1,0:T(8,128)(2,1)S(1)}, u32[]{:S(2)}, u32[]{:S(2)}) collective-permute-start(bf16[16,2048]{1,0:T(8,128)(2,1)S(1)} %shard_map.114.refs_0_.refs_9_), channel_id=1, source_target_pairs={{0,2},{1,3},{2,4},{3,5},{4,6},{5,7},{6,0},{7,1},{8,10},{9,11},{10,... | collective-permute-start | bytes 196616 | tf_op jit(solution)/shard_map/ppermute | solution.py:345
  30.9 6.8 %collective-permute-start.8 = (bf16[16,2048]{1,0:T(8,128)(2,1)S(1)}, bf16[16,2048]{1,0:T(8,128)(2,1)S(1)}, u32[]{:S(2)}, u32[]{:S(2)}) collective-permute-start(bf16[16,2048]{1,0:T(8,128)(2,1)S(1)} %shard_map.114.refs_0_.refs_9_), channel_id=1, source_target_pairs={{0,4},{1,5},{2,6},{3,7},{4,0},{5,1},{6,2},{7,3},{8,12},{9,13},{10,... | collective-permute-start | bytes 196616 | tf_op jit(solution)/shard_map/ppermute | solution.py:345
  30.9 6.8 %collective-permute-start.7 = (bf16[16,2048]{1,0:T(8,128)(2,1)S(1)}, bf16[16,2048]{1,0:T(8,128)(2,1)S(1)}, u32[]{:S(2)}, u32[]{:S(2)}) collective-permute-start(bf16[16,2048]{1,0:T(8,128)(2,1)S(1)} %shard_map.114.refs_0_.refs_9_), channel_id=1, source_target_pairs={{0,6},{1,7},{2,0},{3,1},{4,2},{5,3},{6,4},{7,5},{8,14},{9,15},{10,... | collective-permute-start | bytes 196616 | tf_op jit(solution)/shard_map/ppermute | solution.py:345
  33.4 4.4 %collective-permute-start.18 = (bf16[64,2048]{1,0:T(8,128)(2,1)S(1)}, bf16[64,2048]{1,0:T(8,128)(2,1)S(1)}, u32[]{:S(2)}, u32[]{:S(2)}) collective-permute-start(bf16[64,2048]{1,0:T(8,128)(2,1)S(1)} %shard_map.118._.own_ref), channel_id=1, source_target_pairs={{0,1},{1,0},{2,3},{3,2},{4,5},{5,4},{6,7},{7,6},{8,9},{9,8},{10,11... | collective-permute-start | bytes 786440 | tf_op jit(solution)/shard_map/ppermute | solution.py:348
  37.7 1.6 %collective-permute-start.17 = (bf16[64,2048]{1,0:T(8,128)(2,1)S(1)}, bf16[64,2048]{1,0:T(8,128)(2,1)S(1)}, u32[]{:S(2)}, u32[]{:S(2)}) collective-permute-start(bf16[64,2048]{1,0:T(8,128)(2,1)S(1)} %shard_map.120.own_ref), channel_id=1, source_target_pairs={{0,1},{1,0},{2,3},{3,2},{4,5},{5,4},{6,7},{7,6},{8,9},{9,8},{10,11... | collective-permute-start | bytes 786440 | tf_op jit(solution)/shard_map/ppermute | solution.py:348
  40.7 1.6 %collective-permute-start.23 = (bf16[64,2048]{1,0:T(8,128)(2,1)S(1)}, bf16[64,2048]{1,0:T(8,128)(2,1)S(1)}, u32[]{:S(2)}, u32[]{:S(2)}) collective-permute-start(bf16[64,2048]{1,0:T(8,128)(2,1)S(1)} %get-tuple-element.66), channel_id=1, source_target_pairs={{0,1},{1,0},{2,3},{3,2},{4,5},{5,4},{6,7},{7,6},{8,9},{9,8},{10,11... | collective-permute-start | bytes 786440 | tf_op jit(solution)/shard_map/ppermute | solution.py:348
  41.4 5.4 %collective-permute-start.19 = (bf16[64,2048]{1,0:T(8,128)(2,1)S(1)}, bf16[64,2048]{1,0:T(8,128)(2,1)S(1)}, u32[]{:S(2)}, u32[]{:S(2)}) collective-permute-start(bf16[64,2048]{1,0:T(8,128)(2,1)S(1)} %get-tuple-element.60), channel_id=1, source_target_pairs={{0,1},{1,0},{2,3},{3,2},{4,5},{5,4},{6,7},{7,6},{8,9},{9,8},{10,11... | collective-permute-start | bytes 786440 | tf_op jit(solution)/shard_map/ppermute | solution.py:348
  42.4 7.0 %collective-permute-start.24 = (bf16[16,2048]{1,0:T(8,128)(2,1)S(1)}, bf16[16,2048]{1,0:T(8,128)(2,1)S(1)}, u32[]{:S(2)}, u32[]{:S(2)}) collective-permute-start(bf16[16,2048]{1,0:T(8,128)(2,1)S(1)} %get-tuple-element.68), channel_id=1, source_target_pairs={{0,2},{1,3},{2,4},{3,5},{4,6},{5,7},{6,0},{7,1},{8,10},{9,11},{10,... | collective-permute-start | bytes 196616 | tf_op jit(solution)/shard_map/ppermute | solution.py:345
  44.3 8.8 %collective-permute-start.25 = (bf16[16,2048]{1,0:T(8,128)(2,1)S(1)}, bf16[16,2048]{1,0:T(8,128)(2,1)S(1)}, u32[]{:S(2)}, u32[]{:S(2)}) collective-permute-start(bf16[16,2048]{1,0:T(8,128)(2,1)S(1)} %get-tuple-element.69), channel_id=1, source_target_pairs={{0,4},{1,5},{2,6},{3,7},{4,0},{5,1},{6,2},{7,3},{8,12},{9,13},{10,... | collective-permute-start | bytes 196616 | tf_op jit(solution)/shard_map/ppermute | solution.py:345
  46.1 7.0 %collective-permute-start.26 = (bf16[16,2048]{1,0:T(8,128)(2,1)S(1)}, bf16[16,2048]{1,0:T(8,128)(2,1)S(1)}, u32[]{:S(2)}, u32[]{:S(2)}) collective-permute-start(bf16[16,2048]{1,0:T(8,128)(2,1)S(1)} %get-tuple-element.70), channel_id=1, source_target_pairs={{0,6},{1,7},{2,0},{3,1},{4,2},{5,3},{6,4},{7,5},{8,14},{9,15},{10,... | collective-permute-start | bytes 196616 | tf_op jit(solution)/shard_map/ppermute | solution.py:345
  46.8 6.9 %collective-permute-start.20 = (bf16[16,2048]{1,0:T(8,128)(2,1)S(1)}, bf16[16,2048]{1,0:T(8,128)(2,1)S(1)}, u32[]{:S(2)}, u32[]{:S(2)}) collective-permute-start(bf16[16,2048]{1,0:T(8,128)(2,1)S(1)} %get-tuple-element.62), channel_id=1, source_target_pairs={{0,2},{1,3},{2,4},{3,5},{4,6},{5,7},{6,0},{7,1},{8,10},{9,11},{10,... | collective-permute-start | bytes 196616 | tf_op jit(solution)/shard_map/ppermute | solution.py:345
  48.2 8.7 %collective-permute-start.21 = (bf16[16,2048]{1,0:T(8,128)(2,1)S(1)}, bf16[16,2048]{1,0:T(8,128)(2,1)S(1)}, u32[]{:S(2)}, u32[]{:S(2)}) collective-permute-start(bf16[16,2048]{1,0:T(8,128)(2,1)S(1)} %get-tuple-element.63), channel_id=1, source_target_pairs={{0,4},{1,5},{2,6},{3,7},{4,0},{5,1},{6,2},{7,3},{8,12},{9,13},{10,... | collective-permute-start | bytes 196616 | tf_op jit(solution)/shard_map/ppermute | solution.py:345
  49.4 7.5 %collective-permute-start.22 = (bf16[16,2048]{1,0:T(8,128)(2,1)S(1)}, bf16[16,2048]{1,0:T(8,128)(2,1)S(1)}, u32[]{:S(2)}, u32[]{:S(2)}) collective-permute-start(bf16[16,2048]{1,0:T(8,128)(2,1)S(1)} %get-tuple-element.64), channel_id=1, source_target_pairs={{0,6},{1,7},{2,0},{3,1},{4,2},{5,3},{6,4},{7,5},{8,14},{9,15},{10,... | collective-permute-start | bytes 196616 | tf_op jit(solution)/shard_map/ppermute | solution.py:345

commit v2 on v1

--- a/solution.py
+++ b/solution.py
@@ -216,7 +216,7 @@
     size = 2 * n_pair * rows
     i, j = iota2((size, size), 0), iota2((size, size), 1)
     half, inner = i // (n_pair * rows), i % (n_pair * rows)
-    who = (inner // rows + pair) % n_pair
+    who = jnp.bitwise_xor((n_pair - inner // rows) % n_pair, pair)
     source = (2 * who + (core + half) % 2) * rows + inner % rows
     return jnp.where(source == j, 1.0, 0.0).astype(BF16)
 
@@ -341,8 +341,9 @@
     out = jax.ShapeDtypeStruct
     dma = pltpu.SemaphoreType.DMA
 
-    def shift(x, r):
-        return lax.ppermute(x, "exp", [(e, (e + 2 * r) % exp_count) for e in range(exp_count)])
+    def swap(x, r):
+        flip = 2 * (n_pair - r)
+        return lax.ppermute(x, "exp", [(e, e ^ flip) for e in range(exp_count)])
 
     def across(x):
         return lax.ppermute(x, "exp", [(e, e ^ 1) for e in range(exp_count)])
@@ -359,7 +360,7 @@
             call(functools.partial(add_kernel, [[r] for r in range(n_pair)]), [rows_of(1)] * n_pair, (mine, other))
             for (mine, _), other in zip(products, others)
         ]
-        return [[term[0]] + [shift(term[r], r) for r in range(1, n_pair)] for term in terms]
+        return [[term[0]] + [swap(term[r], r) for r in reversed(range(1, n_pair))] for term in terms]
 
     def products_of(x, w):
         return [call(functools.partial(product_kernel, at), [rows_of(n_pair)] * 2, (x, w)) for at in ranges]
@@ -406,7 +407,7 @@
     )
     terms = reduce(products_of(normed, w_out_near))
     mixed = [call(functools.partial(sum_kernel, n_pair), [rows_of(1)], term)[0] for term in terms]
-    gathered = [[shift(m, -r) if r else m for r in range(n_pair)] for m in mixed]
+    gathered = [[swap(m, r) if r else m for r in range(n_pair)] for m in mixed]
     own, after = [], ()
     for blocks in gathered:
         own += call(functools.partial(join_kernel, n_pair), [rows_of(n_pair)], (*blocks, *after))

time: 57.9 us -> 60.9 us (1.052)
  waiting for transfers between devices: 10.9 us -> 13.9 us
    ppermute x18, waiting for transfers between devices: 8.13 us -> 11.1 us  [swap(): return lax.ppermute(x, 'exp', [(e, e ^ flip) for e in range(exp_count)])]
  transfers between devices with their start and end apart: 27 -> 27, of which waited for: 9 -> 12; matrix products, arithmetic and copies ran while one was open for 0% -> 0% of each run, Pallas kernels for 11% -> 11%
where the time goes in v2:
time: 60.9 us; the launch traced here: 60.7 us
  starting transfers between devices  36.2 us (59%)
  waiting for transfers between devices  13.9 us (23%)
  Pallas kernels  10.4 us (17%)
    ppermute x18, starting transfers between devices, swap(): return lax.ppermute(x, 'exp', [(e, e ^ flip) for e in range(exp_count)])  30.2 us
    ppermute x18, waiting for transfers between devices, swap(): return lax.ppermute(x, 'exp', [(e, e ^ flip) for e in range(exp_count)])  11.1 us
    pallas_call x19, Pallas kernels, call(): pl.pallas_call(kernel, out_shape=outs, in_specs=[pl.BlockSpec(memory_spac...  10.4 us
    ppermute x3, starting transfers between devices, local(): lax.ppermute(state, 'seq', [(move(i), i) for i in range(seq_count)])  4.6 us
    ppermute x6, waiting for transfers between devices, across(): return lax.ppermute(x, 'exp', [(e, e ^ 1) for e in range(exp_count)])  1.91 us
    ppermute x6, starting transfers between devices, across(): return lax.ppermute(x, 'exp', [(e, e ^ 1) for e in range(exp_count)])  1.41 us
  transfers between devices with their start and end apart: 27, of which 12 were waited for; matrix products, arithmetic and copies ran while one was open for 0% of the time, Pallas kernels for 11%

profile of v2, /device:TPU:0, one launch (start us, length us, event | category | flops | bytes accessed | tf_op | source)
XLA Modules:
  0.0 60.7 jit_solution(15545686851905613206)
XLA Ops:
  0.0 1.1 %shard_map.109._ = bf16[144,128]{1,0:T(8,128)(2,1)S(1)} custom-call(bf16[128,128]{1,0:T(8,128)(2,1)} %key_hbm.3, bf16[128,128]{1,0:T(8,128)(2,1)} %value_hbm.3, f32[1,128]{1,0:T(1,128)} %bitcast.15), custom_call_target="tpu_custom_call" | custom-call | tf_op jit(solution)/shard_map/pallas_call | solution.py:321
  1.1 4.0 %collective-permute-start.2 = (bf16[144,128]{1,0:T(8,128)(2,1)S(1)}, bf16[144,128]{1,0:T(8,128)(2,1)S(1)}, u32[]{:S(2)}, u32[]{:S(2)}) collective-permute-start(bf16[144,128]{1,0:T(8,128)(2,1)S(1)} %shard_map.109._), channel_id=1, source_target_pairs={{24,0},{16,8},{8,16},{0,24},{25,1},{17,9},{9,17},{1,25},{26,2},{18... | collective-permute-start | bytes 110600 | tf_op jit(solution)/shard_map/ppermute | solution.py:379
  5.1 0.5 collective-permute-start.1
  5.6 0.1 collective-permute-start
  5.7 2.9 %shard_map.110 = (f32[128,128]{1,0:T(8,128)S(1)}, f32[128,128]{1,0:T(8,128)S(1)}, bf16[128,128]{1,0:T(8,128)(2,1)S(1)}, f32[8,128]{1,0:T(8,128)S(1)}, bf16[128,4...) custom-call(bf16[128,128]{1,0:T(8,128)(2,1)} %query_hbm.1, bf16[128,128]{1,0:T(8,128)(2,1)} %key_hbm.3, ...), custom_call_target="tpu_custom_call" | custom-call | tf_op jit(solution)/shard_map/pallas_call | solution.py:321
  8.6 0.4 collective-permute-done.1.refs_1_
  9.0 0.5 collective-permute-done.refs_0_
  9.5 0.4 shard_map.111.x_ref
  10.0 0.3 shard_map.115
  10.3 0.3 shard_map.112
  10.6 0.6 collective-permute-start.3
  11.2 0.7 %collective-permute-done.10.b_ref = bf16[64,2048]{1,0:T(8,128)(2,1)S(1)} collective-permute-done((bf16[64,2048]{1,0:T(8,128)(2,1)S(1)}, bf16[64,2048]{1,0:T(8,128)(2,1)S(1)}, u32[]{:S(2)}, u32[]{:S(2)}) %collective-permute-start.10) | collective-permute-done | bytes 262176 | tf_op jit(solution)/shard_map/ppermute | solution.py:349
  11.9 1.6 %collective-permute-start.11 = (bf16[16,2048]{1,0:T(8,128)(2,1)S(1)}, bf16[16,2048]{1,0:T(8,128)(2,1)S(1)}, u32[]{:S(2)}, u32[]{:S(2)}) collective-permute-start(bf16[16,2048]{1,0:T(8,128)(2,1)S(1)} %get-tuple-element.53), channel_id=1, source_target_pairs={{0,2},{1,3},{2,0},{3,1},{4,6},{5,7},{6,4},{7,5},{8,10},{9,11},{10,... | collective-permute-start | bytes 196616 | tf_op jit(solution)/shard_map/ppermute | solution.py:346
  13.6 2.6 %collective-permute-start.12 = (bf16[16,2048]{1,0:T(8,128)(2,1)S(1)}, bf16[16,2048]{1,0:T(8,128)(2,1)S(1)}, u32[]{:S(2)}, u32[]{:S(2)}) collective-permute-start(bf16[16,2048]{1,0:T(8,128)(2,1)S(1)} %get-tuple-element.54), channel_id=1, source_target_pairs={{0,4},{1,5},{2,6},{3,7},{4,0},{5,1},{6,2},{7,3},{8,12},{9,13},{10,... | collective-permute-start | bytes 196616 | tf_op jit(solution)/shard_map/ppermute | solution.py:346
  16.1 0.2 collective-permute-start.13
  16.4 0.7 %collective-permute-start.4 = (bf16[16,2048]{1,0:T(8,128)(2,1)S(1)}, bf16[16,2048]{1,0:T(8,128)(2,1)S(1)}, u32[]{:S(2)}, u32[]{:S(2)}) collective-permute-start(bf16[16,2048]{1,0:T(8,128)(2,1)S(1)} %get-tuple-element.47), channel_id=1, source_target_pairs={{0,2},{1,3},{2,0},{3,1},{4,6},{5,7},{6,4},{7,5},{8,10},{9,11},{10,... | collective-permute-start | bytes 196616 | tf_op jit(solution)/shard_map/ppermute | solution.py:346
  17.2 3.5 %collective-permute-start.5 = (bf16[16,2048]{1,0:T(8,128)(2,1)S(1)}, bf16[16,2048]{1,0:T(8,128)(2,1)S(1)}, u32[]{:S(2)}, u32[]{:S(2)}) collective-permute-start(bf16[16,2048]{1,0:T(8,128)(2,1)S(1)} %get-tuple-element.48), channel_id=1, source_target_pairs={{0,4},{1,5},{2,6},{3,7},{4,0},{5,1},{6,2},{7,3},{8,12},{9,13},{10,... | collective-permute-start | bytes 196616 | tf_op jit(solution)/shard_map/ppermute | solution.py:346
  20.7 0.2 collective-permute-start.6
  20.9 0.2 collective-permute-done.12.refs_2_
  21.1 1.9 %collective-permute-done.13.refs_3_ = bf16[16,2048]{1,0:T(8,128)(2,1)S(1)} collective-permute-done((bf16[16,2048]{1,0:T(8,128)(2,1)S(1)}, bf16[16,2048]{1,0:T(8,128)(2,1)S(1)}, u32[]{:S(2)}, u32[]{:S(2)}) %collective-permute-start.13) | collective-permute-done | bytes 65568 | tf_op jit(solution)/shard_map/ppermute | solution.py:346
  23.1 4.4 %collective-permute-start.16 = (bf16[16,2048]{1,0:T(8,128)(2,1)S(1)}, bf16[16,2048]{1,0:T(8,128)(2,1)S(1)}, u32[]{:S(2)}, u32[]{:S(2)}) collective-permute-start(bf16[16,2048]{1,0:T(8,128)(2,1)S(1)} %shard_map.117.refs_0_.refs_4_), channel_id=1, source_target_pairs={{0,2},{1,3},{2,0},{3,1},{4,6},{5,7},{6,4},{7,5},{8,10},{9,11},{10,... | collective-permute-start | bytes 196616 | tf_op jit(solution)/shard_map/ppermute | solution.py:346
  27.5 2.1 %collective-permute-start.15 = (bf16[16,2048]{1,0:T(8,128)(2,1)S(1)}, bf16[16,2048]{1,0:T(8,128)(2,1)S(1)}, u32[]{:S(2)}, u32[]{:S(2)}) collective-permute-start(bf16[16,2048]{1,0:T(8,128)(2,1)S(1)} %shard_map.117.refs_0_.refs_4_), channel_id=1, source_target_pairs={{0,4},{1,5},{2,6},{3,7},{4,0},{5,1},{6,2},{7,3},{8,12},{9,13},{10,... | collective-permute-start | bytes 196616 | tf_op jit(solution)/shard_map/ppermute | solution.py:346
  29.6 1.4 %collective-permute-start.14 = (bf16[16,2048]{1,0:T(8,128)(2,1)S(1)}, bf16[16,2048]{1,0:T(8,128)(2,1)S(1)}, u32[]{:S(2)}, u32[]{:S(2)}) collective-permute-start(bf16[16,2048]{1,0:T(8,128)(2,1)S(1)} %shard_map.117.refs_0_.refs_4_), channel_id=1, source_target_pairs={{0,6},{1,7},{2,4},{3,5},{4,2},{5,3},{6,0},{7,1},{8,14},{9,15},{10,... | collective-permute-start | bytes 196616 | tf_op jit(solution)/shard_map/ppermute | solution.py:346
  31.0 0.6 %collective-permute-start.9 = (bf16[16,2048]{1,0:T(8,128)(2,1)S(1)}, bf16[16,2048]{1,0:T(8,128)(2,1)S(1)}, u32[]{:S(2)}, u32[]{:S(2)}) collective-permute-start(bf16[16,2048]{1,0:T(8,128)(2,1)S(1)} %shard_map.114.refs_0_.refs_9_), channel_id=1, source_target_pairs={{0,2},{1,3},{2,0},{3,1},{4,6},{5,7},{6,4},{7,5},{8,10},{9,11},{10,... | collective-permute-start | bytes 196616 | tf_op jit(solution)/shard_map/ppermute | solution.py:346
  31.7 2.4 %collective-permute-start.8 = (bf16[16,2048]{1,0:T(8,128)(2,1)S(1)}, bf16[16,2048]{1,0:T(8,128)(2,1)S(1)}, u32[]{:S(2)}, u32[]{:S(2)}) collective-permute-start(bf16[16,2048]{1,0:T(8,128)(2,1)S(1)} %shard_map.114.refs_0_.refs_9_), channel_id=1, source_target_pairs={{0,4},{1,5},{2,6},{3,7},{4,0},{5,1},{6,2},{7,3},{8,12},{9,13},{10,... | collective-permute-start | bytes 196616 | tf_op jit(solution)/shard_map/ppermute | solution.py:346
  34.1 1.4 %collective-permute-start.7 = (bf16[16,2048]{1,0:T(8,128)(2,1)S(1)}, bf16[16,2048]{1,0:T(8,128)(2,1)S(1)}, u32[]{:S(2)}, u32[]{:S(2)}) collective-permute-start(bf16[16,2048]{1,0:T(8,128)(2,1)S(1)} %shard_map.114.refs_0_.refs_9_), channel_id=1, source_target_pairs={{0,6},{1,7},{2,4},{3,5},{4,2},{5,3},{6,0},{7,1},{8,14},{9,15},{10,... | collective-permute-start | bytes 196616 | tf_op jit(solution)/shard_map/ppermute | solution.py:346
  35.5 0.9 %collective-permute-done.14.refs_1_ = bf16[16,2048]{1,0:T(8,128)(2,1)S(1)} collective-permute-done((bf16[16,2048]{1,0:T(8,128)(2,1)S(1)}, bf16[16,2048]{1,0:T(8,128)(2,1)S(1)}, u32[]{:S(2)}, u32[]{:S(2)}) %collective-permute-start.14) | collective-permute-done | bytes 65568 | tf_op jit(solution)/shard_map/ppermute | solution.py:346
  36.4 0.1 collective-permute-start.18
  36.5 1.7 %shard_map.119 = (bf16[288,4096]{1,0:T(8,128)(2,1)S(1)}, f32[8,128]{1,0:T(8,128)S(1)}) custom-call(bf16[288,4096]{1,0:T(8,128)(2,1)} %bitcast.13, bf16[64,2048]{1,0:T(8,128)(2,1)S(1)} %shard_map.118._.own_ref), custom_call_target="tpu_custom_call" | custom-call | tf_op jit(solution)/shard_map/pallas_call | solution.py:321
  38.2 1.1 %collective-permute-done.8.refs_2_ = bf16[16,2048]{1,0:T(8,128)(2,1)S(1)} collective-permute-done((bf16[16,2048]{1,0:T(8,128)(2,1)S(1)}, bf16[16,2048]{1,0:T(8,128)(2,1)S(1)}, u32[]{:S(2)}, u32[]{:S(2)}) %collective-permute-start.8) | collective-permute-done | bytes 65568 | tf_op jit(solution)/shard_map/ppermute | solution.py:346
  39.3 1.0 %collective-permute-done.7.refs_1_ = bf16[16,2048]{1,0:T(8,128)(2,1)S(1)} collective-permute-done((bf16[16,2048]{1,0:T(8,128)(2,1)S(1)}, bf16[16,2048]{1,0:T(8,128)(2,1)S(1)}, u32[]{:S(2)}, u32[]{:S(2)}) %collective-permute-start.7) | collective-permute-done | bytes 65568 | tf_op jit(solution)/shard_map/ppermute | solution.py:346
  40.4 0.8 %shard_map.121.before_ref = f32[592,128]{1,0:T(8,128)S(1)} custom-call(bf16[592,4096]{1,0:T(8,128)(2,1)S(1)} %get-tuple-element.38.in_ref, bf16[64,2048]{1,0:T(8,128)(2,1)S(1)} %shard_map.118._.own_ref, bf16[64,2048]{1,0:T(8,128)(2,1)S(1)} %collective-permute-done.18.other_ref), custom_call_target="tpu_custom_call" | custom-call | tf_op jit(solution)/shard_map/pallas_call | solution.py:321
  41.2 0.7 %collective-permute-done.17.other_ref = bf16[64,2048]{1,0:T(8,128)(2,1)S(1)} collective-permute-done((bf16[64,2048]{1,0:T(8,128)(2,1)S(1)}, bf16[64,2048]{1,0:T(8,128)(2,1)S(1)}, u32[]{:S(2)}, u32[]{:S(2)}) %collective-permute-start.17) | collective-permute-done | bytes 262176 | tf_op jit(solution)/shard_map/ppermute | solution.py:349
  41.9 0.9 %shard_map.122.x_ref = bf16[128,288]{1,0:T(8,128)(2,1)S(1)} custom-call(bf16[592,4096]{1,0:T(8,128)(2,1)S(1)} %get-tuple-element.38.in_ref, bf16[64,2048]{1,0:T(8,128)(2,1)S(1)} %shard_map.120.own_ref, bf16[64,2048]{1,0:T(8,128)(2,1)S(1)} %collective-permute-done.17.other_ref, f32[592,128]{1,0:T(8,128)S(1)} %shard_map.121.before_ref, ...), custom_call_target="tpu_custom_call" | custom-call | tf_op jit(solution)/shard_map/pallas_call | solution.py:321
  42.8 0.4 shard_map.125
  43.3 0.2 collective-permute-start.23
  43.5 0.4 shard_map.123
  43.9 0.4 collective-permute-start.19
  44.4 0.5 collective-permute-done.23.b_ref
  44.9 1.1 %collective-permute-start.24 = (bf16[16,2048]{1,0:T(8,128)(2,1)S(1)}, bf16[16,2048]{1,0:T(8,128)(2,1)S(1)}, u32[]{:S(2)}, u32[]{:S(2)}) collective-permute-start(bf16[16,2048]{1,0:T(8,128)(2,1)S(1)} %get-tuple-element.68), channel_id=1, source_target_pairs={{0,2},{1,3},{2,0},{3,1},{4,6},{5,7},{6,4},{7,5},{8,10},{9,11},{10,... | collective-permute-start | bytes 196616 | tf_op jit(solution)/shard_map/ppermute | solution.py:346
  46.0 1.6 %collective-permute-start.25 = (bf16[16,2048]{1,0:T(8,128)(2,1)S(1)}, bf16[16,2048]{1,0:T(8,128)(2,1)S(1)}, u32[]{:S(2)}, u32[]{:S(2)}) collective-permute-start(bf16[16,2048]{1,0:T(8,128)(2,1)S(1)} %get-tuple-element.69), channel_id=1, source_target_pairs={{0,4},{1,5},{2,6},{3,7},{4,0},{5,1},{6,2},{7,3},{8,12},{9,13},{10,... | collective-permute-start | bytes 196616 | tf_op jit(solution)/shard_map/ppermute | solution.py:346
  47.7 1.7 %collective-permute-start.26 = (bf16[16,2048]{1,0:T(8,128)(2,1)S(1)}, bf16[16,2048]{1,0:T(8,128)(2,1)S(1)}, u32[]{:S(2)}, u32[]{:S(2)}) collective-permute-start(bf16[16,2048]{1,0:T(8,128)(2,1)S(1)} %get-tuple-element.70), channel_id=1, source_target_pairs={{0,6},{1,7},{2,4},{3,5},{4,2},{5,3},{6,0},{7,1},{8,14},{9,15},{10,... | collective-permute-start | bytes 196616 | tf_op jit(solution)/shard_map/ppermute | solution.py:346
  49.5 0.2 collective-permute-start.20
  49.7 2.5 %collective-permute-start.21 = (bf16[16,2048]{1,0:T(8,128)(2,1)S(1)}, bf16[16,2048]{1,0:T(8,128)(2,1)S(1)}, u32[]{:S(2)}, u32[]{:S(2)}) collective-permute-start(bf16[16,2048]{1,0:T(8,128)(2,1)S(1)} %get-tuple-element.63), channel_id=1, source_target_pairs={{0,4},{1,5},{2,6},{3,7},{4,0},{5,1},{6,2},{7,3},{8,12},{9,13},{10,... | collective-permute-start | bytes 196616 | tf_op jit(solution)/shard_map/ppermute | solution.py:346
  52.2 1.7 %collective-permute-start.22 = (bf16[16,2048]{1,0:T(8,128)(2,1)S(1)}, bf16[16,2048]{1,0:T(8,128)(2,1)S(1)}, u32[]{:S(2)}, u32[]{:S(2)}) collective-permute-start(bf16[16,2048]{1,0:T(8,128)(2,1)S(1)} %get-tuple-element.64), channel_id=1, source_target_pairs={{0,6},{1,7},{2,4},{3,5},{4,2},{5,3},{6,0},{7,1},{8,14},{9,15},{10,... | collective-permute-start | bytes 196616 | tf_op jit(solution)/shard_map/ppermute | solution.py:346
  53.9 1.0 %collective-permute-done.25.refs_7_ = bf16[16,2048]{1,0:T(8,128)(2,1)S(1)} collective-permute-done((bf16[16,2048]{1,0:T(8,128)(2,1)S(1)}, bf16[16,2048]{1,0:T(8,128)(2,1)S(1)}, u32[]{:S(2)}, u32[]{:S(2)}) %collective-permute-start.25) | collective-permute-done | bytes 65568 | tf_op jit(solution)/shard_map/ppermute | solution.py:346
  55.0 5.0 %collective-permute-done.21.refs_2_ = bf16[16,2048]{1,0:T(8,128)(2,1)S(1)} collective-permute-done((bf16[16,2048]{1,0:T(8,128)(2,1)S(1)}, bf16[16,2048]{1,0:T(8,128)(2,1)S(1)}, u32[]{:S(2)}, u32[]{:S(2)}) %collective-permute-start.21) | collective-permute-done | bytes 65568 | tf_op jit(solution)/shard_map/ppermute | solution.py:346
  59.9 0.7 %shard_map.127 = bf16[16,4096]{1,0:T(8,128)(2,1)} custom-call(bf16[16,2048]{1,0:T(8,128)(2,1)S(1)} %get-tuple-element.61.refs_0_, bf16[16,2048]{1,0:T(8,128)(2,1)S(1)} %collective-permute-done.20.refs_1_, bf16[16,2048]{1,0:T(8,128)(2,1)S(1)} %collective-permute-done.21.refs_2_, bf16[16,2048]{1,0:T(8,128)(2,1)S(1)} %collective-permute-done.22.refs_3_, ...), custom_call_target="tpu_custom_call" | custom-call | tf_op jit(solution)/shard_map/pallas_call | solution.py:321
  (25 shorter events, 0.5 us)
Async XLA Ops:
  1.1 7.5 %collective-permute-start.2 = (bf16[144,128]{1,0:T(8,128)(2,1)S(1)}, bf16[144,128]{1,0:T(8,128)(2,1)S(1)}, u32[]{:S(2)}, u32[]{:S(2)}) collective-permute-start(bf16[144,128]{1,0:T(8,128)(2,1)S(1)} %shard_map.109._), channel_id=1, source_target_pairs={{24,0},{16,8},{8,16},{0,24},{25,1},{17,9},{9,17},{1,25},{26,2},{18... | collective-permute-start | bytes 110600 | tf_op jit(solution)/shard_map/ppermute | solution.py:379
  5.1 4.0 %collective-permute-start.1 = (bf16[144,128]{1,0:T(8,128)(2,1)S(1)}, bf16[144,128]{1,0:T(8,128)(2,1)S(1)}, u32[]{:S(2)}, u32[]{:S(2)}) collective-permute-start(bf16[144,128]{1,0:T(8,128)(2,1)S(1)} %shard_map.109._), channel_id=1, source_target_pairs={{16,0},{24,8},{0,16},{8,24},{17,1},{25,9},{1,17},{9,25},{18,2},{26... | collective-permute-start | bytes 110600 | tf_op jit(solution)/shard_map/ppermute | solution.py:379
  5.6 4.0 %collective-permute-start = (bf16[144,128]{1,0:T(8,128)(2,1)S(1)}, bf16[144,128]{1,0:T(8,128)(2,1)S(1)}, u32[]{:S(2)}, u32[]{:S(2)}) collective-permute-start(bf16[144,128]{1,0:T(8,128)(2,1)S(1)} %shard_map.109._), channel_id=1, source_target_pairs={{8,0},{0,8},{24,16},{16,24},{9,1},{1,9},{25,17},{17,25},{10,2},{2,... | collective-permute-start | bytes 110600 | tf_op jit(solution)/shard_map/ppermute | solution.py:379
  10.3 1.6 %collective-permute-start.10 = (bf16[64,2048]{1,0:T(8,128)(2,1)S(1)}, bf16[64,2048]{1,0:T(8,128)(2,1)S(1)}, u32[]{:S(2)}, u32[]{:S(2)}) collective-permute-start(bf16[64,2048]{1,0:T(8,128)(2,1)S(1)} %get-tuple-element.51), channel_id=1, source_target_pairs={{0,1},{1,0},{2,3},{3,2},{4,5},{5,4},{6,7},{7,6},{8,9},{9,8},{10,11... | collective-permute-start | bytes 786440 | tf_op jit(solution)/shard_map/ppermute | solution.py:349
  10.6 5.8 %collective-permute-start.3 = (bf16[64,2048]{1,0:T(8,128)(2,1)S(1)}, bf16[64,2048]{1,0:T(8,128)(2,1)S(1)}, u32[]{:S(2)}, u32[]{:S(2)}) collective-permute-start(bf16[64,2048]{1,0:T(8,128)(2,1)S(1)} %get-tuple-element.45), channel_id=1, source_target_pairs={{0,1},{1,0},{2,3},{3,2},{4,5},{5,4},{6,7},{7,6},{8,9},{9,8},{10,11... | collective-permute-start | bytes 786440 | tf_op jit(solution)/shard_map/ppermute | solution.py:349
  11.9 8.8 %collective-permute-start.11 = (bf16[16,2048]{1,0:T(8,128)(2,1)S(1)}, bf16[16,2048]{1,0:T(8,128)(2,1)S(1)}, u32[]{:S(2)}, u32[]{:S(2)}) collective-permute-start(bf16[16,2048]{1,0:T(8,128)(2,1)S(1)} %get-tuple-element.53), channel_id=1, source_target_pairs={{0,2},{1,3},{2,0},{3,1},{4,6},{5,7},{6,4},{7,5},{8,10},{9,11},{10,... | collective-permute-start | bytes 196616 | tf_op jit(solution)/shard_map/ppermute | solution.py:346
  13.6 7.5 %collective-permute-start.12 = (bf16[16,2048]{1,0:T(8,128)(2,1)S(1)}, bf16[16,2048]{1,0:T(8,128)(2,1)S(1)}, u32[]{:S(2)}, u32[]{:S(2)}) collective-permute-start(bf16[16,2048]{1,0:T(8,128)(2,1)S(1)} %get-tuple-element.54), channel_id=1, source_target_pairs={{0,4},{1,5},{2,6},{3,7},{4,0},{5,1},{6,2},{7,3},{8,12},{9,13},{10,... | collective-permute-start | bytes 196616 | tf_op jit(solution)/shard_map/ppermute | solution.py:346
  16.1 6.9 %collective-permute-start.13 = (bf16[16,2048]{1,0:T(8,128)(2,1)S(1)}, bf16[16,2048]{1,0:T(8,128)(2,1)S(1)}, u32[]{:S(2)}, u32[]{:S(2)}) collective-permute-start(bf16[16,2048]{1,0:T(8,128)(2,1)S(1)} %get-tuple-element.55), channel_id=1, source_target_pairs={{0,6},{1,7},{2,4},{3,5},{4,2},{5,3},{6,0},{7,1},{8,14},{9,15},{10,... | collective-permute-start | bytes 196616 | tf_op jit(solution)/shard_map/ppermute | solution.py:346
  16.4 13.2 %collective-permute-start.4 = (bf16[16,2048]{1,0:T(8,128)(2,1)S(1)}, bf16[16,2048]{1,0:T(8,128)(2,1)S(1)}, u32[]{:S(2)}, u32[]{:S(2)}) collective-permute-start(bf16[16,2048]{1,0:T(8,128)(2,1)S(1)} %get-tuple-element.47), channel_id=1, source_target_pairs={{0,2},{1,3},{2,0},{3,1},{4,6},{5,7},{6,4},{7,5},{8,10},{9,11},{10,... | collective-permute-start | bytes 196616 | tf_op jit(solution)/shard_map/ppermute | solution.py:346
  17.2 13.8 %collective-permute-start.5 = (bf16[16,2048]{1,0:T(8,128)(2,1)S(1)}, bf16[16,2048]{1,0:T(8,128)(2,1)S(1)}, u32[]{:S(2)}, u32[]{:S(2)}) collective-permute-start(bf16[16,2048]{1,0:T(8,128)(2,1)S(1)} %get-tuple-element.48), channel_id=1, source_target_pairs={{0,4},{1,5},{2,6},{3,7},{4,0},{5,1},{6,2},{7,3},{8,12},{9,13},{10,... | collective-permute-start | bytes 196616 | tf_op jit(solution)/shard_map/ppermute | solution.py:346
  20.7 10.3 %collective-permute-start.6 = (bf16[16,2048]{1,0:T(8,128)(2,1)S(1)}, bf16[16,2048]{1,0:T(8,128)(2,1)S(1)}, u32[]{:S(2)}, u32[]{:S(2)}) collective-permute-start(bf16[16,2048]{1,0:T(8,128)(2,1)S(1)} %get-tuple-element.49), channel_id=1, source_target_pairs={{0,6},{1,7},{2,4},{3,5},{4,2},{5,3},{6,0},{7,1},{8,14},{9,15},{10,... | collective-permute-start | bytes 196616 | tf_op jit(solution)/shard_map/ppermute | solution.py:346
  23.1 11.1 %collective-permute-start.16 = (bf16[16,2048]{1,0:T(8,128)(2,1)S(1)}, bf16[16,2048]{1,0:T(8,128)(2,1)S(1)}, u32[]{:S(2)}, u32[]{:S(2)}) collective-permute-start(bf16[16,2048]{1,0:T(8,128)(2,1)S(1)} %shard_map.117.refs_0_.refs_4_), channel_id=1, source_target_pairs={{0,2},{1,3},{2,0},{3,1},{4,6},{5,7},{6,4},{7,5},{8,10},{9,11},{10,... | collective-permute-start | bytes 196616 | tf_op jit(solution)/shard_map/ppermute | solution.py:346
  27.5 8.0 %collective-permute-start.15 = (bf16[16,2048]{1,0:T(8,128)(2,1)S(1)}, bf16[16,2048]{1,0:T(8,128)(2,1)S(1)}, u32[]{:S(2)}, u32[]{:S(2)}) collective-permute-start(bf16[16,2048]{1,0:T(8,128)(2,1)S(1)} %shard_map.117.refs_0_.refs_4_), channel_id=1, source_target_pairs={{0,4},{1,5},{2,6},{3,7},{4,0},{5,1},{6,2},{7,3},{8,12},{9,13},{10,... | collective-permute-start | bytes 196616 | tf_op jit(solution)/shard_map/ppermute | solution.py:346
  29.6 6.8 %collective-permute-start.14 = (bf16[16,2048]{1,0:T(8,128)(2,1)S(1)}, bf16[16,2048]{1,0:T(8,128)(2,1)S(1)}, u32[]{:S(2)}, u32[]{:S(2)}) collective-permute-start(bf16[16,2048]{1,0:T(8,128)(2,1)S(1)} %shard_map.117.refs_0_.refs_4_), channel_id=1, source_target_pairs={{0,6},{1,7},{2,4},{3,5},{4,2},{5,3},{6,0},{7,1},{8,14},{9,15},{10,... | collective-permute-start | bytes 196616 | tf_op jit(solution)/shard_map/ppermute | solution.py:346
  31.0 7.1 %collective-permute-start.9 = (bf16[16,2048]{1,0:T(8,128)(2,1)S(1)}, bf16[16,2048]{1,0:T(8,128)(2,1)S(1)}, u32[]{:S(2)}, u32[]{:S(2)}) collective-permute-start(bf16[16,2048]{1,0:T(8,128)(2,1)S(1)} %shard_map.114.refs_0_.refs_9_), channel_id=1, source_target_pairs={{0,2},{1,3},{2,0},{3,1},{4,6},{5,7},{6,4},{7,5},{8,10},{9,11},{10,... | collective-permute-start | bytes 196616 | tf_op jit(solution)/shard_map/ppermute | solution.py:346
  31.7 7.6 %collective-permute-start.8 = (bf16[16,2048]{1,0:T(8,128)(2,1)S(1)}, bf16[16,2048]{1,0:T(8,128)(2,1)S(1)}, u32[]{:S(2)}, u32[]{:S(2)}) collective-permute-start(bf16[16,2048]{1,0:T(8,128)(2,1)S(1)} %shard_map.114.refs_0_.refs_9_), channel_id=1, source_target_pairs={{0,4},{1,5},{2,6},{3,7},{4,0},{5,1},{6,2},{7,3},{8,12},{9,13},{10,... | collective-permute-start | bytes 196616 | tf_op jit(solution)/shard_map/ppermute | solution.py:346
  34.1 6.2 %collective-permute-start.7 = (bf16[16,2048]{1,0:T(8,128)(2,1)S(1)}, bf16[16,2048]{1,0:T(8,128)(2,1)S(1)}, u32[]{:S(2)}, u32[]{:S(2)}) collective-permute-start(bf16[16,2048]{1,0:T(8,128)(2,1)S(1)} %shard_map.114.refs_0_.refs_9_), channel_id=1, source_target_pairs={{0,6},{1,7},{2,4},{3,5},{4,2},{5,3},{6,0},{7,1},{8,14},{9,15},{10,... | collective-permute-start | bytes 196616 | tf_op jit(solution)/shard_map/ppermute | solution.py:346
  36.4 4.0 %collective-permute-start.18 = (bf16[64,2048]{1,0:T(8,128)(2,1)S(1)}, bf16[64,2048]{1,0:T(8,128)(2,1)S(1)}, u32[]{:S(2)}, u32[]{:S(2)}) collective-permute-start(bf16[64,2048]{1,0:T(8,128)(2,1)S(1)} %shard_map.118._.own_ref), channel_id=1, source_target_pairs={{0,1},{1,0},{2,3},{3,2},{4,5},{5,4},{6,7},{7,6},{8,9},{9,8},{10,11... | collective-permute-start | bytes 786440 | tf_op jit(solution)/shard_map/ppermute | solution.py:349
  40.3 1.6 %collective-permute-start.17 = (bf16[64,2048]{1,0:T(8,128)(2,1)S(1)}, bf16[64,2048]{1,0:T(8,128)(2,1)S(1)}, u32[]{:S(2)}, u32[]{:S(2)}) collective-permute-start(bf16[64,2048]{1,0:T(8,128)(2,1)S(1)} %shard_map.120.own_ref), channel_id=1, source_target_pairs={{0,1},{1,0},{2,3},{3,2},{4,5},{5,4},{6,7},{7,6},{8,9},{9,8},{10,11... | collective-permute-start | bytes 786440 | tf_op jit(solution)/shard_map/ppermute | solution.py:349
  43.3 1.6 %collective-permute-start.23 = (bf16[64,2048]{1,0:T(8,128)(2,1)S(1)}, bf16[64,2048]{1,0:T(8,128)(2,1)S(1)}, u32[]{:S(2)}, u32[]{:S(2)}) collective-permute-start(bf16[64,2048]{1,0:T(8,128)(2,1)S(1)} %get-tuple-element.66), channel_id=1, source_target_pairs={{0,1},{1,0},{2,3},{3,2},{4,5},{5,4},{6,7},{7,6},{8,9},{9,8},{10,11... | collective-permute-start | bytes 786440 | tf_op jit(solution)/shard_map/ppermute | solution.py:349
  43.9 5.5 %collective-permute-start.19 = (bf16[64,2048]{1,0:T(8,128)(2,1)S(1)}, bf16[64,2048]{1,0:T(8,128)(2,1)S(1)}, u32[]{:S(2)}, u32[]{:S(2)}) collective-permute-start(bf16[64,2048]{1,0:T(8,128)(2,1)S(1)} %get-tuple-element.60), channel_id=1, source_target_pairs={{0,1},{1,0},{2,3},{3,2},{4,5},{5,4},{6,7},{7,6},{8,9},{9,8},{10,11... | collective-permute-start | bytes 786440 | tf_op jit(solution)/shard_map/ppermute | solution.py:349
  44.9 7.2 %collective-permute-start.24 = (bf16[16,2048]{1,0:T(8,128)(2,1)S(1)}, bf16[16,2048]{1,0:T(8,128)(2,1)S(1)}, u32[]{:S(2)}, u32[]{:S(2)}) collective-permute-start(bf16[16,2048]{1,0:T(8,128)(2,1)S(1)} %get-tuple-element.68), channel_id=1, source_target_pairs={{0,2},{1,3},{2,0},{3,1},{4,6},{5,7},{6,4},{7,5},{8,10},{9,11},{10,... | collective-permute-start | bytes 196616 | tf_op jit(solution)/shard_map/ppermute | solution.py:346
  46.0 8.9 %collective-permute-start.25 = (bf16[16,2048]{1,0:T(8,128)(2,1)S(1)}, bf16[16,2048]{1,0:T(8,128)(2,1)S(1)}, u32[]{:S(2)}, u32[]{:S(2)}) collective-permute-start(bf16[16,2048]{1,0:T(8,128)(2,1)S(1)} %get-tuple-element.69), channel_id=1, source_target_pairs={{0,4},{1,5},{2,6},{3,7},{4,0},{5,1},{6,2},{7,3},{8,12},{9,13},{10,... | collective-permute-start | bytes 196616 | tf_op jit(solution)/shard_map/ppermute | solution.py:346
  47.7 7.3 %collective-permute-start.26 = (bf16[16,2048]{1,0:T(8,128)(2,1)S(1)}, bf16[16,2048]{1,0:T(8,128)(2,1)S(1)}, u32[]{:S(2)}, u32[]{:S(2)}) collective-permute-start(bf16[16,2048]{1,0:T(8,128)(2,1)S(1)} %get-tuple-element.70), channel_id=1, source_target_pairs={{0,6},{1,7},{2,4},{3,5},{4,2},{5,3},{6,0},{7,1},{8,14},{9,15},{10,... | collective-permute-start | bytes 196616 | tf_op jit(solution)/shard_map/ppermute | solution.py:346
  49.5 5.5 %collective-permute-start.20 = (bf16[16,2048]{1,0:T(8,128)(2,1)S(1)}, bf16[16,2048]{1,0:T(8,128)(2,1)S(1)}, u32[]{:S(2)}, u32[]{:S(2)}) collective-permute-start(bf16[16,2048]{1,0:T(8,128)(2,1)S(1)} %get-tuple-element.62), channel_id=1, source_target_pairs={{0,2},{1,3},{2,0},{3,1},{4,6},{5,7},{6,4},{7,5},{8,10},{9,11},{10,... | collective-permute-start | bytes 196616 | tf_op jit(solution)/shard_map/ppermute | solution.py:346
  49.7 10.3 %collective-permute-start.21 = (bf16[16,2048]{1,0:T(8,128)(2,1)S(1)}, bf16[16,2048]{1,0:T(8,128)(2,1)S(1)}, u32[]{:S(2)}, u32[]{:S(2)}) collective-permute-start(bf16[16,2048]{1,0:T(8,128)(2,1)S(1)} %get-tuple-element.63), channel_id=1, source_target_pairs={{0,4},{1,5},{2,6},{3,7},{4,0},{5,1},{6,2},{7,3},{8,12},{9,13},{10,... | collective-permute-start | bytes 196616 | tf_op jit(solution)/shard_map/ppermute | solution.py:346
  52.2 7.7 %collective-permute-start.22 = (bf16[16,2048]{1,0:T(8,128)(2,1)S(1)}, bf16[16,2048]{1,0:T(8,128)(2,1)S(1)}, u32[]{:S(2)}, u32[]{:S(2)}) collective-permute-start(bf16[16,2048]{1,0:T(8,128)(2,1)S(1)} %get-tuple-element.64), channel_id=1, source_target_pairs={{0,6},{1,7},{2,4},{3,5},{4,2},{5,3},{6,0},{7,1},{8,14},{9,15},{10,... | collective-permute-start | bytes 196616 | tf_op jit(solution)/shard_map/ppermute | solution.py:346

commit v3 on v1

--- a/solution.py
+++ b/solution.py
@@ -11,7 +11,9 @@
 BF16 = jnp.bfloat16
 TILE_ROWS = 16
 COLUMNS = 1024
-PARTS = 2
+LANES = 128
+MIX_PARTS = 3
+OUT_PARTS = 2
 VMEM_LIMIT = 16 * 1024 * 1024
 
 
@@ -256,9 +258,10 @@
 def product_kernel(at, x_ref, w_ref, mine_ref, theirs_ref):
     half = mine_ref.shape[0]
     for i in range(at.start, at.stop, COLUMNS):
-        part = dot_f32(x_ref[...], w_ref[:, i : i + COLUMNS], ((1,), (0,))).astype(BF16)
-        mine_ref[:, i - at.start : i - at.start + COLUMNS] = part[:half]
-        theirs_ref[:, i - at.start : i - at.start + COLUMNS] = part[half:]
+        j = min(i + COLUMNS, at.stop)
+        part = dot_f32(x_ref[...], w_ref[:, i:j], ((1,), (0,))).astype(BF16)
+        mine_ref[:, i - at.start : j - at.start] = part[:half]
+        theirs_ref[:, i - at.start : j - at.start] = part[half:]
 
 
 def add_kernel(groups, a_ref, b_ref, *refs):
@@ -290,8 +293,11 @@
     return dot_f32(in_ref[:, at], x, ((1,), (1,)))
 
 
-def enter_kernel(at, in_ref, own_ref, other_ref, out_ref):
-    out_ref[...] = enter_part(at, in_ref, own_ref, other_ref)
+def enter_kernel(at, in_ref, own_ref, other_ref, *refs):
+    total = enter_part(at, in_ref, own_ref, other_ref)
+    for ref in refs[:-1]:
+        total = total + ref[...]
+    refs[-1][...] = total
 
 
 def hidden_kernel(at, slices, experts, in_ref, own_ref, other_ref, before_ref, member_ref, out_ref):
@@ -304,14 +310,22 @@
     out_ref[...] = (gate / (1.0 + jnp.exp(-gate)) * up * prob).T.astype(BF16)
 
 
-def result_kernel(count, *refs):
-    out_ref = refs[-1]
-    width = refs[0].shape[1]
-    for i in range(len(refs) // count):
-        total = refs[i * count][...].astype(F32)
-        for ref in refs[i * count + 1 : (i + 1) * count]:
-            total = total + ref[...].astype(F32)
-        out_ref[:, i * width : (i + 1) * width] = total.astype(BF16)
+def result_kernel(out_ranges, mix_ranges, *refs):
+    out_ref, mixed = refs[-1], refs[-1 - len(mix_ranges) : -1]
+    count = (len(refs) - 1 - len(mixed)) // len(out_ranges)
+    edges = sorted({at.start for at in out_ranges + mix_ranges} | {out_ref.shape[1]})
+    for start, stop in zip(edges, edges[1:]):
+        ((i, at),) = [(i, at) for i, at in enumerate(out_ranges) if at.start <= start < at.stop]
+        ((m, by),) = [(ref, by) for ref, by in zip(mixed, mix_ranges) if by.start <= start < by.stop]
+        total = m[:, start - by.start : stop - by.start].astype(F32)
+        for ref in refs[i * count : (i + 1) * count]:
+            total = total + ref[:, start - at.start : stop - at.start].astype(F32)
+        out_ref[:, start:stop] = total.astype(BF16)
+
+
+def split(width, parts):
+    edges = [-(-width * i // parts // LANES) * LANES for i in range(parts)] + [width]
+    return [slice(a, b) for a, b in zip(edges, edges[1:])]
 
 
 def call(kernel, outs, args, scratch=(), far=0):
@@ -347,22 +361,19 @@
     def across(x):
         return lax.ppermute(x, "exp", [(e, e ^ 1) for e in range(exp_count)])
 
-    size = width // PARTS
-    ranges = [slice(i * size, (i + 1) * size) for i in range(PARTS)]
-
-    def rows_of(count):
-        return out((count * rows, size), BF16)
-
-    def reduce(products):
+    mix_ranges, out_ranges = split(width, MIX_PARTS), split(width, OUT_PARTS)
+
+    def rows_of(count, at):
+        return out((count * rows, at.stop - at.start), BF16)
+
+    def reduce(x, w, ranges):
+        products = [call(functools.partial(product_kernel, at), [rows_of(n_pair, at)] * 2, (x, w)) for at in ranges]
         others = [across(theirs) for _, theirs in products]
         terms = [
-            call(functools.partial(add_kernel, [[r] for r in range(n_pair)]), [rows_of(1)] * n_pair, (mine, other))
-            for (mine, _), other in zip(products, others)
+            call(functools.partial(add_kernel, [[r] for r in range(n_pair)]), [rows_of(1, at)] * n_pair, (mine, other))
+            for at, (mine, _), other in zip(ranges, products, others)
         ]
         return [[term[0]] + [shift(term[r], r) for r in range(1, n_pair)] for term in terms]
-
-    def products_of(x, w):
-        return [call(functools.partial(product_kernel, at), [rows_of(n_pair)] * 2, (x, w)) for at in ranges]
 
     decay_row = decay_log.T
     block = pltpu.VMEM((t, d), BF16)
@@ -404,28 +415,36 @@
         [out((t, d), BF16)],
         (*states, intra, grown, query_near, gain),
     )
-    terms = reduce(products_of(normed, w_out_near))
-    mixed = [call(functools.partial(sum_kernel, n_pair), [rows_of(1)], term)[0] for term in terms]
+    terms = reduce(normed, w_out_near, mix_ranges)
+    mixed = [
+        call(functools.partial(sum_kernel, n_pair), [rows_of(1, at)], term)[0] for at, term in zip(mix_ranges, terms)
+    ]
     gathered = [[shift(m, -r) if r else m for r in range(n_pair)] for m in mixed]
-    own, after = [], ()
-    for blocks in gathered:
-        own += call(functools.partial(join_kernel, n_pair), [rows_of(n_pair)], (*blocks, *after))
-        if not after:
-            w_down_near, token = call(
-                fetch_down_kernel, [out((hid, width), BF16), out((8, 128), F32)], (w_down[0], own[0]), [dma], far=1
-            )
-            after = (token,)
+    (own,) = call(functools.partial(join_kernel, n_pair), [rows_of(n_pair, mix_ranges[0])], gathered[0])
+    w_down_near, token = call(
+        fetch_down_kernel, [out((hid, width), BF16), out((8, 128), F32)], (w_down[0], own), [dma], far=1
+    )
+    whole = [own]
+    for at, blocks in zip(mix_ranges[1:], gathered[1:]):
+        whole += call(functools.partial(join_kernel, n_pair), [rows_of(n_pair, at)], (*blocks, token))
     total = ()
-    for at, x in zip(ranges, own):
-        if at.stop < width:
-            kernel, shape = functools.partial(enter_kernel, at), out((w_in.shape[0], t), F32)
-        else:
-            kernel, shape = functools.partial(hidden_kernel, at, slices, experts), out((t, hid), BF16)
-            total = (*total, member)
-        total = call(kernel, [shape], (w_in, x, across(x), *total))
-    sums = reduce(products_of(total[0], w_down_near))
-    args = [x for some, m in zip(sums, mixed) for x in (*some, m)]
-    return call(functools.partial(result_kernel, n_pair + 1), [out((rows, width), BF16)], args)[0]
+    for at, own in zip(mix_ranges[:-1], whole):
+        total = call(
+            functools.partial(enter_kernel, at),
+            [out((w_in.shape[0], t), F32)],
+            (w_in, own, across(own), *total),
+        )
+    (hidden,) = call(
+        functools.partial(hidden_kernel, mix_ranges[-1], slices, experts),
+        [out((t, hid), BF16)],
+        (w_in, whole[-1], across(whole[-1]), *total, member),
+    )
+    sums = reduce(hidden, w_down_near, out_ranges)
+    return call(
+        functools.partial(result_kernel, out_ranges, mix_ranges),
+        [out((rows, width), BF16)],
+        [x for some in sums for x in some] + mixed,
+    )[0]
 
 
 def solution(mesh):

time: 57.9 us -> 61.2 us (1.057)
  starting transfers between devices: 36.2 us -> 41.7 us
  waiting for transfers between devices: 10.9 us -> 8.28 us
    ppermute x18 -> x24, starting transfers between devices: 30.2 us -> 35 us  [shift(): lax.ppermute(x, 'exp', [(e, (e + 2 * r) % exp_count) for e in range(exp_c...]
    ppermute x18 -> x24, waiting for transfers between devices: 8.13 us -> 6.23 us  [shift(): lax.ppermute(x, 'exp', [(e, (e + 2 * r) % exp_count) for e in range(exp_c...]
    ppermute x6 -> x8, waiting for transfers between devices: 1.9 us -> 1.15 us  [across(): return lax.ppermute(x, 'exp', [(e, e ^ 1) for e in range(exp_count)])]
    ppermute x6 -> x8, starting transfers between devices: 1.42 us -> 2.05 us  [across(): return lax.ppermute(x, 'exp', [(e, e ^ 1) for e in range(exp_count)])]
    pallas_call x19 -> x24, Pallas kernels: 10.4 us -> 10.8 us  [call(): pl.pallas_call(kernel, out_shape=outs, in_specs=[pl.BlockSpec(memory_spac...]
  transfers between devices with their start and end apart: 27 -> 35, of which waited for: 9 -> 11; matrix products, arithmetic and copies ran while one was open for 0% -> 0% of each run, Pallas kernels for 11% -> 12%
where the time goes in v3:
time: 61.2 us; the launch traced here: 61 us
  starting transfers between devices  41.7 us (68%)
  Pallas kernels  10.8 us (18%)
  waiting for transfers between devices  8.28 us (14%)
    ppermute x24, starting transfers between devices, shift(): lax.ppermute(x, 'exp', [(e, (e + 2 * r) % exp_count) for e in range(exp_c...  35 us
    pallas_call x24, Pallas kernels, call(): pl.pallas_call(kernel, out_shape=outs, in_specs=[pl.BlockSpec(memory_spac...  10.8 us
    ppermute x24, waiting for transfers between devices, shift(): lax.ppermute(x, 'exp', [(e, (e + 2 * r) % exp_count) for e in range(exp_c...  6.23 us
    ppermute x3, starting transfers between devices, local(): lax.ppermute(state, 'seq', [(move(i), i) for i in range(seq_count)])  4.6 us
    ppermute x8, starting transfers between devices, across(): return lax.ppermute(x, 'exp', [(e, e ^ 1) for e in range(exp_count)])  2.05 us
  transfers between devices with their start and end apart: 35, of which 11 were waited for; matrix products, arithmetic and copies ran while one was open for 0% of the time, Pallas kernels for 12%

profile of v3, /device:TPU:0, one launch (start us, length us, event | category | flops | bytes accessed | tf_op | source)
XLA Modules:
  0.0 61.0 jit_solution(13593184647675650148)
XLA Ops:
  0.0 1.1 %shard_map.109._ = bf16[144,128]{1,0:T(8,128)(2,1)S(1)} custom-call(bf16[128,128]{1,0:T(8,128)(2,1)} %key_hbm.3, bf16[128,128]{1,0:T(8,128)(2,1)} %value_hbm.3, f32[1,128]{1,0:T(1,128)} %bitcast.15), custom_call_target="tpu_custom_call" | custom-call | tf_op jit(solution)/shard_map/pallas_call | solution.py:335
  1.1 4.0 %collective-permute-start.2 = (bf16[144,128]{1,0:T(8,128)(2,1)S(1)}, bf16[144,128]{1,0:T(8,128)(2,1)S(1)}, u32[]{:S(2)}, u32[]{:S(2)}) collective-permute-start(bf16[144,128]{1,0:T(8,128)(2,1)S(1)} %shard_map.109._), channel_id=1, source_target_pairs={{24,0},{16,8},{8,16},{0,24},{25,1},{17,9},{9,17},{1,25},{26,2},{18... | collective-permute-start | bytes 110600 | tf_op jit(solution)/shard_map/ppermute | solution.py:389
  5.1 0.5 collective-permute-start.1
  5.7 2.9 %shard_map.110 = (f32[128,128]{1,0:T(8,128)S(1)}, f32[128,128]{1,0:T(8,128)S(1)}, bf16[128,128]{1,0:T(8,128)(2,1)S(1)}, f32[8,128]{1,0:T(8,128)S(1)}, bf16[128,4...) custom-call(bf16[128,128]{1,0:T(8,128)(2,1)} %query_hbm.1, bf16[128,128]{1,0:T(8,128)(2,1)} %key_hbm.3, ...), custom_call_target="tpu_custom_call" | custom-call | tf_op jit(solution)/shard_map/pallas_call | solution.py:335
  8.6 0.4 collective-permute-done.1.refs_1_
  9.0 0.5 collective-permute-done.refs_0_
  9.5 0.4 shard_map.111.x_ref
  10.6 0.6 collective-permute-start.10
  11.8 1.6 %collective-permute-start.19 = (bf16[16,1408]{1,0:T(8,128)(2,1)S(1)}, bf16[16,1408]{1,0:T(8,128)(2,1)S(1)}, u32[]{:S(2)}, u32[]{:S(2)}) collective-permute-start(bf16[16,1408]{1,0:T(8,128)(2,1)S(1)} %get-tuple-element.66), channel_id=1, source_target_pairs={{0,2},{1,3},{2,4},{3,5},{4,6},{5,7},{6,0},{7,1},{8,10},{9,11},{10,... | collective-permute-start | bytes 135176 | tf_op jit(solution)/shard_map/ppermute | solution.py:359
  13.4 2.6 %collective-permute-start.20 = (bf16[16,1408]{1,0:T(8,128)(2,1)S(1)}, bf16[16,1408]{1,0:T(8,128)(2,1)S(1)}, u32[]{:S(2)}, u32[]{:S(2)}) collective-permute-start(bf16[16,1408]{1,0:T(8,128)(2,1)S(1)} %get-tuple-element.67), channel_id=1, source_target_pairs={{0,4},{1,5},{2,6},{3,7},{4,0},{5,1},{6,2},{7,3},{8,12},{9,13},{10,... | collective-permute-start | bytes 135176 | tf_op jit(solution)/shard_map/ppermute | solution.py:359
  16.0 1.3 %collective-permute-start.21 = (bf16[16,1408]{1,0:T(8,128)(2,1)S(1)}, bf16[16,1408]{1,0:T(8,128)(2,1)S(1)}, u32[]{:S(2)}, u32[]{:S(2)}) collective-permute-start(bf16[16,1408]{1,0:T(8,128)(2,1)S(1)} %get-tuple-element.68), channel_id=1, source_target_pairs={{0,6},{1,7},{2,0},{3,1},{4,2},{5,3},{6,4},{7,5},{8,14},{9,15},{10,... | collective-permute-start | bytes 135176 | tf_op jit(solution)/shard_map/ppermute | solution.py:359
  17.4 0.7 %collective-permute-start.11 = (bf16[16,1408]{1,0:T(8,128)(2,1)S(1)}, bf16[16,1408]{1,0:T(8,128)(2,1)S(1)}, u32[]{:S(2)}, u32[]{:S(2)}) collective-permute-start(bf16[16,1408]{1,0:T(8,128)(2,1)S(1)} %get-tuple-element.59), channel_id=1, source_target_pairs={{0,2},{1,3},{2,4},{3,5},{4,6},{5,7},{6,0},{7,1},{8,10},{9,11},{10,... | collective-permute-start | bytes 135176 | tf_op jit(solution)/shard_map/ppermute | solution.py:359
  18.1 0.3 collective-permute-start.12
  18.4 2.9 %collective-permute-start.13 = (bf16[16,1408]{1,0:T(8,128)(2,1)S(1)}, bf16[16,1408]{1,0:T(8,128)(2,1)S(1)}, u32[]{:S(2)}, u32[]{:S(2)}) collective-permute-start(bf16[16,1408]{1,0:T(8,128)(2,1)S(1)} %get-tuple-element.61), channel_id=1, source_target_pairs={{0,6},{1,7},{2,0},{3,1},{4,2},{5,3},{6,4},{7,5},{8,14},{9,15},{10,... | collective-permute-start | bytes 135176 | tf_op jit(solution)/shard_map/ppermute | solution.py:359
  21.4 0.6 collective-permute-start.4
  21.9 1.5 %collective-permute-start.5 = (bf16[16,1280]{1,0:T(8,128)(2,1)S(1)}, bf16[16,1280]{1,0:T(8,128)(2,1)S(1)}, u32[]{:S(2)}, u32[]{:S(2)}) collective-permute-start(bf16[16,1280]{1,0:T(8,128)(2,1)S(1)} %get-tuple-element.54), channel_id=1, source_target_pairs={{0,4},{1,5},{2,6},{3,7},{4,0},{5,1},{6,2},{7,3},{8,12},{9,13},{10,... | collective-permute-start | bytes 122888 | tf_op jit(solution)/shard_map/ppermute | solution.py:359
  23.5 2.4 %collective-permute-start.24 = (bf16[16,1408]{1,0:T(8,128)(2,1)S(1)}, bf16[16,1408]{1,0:T(8,128)(2,1)S(1)}, u32[]{:S(2)}, u32[]{:S(2)}) collective-permute-start(bf16[16,1408]{1,0:T(8,128)(2,1)S(1)} %shard_map.123.refs_0_.refs_9_), channel_id=1, source_target_pairs={{0,2},{1,3},{2,4},{3,5},{4,6},{5,7},{6,0},{7,1},{8,10},{9,11},{10,... | collective-permute-start | bytes 135176 | tf_op jit(solution)/shard_map/ppermute | solution.py:359
  25.9 1.5 %collective-permute-start.6 = (bf16[16,1280]{1,0:T(8,128)(2,1)S(1)}, bf16[16,1280]{1,0:T(8,128)(2,1)S(1)}, u32[]{:S(2)}, u32[]{:S(2)}) collective-permute-start(bf16[16,1280]{1,0:T(8,128)(2,1)S(1)} %get-tuple-element.55), channel_id=1, source_target_pairs={{0,6},{1,7},{2,0},{3,1},{4,2},{5,3},{6,4},{7,5},{8,14},{9,15},{10,... | collective-permute-start | bytes 122888 | tf_op jit(solution)/shard_map/ppermute | solution.py:359
  27.4 0.6 collective-permute-start.16
  28.0 1.1 %collective-permute-start.15 = (bf16[16,1408]{1,0:T(8,128)(2,1)S(1)}, bf16[16,1408]{1,0:T(8,128)(2,1)S(1)}, u32[]{:S(2)}, u32[]{:S(2)}) collective-permute-start(bf16[16,1408]{1,0:T(8,128)(2,1)S(1)} %shard_map.117.refs_0_.refs_8_), channel_id=1, source_target_pairs={{0,4},{1,5},{2,6},{3,7},{4,0},{5,1},{6,2},{7,3},{8,12},{9,13},{10,... | collective-permute-start | bytes 135176 | tf_op jit(solution)/shard_map/ppermute | solution.py:359
  29.1 2.3 %collective-permute-start.14 = (bf16[16,1408]{1,0:T(8,128)(2,1)S(1)}, bf16[16,1408]{1,0:T(8,128)(2,1)S(1)}, u32[]{:S(2)}, u32[]{:S(2)}) collective-permute-start(bf16[16,1408]{1,0:T(8,128)(2,1)S(1)} %shard_map.117.refs_0_.refs_8_), channel_id=1, source_target_pairs={{0,6},{1,7},{2,0},{3,1},{4,2},{5,3},{6,4},{7,5},{8,14},{9,15},{10,... | collective-permute-start | bytes 135176 | tf_op jit(solution)/shard_map/ppermute | solution.py:359
  31.4 2.0 %collective-permute-start.23 = (bf16[16,1408]{1,0:T(8,128)(2,1)S(1)}, bf16[16,1408]{1,0:T(8,128)(2,1)S(1)}, u32[]{:S(2)}, u32[]{:S(2)}) collective-permute-start(bf16[16,1408]{1,0:T(8,128)(2,1)S(1)} %shard_map.123.refs_0_.refs_9_), channel_id=1, source_target_pairs={{0,4},{1,5},{2,6},{3,7},{4,0},{5,1},{6,2},{7,3},{8,12},{9,13},{10,... | collective-permute-start | bytes 135176 | tf_op jit(solution)/shard_map/ppermute | solution.py:359
  33.4 1.0 %collective-permute-start.22 = (bf16[16,1408]{1,0:T(8,128)(2,1)S(1)}, bf16[16,1408]{1,0:T(8,128)(2,1)S(1)}, u32[]{:S(2)}, u32[]{:S(2)}) collective-permute-start(bf16[16,1408]{1,0:T(8,128)(2,1)S(1)} %shard_map.123.refs_0_.refs_9_), channel_id=1, source_target_pairs={{0,6},{1,7},{2,0},{3,1},{4,2},{5,3},{6,4},{7,5},{8,14},{9,15},{10,... | collective-permute-start | bytes 135176 | tf_op jit(solution)/shard_map/ppermute | solution.py:359
  34.4 1.1 %collective-permute-start.9 = (bf16[16,1280]{1,0:T(8,128)(2,1)S(1)}, bf16[16,1280]{1,0:T(8,128)(2,1)S(1)}, u32[]{:S(2)}, u32[]{:S(2)}) collective-permute-start(bf16[16,1280]{1,0:T(8,128)(2,1)S(1)} %shard_map.114.refs_0_.refs_10_), channel_id=1, source_target_pairs={{0,2},{1,3},{2,4},{3,5},{4,6},{5,7},{6,0},{7,1},{8,10},{9,11},{10,... | collective-permute-start | bytes 122888 | tf_op jit(solution)/shard_map/ppermute | solution.py:359
  35.5 1.0 %collective-permute-start.8 = (bf16[16,1280]{1,0:T(8,128)(2,1)S(1)}, bf16[16,1280]{1,0:T(8,128)(2,1)S(1)}, u32[]{:S(2)}, u32[]{:S(2)}) collective-permute-start(bf16[16,1280]{1,0:T(8,128)(2,1)S(1)} %shard_map.114.refs_0_.refs_10_), channel_id=1, source_target_pairs={{0,4},{1,5},{2,6},{3,7},{4,0},{5,1},{6,2},{7,3},{8,12},{9,13},{10,... | collective-permute-start | bytes 122888 | tf_op jit(solution)/shard_map/ppermute | solution.py:359
  36.4 2.0 %collective-permute-start.7 = (bf16[16,1280]{1,0:T(8,128)(2,1)S(1)}, bf16[16,1280]{1,0:T(8,128)(2,1)S(1)}, u32[]{:S(2)}, u32[]{:S(2)}) collective-permute-start(bf16[16,1280]{1,0:T(8,128)(2,1)S(1)} %shard_map.114.refs_0_.refs_10_), channel_id=1, source_target_pairs={{0,6},{1,7},{2,0},{3,1},{4,2},{5,3},{6,4},{7,5},{8,14},{9,15},{10,... | collective-permute-start | bytes 122888 | tf_op jit(solution)/shard_map/ppermute | solution.py:359
  38.5 1.7 %shard_map.119 = (bf16[288,4096]{1,0:T(8,128)(2,1)S(1)}, f32[8,128]{1,0:T(8,128)S(1)}) custom-call(bf16[288,4096]{1,0:T(8,128)(2,1)} %bitcast.13, bf16[64,1408]{1,0:T(8,128)(2,1)S(1)} %shard_map.118._.own_ref), custom_call_target="tpu_custom_call" | custom-call | tf_op jit(solution)/shard_map/pallas_call | solution.py:335
  40.3 0.5 collective-permute-start.25
  40.8 0.4 collective-permute-done.8.refs_2_
  41.3 0.4 collective-permute-done.26.other_ref
  41.6 0.6 %shard_map.125.refs_0_ = f32[592,128]{1,0:T(8,128)S(1)} custom-call(bf16[592,4096]{1,0:T(8,128)(2,1)S(1)} %get-tuple-element.44.in_ref, bf16[64,1408]{1,0:T(8,128)(2,1)S(1)} %shard_map.118._.own_ref, bf16[64,1408]{1,0:T(8,128)(2,1)S(1)} %collective-permute-done.26.other_ref), custom_call_target="tpu_custom_call" | custom-call | tf_op jit(solution)/shard_map/pallas_call | solution.py:335
  42.3 0.6 %shard_map.126.before_ref = f32[592,128]{1,0:T(8,128)S(1)} custom-call(bf16[592,4096]{1,0:T(8,128)(2,1)S(1)} %get-tuple-element.44.in_ref, bf16[64,1408]{1,0:T(8,128)(2,1)S(1)} %shard_map.124.own_ref, bf16[64,1408]{1,0:T(8,128)(2,1)S(1)} %collective-permute-done.25.other_ref, f32[592,128]{1,0:T(8,128)S(1)} %shard_map.125.refs_0_), custom_call_target="tpu_custom_call" | custom-call | tf_op jit(solution)/shard_map/pallas_call | solution.py:335
  42.9 0.7 %shard_map.127.x_ref = bf16[128,288]{1,0:T(8,128)(2,1)S(1)} custom-call(bf16[592,4096]{1,0:T(8,128)(2,1)S(1)} %get-tuple-element.44.in_ref, bf16[64,1280]{1,0:T(8,128)(2,1)S(1)} %shard_map.120.own_ref, bf16[64,1280]{1,0:T(8,128)(2,1)S(1)} %collective-permute-done.17.other_ref, f32[592,128]{1,0:T(8,128)S(1)} %shard_map.126.before_ref, ...), custom_call_target="tpu_custom_call" | custom-call | tf_op jit(solution)/shard_map/pallas_call | solution.py:335
  43.6 0.4 shard_map.130
  44.3 0.4 shard_map.128
  44.7 0.4 collective-permute-start.27
  45.2 0.5 collective-permute-done.31.b_ref
  45.8 1.5 %collective-permute-start.32 = (bf16[16,2048]{1,0:T(8,128)(2,1)S(1)}, bf16[16,2048]{1,0:T(8,128)(2,1)S(1)}, u32[]{:S(2)}, u32[]{:S(2)}) collective-permute-start(bf16[16,2048]{1,0:T(8,128)(2,1)S(1)} %get-tuple-element.80), channel_id=1, source_target_pairs={{0,2},{1,3},{2,4},{3,5},{4,6},{5,7},{6,0},{7,1},{8,10},{9,11},{10,... | collective-permute-start | bytes 196616 | tf_op jit(solution)/shard_map/ppermute | solution.py:359
  47.2 2.0 %collective-permute-start.33 = (bf16[16,2048]{1,0:T(8,128)(2,1)S(1)}, bf16[16,2048]{1,0:T(8,128)(2,1)S(1)}, u32[]{:S(2)}, u32[]{:S(2)}) collective-permute-start(bf16[16,2048]{1,0:T(8,128)(2,1)S(1)} %get-tuple-element.81), channel_id=1, source_target_pairs={{0,4},{1,5},{2,6},{3,7},{4,0},{5,1},{6,2},{7,3},{8,12},{9,13},{10,... | collective-permute-start | bytes 196616 | tf_op jit(solution)/shard_map/ppermute | solution.py:359
  49.2 1.3 %collective-permute-start.34 = (bf16[16,2048]{1,0:T(8,128)(2,1)S(1)}, bf16[16,2048]{1,0:T(8,128)(2,1)S(1)}, u32[]{:S(2)}, u32[]{:S(2)}) collective-permute-start(bf16[16,2048]{1,0:T(8,128)(2,1)S(1)} %get-tuple-element.82), channel_id=1, source_target_pairs={{0,6},{1,7},{2,0},{3,1},{4,2},{5,3},{6,4},{7,5},{8,14},{9,15},{10,... | collective-permute-start | bytes 196616 | tf_op jit(solution)/shard_map/ppermute | solution.py:359
  50.6 0.7 %collective-permute-start.28 = (bf16[16,2048]{1,0:T(8,128)(2,1)S(1)}, bf16[16,2048]{1,0:T(8,128)(2,1)S(1)}, u32[]{:S(2)}, u32[]{:S(2)}) collective-permute-start(bf16[16,2048]{1,0:T(8,128)(2,1)S(1)} %get-tuple-element.74), channel_id=1, source_target_pairs={{0,2},{1,3},{2,4},{3,5},{4,6},{5,7},{6,0},{7,1},{8,10},{9,11},{10,... | collective-permute-start | bytes 196616 | tf_op jit(solution)/shard_map/ppermute | solution.py:359
  51.4 0.9 %collective-permute-start.29 = (bf16[16,2048]{1,0:T(8,128)(2,1)S(1)}, bf16[16,2048]{1,0:T(8,128)(2,1)S(1)}, u32[]{:S(2)}, u32[]{:S(2)}) collective-permute-start(bf16[16,2048]{1,0:T(8,128)(2,1)S(1)} %get-tuple-element.75), channel_id=1, source_target_pairs={{0,4},{1,5},{2,6},{3,7},{4,0},{5,1},{6,2},{7,3},{8,12},{9,13},{10,... | collective-permute-start | bytes 196616 | tf_op jit(solution)/shard_map/ppermute | solution.py:359
  52.3 0.3 collective-permute-done.32.refs_5_
  52.6 2.1 %collective-permute-start.30 = (bf16[16,2048]{1,0:T(8,128)(2,1)S(1)}, bf16[16,2048]{1,0:T(8,128)(2,1)S(1)}, u32[]{:S(2)}, u32[]{:S(2)}) collective-permute-start(bf16[16,2048]{1,0:T(8,128)(2,1)S(1)} %get-tuple-element.76), channel_id=1, source_target_pairs={{0,6},{1,7},{2,0},{3,1},{4,2},{5,3},{6,4},{7,5},{8,14},{9,15},{10,... | collective-permute-start | bytes 196616 | tf_op jit(solution)/shard_map/ppermute | solution.py:359
  54.8 0.9 %collective-permute-done.34.refs_7_ = bf16[16,2048]{1,0:T(8,128)(2,1)S(1)} collective-permute-done((bf16[16,2048]{1,0:T(8,128)(2,1)S(1)}, bf16[16,2048]{1,0:T(8,128)(2,1)S(1)}, u32[]{:S(2)}, u32[]{:S(2)}) %collective-permute-start.34) | collective-permute-done | bytes 65568 | tf_op jit(solution)/shard_map/ppermute | solution.py:359
  55.7 1.8 %collective-permute-done.28.refs_1_ = bf16[16,2048]{1,0:T(8,128)(2,1)S(1)} collective-permute-done((bf16[16,2048]{1,0:T(8,128)(2,1)S(1)}, bf16[16,2048]{1,0:T(8,128)(2,1)S(1)}, u32[]{:S(2)}, u32[]{:S(2)}) %collective-permute-start.28) | collective-permute-done | bytes 65568 | tf_op jit(solution)/shard_map/ppermute | solution.py:359
  57.5 2.7 %collective-permute-done.29.refs_2_ = bf16[16,2048]{1,0:T(8,128)(2,1)S(1)} collective-permute-done((bf16[16,2048]{1,0:T(8,128)(2,1)S(1)}, bf16[16,2048]{1,0:T(8,128)(2,1)S(1)}, u32[]{:S(2)}, u32[]{:S(2)}) %collective-permute-start.29) | collective-permute-done | bytes 65568 | tf_op jit(solution)/shard_map/ppermute | solution.py:359
  60.3 0.7 %shard_map.132 = bf16[16,4096]{1,0:T(8,128)(2,1)} custom-call(bf16[16,2048]{1,0:T(8,128)(2,1)S(1)} %get-tuple-element.73.refs_0_, bf16[16,2048]{1,0:T(8,128)(2,1)S(1)} %collective-permute-done.28.refs_1_, bf16[16,2048]{1,0:T(8,128)(2,1)S(1)} %collective-permute-done.29.refs_2_, bf16[16,2048]{1,0:T(8,128)(2,1)S(1)} %collective-permute-done.30.refs_3_, ...), custom_call_target="tpu_custom_call" | custom-call | tf_op jit(solution)/shard_map/pallas_call | solution.py:335
  (46 shorter events, 2.1 us)
Async XLA Ops:
  1.1 7.5 %collective-permute-start.2 = (bf16[144,128]{1,0:T(8,128)(2,1)S(1)}, bf16[144,128]{1,0:T(8,128)(2,1)S(1)}, u32[]{:S(2)}, u32[]{:S(2)}) collective-permute-start(bf16[144,128]{1,0:T(8,128)(2,1)S(1)} %shard_map.109._), channel_id=1, source_target_pairs={{24,0},{16,8},{8,16},{0,24},{25,1},{17,9},{9,17},{1,25},{26,2},{18... | collective-permute-start | bytes 110600 | tf_op jit(solution)/shard_map/ppermute | solution.py:389
  5.1 4.0 %collective-permute-start.1 = (bf16[144,128]{1,0:T(8,128)(2,1)S(1)}, bf16[144,128]{1,0:T(8,128)(2,1)S(1)}, u32[]{:S(2)}, u32[]{:S(2)}) collective-permute-start(bf16[144,128]{1,0:T(8,128)(2,1)S(1)} %shard_map.109._), channel_id=1, source_target_pairs={{16,0},{24,8},{0,16},{8,24},{17,1},{25,9},{1,17},{9,25},{18,2},{26... | collective-permute-start | bytes 110600 | tf_op jit(solution)/shard_map/ppermute | solution.py:389
  5.6 4.0 %collective-permute-start = (bf16[144,128]{1,0:T(8,128)(2,1)S(1)}, bf16[144,128]{1,0:T(8,128)(2,1)S(1)}, u32[]{:S(2)}, u32[]{:S(2)}) collective-permute-start(bf16[144,128]{1,0:T(8,128)(2,1)S(1)} %shard_map.109._), channel_id=1, source_target_pairs={{8,0},{0,8},{24,16},{16,24},{9,1},{1,9},{25,17},{17,25},{10,2},{2,... | collective-permute-start | bytes 110600 | tf_op jit(solution)/shard_map/ppermute | solution.py:389
  10.2 1.5 %collective-permute-start.18 = (bf16[64,1408]{1,0:T(8,128)(2,1)S(1)}, bf16[64,1408]{1,0:T(8,128)(2,1)S(1)}, u32[]{:S(2)}, u32[]{:S(2)}) collective-permute-start(bf16[64,1408]{1,0:T(8,128)(2,1)S(1)} %get-tuple-element.64), channel_id=1, source_target_pairs={{0,1},{1,0},{2,3},{3,2},{4,5},{5,4},{6,7},{7,6},{8,9},{9,8},{10,11... | collective-permute-start | bytes 540680 | tf_op jit(solution)/shard_map/ppermute | solution.py:362
  10.6 6.8 %collective-permute-start.10 = (bf16[64,1408]{1,0:T(8,128)(2,1)S(1)}, bf16[64,1408]{1,0:T(8,128)(2,1)S(1)}, u32[]{:S(2)}, u32[]{:S(2)}) collective-permute-start(bf16[64,1408]{1,0:T(8,128)(2,1)S(1)} %get-tuple-element.57), channel_id=1, source_target_pairs={{0,1},{1,0},{2,3},{3,2},{4,5},{5,4},{6,7},{7,6},{8,9},{9,8},{10,11... | collective-permute-start | bytes 540680 | tf_op jit(solution)/shard_map/ppermute | solution.py:362
  11.4 6.8 %collective-permute-start.3 = (bf16[64,1280]{1,0:T(8,128)(2,1)S(1)}, bf16[64,1280]{1,0:T(8,128)(2,1)S(1)}, u32[]{:S(2)}, u32[]{:S(2)}) collective-permute-start(bf16[64,1280]{1,0:T(8,128)(2,1)S(1)} %get-tuple-element.51), channel_id=1, source_target_pairs={{0,1},{1,0},{2,3},{3,2},{4,5},{5,4},{6,7},{7,6},{8,9},{9,8},{10,11... | collective-permute-start | bytes 491528 | tf_op jit(solution)/shard_map/ppermute | solution.py:362
  11.8 6.7 %collective-permute-start.19 = (bf16[16,1408]{1,0:T(8,128)(2,1)S(1)}, bf16[16,1408]{1,0:T(8,128)(2,1)S(1)}, u32[]{:S(2)}, u32[]{:S(2)}) collective-permute-start(bf16[16,1408]{1,0:T(8,128)(2,1)S(1)} %get-tuple-element.66), channel_id=1, source_target_pairs={{0,2},{1,3},{2,4},{3,5},{4,6},{5,7},{6,0},{7,1},{8,10},{9,11},{10,... | collective-permute-start | bytes 135176 | tf_op jit(solution)/shard_map/ppermute | solution.py:359
  13.4 8.0 %collective-permute-start.20 = (bf16[16,1408]{1,0:T(8,128)(2,1)S(1)}, bf16[16,1408]{1,0:T(8,128)(2,1)S(1)}, u32[]{:S(2)}, u32[]{:S(2)}) collective-permute-start(bf16[16,1408]{1,0:T(8,128)(2,1)S(1)} %get-tuple-element.67), channel_id=1, source_target_pairs={{0,4},{1,5},{2,6},{3,7},{4,0},{5,1},{6,2},{7,3},{8,12},{9,13},{10,... | collective-permute-start | bytes 135176 | tf_op jit(solution)/shard_map/ppermute | solution.py:359
  16.0 6.0 %collective-permute-start.21 = (bf16[16,1408]{1,0:T(8,128)(2,1)S(1)}, bf16[16,1408]{1,0:T(8,128)(2,1)S(1)}, u32[]{:S(2)}, u32[]{:S(2)}) collective-permute-start(bf16[16,1408]{1,0:T(8,128)(2,1)S(1)} %get-tuple-element.68), channel_id=1, source_target_pairs={{0,6},{1,7},{2,0},{3,1},{4,2},{5,3},{6,4},{7,5},{8,14},{9,15},{10,... | collective-permute-start | bytes 135176 | tf_op jit(solution)/shard_map/ppermute | solution.py:359
  17.4 6.1 %collective-permute-start.11 = (bf16[16,1408]{1,0:T(8,128)(2,1)S(1)}, bf16[16,1408]{1,0:T(8,128)(2,1)S(1)}, u32[]{:S(2)}, u32[]{:S(2)}) collective-permute-start(bf16[16,1408]{1,0:T(8,128)(2,1)S(1)} %get-tuple-element.59), channel_id=1, source_target_pairs={{0,2},{1,3},{2,4},{3,5},{4,6},{5,7},{6,0},{7,1},{8,10},{9,11},{10,... | collective-permute-start | bytes 135176 | tf_op jit(solution)/shard_map/ppermute | solution.py:359
  18.1 7.8 %collective-permute-start.12 = (bf16[16,1408]{1,0:T(8,128)(2,1)S(1)}, bf16[16,1408]{1,0:T(8,128)(2,1)S(1)}, u32[]{:S(2)}, u32[]{:S(2)}) collective-permute-start(bf16[16,1408]{1,0:T(8,128)(2,1)S(1)} %get-tuple-element.60), channel_id=1, source_target_pairs={{0,4},{1,5},{2,6},{3,7},{4,0},{5,1},{6,2},{7,3},{8,12},{9,13},{10,... | collective-permute-start | bytes 135176 | tf_op jit(solution)/shard_map/ppermute | solution.py:359
  18.4 9.0 %collective-permute-start.13 = (bf16[16,1408]{1,0:T(8,128)(2,1)S(1)}, bf16[16,1408]{1,0:T(8,128)(2,1)S(1)}, u32[]{:S(2)}, u32[]{:S(2)}) collective-permute-start(bf16[16,1408]{1,0:T(8,128)(2,1)S(1)} %get-tuple-element.61), channel_id=1, source_target_pairs={{0,6},{1,7},{2,0},{3,1},{4,2},{5,3},{6,4},{7,5},{8,14},{9,15},{10,... | collective-permute-start | bytes 135176 | tf_op jit(solution)/shard_map/ppermute | solution.py:359
  21.4 6.7 %collective-permute-start.4 = (bf16[16,1280]{1,0:T(8,128)(2,1)S(1)}, bf16[16,1280]{1,0:T(8,128)(2,1)S(1)}, u32[]{:S(2)}, u32[]{:S(2)}) collective-permute-start(bf16[16,1280]{1,0:T(8,128)(2,1)S(1)} %get-tuple-element.53), channel_id=1, source_target_pairs={{0,2},{1,3},{2,4},{3,5},{4,6},{5,7},{6,0},{7,1},{8,10},{9,11},{10,... | collective-permute-start | bytes 122888 | tf_op jit(solution)/shard_map/ppermute | solution.py:359
  21.9 7.2 %collective-permute-start.5 = (bf16[16,1280]{1,0:T(8,128)(2,1)S(1)}, bf16[16,1280]{1,0:T(8,128)(2,1)S(1)}, u32[]{:S(2)}, u32[]{:S(2)}) collective-permute-start(bf16[16,1280]{1,0:T(8,128)(2,1)S(1)} %get-tuple-element.54), channel_id=1, source_target_pairs={{0,4},{1,5},{2,6},{3,7},{4,0},{5,1},{6,2},{7,3},{8,12},{9,13},{10,... | collective-permute-start | bytes 122888 | tf_op jit(solution)/shard_map/ppermute | solution.py:359
  23.5 9.8 %collective-permute-start.24 = (bf16[16,1408]{1,0:T(8,128)(2,1)S(1)}, bf16[16,1408]{1,0:T(8,128)(2,1)S(1)}, u32[]{:S(2)}, u32[]{:S(2)}) collective-permute-start(bf16[16,1408]{1,0:T(8,128)(2,1)S(1)} %shard_map.123.refs_0_.refs_9_), channel_id=1, source_target_pairs={{0,2},{1,3},{2,4},{3,5},{4,6},{5,7},{6,0},{7,1},{8,10},{9,11},{10,... | collective-permute-start | bytes 135176 | tf_op jit(solution)/shard_map/ppermute | solution.py:359
  25.9 5.5 %collective-permute-start.6 = (bf16[16,1280]{1,0:T(8,128)(2,1)S(1)}, bf16[16,1280]{1,0:T(8,128)(2,1)S(1)}, u32[]{:S(2)}, u32[]{:S(2)}) collective-permute-start(bf16[16,1280]{1,0:T(8,128)(2,1)S(1)} %get-tuple-element.55), channel_id=1, source_target_pairs={{0,6},{1,7},{2,0},{3,1},{4,2},{5,3},{6,4},{7,5},{8,14},{9,15},{10,... | collective-permute-start | bytes 122888 | tf_op jit(solution)/shard_map/ppermute | solution.py:359
  27.4 6.9 %collective-permute-start.16 = (bf16[16,1408]{1,0:T(8,128)(2,1)S(1)}, bf16[16,1408]{1,0:T(8,128)(2,1)S(1)}, u32[]{:S(2)}, u32[]{:S(2)}) collective-permute-start(bf16[16,1408]{1,0:T(8,128)(2,1)S(1)} %shard_map.117.refs_0_.refs_8_), channel_id=1, source_target_pairs={{0,2},{1,3},{2,4},{3,5},{4,6},{5,7},{6,0},{7,1},{8,10},{9,11},{10,... | collective-permute-start | bytes 135176 | tf_op jit(solution)/shard_map/ppermute | solution.py:359
  28.0 7.4 %collective-permute-start.15 = (bf16[16,1408]{1,0:T(8,128)(2,1)S(1)}, bf16[16,1408]{1,0:T(8,128)(2,1)S(1)}, u32[]{:S(2)}, u32[]{:S(2)}) collective-permute-start(bf16[16,1408]{1,0:T(8,128)(2,1)S(1)} %shard_map.117.refs_0_.refs_8_), channel_id=1, source_target_pairs={{0,4},{1,5},{2,6},{3,7},{4,0},{5,1},{6,2},{7,3},{8,12},{9,13},{10,... | collective-permute-start | bytes 135176 | tf_op jit(solution)/shard_map/ppermute | solution.py:359
  29.1 7.3 %collective-permute-start.14 = (bf16[16,1408]{1,0:T(8,128)(2,1)S(1)}, bf16[16,1408]{1,0:T(8,128)(2,1)S(1)}, u32[]{:S(2)}, u32[]{:S(2)}) collective-permute-start(bf16[16,1408]{1,0:T(8,128)(2,1)S(1)} %shard_map.117.refs_0_.refs_8_), channel_id=1, source_target_pairs={{0,6},{1,7},{2,0},{3,1},{4,2},{5,3},{6,4},{7,5},{8,14},{9,15},{10,... | collective-permute-start | bytes 135176 | tf_op jit(solution)/shard_map/ppermute | solution.py:359
  31.4 8.8 %collective-permute-start.23 = (bf16[16,1408]{1,0:T(8,128)(2,1)S(1)}, bf16[16,1408]{1,0:T(8,128)(2,1)S(1)}, u32[]{:S(2)}, u32[]{:S(2)}) collective-permute-start(bf16[16,1408]{1,0:T(8,128)(2,1)S(1)} %shard_map.123.refs_0_.refs_9_), channel_id=1, source_target_pairs={{0,4},{1,5},{2,6},{3,7},{4,0},{5,1},{6,2},{7,3},{8,12},{9,13},{10,... | collective-permute-start | bytes 135176 | tf_op jit(solution)/shard_map/ppermute | solution.py:359
  33.4 6.9 %collective-permute-start.22 = (bf16[16,1408]{1,0:T(8,128)(2,1)S(1)}, bf16[16,1408]{1,0:T(8,128)(2,1)S(1)}, u32[]{:S(2)}, u32[]{:S(2)}) collective-permute-start(bf16[16,1408]{1,0:T(8,128)(2,1)S(1)} %shard_map.123.refs_0_.refs_9_), channel_id=1, source_target_pairs={{0,6},{1,7},{2,0},{3,1},{4,2},{5,3},{6,4},{7,5},{8,14},{9,15},{10,... | collective-permute-start | bytes 135176 | tf_op jit(solution)/shard_map/ppermute | solution.py:359
  34.4 6.5 %collective-permute-start.9 = (bf16[16,1280]{1,0:T(8,128)(2,1)S(1)}, bf16[16,1280]{1,0:T(8,128)(2,1)S(1)}, u32[]{:S(2)}, u32[]{:S(2)}) collective-permute-start(bf16[16,1280]{1,0:T(8,128)(2,1)S(1)} %shard_map.114.refs_0_.refs_10_), channel_id=1, source_target_pairs={{0,2},{1,3},{2,4},{3,5},{4,6},{5,7},{6,0},{7,1},{8,10},{9,11},{10,... | collective-permute-start | bytes 122888 | tf_op jit(solution)/shard_map/ppermute | solution.py:359
  35.5 5.7 %collective-permute-start.8 = (bf16[16,1280]{1,0:T(8,128)(2,1)S(1)}, bf16[16,1280]{1,0:T(8,128)(2,1)S(1)}, u32[]{:S(2)}, u32[]{:S(2)}) collective-permute-start(bf16[16,1280]{1,0:T(8,128)(2,1)S(1)} %shard_map.114.refs_0_.refs_10_), channel_id=1, source_target_pairs={{0,4},{1,5},{2,6},{3,7},{4,0},{5,1},{6,2},{7,3},{8,12},{9,13},{10,... | collective-permute-start | bytes 122888 | tf_op jit(solution)/shard_map/ppermute | solution.py:359
  36.4 4.8 %collective-permute-start.7 = (bf16[16,1280]{1,0:T(8,128)(2,1)S(1)}, bf16[16,1280]{1,0:T(8,128)(2,1)S(1)}, u32[]{:S(2)}, u32[]{:S(2)}) collective-permute-start(bf16[16,1280]{1,0:T(8,128)(2,1)S(1)} %shard_map.114.refs_0_.refs_10_), channel_id=1, source_target_pairs={{0,6},{1,7},{2,0},{3,1},{4,2},{5,3},{6,4},{7,5},{8,14},{9,15},{10,... | collective-permute-start | bytes 122888 | tf_op jit(solution)/shard_map/ppermute | solution.py:359
  40.2 1.5 %collective-permute-start.26 = (bf16[64,1408]{1,0:T(8,128)(2,1)S(1)}, bf16[64,1408]{1,0:T(8,128)(2,1)S(1)}, u32[]{:S(2)}, u32[]{:S(2)}) collective-permute-start(bf16[64,1408]{1,0:T(8,128)(2,1)S(1)} %shard_map.118._.own_ref), channel_id=1, source_target_pairs={{0,1},{1,0},{2,3},{3,2},{4,5},{5,4},{6,7},{7,6},{8,9},{9,8},{10,11... | collective-permute-start | bytes 540680 | tf_op jit(solution)/shard_map/ppermute | solution.py:362
  40.3 2.0 %collective-permute-start.25 = (bf16[64,1408]{1,0:T(8,128)(2,1)S(1)}, bf16[64,1408]{1,0:T(8,128)(2,1)S(1)}, u32[]{:S(2)}, u32[]{:S(2)}) collective-permute-start(bf16[64,1408]{1,0:T(8,128)(2,1)S(1)} %shard_map.124.own_ref), channel_id=1, source_target_pairs={{0,1},{1,0},{2,3},{3,2},{4,5},{5,4},{6,7},{7,6},{8,9},{9,8},{10,11... | collective-permute-start | bytes 540680 | tf_op jit(solution)/shard_map/ppermute | solution.py:362
  41.2 1.7 %collective-permute-start.17 = (bf16[64,1280]{1,0:T(8,128)(2,1)S(1)}, bf16[64,1280]{1,0:T(8,128)(2,1)S(1)}, u32[]{:S(2)}, u32[]{:S(2)}) collective-permute-start(bf16[64,1280]{1,0:T(8,128)(2,1)S(1)} %shard_map.120.own_ref), channel_id=1, source_target_pairs={{0,1},{1,0},{2,3},{3,2},{4,5},{5,4},{6,7},{7,6},{8,9},{9,8},{10,11... | collective-permute-start | bytes 491528 | tf_op jit(solution)/shard_map/ppermute | solution.py:362
  44.1 1.6 %collective-permute-start.31 = (bf16[64,2048]{1,0:T(8,128)(2,1)S(1)}, bf16[64,2048]{1,0:T(8,128)(2,1)S(1)}, u32[]{:S(2)}, u32[]{:S(2)}) collective-permute-start(bf16[64,2048]{1,0:T(8,128)(2,1)S(1)} %get-tuple-element.78), channel_id=1, source_target_pairs={{0,1},{1,0},{2,3},{3,2},{4,5},{5,4},{6,7},{7,6},{8,9},{9,8},{10,11... | collective-permute-start | bytes 786440 | tf_op jit(solution)/shard_map/ppermute | solution.py:362
  44.7 5.8 %collective-permute-start.27 = (bf16[64,2048]{1,0:T(8,128)(2,1)S(1)}, bf16[64,2048]{1,0:T(8,128)(2,1)S(1)}, u32[]{:S(2)}, u32[]{:S(2)}) collective-permute-start(bf16[64,2048]{1,0:T(8,128)(2,1)S(1)} %get-tuple-element.72), channel_id=1, source_target_pairs={{0,1},{1,0},{2,3},{3,2},{4,5},{5,4},{6,7},{7,6},{8,9},{9,8},{10,11... | collective-permute-start | bytes 786440 | tf_op jit(solution)/shard_map/ppermute | solution.py:362
  45.8 6.8 %collective-permute-start.32 = (bf16[16,2048]{1,0:T(8,128)(2,1)S(1)}, bf16[16,2048]{1,0:T(8,128)(2,1)S(1)}, u32[]{:S(2)}, u32[]{:S(2)}) collective-permute-start(bf16[16,2048]{1,0:T(8,128)(2,1)S(1)} %get-tuple-element.80), channel_id=1, source_target_pairs={{0,2},{1,3},{2,4},{3,5},{4,6},{5,7},{6,0},{7,1},{8,10},{9,11},{10,... | collective-permute-start | bytes 196616 | tf_op jit(solution)/shard_map/ppermute | solution.py:359
  47.2 7.6 %collective-permute-start.33 = (bf16[16,2048]{1,0:T(8,128)(2,1)S(1)}, bf16[16,2048]{1,0:T(8,128)(2,1)S(1)}, u32[]{:S(2)}, u32[]{:S(2)}) collective-permute-start(bf16[16,2048]{1,0:T(8,128)(2,1)S(1)} %get-tuple-element.81), channel_id=1, source_target_pairs={{0,4},{1,5},{2,6},{3,7},{4,0},{5,1},{6,2},{7,3},{8,12},{9,13},{10,... | collective-permute-start | bytes 196616 | tf_op jit(solution)/shard_map/ppermute | solution.py:359
  49.2 6.5 %collective-permute-start.34 = (bf16[16,2048]{1,0:T(8,128)(2,1)S(1)}, bf16[16,2048]{1,0:T(8,128)(2,1)S(1)}, u32[]{:S(2)}, u32[]{:S(2)}) collective-permute-start(bf16[16,2048]{1,0:T(8,128)(2,1)S(1)} %get-tuple-element.82), channel_id=1, source_target_pairs={{0,6},{1,7},{2,0},{3,1},{4,2},{5,3},{6,4},{7,5},{8,14},{9,15},{10,... | collective-permute-start | bytes 196616 | tf_op jit(solution)/shard_map/ppermute | solution.py:359
  50.6 6.9 %collective-permute-start.28 = (bf16[16,2048]{1,0:T(8,128)(2,1)S(1)}, bf16[16,2048]{1,0:T(8,128)(2,1)S(1)}, u32[]{:S(2)}, u32[]{:S(2)}) collective-permute-start(bf16[16,2048]{1,0:T(8,128)(2,1)S(1)} %get-tuple-element.74), channel_id=1, source_target_pairs={{0,2},{1,3},{2,4},{3,5},{4,6},{5,7},{6,0},{7,1},{8,10},{9,11},{10,... | collective-permute-start | bytes 196616 | tf_op jit(solution)/shard_map/ppermute | solution.py:359
  51.4 8.9 %collective-permute-start.29 = (bf16[16,2048]{1,0:T(8,128)(2,1)S(1)}, bf16[16,2048]{1,0:T(8,128)(2,1)S(1)}, u32[]{:S(2)}, u32[]{:S(2)}) collective-permute-start(bf16[16,2048]{1,0:T(8,128)(2,1)S(1)} %get-tuple-element.75), channel_id=1, source_target_pairs={{0,4},{1,5},{2,6},{3,7},{4,0},{5,1},{6,2},{7,3},{8,12},{9,13},{10,... | collective-permute-start | bytes 196616 | tf_op jit(solution)/shard_map/ppermute | solution.py:359
  52.6 7.7 %collective-permute-start.30 = (bf16[16,2048]{1,0:T(8,128)(2,1)S(1)}, bf16[16,2048]{1,0:T(8,128)(2,1)S(1)}, u32[]{:S(2)}, u32[]{:S(2)}) collective-permute-start(bf16[16,2048]{1,0:T(8,128)(2,1)S(1)} %get-tuple-element.76), channel_id=1, source_target_pairs={{0,6},{1,7},{2,0},{3,1},{4,2},{5,3},{6,4},{7,5},{8,14},{9,15},{10,... | collective-permute-start | bytes 196616 | tf_op jit(solution)/shard_map/ppermute | solution.py:359

commit v4 on v1

--- a/solution.py
+++ b/solution.py
@@ -11,7 +11,6 @@
 BF16 = jnp.bfloat16
 TILE_ROWS = 16
 COLUMNS = 1024
-PARTS = 2
 VMEM_LIMIT = 16 * 1024 * 1024
 
 
@@ -230,7 +229,7 @@
 
 def normed_kernel(n_pair, moves, *refs):
     states = refs[: len(moves)]
-    intra_ref, grown_ref, query_ref, gain_ref, out_ref = refs[len(moves) :]
+    intra_ref, grown_ref, query_ref, gain_ref, mine_ref, theirs_ref = refs[len(moves) : len(moves) + 4] + refs[-2:]
     t, d = query_ref.shape
     me = lax.axis_index("seq")
     ranks = [move(me) for move in moves]
@@ -250,25 +249,18 @@
     normed = (attended * inverse * gain_ref[0:1, :]).astype(BF16)
     exp_index = lax.axis_index("exp")
     place = place_matrix(t // (2 * n_pair), n_pair, exp_index // 2, exp_index % 2)
-    out_ref[...] = dot_f32(place, normed, ((1,), (0,))).astype(BF16)
-
-
-def product_kernel(at, x_ref, w_ref, mine_ref, theirs_ref):
-    half = mine_ref.shape[0]
+    normed = dot_f32(place, normed, ((1,), (0,))).astype(BF16)
+    mine_ref[...] = normed[: t // 2]
+    theirs_ref[...] = normed[t // 2 :]
+
+
+def product_kernel(at, a_ref, b_ref, wa_ref, wb_ref, *outs):
+    rows = outs[0].shape[0]
     for i in range(at.start, at.stop, COLUMNS):
-        part = dot_f32(x_ref[...], w_ref[:, i : i + COLUMNS], ((1,), (0,))).astype(BF16)
-        mine_ref[:, i - at.start : i - at.start + COLUMNS] = part[:half]
-        theirs_ref[:, i - at.start : i - at.start + COLUMNS] = part[half:]
-
-
-def add_kernel(groups, a_ref, b_ref, *refs):
-    outs = refs[-len(groups) :]
-    rows = outs[0].shape[0] // len(groups[0])
-    for group, ref in zip(groups, outs):
-        for i, block in enumerate(group):
-            at = slice(block * rows, (block + 1) * rows)
-            total = a_ref[at, :].astype(F32) + b_ref[at, :].astype(F32)
-            ref[i * rows : (i + 1) * rows, :] = total.astype(ref.dtype)
+        some, there = slice(i, i + COLUMNS), slice(i - at.start, i - at.start + COLUMNS)
+        part = dot_f32(a_ref[...], wa_ref[:, some], ((1,), (0,))) + dot_f32(b_ref[...], wb_ref[:, some], ((1,), (0,)))
+        for r, ref in enumerate(outs):
+            ref[:, there] = part[r * rows : (r + 1) * rows].astype(BF16)
 
 
 def sum_kernel(count, *refs):
@@ -294,14 +286,17 @@
     out_ref[...] = enter_part(at, in_ref, own_ref, other_ref)
 
 
-def hidden_kernel(at, slices, experts, in_ref, own_ref, other_ref, before_ref, member_ref, out_ref):
+def hidden_kernel(at, slices, experts, in_ref, own_ref, other_ref, before_ref, member_ref, mine_ref, theirs_ref):
     total = before_ref[...] + enter_part(at, in_ref, own_ref, other_ref)
-    t, hid = out_ref.shape
+    half, hid = mine_ref.shape
+    t = 2 * half
     gate, up, logits = total[0:hid], total[hid : 2 * hid], total[2 * hid : 2 * hid + experts]
     raised = jnp.where(member_ref[0:experts, :] > 0.5, jnp.exp(logits), 0.0)
     mine = iota2((experts, t), 0) == lax.axis_index("exp") // slices
     prob = jnp.sum(jnp.where(mine, raised, 0.0), axis=0, keepdims=True) / jnp.sum(raised, axis=0, keepdims=True)
-    out_ref[...] = (gate / (1.0 + jnp.exp(-gate)) * up * prob).T.astype(BF16)
+    hidden = (gate / (1.0 + jnp.exp(-gate)) * up * prob).T.astype(BF16)
+    mine_ref[...] = hidden[:half]
+    theirs_ref[...] = hidden[half:]
 
 
 def result_kernel(count, *refs):
@@ -347,22 +342,18 @@
     def across(x):
         return lax.ppermute(x, "exp", [(e, e ^ 1) for e in range(exp_count)])
 
-    size = width // PARTS
-    ranges = [slice(i * size, (i + 1) * size) for i in range(PARTS)]
+    size = width // 2
+    ranges = [slice(0, size), slice(size, width)]
 
     def rows_of(count):
         return out((count * rows, size), BF16)
 
-    def reduce(products):
-        others = [across(theirs) for _, theirs in products]
+    def reduce(mine, theirs, w, w_other):
+        other = across(theirs)
         terms = [
-            call(functools.partial(add_kernel, [[r] for r in range(n_pair)]), [rows_of(1)] * n_pair, (mine, other))
-            for (mine, _), other in zip(products, others)
+            call(functools.partial(product_kernel, at), [rows_of(1)] * n_pair, (mine, other, w, w_other)) for at in ranges
         ]
         return [[term[0]] + [shift(term[r], r) for r in range(1, n_pair)] for term in terms]
-
-    def products_of(x, w):
-        return [call(functools.partial(product_kernel, at), [rows_of(n_pair)] * 2, (x, w)) for at in ranges]
 
     decay_row = decay_log.T
     block = pltpu.VMEM((t, d), BF16)
@@ -399,12 +390,13 @@
         ],
         far=10,
     )
-    (normed,) = call(
+    w_out_other, w_down_other = across(w_out), across(w_down[0])
+    mine, theirs = call(
         functools.partial(normed_kernel, n_pair, moves),
-        [out((t, d), BF16)],
-        (*states, intra, grown, query_near, gain),
-    )
-    terms = reduce(products_of(normed, w_out_near))
+        [out((t // 2, d), BF16)] * 2,
+        (*states, intra, grown, query_near, gain, w_down_other),
+    )
+    terms = reduce(mine, theirs, w_out_near, w_out_other)
     mixed = [call(functools.partial(sum_kernel, n_pair), [rows_of(1)], term)[0] for term in terms]
     gathered = [[shift(m, -r) if r else m for r in range(n_pair)] for m in mixed]
     own, after = [], ()
@@ -415,15 +407,14 @@
                 fetch_down_kernel, [out((hid, width), BF16), out((8, 128), F32)], (w_down[0], own[0]), [dma], far=1
             )
             after = (token,)
-    total = ()
-    for at, x in zip(ranges, own):
-        if at.stop < width:
-            kernel, shape = functools.partial(enter_kernel, at), out((w_in.shape[0], t), F32)
-        else:
-            kernel, shape = functools.partial(hidden_kernel, at, slices, experts), out((t, hid), BF16)
-            total = (*total, member)
-        total = call(kernel, [shape], (w_in, x, across(x), *total))
-    sums = reduce(products_of(total[0], w_down_near))
+    left, right = ranges
+    (total,) = call(functools.partial(enter_kernel, left), [out((w_in.shape[0], t), F32)], (w_in, own[0], across(own[0])))
+    mine, theirs = call(
+        functools.partial(hidden_kernel, right, slices, experts),
+        [out((t // 2, hid), BF16)] * 2,
+        (w_in, own[1], across(own[1]), total, member),
+    )
+    sums = reduce(mine, theirs, w_down_near, w_down_other)
     args = [x for some, m in zip(sums, mixed) for x in (*some, m)]
     return call(functools.partial(result_kernel, n_pair + 1), [out((rows, width), BF16)], args)[0]
 

time: 57.9 us -> 57.8 us (level)
    ppermute x6, waiting for transfers between devices: 1.9 us -> 2.98 us  [across(): return lax.ppermute(x, 'exp', [(e, e ^ 1) for e in range(exp_count)])]
    ppermute x18, waiting for transfers between devices: 8.13 us -> 7.18 us  [shift(): lax.ppermute(x, 'exp', [(e, (e + 2 * r) % exp_count) for e in range(exp_c...]
    pallas_call x19 -> x15, Pallas kernels: 10.4 us -> 10.5 us  [call(): pl.pallas_call(kernel, out_shape=outs, in_specs=[pl.BlockSpec(memory_spac...]
  transfers between devices with their start and end apart: 27 -> 27, of which waited for: 9 -> 8; matrix products, arithmetic and copies ran while one was open for 0% -> 0% of each run, Pallas kernels for 11% -> 14%
where the time goes in v4:
time: 57.8 us; the launch traced here: 57.6 us
  starting transfers between devices  35.9 us (62%)
  waiting for transfers between devices  11.1 us (19%)
  Pallas kernels  10.5 us (18%)
    ppermute x18, starting transfers between devices, shift(): lax.ppermute(x, 'exp', [(e, (e + 2 * r) % exp_count) for e in range(exp_c...  30.4 us
    pallas_call x15, Pallas kernels, call(): pl.pallas_call(kernel, out_shape=outs, in_specs=[pl.BlockSpec(memory_spac...  10.5 us
    ppermute x18, waiting for transfers between devices, shift(): lax.ppermute(x, 'exp', [(e, (e + 2 * r) % exp_count) for e in range(exp_c...  7.18 us
    ppermute x3, starting transfers between devices, local(): lax.ppermute(state, 'seq', [(move(i), i) for i in range(seq_count)])  4.6 us
    ppermute x6, waiting for transfers between devices, across(): return lax.ppermute(x, 'exp', [(e, e ^ 1) for e in range(exp_count)])  2.98 us
  transfers between devices with their start and end apart: 27, of which 8 were waited for; matrix products, arithmetic and copies ran while one was open for 0% of the time, Pallas kernels for 14%

profile of v4, /device:TPU:0, one launch (start us, length us, event | category | flops | bytes accessed | tf_op | source)
XLA Modules:
  0.0 57.6 jit_solution(11345340350330334136)
XLA Ops:
  0.0 0.5 collective-permute-start.3
  0.5 0.1 collective-permute-start.5
  0.5 1.1 %shard_map.109._ = bf16[144,128]{1,0:T(8,128)(2,1)S(1)} custom-call(bf16[128,128]{1,0:T(8,128)(2,1)} %key_hbm.3, bf16[128,128]{1,0:T(8,128)(2,1)} %value_hbm.3, f32[1,128]{1,0:T(1,128)} %bitcast.16), custom_call_target="tpu_custom_call" | custom-call | tf_op jit(solution)/shard_map/pallas_call | solution.py:316
  1.6 4.0 %collective-permute-start.2 = (bf16[144,128]{1,0:T(8,128)(2,1)S(1)}, bf16[144,128]{1,0:T(8,128)(2,1)S(1)}, u32[]{:S(2)}, u32[]{:S(2)}) collective-permute-start(bf16[144,128]{1,0:T(8,128)(2,1)S(1)} %shard_map.109._), channel_id=1, source_target_pairs={{24,0},{16,8},{8,16},{0,24},{25,1},{17,9},{9,17},{1,25},{26,2},{18... | collective-permute-start | bytes 110600 | tf_op jit(solution)/shard_map/ppermute | solution.py:369
  5.6 0.5 collective-permute-start.1
  6.1 0.1 collective-permute-start
  6.2 2.9 %shard_map.110 = (f32[128,128]{1,0:T(8,128)S(1)}, f32[128,128]{1,0:T(8,128)S(1)}, bf16[128,128]{1,0:T(8,128)(2,1)S(1)}, f32[8,128]{1,0:T(8,128)S(1)}, bf16[128,4...) custom-call(bf16[128,128]{1,0:T(8,128)(2,1)} %query_hbm.1, bf16[128,128]{1,0:T(8,128)(2,1)} %key_hbm.3, ...), custom_call_target="tpu_custom_call" | custom-call | tf_op jit(solution)/shard_map/pallas_call | solution.py:316
  9.1 0.0 collective-permute-done.2.refs_2_
  9.2 0.4 collective-permute-done.1.refs_1_
  9.5 0.5 collective-permute-done.refs_0_
  10.1 0.0 collective-permute-done.3.refs_7_.wb_ref
  10.1 0.4 shard_map.111
  10.5 0.1 collective-permute-start.4
  10.6 0.0 collective-permute-done.5.wb_ref
  10.6 1.2 %collective-permute-done.4.b_ref = bf16[64,128]{1,0:T(8,128)(2,1)S(1)} collective-permute-done((bf16[64,128]{1,0:T(8,128)(2,1)S(1)}, bf16[64,128]{1,0:T(8,128)(2,1)S(1)}, u32[]{:S(2)}, u32[]{:S(2)}) %collective-permute-start.4) | collective-permute-done | bytes 16416 | tf_op jit(solution)/shard_map/ppermute | solution.py:343
  11.7 0.3 shard_map.114
  12.0 1.6 %collective-permute-start.12 = (bf16[16,2048]{1,0:T(8,128)(2,1)S(1)}, bf16[16,2048]{1,0:T(8,128)(2,1)S(1)}, u32[]{:S(2)}, u32[]{:S(2)}) collective-permute-start(bf16[16,2048]{1,0:T(8,128)(2,1)S(1)} %get-tuple-element.47), channel_id=1, source_target_pairs={{0,2},{1,3},{2,4},{3,5},{4,6},{5,7},{6,0},{7,1},{8,10},{9,11},{10,... | collective-permute-start | bytes 196616 | tf_op jit(solution)/shard_map/ppermute | solution.py:340
  13.7 2.6 %collective-permute-start.13 = (bf16[16,2048]{1,0:T(8,128)(2,1)S(1)}, bf16[16,2048]{1,0:T(8,128)(2,1)S(1)}, u32[]{:S(2)}, u32[]{:S(2)}) collective-permute-start(bf16[16,2048]{1,0:T(8,128)(2,1)S(1)} %get-tuple-element.48), channel_id=1, source_target_pairs={{0,4},{1,5},{2,6},{3,7},{4,0},{5,1},{6,2},{7,3},{8,12},{9,13},{10,... | collective-permute-start | bytes 196616 | tf_op jit(solution)/shard_map/ppermute | solution.py:340
  16.2 1.3 %collective-permute-start.14 = (bf16[16,2048]{1,0:T(8,128)(2,1)S(1)}, bf16[16,2048]{1,0:T(8,128)(2,1)S(1)}, u32[]{:S(2)}, u32[]{:S(2)}) collective-permute-start(bf16[16,2048]{1,0:T(8,128)(2,1)S(1)} %get-tuple-element.49), channel_id=1, source_target_pairs={{0,6},{1,7},{2,0},{3,1},{4,2},{5,3},{6,4},{7,5},{8,14},{9,15},{10,... | collective-permute-start | bytes 196616 | tf_op jit(solution)/shard_map/ppermute | solution.py:340
  17.6 0.3 shard_map.112
  17.9 0.7 %collective-permute-start.6 = (bf16[16,2048]{1,0:T(8,128)(2,1)S(1)}, bf16[16,2048]{1,0:T(8,128)(2,1)S(1)}, u32[]{:S(2)}, u32[]{:S(2)}) collective-permute-start(bf16[16,2048]{1,0:T(8,128)(2,1)S(1)} %get-tuple-element.43), channel_id=1, source_target_pairs={{0,2},{1,3},{2,4},{3,5},{4,6},{5,7},{6,0},{7,1},{8,10},{9,11},{10,... | collective-permute-start | bytes 196616 | tf_op jit(solution)/shard_map/ppermute | solution.py:340
  18.6 0.3 collective-permute-start.7
  19.0 2.8 %collective-permute-start.8 = (bf16[16,2048]{1,0:T(8,128)(2,1)S(1)}, bf16[16,2048]{1,0:T(8,128)(2,1)S(1)}, u32[]{:S(2)}, u32[]{:S(2)}) collective-permute-start(bf16[16,2048]{1,0:T(8,128)(2,1)S(1)} %get-tuple-element.45), channel_id=1, source_target_pairs={{0,6},{1,7},{2,0},{3,1},{4,2},{5,3},{6,4},{7,5},{8,14},{9,15},{10,... | collective-permute-start | bytes 196616 | tf_op jit(solution)/shard_map/ppermute | solution.py:340
  21.8 4.1 %collective-permute-start.17 = (bf16[16,2048]{1,0:T(8,128)(2,1)S(1)}, bf16[16,2048]{1,0:T(8,128)(2,1)S(1)}, u32[]{:S(2)}, u32[]{:S(2)}) collective-permute-start(bf16[16,2048]{1,0:T(8,128)(2,1)S(1)} %shard_map.115.refs_0_.refs_4_), channel_id=1, source_target_pairs={{0,2},{1,3},{2,4},{3,5},{4,6},{5,7},{6,0},{7,1},{8,10},{9,11},{10,... | collective-permute-start | bytes 196616 | tf_op jit(solution)/shard_map/ppermute | solution.py:340
  25.9 2.4 %collective-permute-start.15 = (bf16[16,2048]{1,0:T(8,128)(2,1)S(1)}, bf16[16,2048]{1,0:T(8,128)(2,1)S(1)}, u32[]{:S(2)}, u32[]{:S(2)}) collective-permute-start(bf16[16,2048]{1,0:T(8,128)(2,1)S(1)} %shard_map.115.refs_0_.refs_4_), channel_id=1, source_target_pairs={{0,6},{1,7},{2,0},{3,1},{4,2},{5,3},{6,4},{7,5},{8,14},{9,15},{10,... | collective-permute-start | bytes 196616 | tf_op jit(solution)/shard_map/ppermute | solution.py:340
  28.4 3.1 %collective-permute-start.11 = (bf16[16,2048]{1,0:T(8,128)(2,1)S(1)}, bf16[16,2048]{1,0:T(8,128)(2,1)S(1)}, u32[]{:S(2)}, u32[]{:S(2)}) collective-permute-start(bf16[16,2048]{1,0:T(8,128)(2,1)S(1)} %shard_map.113.refs_0_.refs_9_), channel_id=1, source_target_pairs={{0,2},{1,3},{2,4},{3,5},{4,6},{5,7},{6,0},{7,1},{8,10},{9,11},{10,... | collective-permute-start | bytes 196616 | tf_op jit(solution)/shard_map/ppermute | solution.py:340
  31.5 0.1 collective-permute-start.10
  31.5 2.4 %collective-permute-start.9 = (bf16[16,2048]{1,0:T(8,128)(2,1)S(1)}, bf16[16,2048]{1,0:T(8,128)(2,1)S(1)}, u32[]{:S(2)}, u32[]{:S(2)}) collective-permute-start(bf16[16,2048]{1,0:T(8,128)(2,1)S(1)} %shard_map.113.refs_0_.refs_9_), channel_id=1, source_target_pairs={{0,6},{1,7},{2,0},{3,1},{4,2},{5,3},{6,4},{7,5},{8,14},{9,15},{10,... | collective-permute-start | bytes 196616 | tf_op jit(solution)/shard_map/ppermute | solution.py:340
  34.0 0.1 collective-permute-start.19
  34.0 1.7 %shard_map.117 = (bf16[288,4096]{1,0:T(8,128)(2,1)S(1)}, f32[8,128]{1,0:T(8,128)S(1)}) custom-call(bf16[288,4096]{1,0:T(8,128)(2,1)} %bitcast.14, bf16[64,2048]{1,0:T(8,128)(2,1)S(1)} %shard_map.116._.own_ref), custom_call_target="tpu_custom_call" | custom-call | tf_op jit(solution)/shard_map/pallas_call | solution.py:316
  35.7 2.1 %collective-permute-done.10.refs_2_ = bf16[16,2048]{1,0:T(8,128)(2,1)S(1)} collective-permute-done((bf16[16,2048]{1,0:T(8,128)(2,1)S(1)}, bf16[16,2048]{1,0:T(8,128)(2,1)S(1)}, u32[]{:S(2)}, u32[]{:S(2)}) %collective-permute-start.10) | collective-permute-done | bytes 65568 | tf_op jit(solution)/shard_map/ppermute | solution.py:340
  37.9 0.1 collective-permute-start.18
  38.0 0.8 %shard_map.119.before_ref = f32[592,128]{1,0:T(8,128)S(1)} custom-call(bf16[592,4096]{1,0:T(8,128)(2,1)S(1)} %get-tuple-element.34.in_ref, bf16[64,2048]{1,0:T(8,128)(2,1)S(1)} %shard_map.116._.own_ref, bf16[64,2048]{1,0:T(8,128)(2,1)S(1)} %collective-permute-done.19.other_ref), custom_call_target="tpu_custom_call" | custom-call | tf_op jit(solution)/shard_map/pallas_call | solution.py:316
  38.8 0.7 %collective-permute-done.18.other_ref = bf16[64,2048]{1,0:T(8,128)(2,1)S(1)} collective-permute-done((bf16[64,2048]{1,0:T(8,128)(2,1)S(1)}, bf16[64,2048]{1,0:T(8,128)(2,1)S(1)}, u32[]{:S(2)}, u32[]{:S(2)}) %collective-permute-start.18) | collective-permute-done | bytes 262176 | tf_op jit(solution)/shard_map/ppermute | solution.py:343
  39.5 0.9 %shard_map.120 = (bf16[64,288]{1,0:T(8,128)(2,1)S(1)}, bf16[64,288]{1,0:T(8,128)(2,1)S(1)}) custom-call(bf16[592,4096]{1,0:T(8,128)(2,1)S(1)} %get-tuple-element.34.in_ref, bf16[64,2048]{1,0:T(8,128)(2,1)S(1)} %shard_map.118.own_ref, bf16[64,2048]{1,0:T(8,128)(2,1)S(1)} %collective-permute-done.18.other_ref, f32[592,128]{1,0:T(8,128)S(1)} %shard_map.119.before_ref, ...), custom_call_target="tpu_custom_call" | custom-call | tf_op jit(solution)/shard_map/pallas_call | solution.py:316
  40.4 0.2 collective-permute-start.20
  40.6 1.1 %collective-permute-done.20.b_ref = bf16[64,288]{1,0:T(8,128)(2,1)S(1)} collective-permute-done((bf16[64,288]{1,0:T(8,128)(2,1)S(1)}, bf16[64,288]{1,0:T(8,128)(2,1)S(1)}, u32[]{:S(2)}, u32[]{:S(2)}) %collective-permute-start.20) | collective-permute-done | bytes 36896 | tf_op jit(solution)/shard_map/ppermute | solution.py:343
  41.7 0.6 %shard_map.122 = (bf16[16,2048]{1,0:T(8,128)(2,1)S(1)}, bf16[16,2048]{1,0:T(8,128)(2,1)S(1)}, bf16[16,2048]{1,0:T(8,128)(2,1)S(1)}, bf16[16,2048]{1,0:T(8,128)(2,1)S(1)}) custom-call(bf16[64,288]{1,0:T(8,128)(2,1)S(1)} %get-tuple-element.52.a_ref, bf16[64,288]{1,0:T(8,128)(2,1)S(1)} %collective-permute-done.20.b_ref, ...), custom_call_target="tpu_custom_call" | custom-call | tf_op jit(solution)/shard_map/pallas_call | solution.py:316
  42.3 1.9 %collective-permute-start.24 = (bf16[16,2048]{1,0:T(8,128)(2,1)S(1)}, bf16[16,2048]{1,0:T(8,128)(2,1)S(1)}, u32[]{:S(2)}, u32[]{:S(2)}) collective-permute-start(bf16[16,2048]{1,0:T(8,128)(2,1)S(1)} %get-tuple-element.60), channel_id=1, source_target_pairs={{0,2},{1,3},{2,4},{3,5},{4,6},{5,7},{6,0},{7,1},{8,10},{9,11},{10,... | collective-permute-start | bytes 196616 | tf_op jit(solution)/shard_map/ppermute | solution.py:340
  44.3 1.7 %collective-permute-start.25 = (bf16[16,2048]{1,0:T(8,128)(2,1)S(1)}, bf16[16,2048]{1,0:T(8,128)(2,1)S(1)}, u32[]{:S(2)}, u32[]{:S(2)}) collective-permute-start(bf16[16,2048]{1,0:T(8,128)(2,1)S(1)} %get-tuple-element.61), channel_id=1, source_target_pairs={{0,4},{1,5},{2,6},{3,7},{4,0},{5,1},{6,2},{7,3},{8,12},{9,13},{10,... | collective-permute-start | bytes 196616 | tf_op jit(solution)/shard_map/ppermute | solution.py:340
  46.0 0.7 %collective-permute-start.26 = (bf16[16,2048]{1,0:T(8,128)(2,1)S(1)}, bf16[16,2048]{1,0:T(8,128)(2,1)S(1)}, u32[]{:S(2)}, u32[]{:S(2)}) collective-permute-start(bf16[16,2048]{1,0:T(8,128)(2,1)S(1)} %get-tuple-element.62), channel_id=1, source_target_pairs={{0,6},{1,7},{2,0},{3,1},{4,2},{5,3},{6,4},{7,5},{8,14},{9,15},{10,... | collective-permute-start | bytes 196616 | tf_op jit(solution)/shard_map/ppermute | solution.py:340
  46.7 0.6 %shard_map.121 = (bf16[16,2048]{1,0:T(8,128)(2,1)S(1)}, bf16[16,2048]{1,0:T(8,128)(2,1)S(1)}, bf16[16,2048]{1,0:T(8,128)(2,1)S(1)}, bf16[16,2048]{1,0:T(8,128)(2,1)S(1)}) custom-call(bf16[64,288]{1,0:T(8,128)(2,1)S(1)} %get-tuple-element.52.a_ref, bf16[64,288]{1,0:T(8,128)(2,1)S(1)} %collective-permute-done.20.b_ref, ...), custom_call_target="tpu_custom_call" | custom-call | tf_op jit(solution)/shard_map/pallas_call | solution.py:316
  47.3 1.4 %collective-permute-start.21 = (bf16[16,2048]{1,0:T(8,128)(2,1)S(1)}, bf16[16,2048]{1,0:T(8,128)(2,1)S(1)}, u32[]{:S(2)}, u32[]{:S(2)}) collective-permute-start(bf16[16,2048]{1,0:T(8,128)(2,1)S(1)} %get-tuple-element.56), channel_id=1, source_target_pairs={{0,2},{1,3},{2,4},{3,5},{4,6},{5,7},{6,0},{7,1},{8,10},{9,11},{10,... | collective-permute-start | bytes 196616 | tf_op jit(solution)/shard_map/ppermute | solution.py:340
  48.7 1.2 %collective-permute-start.22 = (bf16[16,2048]{1,0:T(8,128)(2,1)S(1)}, bf16[16,2048]{1,0:T(8,128)(2,1)S(1)}, u32[]{:S(2)}, u32[]{:S(2)}) collective-permute-start(bf16[16,2048]{1,0:T(8,128)(2,1)S(1)} %get-tuple-element.57), channel_id=1, source_target_pairs={{0,4},{1,5},{2,6},{3,7},{4,0},{5,1},{6,2},{7,3},{8,12},{9,13},{10,... | collective-permute-start | bytes 196616 | tf_op jit(solution)/shard_map/ppermute | solution.py:340
  49.9 2.0 %collective-permute-start.23 = (bf16[16,2048]{1,0:T(8,128)(2,1)S(1)}, bf16[16,2048]{1,0:T(8,128)(2,1)S(1)}, u32[]{:S(2)}, u32[]{:S(2)}) collective-permute-start(bf16[16,2048]{1,0:T(8,128)(2,1)S(1)} %get-tuple-element.58), channel_id=1, source_target_pairs={{0,6},{1,7},{2,0},{3,1},{4,2},{5,3},{6,4},{7,5},{8,14},{9,15},{10,... | collective-permute-start | bytes 196616 | tf_op jit(solution)/shard_map/ppermute | solution.py:340
  51.9 2.3 %collective-permute-done.21.refs_1_ = bf16[16,2048]{1,0:T(8,128)(2,1)S(1)} collective-permute-done((bf16[16,2048]{1,0:T(8,128)(2,1)S(1)}, bf16[16,2048]{1,0:T(8,128)(2,1)S(1)}, u32[]{:S(2)}, u32[]{:S(2)}) %collective-permute-start.21) | collective-permute-done | bytes 65568 | tf_op jit(solution)/shard_map/ppermute | solution.py:340
  54.2 2.7 %collective-permute-done.22.refs_2_ = bf16[16,2048]{1,0:T(8,128)(2,1)S(1)} collective-permute-done((bf16[16,2048]{1,0:T(8,128)(2,1)S(1)}, bf16[16,2048]{1,0:T(8,128)(2,1)S(1)}, u32[]{:S(2)}, u32[]{:S(2)}) %collective-permute-start.22) | collective-permute-done | bytes 65568 | tf_op jit(solution)/shard_map/ppermute | solution.py:340
  56.9 0.7 %shard_map.123 = bf16[16,4096]{1,0:T(8,128)(2,1)} custom-call(bf16[16,2048]{1,0:T(8,128)(2,1)S(1)} %get-tuple-element.55.refs_0_, bf16[16,2048]{1,0:T(8,128)(2,1)S(1)} %collective-permute-done.21.refs_1_, bf16[16,2048]{1,0:T(8,128)(2,1)S(1)} %collective-permute-done.22.refs_2_, bf16[16,2048]{1,0:T(8,128)(2,1)S(1)} %collective-permute-done.23.refs_3_, ...), custom_call_target="tpu_custom_call" | custom-call | tf_op jit(solution)/shard_map/pallas_call | solution.py:316
  (21 shorter events, 0.2 us)
Async XLA Ops:
  0.0 10.1 %collective-permute-start.3 = (bf16[288,4096]{1,0:T(8,128)(2,1)}, bf16[288,4096]{1,0:T(8,128)(2,1)S(1)}, u32[]{:S(2)}, u32[]{:S(2)}) collective-permute-start(bf16[288,4096]{1,0:T(8,128)(2,1)} %bitcast.13), channel_id=1, source_target_pairs={{0,1},{1,0},{2,3},{3,2},{4,5},{5,4},{6,7},{7,6},{8,9},{9,8},{10,11... | collective-permute-start | bytes 7077896 | tf_op jit(solution)/shard_map/ppermute | solution.py:343
  0.5 10.1 %collective-permute-start.5 = (bf16[128,4096]{1,0:T(8,128)(2,1)}, bf16[128,4096]{1,0:T(8,128)(2,1)S(1)}, u32[]{:S(2)}, u32[]{:S(2)}) collective-permute-start(bf16[128,4096]{1,0:T(8,128)(2,1)} %w_out_hbm.1), channel_id=1, source_target_pairs={{0,1},{1,0},{2,3},{3,2},{4,5},{5,4},{6,7},{7,6},{8,9},{9,8},{10,11... | collective-permute-start | bytes 3145736 | tf_op jit(solution)/shard_map/ppermute | solution.py:343
  1.6 7.5 %collective-permute-start.2 = (bf16[144,128]{1,0:T(8,128)(2,1)S(1)}, bf16[144,128]{1,0:T(8,128)(2,1)S(1)}, u32[]{:S(2)}, u32[]{:S(2)}) collective-permute-start(bf16[144,128]{1,0:T(8,128)(2,1)S(1)} %shard_map.109._), channel_id=1, source_target_pairs={{24,0},{16,8},{8,16},{0,24},{25,1},{17,9},{9,17},{1,25},{26,2},{18... | collective-permute-start | bytes 110600 | tf_op jit(solution)/shard_map/ppermute | solution.py:369
  5.6 4.0 %collective-permute-start.1 = (bf16[144,128]{1,0:T(8,128)(2,1)S(1)}, bf16[144,128]{1,0:T(8,128)(2,1)S(1)}, u32[]{:S(2)}, u32[]{:S(2)}) collective-permute-start(bf16[144,128]{1,0:T(8,128)(2,1)S(1)} %shard_map.109._), channel_id=1, source_target_pairs={{16,0},{24,8},{0,16},{8,24},{17,1},{25,9},{1,17},{9,25},{18,2},{26... | collective-permute-start | bytes 110600 | tf_op jit(solution)/shard_map/ppermute | solution.py:369
  6.1 4.0 %collective-permute-start = (bf16[144,128]{1,0:T(8,128)(2,1)S(1)}, bf16[144,128]{1,0:T(8,128)(2,1)S(1)}, u32[]{:S(2)}, u32[]{:S(2)}) collective-permute-start(bf16[144,128]{1,0:T(8,128)(2,1)S(1)} %shard_map.109._), channel_id=1, source_target_pairs={{8,0},{0,8},{24,16},{16,24},{9,1},{1,9},{25,17},{17,25},{10,2},{2,... | collective-permute-start | bytes 110600 | tf_op jit(solution)/shard_map/ppermute | solution.py:369
  10.5 1.2 %collective-permute-start.4 = (bf16[64,128]{1,0:T(8,128)(2,1)S(1)}, bf16[64,128]{1,0:T(8,128)(2,1)S(1)}, u32[]{:S(2)}, u32[]{:S(2)}) collective-permute-start(bf16[64,128]{1,0:T(8,128)(2,1)S(1)} %get-tuple-element.40), channel_id=1, source_target_pairs={{0,1},{1,0},{2,3},{3,2},{4,5},{5,4},{6,7},{7,6},{8,9},{9,8},{10,11... | collective-permute-start | bytes 49160 | tf_op jit(solution)/shard_map/ppermute | solution.py:343
  12.0 6.9 %collective-permute-start.12 = (bf16[16,2048]{1,0:T(8,128)(2,1)S(1)}, bf16[16,2048]{1,0:T(8,128)(2,1)S(1)}, u32[]{:S(2)}, u32[]{:S(2)}) collective-permute-start(bf16[16,2048]{1,0:T(8,128)(2,1)S(1)} %get-tuple-element.47), channel_id=1, source_target_pairs={{0,2},{1,3},{2,4},{3,5},{4,6},{5,7},{6,0},{7,1},{8,10},{9,11},{10,... | collective-permute-start | bytes 196616 | tf_op jit(solution)/shard_map/ppermute | solution.py:340
  13.7 8.1 %collective-permute-start.13 = (bf16[16,2048]{1,0:T(8,128)(2,1)S(1)}, bf16[16,2048]{1,0:T(8,128)(2,1)S(1)}, u32[]{:S(2)}, u32[]{:S(2)}) collective-permute-start(bf16[16,2048]{1,0:T(8,128)(2,1)S(1)} %get-tuple-element.48), channel_id=1, source_target_pairs={{0,4},{1,5},{2,6},{3,7},{4,0},{5,1},{6,2},{7,3},{8,12},{9,13},{10,... | collective-permute-start | bytes 196616 | tf_op jit(solution)/shard_map/ppermute | solution.py:340
  16.2 5.5 %collective-permute-start.14 = (bf16[16,2048]{1,0:T(8,128)(2,1)S(1)}, bf16[16,2048]{1,0:T(8,128)(2,1)S(1)}, u32[]{:S(2)}, u32[]{:S(2)}) collective-permute-start(bf16[16,2048]{1,0:T(8,128)(2,1)S(1)} %get-tuple-element.49), channel_id=1, source_target_pairs={{0,6},{1,7},{2,0},{3,1},{4,2},{5,3},{6,4},{7,5},{8,14},{9,15},{10,... | collective-permute-start | bytes 196616 | tf_op jit(solution)/shard_map/ppermute | solution.py:340
  17.9 8.0 %collective-permute-start.6 = (bf16[16,2048]{1,0:T(8,128)(2,1)S(1)}, bf16[16,2048]{1,0:T(8,128)(2,1)S(1)}, u32[]{:S(2)}, u32[]{:S(2)}) collective-permute-start(bf16[16,2048]{1,0:T(8,128)(2,1)S(1)} %get-tuple-element.43), channel_id=1, source_target_pairs={{0,2},{1,3},{2,4},{3,5},{4,6},{5,7},{6,0},{7,1},{8,10},{9,11},{10,... | collective-permute-start | bytes 196616 | tf_op jit(solution)/shard_map/ppermute | solution.py:340
  18.6 9.7 %collective-permute-start.7 = (bf16[16,2048]{1,0:T(8,128)(2,1)S(1)}, bf16[16,2048]{1,0:T(8,128)(2,1)S(1)}, u32[]{:S(2)}, u32[]{:S(2)}) collective-permute-start(bf16[16,2048]{1,0:T(8,128)(2,1)S(1)} %get-tuple-element.44), channel_id=1, source_target_pairs={{0,4},{1,5},{2,6},{3,7},{4,0},{5,1},{6,2},{7,3},{8,12},{9,13},{10,... | collective-permute-start | bytes 196616 | tf_op jit(solution)/shard_map/ppermute | solution.py:340
  19.0 9.4 %collective-permute-start.8 = (bf16[16,2048]{1,0:T(8,128)(2,1)S(1)}, bf16[16,2048]{1,0:T(8,128)(2,1)S(1)}, u32[]{:S(2)}, u32[]{:S(2)}) collective-permute-start(bf16[16,2048]{1,0:T(8,128)(2,1)S(1)} %get-tuple-element.45), channel_id=1, source_target_pairs={{0,6},{1,7},{2,0},{3,1},{4,2},{5,3},{6,4},{7,5},{8,14},{9,15},{10,... | collective-permute-start | bytes 196616 | tf_op jit(solution)/shard_map/ppermute | solution.py:340
  21.8 9.7 %collective-permute-start.17 = (bf16[16,2048]{1,0:T(8,128)(2,1)S(1)}, bf16[16,2048]{1,0:T(8,128)(2,1)S(1)}, u32[]{:S(2)}, u32[]{:S(2)}) collective-permute-start(bf16[16,2048]{1,0:T(8,128)(2,1)S(1)} %shard_map.115.refs_0_.refs_4_), channel_id=1, source_target_pairs={{0,2},{1,3},{2,4},{3,5},{4,6},{5,7},{6,0},{7,1},{8,10},{9,11},{10,... | collective-permute-start | bytes 196616 | tf_op jit(solution)/shard_map/ppermute | solution.py:340
  25.9 8.1 %collective-permute-start.16 = (bf16[16,2048]{1,0:T(8,128)(2,1)S(1)}, bf16[16,2048]{1,0:T(8,128)(2,1)S(1)}, u32[]{:S(2)}, u32[]{:S(2)}) collective-permute-start(bf16[16,2048]{1,0:T(8,128)(2,1)S(1)} %shard_map.115.refs_0_.refs_4_), channel_id=1, source_target_pairs={{0,4},{1,5},{2,6},{3,7},{4,0},{5,1},{6,2},{7,3},{8,12},{9,13},{10,... | collective-permute-start | bytes 196616 | tf_op jit(solution)/shard_map/ppermute | solution.py:340
  25.9 8.1 %collective-permute-start.15 = (bf16[16,2048]{1,0:T(8,128)(2,1)S(1)}, bf16[16,2048]{1,0:T(8,128)(2,1)S(1)}, u32[]{:S(2)}, u32[]{:S(2)}) collective-permute-start(bf16[16,2048]{1,0:T(8,128)(2,1)S(1)} %shard_map.115.refs_0_.refs_4_), channel_id=1, source_target_pairs={{0,6},{1,7},{2,0},{3,1},{4,2},{5,3},{6,4},{7,5},{8,14},{9,15},{10,... | collective-permute-start | bytes 196616 | tf_op jit(solution)/shard_map/ppermute | solution.py:340
  28.4 7.4 %collective-permute-start.11 = (bf16[16,2048]{1,0:T(8,128)(2,1)S(1)}, bf16[16,2048]{1,0:T(8,128)(2,1)S(1)}, u32[]{:S(2)}, u32[]{:S(2)}) collective-permute-start(bf16[16,2048]{1,0:T(8,128)(2,1)S(1)} %shard_map.113.refs_0_.refs_9_), channel_id=1, source_target_pairs={{0,2},{1,3},{2,4},{3,5},{4,6},{5,7},{6,0},{7,1},{8,10},{9,11},{10,... | collective-permute-start | bytes 196616 | tf_op jit(solution)/shard_map/ppermute | solution.py:340
  31.5 6.4 %collective-permute-start.10 = (bf16[16,2048]{1,0:T(8,128)(2,1)S(1)}, bf16[16,2048]{1,0:T(8,128)(2,1)S(1)}, u32[]{:S(2)}, u32[]{:S(2)}) collective-permute-start(bf16[16,2048]{1,0:T(8,128)(2,1)S(1)} %shard_map.113.refs_0_.refs_9_), channel_id=1, source_target_pairs={{0,4},{1,5},{2,6},{3,7},{4,0},{5,1},{6,2},{7,3},{8,12},{9,13},{10,... | collective-permute-start | bytes 196616 | tf_op jit(solution)/shard_map/ppermute | solution.py:340
  31.5 6.3 %collective-permute-start.9 = (bf16[16,2048]{1,0:T(8,128)(2,1)S(1)}, bf16[16,2048]{1,0:T(8,128)(2,1)S(1)}, u32[]{:S(2)}, u32[]{:S(2)}) collective-permute-start(bf16[16,2048]{1,0:T(8,128)(2,1)S(1)} %shard_map.113.refs_0_.refs_9_), channel_id=1, source_target_pairs={{0,6},{1,7},{2,0},{3,1},{4,2},{5,3},{6,4},{7,5},{8,14},{9,15},{10,... | collective-permute-start | bytes 196616 | tf_op jit(solution)/shard_map/ppermute | solution.py:340
  34.0 4.0 %collective-permute-start.19 = (bf16[64,2048]{1,0:T(8,128)(2,1)S(1)}, bf16[64,2048]{1,0:T(8,128)(2,1)S(1)}, u32[]{:S(2)}, u32[]{:S(2)}) collective-permute-start(bf16[64,2048]{1,0:T(8,128)(2,1)S(1)} %shard_map.116._.own_ref), channel_id=1, source_target_pairs={{0,1},{1,0},{2,3},{3,2},{4,5},{5,4},{6,7},{7,6},{8,9},{9,8},{10,11... | collective-permute-start | bytes 786440 | tf_op jit(solution)/shard_map/ppermute | solution.py:343
  37.9 1.6 %collective-permute-start.18 = (bf16[64,2048]{1,0:T(8,128)(2,1)S(1)}, bf16[64,2048]{1,0:T(8,128)(2,1)S(1)}, u32[]{:S(2)}, u32[]{:S(2)}) collective-permute-start(bf16[64,2048]{1,0:T(8,128)(2,1)S(1)} %shard_map.118.own_ref), channel_id=1, source_target_pairs={{0,1},{1,0},{2,3},{3,2},{4,5},{5,4},{6,7},{7,6},{8,9},{9,8},{10,11... | collective-permute-start | bytes 786440 | tf_op jit(solution)/shard_map/ppermute | solution.py:343
  40.4 1.3 %collective-permute-start.20 = (bf16[64,288]{1,0:T(8,128)(2,1)S(1)}, bf16[64,288]{1,0:T(8,128)(2,1)S(1)}, u32[]{:S(2)}, u32[]{:S(2)}) collective-permute-start(bf16[64,288]{1,0:T(8,128)(2,1)S(1)} %get-tuple-element.53), channel_id=1, source_target_pairs={{0,1},{1,0},{2,3},{3,2},{4,5},{5,4},{6,7},{7,6},{8,9},{9,8},{10,11... | collective-permute-start | bytes 110600 | tf_op jit(solution)/shard_map/ppermute | solution.py:343
  42.3 7.6 %collective-permute-start.24 = (bf16[16,2048]{1,0:T(8,128)(2,1)S(1)}, bf16[16,2048]{1,0:T(8,128)(2,1)S(1)}, u32[]{:S(2)}, u32[]{:S(2)}) collective-permute-start(bf16[16,2048]{1,0:T(8,128)(2,1)S(1)} %get-tuple-element.60), channel_id=1, source_target_pairs={{0,2},{1,3},{2,4},{3,5},{4,6},{5,7},{6,0},{7,1},{8,10},{9,11},{10,... | collective-permute-start | bytes 196616 | tf_op jit(solution)/shard_map/ppermute | solution.py:340
  44.3 7.6 %collective-permute-start.25 = (bf16[16,2048]{1,0:T(8,128)(2,1)S(1)}, bf16[16,2048]{1,0:T(8,128)(2,1)S(1)}, u32[]{:S(2)}, u32[]{:S(2)}) collective-permute-start(bf16[16,2048]{1,0:T(8,128)(2,1)S(1)} %get-tuple-element.61), channel_id=1, source_target_pairs={{0,4},{1,5},{2,6},{3,7},{4,0},{5,1},{6,2},{7,3},{8,12},{9,13},{10,... | collective-permute-start | bytes 196616 | tf_op jit(solution)/shard_map/ppermute | solution.py:340
  46.0 5.9 %collective-permute-start.26 = (bf16[16,2048]{1,0:T(8,128)(2,1)S(1)}, bf16[16,2048]{1,0:T(8,128)(2,1)S(1)}, u32[]{:S(2)}, u32[]{:S(2)}) collective-permute-start(bf16[16,2048]{1,0:T(8,128)(2,1)S(1)} %get-tuple-element.62), channel_id=1, source_target_pairs={{0,6},{1,7},{2,0},{3,1},{4,2},{5,3},{6,4},{7,5},{8,14},{9,15},{10,... | collective-permute-start | bytes 196616 | tf_op jit(solution)/shard_map/ppermute | solution.py:340
  47.3 6.9 %collective-permute-start.21 = (bf16[16,2048]{1,0:T(8,128)(2,1)S(1)}, bf16[16,2048]{1,0:T(8,128)(2,1)S(1)}, u32[]{:S(2)}, u32[]{:S(2)}) collective-permute-start(bf16[16,2048]{1,0:T(8,128)(2,1)S(1)} %get-tuple-element.56), channel_id=1, source_target_pairs={{0,2},{1,3},{2,4},{3,5},{4,6},{5,7},{6,0},{7,1},{8,10},{9,11},{10,... | collective-permute-start | bytes 196616 | tf_op jit(solution)/shard_map/ppermute | solution.py:340
  48.7 8.2 %collective-permute-start.22 = (bf16[16,2048]{1,0:T(8,128)(2,1)S(1)}, bf16[16,2048]{1,0:T(8,128)(2,1)S(1)}, u32[]{:S(2)}, u32[]{:S(2)}) collective-permute-start(bf16[16,2048]{1,0:T(8,128)(2,1)S(1)} %get-tuple-element.57), channel_id=1, source_target_pairs={{0,4},{1,5},{2,6},{3,7},{4,0},{5,1},{6,2},{7,3},{8,12},{9,13},{10,... | collective-permute-start | bytes 196616 | tf_op jit(solution)/shard_map/ppermute | solution.py:340
  49.9 7.0 %collective-permute-start.23 = (bf16[16,2048]{1,0:T(8,128)(2,1)S(1)}, bf16[16,2048]{1,0:T(8,128)(2,1)S(1)}, u32[]{:S(2)}, u32[]{:S(2)}) collective-permute-start(bf16[16,2048]{1,0:T(8,128)(2,1)S(1)} %get-tuple-element.58), channel_id=1, source_target_pairs={{0,6},{1,7},{2,0},{3,1},{4,2},{5,3},{6,4},{7,5},{8,14},{9,15},{10,... | collective-permute-start | bytes 196616 | tf_op jit(solution)/shard_map/ppermute | solution.py:340

commit v5 on v1

--- a/solution.py
+++ b/solution.py
@@ -216,8 +216,9 @@
     size = 2 * n_pair * rows
     i, j = iota2((size, size), 0), iota2((size, size), 1)
     half, inner = i // (n_pair * rows), i % (n_pair * rows)
-    who = (inner // rows + pair) % n_pair
-    source = (2 * who + (core + half) % 2) * rows + inner % rows
+    whose = (core + half) % 2
+    who = (inner // rows * (1 - 2 * whose) + pair + n_pair) % n_pair
+    source = (2 * who + whose) * rows + inner % rows
     return jnp.where(source == j, 1.0, 0.0).astype(BF16)
 
 
@@ -342,7 +343,7 @@
     dma = pltpu.SemaphoreType.DMA
 
     def shift(x, r):
-        return lax.ppermute(x, "exp", [(e, (e + 2 * r) % exp_count) for e in range(exp_count)])
+        return lax.ppermute(x, "exp", [(e, (e + 2 * r * (1 - 2 * (e % 2))) % exp_count) for e in range(exp_count)])
 
     def across(x):
         return lax.ppermute(x, "exp", [(e, e ^ 1) for e in range(exp_count)])

time: 57.9 us -> 59 us (1.019)
  waiting for transfers between devices: 10.9 us -> 13.9 us
  starting transfers between devices: 36.2 us -> 34.3 us
    ppermute x18, waiting for transfers between devices: 8.13 us -> 11.1 us  [shift(): lax.ppermute(x, 'exp', [(e, (e + 2 * r * (1 - 2 * (e % 2))) % exp_count)...]
    ppermute x18, starting transfers between devices: 30.2 us -> 28.3 us  [shift(): lax.ppermute(x, 'exp', [(e, (e + 2 * r * (1 - 2 * (e % 2))) % exp_count)...]
  transfers between devices with their start and end apart: 27 -> 27, of which waited for: 9 -> 16; matrix products, arithmetic and copies ran while one was open for 0% -> 0% of each run, Pallas kernels for 11% -> 11%
where the time goes in v5:
time: 59 us; the launch traced here: 58.8 us
  starting transfers between devices  34.3 us (58%)
  waiting for transfers between devices  13.9 us (24%)
  Pallas kernels  10.4 us (18%)
    ppermute x18, starting transfers between devices, shift(): lax.ppermute(x, 'exp', [(e, (e + 2 * r * (1 - 2 * (e % 2))) % exp_count)...  28.3 us
    ppermute x18, waiting for transfers between devices, shift(): lax.ppermute(x, 'exp', [(e, (e + 2 * r * (1 - 2 * (e % 2))) % exp_count)...  11.1 us
    pallas_call x19, Pallas kernels, call(): pl.pallas_call(kernel, out_shape=outs, in_specs=[pl.BlockSpec(memory_spac...  10.4 us
    ppermute x3, starting transfers between devices, local(): lax.ppermute(state, 'seq', [(move(i), i) for i in range(seq_count)])  4.6 us
    ppermute x6, waiting for transfers between devices, across(): return lax.ppermute(x, 'exp', [(e, e ^ 1) for e in range(exp_count)])  1.91 us
    ppermute x6, starting transfers between devices, across(): return lax.ppermute(x, 'exp', [(e, e ^ 1) for e in range(exp_count)])  1.41 us
  transfers between devices with their start and end apart: 27, of which 16 were waited for; matrix products, arithmetic and copies ran while one was open for 0% of the time, Pallas kernels for 11%

profile of v5, /device:TPU:0, one launch (start us, length us, event | category | flops | bytes accessed | tf_op | source)
XLA Modules:
  0.0 58.8 jit_solution(9982782360547709151)
XLA Ops:
  0.0 1.1 %shard_map.109._ = bf16[144,128]{1,0:T(8,128)(2,1)S(1)} custom-call(bf16[128,128]{1,0:T(8,128)(2,1)} %key_hbm.3, bf16[128,128]{1,0:T(8,128)(2,1)} %value_hbm.3, f32[1,128]{1,0:T(1,128)} %bitcast.15), custom_call_target="tpu_custom_call" | custom-call | tf_op jit(solution)/shard_map/pallas_call | solution.py:322
  1.1 4.0 %collective-permute-start.2 = (bf16[144,128]{1,0:T(8,128)(2,1)S(1)}, bf16[144,128]{1,0:T(8,128)(2,1)S(1)}, u32[]{:S(2)}, u32[]{:S(2)}) collective-permute-start(bf16[144,128]{1,0:T(8,128)(2,1)S(1)} %shard_map.109._), channel_id=1, source_target_pairs={{24,0},{16,8},{8,16},{0,24},{25,1},{17,9},{9,17},{1,25},{26,2},{18... | collective-permute-start | bytes 110600 | tf_op jit(solution)/shard_map/ppermute | solution.py:379
  5.1 0.5 collective-permute-start.1
  5.7 2.9 %shard_map.110 = (f32[128,128]{1,0:T(8,128)S(1)}, f32[128,128]{1,0:T(8,128)S(1)}, bf16[128,128]{1,0:T(8,128)(2,1)S(1)}, f32[8,128]{1,0:T(8,128)S(1)}, bf16[128,4...) custom-call(bf16[128,128]{1,0:T(8,128)(2,1)} %query_hbm.1, bf16[128,128]{1,0:T(8,128)(2,1)} %key_hbm.3, ...), custom_call_target="tpu_custom_call" | custom-call | tf_op jit(solution)/shard_map/pallas_call | solution.py:322
  8.6 0.4 collective-permute-done.1.refs_1_
  9.0 0.5 collective-permute-done.refs_0_
  9.5 0.4 shard_map.111.x_ref
  10.0 0.3 shard_map.115
  10.3 0.3 shard_map.112
  10.6 0.6 collective-permute-start.3
  11.2 0.7 %collective-permute-done.10.b_ref = bf16[64,2048]{1,0:T(8,128)(2,1)S(1)} collective-permute-done((bf16[64,2048]{1,0:T(8,128)(2,1)S(1)}, bf16[64,2048]{1,0:T(8,128)(2,1)S(1)}, u32[]{:S(2)}, u32[]{:S(2)}) %collective-permute-start.10) | collective-permute-done | bytes 262176 | tf_op jit(solution)/shard_map/ppermute | solution.py:349
  11.9 1.6 %collective-permute-start.11 = (bf16[16,2048]{1,0:T(8,128)(2,1)S(1)}, bf16[16,2048]{1,0:T(8,128)(2,1)S(1)}, u32[]{:S(2)}, u32[]{:S(2)}) collective-permute-start(bf16[16,2048]{1,0:T(8,128)(2,1)S(1)} %get-tuple-element.53), channel_id=1, source_target_pairs={{0,2},{1,7},{2,4},{3,1},{4,6},{5,3},{6,0},{7,5},{8,10},{9,15},{10,... | collective-permute-start | bytes 196616 | tf_op jit(solution)/shard_map/ppermute | solution.py:346
  13.5 2.6 %collective-permute-start.12 = (bf16[16,2048]{1,0:T(8,128)(2,1)S(1)}, bf16[16,2048]{1,0:T(8,128)(2,1)S(1)}, u32[]{:S(2)}, u32[]{:S(2)}) collective-permute-start(bf16[16,2048]{1,0:T(8,128)(2,1)S(1)} %get-tuple-element.54), channel_id=1, source_target_pairs={{0,4},{1,5},{2,6},{3,7},{4,0},{5,1},{6,2},{7,3},{8,12},{9,13},{10,... | collective-permute-start | bytes 196616 | tf_op jit(solution)/shard_map/ppermute | solution.py:346
  16.1 1.3 %collective-permute-start.13 = (bf16[16,2048]{1,0:T(8,128)(2,1)S(1)}, bf16[16,2048]{1,0:T(8,128)(2,1)S(1)}, u32[]{:S(2)}, u32[]{:S(2)}) collective-permute-start(bf16[16,2048]{1,0:T(8,128)(2,1)S(1)} %get-tuple-element.55), channel_id=1, source_target_pairs={{0,6},{1,3},{2,0},{3,5},{4,2},{5,7},{6,4},{7,1},{8,14},{9,11},{10,... | collective-permute-start | bytes 196616 | tf_op jit(solution)/shard_map/ppermute | solution.py:346
  17.6 0.7 %collective-permute-start.4 = (bf16[16,2048]{1,0:T(8,128)(2,1)S(1)}, bf16[16,2048]{1,0:T(8,128)(2,1)S(1)}, u32[]{:S(2)}, u32[]{:S(2)}) collective-permute-start(bf16[16,2048]{1,0:T(8,128)(2,1)S(1)} %get-tuple-element.47), channel_id=1, source_target_pairs={{0,2},{1,7},{2,4},{3,1},{4,6},{5,3},{6,0},{7,5},{8,10},{9,15},{10,... | collective-permute-start | bytes 196616 | tf_op jit(solution)/shard_map/ppermute | solution.py:346
  18.3 0.3 collective-permute-start.5
  18.8 2.7 %collective-permute-start.6 = (bf16[16,2048]{1,0:T(8,128)(2,1)S(1)}, bf16[16,2048]{1,0:T(8,128)(2,1)S(1)}, u32[]{:S(2)}, u32[]{:S(2)}) collective-permute-start(bf16[16,2048]{1,0:T(8,128)(2,1)S(1)} %get-tuple-element.49), channel_id=1, source_target_pairs={{0,6},{1,3},{2,0},{3,5},{4,2},{5,7},{6,4},{7,1},{8,14},{9,11},{10,... | collective-permute-start | bytes 196616 | tf_op jit(solution)/shard_map/ppermute | solution.py:346
  21.4 0.2 collective-permute-done.12.refs_2_
  21.6 1.0 %collective-permute-done.13.refs_3_ = bf16[16,2048]{1,0:T(8,128)(2,1)S(1)} collective-permute-done((bf16[16,2048]{1,0:T(8,128)(2,1)S(1)}, bf16[16,2048]{1,0:T(8,128)(2,1)S(1)}, u32[]{:S(2)}, u32[]{:S(2)}) %collective-permute-start.13) | collective-permute-done | bytes 65568 | tf_op jit(solution)/shard_map/ppermute | solution.py:346
  22.7 3.8 %collective-permute-start.16 = (bf16[16,2048]{1,0:T(8,128)(2,1)S(1)}, bf16[16,2048]{1,0:T(8,128)(2,1)S(1)}, u32[]{:S(2)}, u32[]{:S(2)}) collective-permute-start(bf16[16,2048]{1,0:T(8,128)(2,1)S(1)} %shard_map.117.refs_0_.refs_4_), channel_id=1, source_target_pairs={{0,2},{1,7},{2,4},{3,1},{4,6},{5,3},{6,0},{7,5},{8,10},{9,15},{10,... | collective-permute-start | bytes 196616 | tf_op jit(solution)/shard_map/ppermute | solution.py:346
  26.5 0.6 %collective-permute-start.15 = (bf16[16,2048]{1,0:T(8,128)(2,1)S(1)}, bf16[16,2048]{1,0:T(8,128)(2,1)S(1)}, u32[]{:S(2)}, u32[]{:S(2)}) collective-permute-start(bf16[16,2048]{1,0:T(8,128)(2,1)S(1)} %shard_map.117.refs_0_.refs_4_), channel_id=1, source_target_pairs={{0,4},{1,5},{2,6},{3,7},{4,0},{5,1},{6,2},{7,3},{8,12},{9,13},{10,... | collective-permute-start | bytes 196616 | tf_op jit(solution)/shard_map/ppermute | solution.py:346
  27.1 1.8 %collective-permute-start.14 = (bf16[16,2048]{1,0:T(8,128)(2,1)S(1)}, bf16[16,2048]{1,0:T(8,128)(2,1)S(1)}, u32[]{:S(2)}, u32[]{:S(2)}) collective-permute-start(bf16[16,2048]{1,0:T(8,128)(2,1)S(1)} %shard_map.117.refs_0_.refs_4_), channel_id=1, source_target_pairs={{0,6},{1,3},{2,0},{3,5},{4,2},{5,7},{6,4},{7,1},{8,14},{9,11},{10,... | collective-permute-start | bytes 196616 | tf_op jit(solution)/shard_map/ppermute | solution.py:346
  29.0 1.0 %collective-permute-start.9 = (bf16[16,2048]{1,0:T(8,128)(2,1)S(1)}, bf16[16,2048]{1,0:T(8,128)(2,1)S(1)}, u32[]{:S(2)}, u32[]{:S(2)}) collective-permute-start(bf16[16,2048]{1,0:T(8,128)(2,1)S(1)} %shard_map.114.refs_0_.refs_9_), channel_id=1, source_target_pairs={{0,2},{1,7},{2,4},{3,1},{4,6},{5,3},{6,0},{7,5},{8,10},{9,15},{10,... | collective-permute-start | bytes 196616 | tf_op jit(solution)/shard_map/ppermute | solution.py:346
  30.0 1.5 %collective-permute-start.8 = (bf16[16,2048]{1,0:T(8,128)(2,1)S(1)}, bf16[16,2048]{1,0:T(8,128)(2,1)S(1)}, u32[]{:S(2)}, u32[]{:S(2)}) collective-permute-start(bf16[16,2048]{1,0:T(8,128)(2,1)S(1)} %shard_map.114.refs_0_.refs_9_), channel_id=1, source_target_pairs={{0,4},{1,5},{2,6},{3,7},{4,0},{5,1},{6,2},{7,3},{8,12},{9,13},{10,... | collective-permute-start | bytes 196616 | tf_op jit(solution)/shard_map/ppermute | solution.py:346
  31.5 1.3 %collective-permute-start.7 = (bf16[16,2048]{1,0:T(8,128)(2,1)S(1)}, bf16[16,2048]{1,0:T(8,128)(2,1)S(1)}, u32[]{:S(2)}, u32[]{:S(2)}) collective-permute-start(bf16[16,2048]{1,0:T(8,128)(2,1)S(1)} %shard_map.114.refs_0_.refs_9_), channel_id=1, source_target_pairs={{0,6},{1,3},{2,0},{3,5},{4,2},{5,7},{6,4},{7,1},{8,14},{9,11},{10,... | collective-permute-start | bytes 196616 | tf_op jit(solution)/shard_map/ppermute | solution.py:346
  32.8 0.5 collective-permute-done.15.refs_2_
  33.3 0.3 collective-permute-done.14.refs_1_
  33.7 1.7 %shard_map.119 = (bf16[288,4096]{1,0:T(8,128)(2,1)S(1)}, f32[8,128]{1,0:T(8,128)S(1)}) custom-call(bf16[288,4096]{1,0:T(8,128)(2,1)} %bitcast.13, bf16[64,2048]{1,0:T(8,128)(2,1)S(1)} %shard_map.118._.own_ref), custom_call_target="tpu_custom_call" | custom-call | tf_op jit(solution)/shard_map/pallas_call | solution.py:322
  35.5 3.0 %collective-permute-done.8.refs_2_ = bf16[16,2048]{1,0:T(8,128)(2,1)S(1)} collective-permute-done((bf16[16,2048]{1,0:T(8,128)(2,1)S(1)}, bf16[16,2048]{1,0:T(8,128)(2,1)S(1)}, u32[]{:S(2)}, u32[]{:S(2)}) %collective-permute-start.8) | collective-permute-done | bytes 65568 | tf_op jit(solution)/shard_map/ppermute | solution.py:346
  38.7 0.8 %shard_map.121.before_ref = f32[592,128]{1,0:T(8,128)S(1)} custom-call(bf16[592,4096]{1,0:T(8,128)(2,1)S(1)} %get-tuple-element.38.in_ref, bf16[64,2048]{1,0:T(8,128)(2,1)S(1)} %shard_map.118._.own_ref, bf16[64,2048]{1,0:T(8,128)(2,1)S(1)} %collective-permute-done.18.other_ref), custom_call_target="tpu_custom_call" | custom-call | tf_op jit(solution)/shard_map/pallas_call | solution.py:322
  39.5 0.7 %collective-permute-done.17.other_ref = bf16[64,2048]{1,0:T(8,128)(2,1)S(1)} collective-permute-done((bf16[64,2048]{1,0:T(8,128)(2,1)S(1)}, bf16[64,2048]{1,0:T(8,128)(2,1)S(1)}, u32[]{:S(2)}, u32[]{:S(2)}) %collective-permute-start.17) | collective-permute-done | bytes 262176 | tf_op jit(solution)/shard_map/ppermute | solution.py:349
  40.2 0.9 %shard_map.122.x_ref = bf16[128,288]{1,0:T(8,128)(2,1)S(1)} custom-call(bf16[592,4096]{1,0:T(8,128)(2,1)S(1)} %get-tuple-element.38.in_ref, bf16[64,2048]{1,0:T(8,128)(2,1)S(1)} %shard_map.120.own_ref, bf16[64,2048]{1,0:T(8,128)(2,1)S(1)} %collective-permute-done.17.other_ref, f32[592,128]{1,0:T(8,128)S(1)} %shard_map.121.before_ref, ...), custom_call_target="tpu_custom_call" | custom-call | tf_op jit(solution)/shard_map/pallas_call | solution.py:322
  41.1 0.4 shard_map.125
  41.5 0.2 collective-permute-start.23
  41.8 0.4 shard_map.123
  42.2 0.4 collective-permute-start.19
  42.6 0.5 collective-permute-done.23.b_ref
  43.2 1.5 %collective-permute-start.24 = (bf16[16,2048]{1,0:T(8,128)(2,1)S(1)}, bf16[16,2048]{1,0:T(8,128)(2,1)S(1)}, u32[]{:S(2)}, u32[]{:S(2)}) collective-permute-start(bf16[16,2048]{1,0:T(8,128)(2,1)S(1)} %get-tuple-element.68), channel_id=1, source_target_pairs={{0,2},{1,7},{2,4},{3,1},{4,6},{5,3},{6,0},{7,5},{8,10},{9,15},{10,... | collective-permute-start | bytes 196616 | tf_op jit(solution)/shard_map/ppermute | solution.py:346
  44.8 1.8 %collective-permute-start.25 = (bf16[16,2048]{1,0:T(8,128)(2,1)S(1)}, bf16[16,2048]{1,0:T(8,128)(2,1)S(1)}, u32[]{:S(2)}, u32[]{:S(2)}) collective-permute-start(bf16[16,2048]{1,0:T(8,128)(2,1)S(1)} %get-tuple-element.69), channel_id=1, source_target_pairs={{0,4},{1,5},{2,6},{3,7},{4,0},{5,1},{6,2},{7,3},{8,12},{9,13},{10,... | collective-permute-start | bytes 196616 | tf_op jit(solution)/shard_map/ppermute | solution.py:346
  46.5 1.2 %collective-permute-start.26 = (bf16[16,2048]{1,0:T(8,128)(2,1)S(1)}, bf16[16,2048]{1,0:T(8,128)(2,1)S(1)}, u32[]{:S(2)}, u32[]{:S(2)}) collective-permute-start(bf16[16,2048]{1,0:T(8,128)(2,1)S(1)} %get-tuple-element.70), channel_id=1, source_target_pairs={{0,6},{1,3},{2,0},{3,5},{4,2},{5,7},{6,4},{7,1},{8,14},{9,11},{10,... | collective-permute-start | bytes 196616 | tf_op jit(solution)/shard_map/ppermute | solution.py:346
  47.8 0.9 %collective-permute-start.20 = (bf16[16,2048]{1,0:T(8,128)(2,1)S(1)}, bf16[16,2048]{1,0:T(8,128)(2,1)S(1)}, u32[]{:S(2)}, u32[]{:S(2)}) collective-permute-start(bf16[16,2048]{1,0:T(8,128)(2,1)S(1)} %get-tuple-element.62), channel_id=1, source_target_pairs={{0,2},{1,7},{2,4},{3,1},{4,6},{5,3},{6,0},{7,5},{8,10},{9,15},{10,... | collective-permute-start | bytes 196616 | tf_op jit(solution)/shard_map/ppermute | solution.py:346
  48.7 1.1 %collective-permute-start.21 = (bf16[16,2048]{1,0:T(8,128)(2,1)S(1)}, bf16[16,2048]{1,0:T(8,128)(2,1)S(1)}, u32[]{:S(2)}, u32[]{:S(2)}) collective-permute-start(bf16[16,2048]{1,0:T(8,128)(2,1)S(1)} %get-tuple-element.63), channel_id=1, source_target_pairs={{0,4},{1,5},{2,6},{3,7},{4,0},{5,1},{6,2},{7,3},{8,12},{9,13},{10,... | collective-permute-start | bytes 196616 | tf_op jit(solution)/shard_map/ppermute | solution.py:346
  49.8 2.3 %collective-permute-start.22 = (bf16[16,2048]{1,0:T(8,128)(2,1)S(1)}, bf16[16,2048]{1,0:T(8,128)(2,1)S(1)}, u32[]{:S(2)}, u32[]{:S(2)}) collective-permute-start(bf16[16,2048]{1,0:T(8,128)(2,1)S(1)} %get-tuple-element.64), channel_id=1, source_target_pairs={{0,6},{1,3},{2,0},{3,5},{4,2},{5,7},{6,4},{7,1},{8,14},{9,11},{10,... | collective-permute-start | bytes 196616 | tf_op jit(solution)/shard_map/ppermute | solution.py:346
  52.2 0.3 collective-permute-done.25.refs_7_
  52.4 0.8 %collective-permute-done.26.refs_8_ = bf16[16,2048]{1,0:T(8,128)(2,1)S(1)} collective-permute-done((bf16[16,2048]{1,0:T(8,128)(2,1)S(1)}, bf16[16,2048]{1,0:T(8,128)(2,1)S(1)}, u32[]{:S(2)}, u32[]{:S(2)}) %collective-permute-start.26) | collective-permute-done | bytes 65568 | tf_op jit(solution)/shard_map/ppermute | solution.py:346
  53.2 0.9 %collective-permute-done.20.refs_1_ = bf16[16,2048]{1,0:T(8,128)(2,1)S(1)} collective-permute-done((bf16[16,2048]{1,0:T(8,128)(2,1)S(1)}, bf16[16,2048]{1,0:T(8,128)(2,1)S(1)}, u32[]{:S(2)}, u32[]{:S(2)}) %collective-permute-start.20) | collective-permute-done | bytes 65568 | tf_op jit(solution)/shard_map/ppermute | solution.py:346
  54.1 3.9 %collective-permute-done.21.refs_2_ = bf16[16,2048]{1,0:T(8,128)(2,1)S(1)} collective-permute-done((bf16[16,2048]{1,0:T(8,128)(2,1)S(1)}, bf16[16,2048]{1,0:T(8,128)(2,1)S(1)}, u32[]{:S(2)}, u32[]{:S(2)}) %collective-permute-start.21) | collective-permute-done | bytes 65568 | tf_op jit(solution)/shard_map/ppermute | solution.py:346
  58.0 0.7 %shard_map.127 = bf16[16,4096]{1,0:T(8,128)(2,1)} custom-call(bf16[16,2048]{1,0:T(8,128)(2,1)S(1)} %get-tuple-element.61.refs_0_, bf16[16,2048]{1,0:T(8,128)(2,1)S(1)} %collective-permute-done.20.refs_1_, bf16[16,2048]{1,0:T(8,128)(2,1)S(1)} %collective-permute-done.21.refs_2_, bf16[16,2048]{1,0:T(8,128)(2,1)S(1)} %collective-permute-done.22.refs_3_, ...), custom_call_target="tpu_custom_call" | custom-call | tf_op jit(solution)/shard_map/pallas_call | solution.py:322
  (25 shorter events, 0.9 us)
Async XLA Ops:
  1.1 7.5 %collective-permute-start.2 = (bf16[144,128]{1,0:T(8,128)(2,1)S(1)}, bf16[144,128]{1,0:T(8,128)(2,1)S(1)}, u32[]{:S(2)}, u32[]{:S(2)}) collective-permute-start(bf16[144,128]{1,0:T(8,128)(2,1)S(1)} %shard_map.109._), channel_id=1, source_target_pairs={{24,0},{16,8},{8,16},{0,24},{25,1},{17,9},{9,17},{1,25},{26,2},{18... | collective-permute-start | bytes 110600 | tf_op jit(solution)/shard_map/ppermute | solution.py:379
  5.1 4.0 %collective-permute-start.1 = (bf16[144,128]{1,0:T(8,128)(2,1)S(1)}, bf16[144,128]{1,0:T(8,128)(2,1)S(1)}, u32[]{:S(2)}, u32[]{:S(2)}) collective-permute-start(bf16[144,128]{1,0:T(8,128)(2,1)S(1)} %shard_map.109._), channel_id=1, source_target_pairs={{16,0},{24,8},{0,16},{8,24},{17,1},{25,9},{1,17},{9,25},{18,2},{26... | collective-permute-start | bytes 110600 | tf_op jit(solution)/shard_map/ppermute | solution.py:379
  5.6 4.0 %collective-permute-start = (bf16[144,128]{1,0:T(8,128)(2,1)S(1)}, bf16[144,128]{1,0:T(8,128)(2,1)S(1)}, u32[]{:S(2)}, u32[]{:S(2)}) collective-permute-start(bf16[144,128]{1,0:T(8,128)(2,1)S(1)} %shard_map.109._), channel_id=1, source_target_pairs={{8,0},{0,8},{24,16},{16,24},{9,1},{1,9},{25,17},{17,25},{10,2},{2,... | collective-permute-start | bytes 110600 | tf_op jit(solution)/shard_map/ppermute | solution.py:379
  10.3 1.6 %collective-permute-start.10 = (bf16[64,2048]{1,0:T(8,128)(2,1)S(1)}, bf16[64,2048]{1,0:T(8,128)(2,1)S(1)}, u32[]{:S(2)}, u32[]{:S(2)}) collective-permute-start(bf16[64,2048]{1,0:T(8,128)(2,1)S(1)} %get-tuple-element.51), channel_id=1, source_target_pairs={{0,1},{1,0},{2,3},{3,2},{4,5},{5,4},{6,7},{7,6},{8,9},{9,8},{10,11... | collective-permute-start | bytes 786440 | tf_op jit(solution)/shard_map/ppermute | solution.py:349
  10.6 6.9 %collective-permute-start.3 = (bf16[64,2048]{1,0:T(8,128)(2,1)S(1)}, bf16[64,2048]{1,0:T(8,128)(2,1)S(1)}, u32[]{:S(2)}, u32[]{:S(2)}) collective-permute-start(bf16[64,2048]{1,0:T(8,128)(2,1)S(1)} %get-tuple-element.45), channel_id=1, source_target_pairs={{0,1},{1,0},{2,3},{3,2},{4,5},{5,4},{6,7},{7,6},{8,9},{9,8},{10,11... | collective-permute-start | bytes 786440 | tf_op jit(solution)/shard_map/ppermute | solution.py:349
  11.9 6.8 %collective-permute-start.11 = (bf16[16,2048]{1,0:T(8,128)(2,1)S(1)}, bf16[16,2048]{1,0:T(8,128)(2,1)S(1)}, u32[]{:S(2)}, u32[]{:S(2)}) collective-permute-start(bf16[16,2048]{1,0:T(8,128)(2,1)S(1)} %get-tuple-element.53), channel_id=1, source_target_pairs={{0,2},{1,7},{2,4},{3,1},{4,6},{5,3},{6,0},{7,5},{8,10},{9,15},{10,... | collective-permute-start | bytes 196616 | tf_op jit(solution)/shard_map/ppermute | solution.py:346
  13.5 8.1 %collective-permute-start.12 = (bf16[16,2048]{1,0:T(8,128)(2,1)S(1)}, bf16[16,2048]{1,0:T(8,128)(2,1)S(1)}, u32[]{:S(2)}, u32[]{:S(2)}) collective-permute-start(bf16[16,2048]{1,0:T(8,128)(2,1)S(1)} %get-tuple-element.54), channel_id=1, source_target_pairs={{0,4},{1,5},{2,6},{3,7},{4,0},{5,1},{6,2},{7,3},{8,12},{9,13},{10,... | collective-permute-start | bytes 196616 | tf_op jit(solution)/shard_map/ppermute | solution.py:346
  16.1 6.5 %collective-permute-start.13 = (bf16[16,2048]{1,0:T(8,128)(2,1)S(1)}, bf16[16,2048]{1,0:T(8,128)(2,1)S(1)}, u32[]{:S(2)}, u32[]{:S(2)}) collective-permute-start(bf16[16,2048]{1,0:T(8,128)(2,1)S(1)} %get-tuple-element.55), channel_id=1, source_target_pairs={{0,6},{1,3},{2,0},{3,5},{4,2},{5,7},{6,4},{7,1},{8,14},{9,11},{10,... | collective-permute-start | bytes 196616 | tf_op jit(solution)/shard_map/ppermute | solution.py:346
  17.6 9.5 %collective-permute-start.4 = (bf16[16,2048]{1,0:T(8,128)(2,1)S(1)}, bf16[16,2048]{1,0:T(8,128)(2,1)S(1)}, u32[]{:S(2)}, u32[]{:S(2)}) collective-permute-start(bf16[16,2048]{1,0:T(8,128)(2,1)S(1)} %get-tuple-element.47), channel_id=1, source_target_pairs={{0,2},{1,7},{2,4},{3,1},{4,6},{5,3},{6,0},{7,5},{8,10},{9,15},{10,... | collective-permute-start | bytes 196616 | tf_op jit(solution)/shard_map/ppermute | solution.py:346
  18.3 10.6 %collective-permute-start.5 = (bf16[16,2048]{1,0:T(8,128)(2,1)S(1)}, bf16[16,2048]{1,0:T(8,128)(2,1)S(1)}, u32[]{:S(2)}, u32[]{:S(2)}) collective-permute-start(bf16[16,2048]{1,0:T(8,128)(2,1)S(1)} %get-tuple-element.48), channel_id=1, source_target_pairs={{0,4},{1,5},{2,6},{3,7},{4,0},{5,1},{6,2},{7,3},{8,12},{9,13},{10,... | collective-permute-start | bytes 196616 | tf_op jit(solution)/shard_map/ppermute | solution.py:346
  18.8 10.2 %collective-permute-start.6 = (bf16[16,2048]{1,0:T(8,128)(2,1)S(1)}, bf16[16,2048]{1,0:T(8,128)(2,1)S(1)}, u32[]{:S(2)}, u32[]{:S(2)}) collective-permute-start(bf16[16,2048]{1,0:T(8,128)(2,1)S(1)} %get-tuple-element.49), channel_id=1, source_target_pairs={{0,6},{1,3},{2,0},{3,5},{4,2},{5,7},{6,4},{7,1},{8,14},{9,11},{10,... | collective-permute-start | bytes 196616 | tf_op jit(solution)/shard_map/ppermute | solution.py:346
  22.7 8.8 %collective-permute-start.16 = (bf16[16,2048]{1,0:T(8,128)(2,1)S(1)}, bf16[16,2048]{1,0:T(8,128)(2,1)S(1)}, u32[]{:S(2)}, u32[]{:S(2)}) collective-permute-start(bf16[16,2048]{1,0:T(8,128)(2,1)S(1)} %shard_map.117.refs_0_.refs_4_), channel_id=1, source_target_pairs={{0,2},{1,7},{2,4},{3,1},{4,6},{5,3},{6,0},{7,5},{8,10},{9,15},{10,... | collective-permute-start | bytes 196616 | tf_op jit(solution)/shard_map/ppermute | solution.py:346
  26.5 6.8 %collective-permute-start.15 = (bf16[16,2048]{1,0:T(8,128)(2,1)S(1)}, bf16[16,2048]{1,0:T(8,128)(2,1)S(1)}, u32[]{:S(2)}, u32[]{:S(2)}) collective-permute-start(bf16[16,2048]{1,0:T(8,128)(2,1)S(1)} %shard_map.117.refs_0_.refs_4_), channel_id=1, source_target_pairs={{0,4},{1,5},{2,6},{3,7},{4,0},{5,1},{6,2},{7,3},{8,12},{9,13},{10,... | collective-permute-start | bytes 196616 | tf_op jit(solution)/shard_map/ppermute | solution.py:346
  27.1 6.5 %collective-permute-start.14 = (bf16[16,2048]{1,0:T(8,128)(2,1)S(1)}, bf16[16,2048]{1,0:T(8,128)(2,1)S(1)}, u32[]{:S(2)}, u32[]{:S(2)}) collective-permute-start(bf16[16,2048]{1,0:T(8,128)(2,1)S(1)} %shard_map.117.refs_0_.refs_4_), channel_id=1, source_target_pairs={{0,6},{1,3},{2,0},{3,5},{4,2},{5,7},{6,4},{7,1},{8,14},{9,11},{10,... | collective-permute-start | bytes 196616 | tf_op jit(solution)/shard_map/ppermute | solution.py:346
  29.0 6.5 %collective-permute-start.9 = (bf16[16,2048]{1,0:T(8,128)(2,1)S(1)}, bf16[16,2048]{1,0:T(8,128)(2,1)S(1)}, u32[]{:S(2)}, u32[]{:S(2)}) collective-permute-start(bf16[16,2048]{1,0:T(8,128)(2,1)S(1)} %shard_map.114.refs_0_.refs_9_), channel_id=1, source_target_pairs={{0,2},{1,7},{2,4},{3,1},{4,6},{5,3},{6,0},{7,5},{8,10},{9,15},{10,... | collective-permute-start | bytes 196616 | tf_op jit(solution)/shard_map/ppermute | solution.py:346
  30.0 8.6 %collective-permute-start.8 = (bf16[16,2048]{1,0:T(8,128)(2,1)S(1)}, bf16[16,2048]{1,0:T(8,128)(2,1)S(1)}, u32[]{:S(2)}, u32[]{:S(2)}) collective-permute-start(bf16[16,2048]{1,0:T(8,128)(2,1)S(1)} %shard_map.114.refs_0_.refs_9_), channel_id=1, source_target_pairs={{0,4},{1,5},{2,6},{3,7},{4,0},{5,1},{6,2},{7,3},{8,12},{9,13},{10,... | collective-permute-start | bytes 196616 | tf_op jit(solution)/shard_map/ppermute | solution.py:346
  31.5 7.0 %collective-permute-start.7 = (bf16[16,2048]{1,0:T(8,128)(2,1)S(1)}, bf16[16,2048]{1,0:T(8,128)(2,1)S(1)}, u32[]{:S(2)}, u32[]{:S(2)}) collective-permute-start(bf16[16,2048]{1,0:T(8,128)(2,1)S(1)} %shard_map.114.refs_0_.refs_9_), channel_id=1, source_target_pairs={{0,6},{1,3},{2,0},{3,5},{4,2},{5,7},{6,4},{7,1},{8,14},{9,11},{10,... | collective-permute-start | bytes 196616 | tf_op jit(solution)/shard_map/ppermute | solution.py:346
  33.6 5.0 %collective-permute-start.18 = (bf16[64,2048]{1,0:T(8,128)(2,1)S(1)}, bf16[64,2048]{1,0:T(8,128)(2,1)S(1)}, u32[]{:S(2)}, u32[]{:S(2)}) collective-permute-start(bf16[64,2048]{1,0:T(8,128)(2,1)S(1)} %shard_map.118._.own_ref), channel_id=1, source_target_pairs={{0,1},{1,0},{2,3},{3,2},{4,5},{5,4},{6,7},{7,6},{8,9},{9,8},{10,11... | collective-permute-start | bytes 786440 | tf_op jit(solution)/shard_map/ppermute | solution.py:349
  38.6 1.6 %collective-permute-start.17 = (bf16[64,2048]{1,0:T(8,128)(2,1)S(1)}, bf16[64,2048]{1,0:T(8,128)(2,1)S(1)}, u32[]{:S(2)}, u32[]{:S(2)}) collective-permute-start(bf16[64,2048]{1,0:T(8,128)(2,1)S(1)} %shard_map.120.own_ref), channel_id=1, source_target_pairs={{0,1},{1,0},{2,3},{3,2},{4,5},{5,4},{6,7},{7,6},{8,9},{9,8},{10,11... | collective-permute-start | bytes 786440 | tf_op jit(solution)/shard_map/ppermute | solution.py:349
  41.5 1.6 %collective-permute-start.23 = (bf16[64,2048]{1,0:T(8,128)(2,1)S(1)}, bf16[64,2048]{1,0:T(8,128)(2,1)S(1)}, u32[]{:S(2)}, u32[]{:S(2)}) collective-permute-start(bf16[64,2048]{1,0:T(8,128)(2,1)S(1)} %get-tuple-element.66), channel_id=1, source_target_pairs={{0,1},{1,0},{2,3},{3,2},{4,5},{5,4},{6,7},{7,6},{8,9},{9,8},{10,11... | collective-permute-start | bytes 786440 | tf_op jit(solution)/shard_map/ppermute | solution.py:349
  42.2 5.5 %collective-permute-start.19 = (bf16[64,2048]{1,0:T(8,128)(2,1)S(1)}, bf16[64,2048]{1,0:T(8,128)(2,1)S(1)}, u32[]{:S(2)}, u32[]{:S(2)}) collective-permute-start(bf16[64,2048]{1,0:T(8,128)(2,1)S(1)} %get-tuple-element.60), channel_id=1, source_target_pairs={{0,1},{1,0},{2,3},{3,2},{4,5},{5,4},{6,7},{7,6},{8,9},{9,8},{10,11... | collective-permute-start | bytes 786440 | tf_op jit(solution)/shard_map/ppermute | solution.py:349
  43.2 6.6 %collective-permute-start.24 = (bf16[16,2048]{1,0:T(8,128)(2,1)S(1)}, bf16[16,2048]{1,0:T(8,128)(2,1)S(1)}, u32[]{:S(2)}, u32[]{:S(2)}) collective-permute-start(bf16[16,2048]{1,0:T(8,128)(2,1)S(1)} %get-tuple-element.68), channel_id=1, source_target_pairs={{0,2},{1,7},{2,4},{3,1},{4,6},{5,3},{6,0},{7,5},{8,10},{9,15},{10,... | collective-permute-start | bytes 196616 | tf_op jit(solution)/shard_map/ppermute | solution.py:346
  44.8 7.7 %collective-permute-start.25 = (bf16[16,2048]{1,0:T(8,128)(2,1)S(1)}, bf16[16,2048]{1,0:T(8,128)(2,1)S(1)}, u32[]{:S(2)}, u32[]{:S(2)}) collective-permute-start(bf16[16,2048]{1,0:T(8,128)(2,1)S(1)} %get-tuple-element.69), channel_id=1, source_target_pairs={{0,4},{1,5},{2,6},{3,7},{4,0},{5,1},{6,2},{7,3},{8,12},{9,13},{10,... | collective-permute-start | bytes 196616 | tf_op jit(solution)/shard_map/ppermute | solution.py:346
  46.5 6.7 %collective-permute-start.26 = (bf16[16,2048]{1,0:T(8,128)(2,1)S(1)}, bf16[16,2048]{1,0:T(8,128)(2,1)S(1)}, u32[]{:S(2)}, u32[]{:S(2)}) collective-permute-start(bf16[16,2048]{1,0:T(8,128)(2,1)S(1)} %get-tuple-element.70), channel_id=1, source_target_pairs={{0,6},{1,3},{2,0},{3,5},{4,2},{5,7},{6,4},{7,1},{8,14},{9,11},{10,... | collective-permute-start | bytes 196616 | tf_op jit(solution)/shard_map/ppermute | solution.py:346
  47.8 6.3 %collective-permute-start.20 = (bf16[16,2048]{1,0:T(8,128)(2,1)S(1)}, bf16[16,2048]{1,0:T(8,128)(2,1)S(1)}, u32[]{:S(2)}, u32[]{:S(2)}) collective-permute-start(bf16[16,2048]{1,0:T(8,128)(2,1)S(1)} %get-tuple-element.62), channel_id=1, source_target_pairs={{0,2},{1,7},{2,4},{3,1},{4,6},{5,3},{6,0},{7,5},{8,10},{9,15},{10,... | collective-permute-start | bytes 196616 | tf_op jit(solution)/shard_map/ppermute | solution.py:346
  48.7 9.3 %collective-permute-start.21 = (bf16[16,2048]{1,0:T(8,128)(2,1)S(1)}, bf16[16,2048]{1,0:T(8,128)(2,1)S(1)}, u32[]{:S(2)}, u32[]{:S(2)}) collective-permute-start(bf16[16,2048]{1,0:T(8,128)(2,1)S(1)} %get-tuple-element.63), channel_id=1, source_target_pairs={{0,4},{1,5},{2,6},{3,7},{4,0},{5,1},{6,2},{7,3},{8,12},{9,13},{10,... | collective-permute-start | bytes 196616 | tf_op jit(solution)/shard_map/ppermute | solution.py:346
  49.8 8.2 %collective-permute-start.22 = (bf16[16,2048]{1,0:T(8,128)(2,1)S(1)}, bf16[16,2048]{1,0:T(8,128)(2,1)S(1)}, u32[]{:S(2)}, u32[]{:S(2)}) collective-permute-start(bf16[16,2048]{1,0:T(8,128)(2,1)S(1)} %get-tuple-element.64), channel_id=1, source_target_pairs={{0,6},{1,3},{2,0},{3,5},{4,2},{5,7},{6,4},{7,1},{8,14},{9,11},{10,... | collective-permute-start | bytes 196616 | tf_op jit(solution)/shard_map/ppermute | solution.py:346

commit v6 on v4

--- a/solution.py
+++ b/solution.py
@@ -229,7 +229,7 @@
 
 def normed_kernel(n_pair, moves, *refs):
     states = refs[: len(moves)]
-    intra_ref, grown_ref, query_ref, gain_ref, mine_ref, theirs_ref = refs[len(moves) : len(moves) + 4] + refs[-2:]
+    intra_ref, grown_ref, query_ref, gain_ref, mine_ref, theirs_ref = refs[len(moves) :]
     t, d = query_ref.shape
     me = lax.axis_index("seq")
     ranks = [move(me) for move in moves]
@@ -263,6 +263,24 @@
             ref[:, there] = part[r * rows : (r + 1) * rows].astype(BF16)
 
 
+def halves_kernel(at, x_ref, w_ref, mine_ref, theirs_ref):
+    half = mine_ref.shape[0]
+    for i in range(at.start, at.stop, COLUMNS):
+        part = dot_f32(x_ref[...], w_ref[:, i : i + COLUMNS], ((1,), (0,))).astype(BF16)
+        mine_ref[:, i - at.start : i - at.start + COLUMNS] = part[:half]
+        theirs_ref[:, i - at.start : i - at.start + COLUMNS] = part[half:]
+
+
+def add_kernel(groups, a_ref, b_ref, *refs):
+    outs = refs[-len(groups) :]
+    rows = outs[0].shape[0] // len(groups[0])
+    for group, ref in zip(groups, outs):
+        for i, block in enumerate(group):
+            at = slice(block * rows, (block + 1) * rows)
+            total = a_ref[at, :].astype(F32) + b_ref[at, :].astype(F32)
+            ref[i * rows : (i + 1) * rows, :] = total.astype(ref.dtype)
+
+
 def sum_kernel(count, *refs):
     total = refs[0][...].astype(F32)
     for ref in refs[1:count]:
@@ -286,17 +304,14 @@
     out_ref[...] = enter_part(at, in_ref, own_ref, other_ref)
 
 
-def hidden_kernel(at, slices, experts, in_ref, own_ref, other_ref, before_ref, member_ref, mine_ref, theirs_ref):
+def hidden_kernel(at, slices, experts, in_ref, own_ref, other_ref, before_ref, member_ref, out_ref):
     total = before_ref[...] + enter_part(at, in_ref, own_ref, other_ref)
-    half, hid = mine_ref.shape
-    t = 2 * half
+    t, hid = out_ref.shape
     gate, up, logits = total[0:hid], total[hid : 2 * hid], total[2 * hid : 2 * hid + experts]
     raised = jnp.where(member_ref[0:experts, :] > 0.5, jnp.exp(logits), 0.0)
     mine = iota2((experts, t), 0) == lax.axis_index("exp") // slices
     prob = jnp.sum(jnp.where(mine, raised, 0.0), axis=0, keepdims=True) / jnp.sum(raised, axis=0, keepdims=True)
-    hidden = (gate / (1.0 + jnp.exp(-gate)) * up * prob).T.astype(BF16)
-    mine_ref[...] = hidden[:half]
-    theirs_ref[...] = hidden[half:]
+    out_ref[...] = (gate / (1.0 + jnp.exp(-gate)) * up * prob).T.astype(BF16)
 
 
 def result_kernel(count, *refs):
@@ -348,11 +363,7 @@
     def rows_of(count):
         return out((count * rows, size), BF16)
 
-    def reduce(mine, theirs, w, w_other):
-        other = across(theirs)
-        terms = [
-            call(functools.partial(product_kernel, at), [rows_of(1)] * n_pair, (mine, other, w, w_other)) for at in ranges
-        ]
+    def send(terms):
         return [[term[0]] + [shift(term[r], r) for r in range(1, n_pair)] for term in terms]
 
     decay_row = decay_log.T
@@ -390,13 +401,17 @@
         ],
         far=10,
     )
-    w_out_other, w_down_other = across(w_out), across(w_down[0])
+    w_out_other = across(w_out)
     mine, theirs = call(
         functools.partial(normed_kernel, n_pair, moves),
         [out((t // 2, d), BF16)] * 2,
-        (*states, intra, grown, query_near, gain, w_down_other),
-    )
-    terms = reduce(mine, theirs, w_out_near, w_out_other)
+        (*states, intra, grown, query_near, gain),
+    )
+    other = across(theirs)
+    terms = send(
+        call(functools.partial(product_kernel, at), [rows_of(1)] * n_pair, (mine, other, w_out_near, w_out_other))
+        for at in ranges
+    )
     mixed = [call(functools.partial(sum_kernel, n_pair), [rows_of(1)], term)[0] for term in terms]
     gathered = [[shift(m, -r) if r else m for r in range(n_pair)] for m in mixed]
     own, after = [], ()
@@ -409,12 +424,19 @@
             after = (token,)
     left, right = ranges
     (total,) = call(functools.partial(enter_kernel, left), [out((w_in.shape[0], t), F32)], (w_in, own[0], across(own[0])))
-    mine, theirs = call(
+    (hidden,) = call(
         functools.partial(hidden_kernel, right, slices, experts),
-        [out((t // 2, hid), BF16)] * 2,
+        [out((t, hid), BF16)],
         (w_in, own[1], across(own[1]), total, member),
     )
-    sums = reduce(mine, theirs, w_down_near, w_down_other)
+    products = [
+        call(functools.partial(halves_kernel, at), [rows_of(n_pair)] * 2, (hidden, w_down_near)) for at in ranges
+    ]
+    others = [across(theirs) for _, theirs in products]
+    sums = send(
+        call(functools.partial(add_kernel, [[r] for r in range(n_pair)]), [rows_of(1)] * n_pair, (mine, other))
+        for (mine, _), other in zip(products, others)
+    )
     args = [x for some, m in zip(sums, mixed) for x in (*some, m)]
     return call(functools.partial(result_kernel, n_pair + 1), [out((rows, width), BF16)], args)[0]
 

time: 57.8 us -> 57.5 us (level)
    pallas_call x15 -> x17, Pallas kernels: 10.5 us -> 10.2 us  [call(): pl.pallas_call(kernel, out_shape=outs, in_specs=[pl.BlockSpec(memory_spac...]
  transfers between devices with their start and end apart: 27 -> 27, of which waited for: 8 -> 9; matrix products, arithmetic and copies ran while one was open for 0% -> 0% of each run, Pallas kernels for 14% -> 14%
where the time goes in v6:
time: 57.5 us; the launch traced here: 57.3 us
  starting transfers between devices  35.8 us (62%)
  waiting for transfers between devices  11 us (19%)
  Pallas kernels  10.2 us (18%)
    ppermute x18, starting transfers between devices, shift(): lax.ppermute(x, 'exp', [(e, (e + 2 * r) % exp_count) for e in range(exp_c...  30.4 us
    pallas_call x17, Pallas kernels, call(): pl.pallas_call(kernel, out_shape=outs, in_specs=[pl.BlockSpec(memory_spac...  10.2 us
    ppermute x18, waiting for transfers between devices, shift(): lax.ppermute(x, 'exp', [(e, (e + 2 * r) % exp_count) for e in range(exp_c...  7.71 us
    ppermute x3, starting transfers between devices, local(): lax.ppermute(state, 'seq', [(move(i), i) for i in range(seq_count)])  4.15 us
    ppermute x6, waiting for transfers between devices, across(): return lax.ppermute(x, 'exp', [(e, e ^ 1) for e in range(exp_count)])  2.4 us
    ppermute x6, starting transfers between devices, across(): return lax.ppermute(x, 'exp', [(e, e ^ 1) for e in range(exp_count)])  1.31 us
  transfers between devices with their start and end apart: 27, of which 9 were waited for; matrix products, arithmetic and copies ran while one was open for 0% of the time, Pallas kernels for 14%

profile of v6, /device:TPU:0, one launch (start us, length us, event | category | flops | bytes accessed | tf_op | source)
XLA Modules:
  0.0 57.3 jit_solution(3235602654935909847)
XLA Ops:
  0.0 0.5 collective-permute-start.4
  0.5 1.1 %shard_map.109._ = bf16[144,128]{1,0:T(8,128)(2,1)S(1)} custom-call(bf16[128,128]{1,0:T(8,128)(2,1)} %key_hbm.3, bf16[128,128]{1,0:T(8,128)(2,1)} %value_hbm.3, f32[1,128]{1,0:T(1,128)} %bitcast.15), custom_call_target="tpu_custom_call" | custom-call | tf_op jit(solution)/shard_map/pallas_call | solution.py:331
  1.6 3.5 %collective-permute-start.2 = (bf16[144,128]{1,0:T(8,128)(2,1)S(1)}, bf16[144,128]{1,0:T(8,128)(2,1)S(1)}, u32[]{:S(2)}, u32[]{:S(2)}) collective-permute-start(bf16[144,128]{1,0:T(8,128)(2,1)S(1)} %shard_map.109._), channel_id=1, source_target_pairs={{24,0},{16,8},{8,16},{0,24},{25,1},{17,9},{9,17},{1,25},{26,2},{18... | collective-permute-start | bytes 110600 | tf_op jit(solution)/shard_map/ppermute | solution.py:380
  5.1 0.5 collective-permute-start.1
  5.6 0.1 collective-permute-start
  5.7 2.9 %shard_map.110 = (f32[128,128]{1,0:T(8,128)S(1)}, f32[128,128]{1,0:T(8,128)S(1)}, bf16[128,128]{1,0:T(8,128)(2,1)S(1)}, f32[8,128]{1,0:T(8,128)S(1)}, bf16[128,4...) custom-call(bf16[128,128]{1,0:T(8,128)(2,1)} %query_hbm.1, bf16[128,128]{1,0:T(8,128)(2,1)} %key_hbm.3, ...), custom_call_target="tpu_custom_call" | custom-call | tf_op jit(solution)/shard_map/pallas_call | solution.py:331
  8.6 0.4 collective-permute-done.1.refs_1_
  9.0 0.5 collective-permute-done.refs_0_
  9.5 0.4 shard_map.111
  10.0 0.1 collective-permute-start.3
  10.0 1.2 %collective-permute-done.3.b_ref = bf16[64,128]{1,0:T(8,128)(2,1)S(1)} collective-permute-done((bf16[64,128]{1,0:T(8,128)(2,1)S(1)}, bf16[64,128]{1,0:T(8,128)(2,1)S(1)}, u32[]{:S(2)}, u32[]{:S(2)}) %collective-permute-start.3) | collective-permute-done | bytes 16416 | tf_op jit(solution)/shard_map/ppermute | solution.py:358
  11.2 0.3 shard_map.114
  11.5 1.6 %collective-permute-start.11 = (bf16[16,2048]{1,0:T(8,128)(2,1)S(1)}, bf16[16,2048]{1,0:T(8,128)(2,1)S(1)}, u32[]{:S(2)}, u32[]{:S(2)}) collective-permute-start(bf16[16,2048]{1,0:T(8,128)(2,1)S(1)} %get-tuple-element.49), channel_id=1, source_target_pairs={{0,2},{1,3},{2,4},{3,5},{4,6},{5,7},{6,0},{7,1},{8,10},{9,11},{10,... | collective-permute-start | bytes 196616 | tf_op jit(solution)/shard_map/ppermute | solution.py:355
  13.1 2.6 %collective-permute-start.12 = (bf16[16,2048]{1,0:T(8,128)(2,1)S(1)}, bf16[16,2048]{1,0:T(8,128)(2,1)S(1)}, u32[]{:S(2)}, u32[]{:S(2)}) collective-permute-start(bf16[16,2048]{1,0:T(8,128)(2,1)S(1)} %get-tuple-element.50), channel_id=1, source_target_pairs={{0,4},{1,5},{2,6},{3,7},{4,0},{5,1},{6,2},{7,3},{8,12},{9,13},{10,... | collective-permute-start | bytes 196616 | tf_op jit(solution)/shard_map/ppermute | solution.py:355
  15.7 1.3 %collective-permute-start.13 = (bf16[16,2048]{1,0:T(8,128)(2,1)S(1)}, bf16[16,2048]{1,0:T(8,128)(2,1)S(1)}, u32[]{:S(2)}, u32[]{:S(2)}) collective-permute-start(bf16[16,2048]{1,0:T(8,128)(2,1)S(1)} %get-tuple-element.51), channel_id=1, source_target_pairs={{0,6},{1,7},{2,0},{3,1},{4,2},{5,3},{6,4},{7,5},{8,14},{9,15},{10,... | collective-permute-start | bytes 196616 | tf_op jit(solution)/shard_map/ppermute | solution.py:355
  17.1 0.3 shard_map.112
  17.4 0.7 %collective-permute-start.5 = (bf16[16,2048]{1,0:T(8,128)(2,1)S(1)}, bf16[16,2048]{1,0:T(8,128)(2,1)S(1)}, u32[]{:S(2)}, u32[]{:S(2)}) collective-permute-start(bf16[16,2048]{1,0:T(8,128)(2,1)S(1)} %get-tuple-element.45), channel_id=1, source_target_pairs={{0,2},{1,3},{2,4},{3,5},{4,6},{5,7},{6,0},{7,1},{8,10},{9,11},{10,... | collective-permute-start | bytes 196616 | tf_op jit(solution)/shard_map/ppermute | solution.py:355
  18.1 0.3 collective-permute-start.6
  18.5 2.8 %collective-permute-start.7 = (bf16[16,2048]{1,0:T(8,128)(2,1)S(1)}, bf16[16,2048]{1,0:T(8,128)(2,1)S(1)}, u32[]{:S(2)}, u32[]{:S(2)}) collective-permute-start(bf16[16,2048]{1,0:T(8,128)(2,1)S(1)} %get-tuple-element.47), channel_id=1, source_target_pairs={{0,6},{1,7},{2,0},{3,1},{4,2},{5,3},{6,4},{7,5},{8,14},{9,15},{10,... | collective-permute-start | bytes 196616 | tf_op jit(solution)/shard_map/ppermute | solution.py:355
  21.3 3.1 %collective-permute-start.16 = (bf16[16,2048]{1,0:T(8,128)(2,1)S(1)}, bf16[16,2048]{1,0:T(8,128)(2,1)S(1)}, u32[]{:S(2)}, u32[]{:S(2)}) collective-permute-start(bf16[16,2048]{1,0:T(8,128)(2,1)S(1)} %shard_map.115.refs_0_.refs_4_), channel_id=1, source_target_pairs={{0,2},{1,3},{2,4},{3,5},{4,6},{5,7},{6,0},{7,1},{8,10},{9,11},{10,... | collective-permute-start | bytes 196616 | tf_op jit(solution)/shard_map/ppermute | solution.py:355
  24.4 0.5 collective-permute-start.15
  24.9 1.9 %collective-permute-start.14 = (bf16[16,2048]{1,0:T(8,128)(2,1)S(1)}, bf16[16,2048]{1,0:T(8,128)(2,1)S(1)}, u32[]{:S(2)}, u32[]{:S(2)}) collective-permute-start(bf16[16,2048]{1,0:T(8,128)(2,1)S(1)} %shard_map.115.refs_0_.refs_4_), channel_id=1, source_target_pairs={{0,6},{1,7},{2,0},{3,1},{4,2},{5,3},{6,4},{7,5},{8,14},{9,15},{10,... | collective-permute-start | bytes 196616 | tf_op jit(solution)/shard_map/ppermute | solution.py:355
  26.9 4.1 %collective-permute-start.10 = (bf16[16,2048]{1,0:T(8,128)(2,1)S(1)}, bf16[16,2048]{1,0:T(8,128)(2,1)S(1)}, u32[]{:S(2)}, u32[]{:S(2)}) collective-permute-start(bf16[16,2048]{1,0:T(8,128)(2,1)S(1)} %shard_map.113.refs_0_.refs_9_), channel_id=1, source_target_pairs={{0,2},{1,3},{2,4},{3,5},{4,6},{5,7},{6,0},{7,1},{8,10},{9,11},{10,... | collective-permute-start | bytes 196616 | tf_op jit(solution)/shard_map/ppermute | solution.py:355
  31.0 2.4 %collective-permute-start.8 = (bf16[16,2048]{1,0:T(8,128)(2,1)S(1)}, bf16[16,2048]{1,0:T(8,128)(2,1)S(1)}, u32[]{:S(2)}, u32[]{:S(2)}) collective-permute-start(bf16[16,2048]{1,0:T(8,128)(2,1)S(1)} %shard_map.113.refs_0_.refs_9_), channel_id=1, source_target_pairs={{0,6},{1,7},{2,0},{3,1},{4,2},{5,3},{6,4},{7,5},{8,14},{9,15},{10,... | collective-permute-start | bytes 196616 | tf_op jit(solution)/shard_map/ppermute | solution.py:355
  33.5 0.1 collective-permute-start.18
  33.5 1.7 %shard_map.117 = (bf16[288,4096]{1,0:T(8,128)(2,1)S(1)}, f32[8,128]{1,0:T(8,128)S(1)}) custom-call(bf16[288,4096]{1,0:T(8,128)(2,1)} %bitcast.13, bf16[64,2048]{1,0:T(8,128)(2,1)S(1)} %shard_map.116._.own_ref), custom_call_target="tpu_custom_call" | custom-call | tf_op jit(solution)/shard_map/pallas_call | solution.py:331
  35.2 2.1 %collective-permute-done.9.refs_2_ = bf16[16,2048]{1,0:T(8,128)(2,1)S(1)} collective-permute-done((bf16[16,2048]{1,0:T(8,128)(2,1)S(1)}, bf16[16,2048]{1,0:T(8,128)(2,1)S(1)}, u32[]{:S(2)}, u32[]{:S(2)}) %collective-permute-start.9) | collective-permute-done | bytes 65568 | tf_op jit(solution)/shard_map/ppermute | solution.py:355
  37.4 0.1 collective-permute-start.17
  37.5 0.8 %shard_map.119.before_ref = f32[592,128]{1,0:T(8,128)S(1)} custom-call(bf16[592,4096]{1,0:T(8,128)(2,1)S(1)} %get-tuple-element.36.in_ref, bf16[64,2048]{1,0:T(8,128)(2,1)S(1)} %shard_map.116._.own_ref, bf16[64,2048]{1,0:T(8,128)(2,1)S(1)} %collective-permute-done.18.other_ref), custom_call_target="tpu_custom_call" | custom-call | tf_op jit(solution)/shard_map/pallas_call | solution.py:331
  38.3 0.7 %collective-permute-done.17.other_ref = bf16[64,2048]{1,0:T(8,128)(2,1)S(1)} collective-permute-done((bf16[64,2048]{1,0:T(8,128)(2,1)S(1)}, bf16[64,2048]{1,0:T(8,128)(2,1)S(1)}, u32[]{:S(2)}, u32[]{:S(2)}) %collective-permute-start.17) | collective-permute-done | bytes 262176 | tf_op jit(solution)/shard_map/ppermute | solution.py:358
  39.0 0.9 %shard_map.120.x_ref = bf16[128,288]{1,0:T(8,128)(2,1)S(1)} custom-call(bf16[592,4096]{1,0:T(8,128)(2,1)S(1)} %get-tuple-element.36.in_ref, bf16[64,2048]{1,0:T(8,128)(2,1)S(1)} %shard_map.118.own_ref, bf16[64,2048]{1,0:T(8,128)(2,1)S(1)} %collective-permute-done.17.other_ref, f32[592,128]{1,0:T(8,128)S(1)} %shard_map.119.before_ref, ...), custom_call_target="tpu_custom_call" | custom-call | tf_op jit(solution)/shard_map/pallas_call | solution.py:331
  39.9 0.4 shard_map.123
  40.4 0.2 collective-permute-start.23
  40.6 0.4 shard_map.121
  41.0 0.4 collective-permute-start.19
  41.4 0.5 collective-permute-done.23.b_ref
  42.0 0.1 shard_map.124
  42.0 1.9 %collective-permute-start.24 = (bf16[16,2048]{1,0:T(8,128)(2,1)S(1)}, bf16[16,2048]{1,0:T(8,128)(2,1)S(1)}, u32[]{:S(2)}, u32[]{:S(2)}) collective-permute-start(bf16[16,2048]{1,0:T(8,128)(2,1)S(1)} %get-tuple-element.64), channel_id=1, source_target_pairs={{0,2},{1,3},{2,4},{3,5},{4,6},{5,7},{6,0},{7,1},{8,10},{9,11},{10,... | collective-permute-start | bytes 196616 | tf_op jit(solution)/shard_map/ppermute | solution.py:355
  43.9 1.7 %collective-permute-start.25 = (bf16[16,2048]{1,0:T(8,128)(2,1)S(1)}, bf16[16,2048]{1,0:T(8,128)(2,1)S(1)}, u32[]{:S(2)}, u32[]{:S(2)}) collective-permute-start(bf16[16,2048]{1,0:T(8,128)(2,1)S(1)} %get-tuple-element.65), channel_id=1, source_target_pairs={{0,4},{1,5},{2,6},{3,7},{4,0},{5,1},{6,2},{7,3},{8,12},{9,13},{10,... | collective-permute-start | bytes 196616 | tf_op jit(solution)/shard_map/ppermute | solution.py:355
  45.7 0.7 %collective-permute-start.26 = (bf16[16,2048]{1,0:T(8,128)(2,1)S(1)}, bf16[16,2048]{1,0:T(8,128)(2,1)S(1)}, u32[]{:S(2)}, u32[]{:S(2)}) collective-permute-start(bf16[16,2048]{1,0:T(8,128)(2,1)S(1)} %get-tuple-element.66), channel_id=1, source_target_pairs={{0,6},{1,7},{2,0},{3,1},{4,2},{5,3},{6,4},{7,5},{8,14},{9,15},{10,... | collective-permute-start | bytes 196616 | tf_op jit(solution)/shard_map/ppermute | solution.py:355
  46.4 0.1 shard_map.122
  46.5 1.4 %collective-permute-start.20 = (bf16[16,2048]{1,0:T(8,128)(2,1)S(1)}, bf16[16,2048]{1,0:T(8,128)(2,1)S(1)}, u32[]{:S(2)}, u32[]{:S(2)}) collective-permute-start(bf16[16,2048]{1,0:T(8,128)(2,1)S(1)} %get-tuple-element.58), channel_id=1, source_target_pairs={{0,2},{1,3},{2,4},{3,5},{4,6},{5,7},{6,0},{7,1},{8,10},{9,11},{10,... | collective-permute-start | bytes 196616 | tf_op jit(solution)/shard_map/ppermute | solution.py:355
  47.8 1.2 %collective-permute-start.21 = (bf16[16,2048]{1,0:T(8,128)(2,1)S(1)}, bf16[16,2048]{1,0:T(8,128)(2,1)S(1)}, u32[]{:S(2)}, u32[]{:S(2)}) collective-permute-start(bf16[16,2048]{1,0:T(8,128)(2,1)S(1)} %get-tuple-element.59), channel_id=1, source_target_pairs={{0,4},{1,5},{2,6},{3,7},{4,0},{5,1},{6,2},{7,3},{8,12},{9,13},{10,... | collective-permute-start | bytes 196616 | tf_op jit(solution)/shard_map/ppermute | solution.py:355
  49.0 2.0 %collective-permute-start.22 = (bf16[16,2048]{1,0:T(8,128)(2,1)S(1)}, bf16[16,2048]{1,0:T(8,128)(2,1)S(1)}, u32[]{:S(2)}, u32[]{:S(2)}) collective-permute-start(bf16[16,2048]{1,0:T(8,128)(2,1)S(1)} %get-tuple-element.60), channel_id=1, source_target_pairs={{0,6},{1,7},{2,0},{3,1},{4,2},{5,3},{6,4},{7,5},{8,14},{9,15},{10,... | collective-permute-start | bytes 196616 | tf_op jit(solution)/shard_map/ppermute | solution.py:355
  51.0 1.7 %collective-permute-done.25.refs_7_ = bf16[16,2048]{1,0:T(8,128)(2,1)S(1)} collective-permute-done((bf16[16,2048]{1,0:T(8,128)(2,1)S(1)}, bf16[16,2048]{1,0:T(8,128)(2,1)S(1)}, u32[]{:S(2)}, u32[]{:S(2)}) %collective-permute-start.25) | collective-permute-done | bytes 65568 | tf_op jit(solution)/shard_map/ppermute | solution.py:355
  52.7 0.6 %collective-permute-done.20.refs_1_ = bf16[16,2048]{1,0:T(8,128)(2,1)S(1)} collective-permute-done((bf16[16,2048]{1,0:T(8,128)(2,1)S(1)}, bf16[16,2048]{1,0:T(8,128)(2,1)S(1)}, u32[]{:S(2)}, u32[]{:S(2)}) %collective-permute-start.20) | collective-permute-done | bytes 65568 | tf_op jit(solution)/shard_map/ppermute | solution.py:355
  53.3 3.2 %collective-permute-done.21.refs_2_ = bf16[16,2048]{1,0:T(8,128)(2,1)S(1)} collective-permute-done((bf16[16,2048]{1,0:T(8,128)(2,1)S(1)}, bf16[16,2048]{1,0:T(8,128)(2,1)S(1)}, u32[]{:S(2)}, u32[]{:S(2)}) %collective-permute-start.21) | collective-permute-done | bytes 65568 | tf_op jit(solution)/shard_map/ppermute | solution.py:355
  56.5 0.7 %shard_map.125 = bf16[16,4096]{1,0:T(8,128)(2,1)} custom-call(bf16[16,2048]{1,0:T(8,128)(2,1)S(1)} %get-tuple-element.57.refs_0_, bf16[16,2048]{1,0:T(8,128)(2,1)S(1)} %collective-permute-done.20.refs_1_, bf16[16,2048]{1,0:T(8,128)(2,1)S(1)} %collective-permute-done.21.refs_2_, bf16[16,2048]{1,0:T(8,128)(2,1)S(1)} %collective-permute-done.22.refs_3_, ...), custom_call_target="tpu_custom_call" | custom-call | tf_op jit(solution)/shard_map/pallas_call | solution.py:331
  (23 shorter events, 0.2 us)
Async XLA Ops:
  0.0 11.2 %collective-permute-start.4 = (bf16[128,4096]{1,0:T(8,128)(2,1)}, bf16[128,4096]{1,0:T(8,128)(2,1)S(1)}, u32[]{:S(2)}, u32[]{:S(2)}) collective-permute-start(bf16[128,4096]{1,0:T(8,128)(2,1)} %w_out_hbm.1), channel_id=1, source_target_pairs={{0,1},{1,0},{2,3},{3,2},{4,5},{5,4},{6,7},{7,6},{8,9},{9,8},{10,11... | collective-permute-start | bytes 3145736 | tf_op jit(solution)/shard_map/ppermute | solution.py:358
  1.6 7.1 %collective-permute-start.2 = (bf16[144,128]{1,0:T(8,128)(2,1)S(1)}, bf16[144,128]{1,0:T(8,128)(2,1)S(1)}, u32[]{:S(2)}, u32[]{:S(2)}) collective-permute-start(bf16[144,128]{1,0:T(8,128)(2,1)S(1)} %shard_map.109._), channel_id=1, source_target_pairs={{24,0},{16,8},{8,16},{0,24},{25,1},{17,9},{9,17},{1,25},{26,2},{18... | collective-permute-start | bytes 110600 | tf_op jit(solution)/shard_map/ppermute | solution.py:380
  5.1 4.0 %collective-permute-start.1 = (bf16[144,128]{1,0:T(8,128)(2,1)S(1)}, bf16[144,128]{1,0:T(8,128)(2,1)S(1)}, u32[]{:S(2)}, u32[]{:S(2)}) collective-permute-start(bf16[144,128]{1,0:T(8,128)(2,1)S(1)} %shard_map.109._), channel_id=1, source_target_pairs={{16,0},{24,8},{0,16},{8,24},{17,1},{25,9},{1,17},{9,25},{18,2},{26... | collective-permute-start | bytes 110600 | tf_op jit(solution)/shard_map/ppermute | solution.py:380
  5.6 4.0 %collective-permute-start = (bf16[144,128]{1,0:T(8,128)(2,1)S(1)}, bf16[144,128]{1,0:T(8,128)(2,1)S(1)}, u32[]{:S(2)}, u32[]{:S(2)}) collective-permute-start(bf16[144,128]{1,0:T(8,128)(2,1)S(1)} %shard_map.109._), channel_id=1, source_target_pairs={{8,0},{0,8},{24,16},{16,24},{9,1},{1,9},{25,17},{17,25},{10,2},{2,... | collective-permute-start | bytes 110600 | tf_op jit(solution)/shard_map/ppermute | solution.py:380
  10.0 1.2 %collective-permute-start.3 = (bf16[64,128]{1,0:T(8,128)(2,1)S(1)}, bf16[64,128]{1,0:T(8,128)(2,1)S(1)}, u32[]{:S(2)}, u32[]{:S(2)}) collective-permute-start(bf16[64,128]{1,0:T(8,128)(2,1)S(1)} %get-tuple-element.42), channel_id=1, source_target_pairs={{0,1},{1,0},{2,3},{3,2},{4,5},{5,4},{6,7},{7,6},{8,9},{9,8},{10,11... | collective-permute-start | bytes 49160 | tf_op jit(solution)/shard_map/ppermute | solution.py:358
  11.5 6.9 %collective-permute-start.11 = (bf16[16,2048]{1,0:T(8,128)(2,1)S(1)}, bf16[16,2048]{1,0:T(8,128)(2,1)S(1)}, u32[]{:S(2)}, u32[]{:S(2)}) collective-permute-start(bf16[16,2048]{1,0:T(8,128)(2,1)S(1)} %get-tuple-element.49), channel_id=1, source_target_pairs={{0,2},{1,3},{2,4},{3,5},{4,6},{5,7},{6,0},{7,1},{8,10},{9,11},{10,... | collective-permute-start | bytes 196616 | tf_op jit(solution)/shard_map/ppermute | solution.py:355
  13.1 8.1 %collective-permute-start.12 = (bf16[16,2048]{1,0:T(8,128)(2,1)S(1)}, bf16[16,2048]{1,0:T(8,128)(2,1)S(1)}, u32[]{:S(2)}, u32[]{:S(2)}) collective-permute-start(bf16[16,2048]{1,0:T(8,128)(2,1)S(1)} %get-tuple-element.50), channel_id=1, source_target_pairs={{0,4},{1,5},{2,6},{3,7},{4,0},{5,1},{6,2},{7,3},{8,12},{9,13},{10,... | collective-permute-start | bytes 196616 | tf_op jit(solution)/shard_map/ppermute | solution.py:355
  15.7 5.5 %collective-permute-start.13 = (bf16[16,2048]{1,0:T(8,128)(2,1)S(1)}, bf16[16,2048]{1,0:T(8,128)(2,1)S(1)}, u32[]{:S(2)}, u32[]{:S(2)}) collective-permute-start(bf16[16,2048]{1,0:T(8,128)(2,1)S(1)} %get-tuple-element.51), channel_id=1, source_target_pairs={{0,6},{1,7},{2,0},{3,1},{4,2},{5,3},{6,4},{7,5},{8,14},{9,15},{10,... | collective-permute-start | bytes 196616 | tf_op jit(solution)/shard_map/ppermute | solution.py:355
  17.4 7.5 %collective-permute-start.5 = (bf16[16,2048]{1,0:T(8,128)(2,1)S(1)}, bf16[16,2048]{1,0:T(8,128)(2,1)S(1)}, u32[]{:S(2)}, u32[]{:S(2)}) collective-permute-start(bf16[16,2048]{1,0:T(8,128)(2,1)S(1)} %get-tuple-element.45), channel_id=1, source_target_pairs={{0,2},{1,3},{2,4},{3,5},{4,6},{5,7},{6,0},{7,1},{8,10},{9,11},{10,... | collective-permute-start | bytes 196616 | tf_op jit(solution)/shard_map/ppermute | solution.py:355
  18.1 8.7 %collective-permute-start.6 = (bf16[16,2048]{1,0:T(8,128)(2,1)S(1)}, bf16[16,2048]{1,0:T(8,128)(2,1)S(1)}, u32[]{:S(2)}, u32[]{:S(2)}) collective-permute-start(bf16[16,2048]{1,0:T(8,128)(2,1)S(1)} %get-tuple-element.46), channel_id=1, source_target_pairs={{0,4},{1,5},{2,6},{3,7},{4,0},{5,1},{6,2},{7,3},{8,12},{9,13},{10,... | collective-permute-start | bytes 196616 | tf_op jit(solution)/shard_map/ppermute | solution.py:355
  18.5 8.4 %collective-permute-start.7 = (bf16[16,2048]{1,0:T(8,128)(2,1)S(1)}, bf16[16,2048]{1,0:T(8,128)(2,1)S(1)}, u32[]{:S(2)}, u32[]{:S(2)}) collective-permute-start(bf16[16,2048]{1,0:T(8,128)(2,1)S(1)} %get-tuple-element.47), channel_id=1, source_target_pairs={{0,6},{1,7},{2,0},{3,1},{4,2},{5,3},{6,4},{7,5},{8,14},{9,15},{10,... | collective-permute-start | bytes 196616 | tf_op jit(solution)/shard_map/ppermute | solution.py:355
  21.3 9.7 %collective-permute-start.16 = (bf16[16,2048]{1,0:T(8,128)(2,1)S(1)}, bf16[16,2048]{1,0:T(8,128)(2,1)S(1)}, u32[]{:S(2)}, u32[]{:S(2)}) collective-permute-start(bf16[16,2048]{1,0:T(8,128)(2,1)S(1)} %shard_map.115.refs_0_.refs_4_), channel_id=1, source_target_pairs={{0,2},{1,3},{2,4},{3,5},{4,6},{5,7},{6,0},{7,1},{8,10},{9,11},{10,... | collective-permute-start | bytes 196616 | tf_op jit(solution)/shard_map/ppermute | solution.py:355
  24.4 9.0 %collective-permute-start.15 = (bf16[16,2048]{1,0:T(8,128)(2,1)S(1)}, bf16[16,2048]{1,0:T(8,128)(2,1)S(1)}, u32[]{:S(2)}, u32[]{:S(2)}) collective-permute-start(bf16[16,2048]{1,0:T(8,128)(2,1)S(1)} %shard_map.115.refs_0_.refs_4_), channel_id=1, source_target_pairs={{0,4},{1,5},{2,6},{3,7},{4,0},{5,1},{6,2},{7,3},{8,12},{9,13},{10,... | collective-permute-start | bytes 196616 | tf_op jit(solution)/shard_map/ppermute | solution.py:355
  24.9 8.5 %collective-permute-start.14 = (bf16[16,2048]{1,0:T(8,128)(2,1)S(1)}, bf16[16,2048]{1,0:T(8,128)(2,1)S(1)}, u32[]{:S(2)}, u32[]{:S(2)}) collective-permute-start(bf16[16,2048]{1,0:T(8,128)(2,1)S(1)} %shard_map.115.refs_0_.refs_4_), channel_id=1, source_target_pairs={{0,6},{1,7},{2,0},{3,1},{4,2},{5,3},{6,4},{7,5},{8,14},{9,15},{10,... | collective-permute-start | bytes 196616 | tf_op jit(solution)/shard_map/ppermute | solution.py:355
  26.9 8.3 %collective-permute-start.10 = (bf16[16,2048]{1,0:T(8,128)(2,1)S(1)}, bf16[16,2048]{1,0:T(8,128)(2,1)S(1)}, u32[]{:S(2)}, u32[]{:S(2)}) collective-permute-start(bf16[16,2048]{1,0:T(8,128)(2,1)S(1)} %shard_map.113.refs_0_.refs_9_), channel_id=1, source_target_pairs={{0,2},{1,3},{2,4},{3,5},{4,6},{5,7},{6,0},{7,1},{8,10},{9,11},{10,... | collective-permute-start | bytes 196616 | tf_op jit(solution)/shard_map/ppermute | solution.py:355
  31.0 6.4 %collective-permute-start.9 = (bf16[16,2048]{1,0:T(8,128)(2,1)S(1)}, bf16[16,2048]{1,0:T(8,128)(2,1)S(1)}, u32[]{:S(2)}, u32[]{:S(2)}) collective-permute-start(bf16[16,2048]{1,0:T(8,128)(2,1)S(1)} %shard_map.113.refs_0_.refs_9_), channel_id=1, source_target_pairs={{0,4},{1,5},{2,6},{3,7},{4,0},{5,1},{6,2},{7,3},{8,12},{9,13},{10,... | collective-permute-start | bytes 196616 | tf_op jit(solution)/shard_map/ppermute | solution.py:355
  31.0 6.3 %collective-permute-start.8 = (bf16[16,2048]{1,0:T(8,128)(2,1)S(1)}, bf16[16,2048]{1,0:T(8,128)(2,1)S(1)}, u32[]{:S(2)}, u32[]{:S(2)}) collective-permute-start(bf16[16,2048]{1,0:T(8,128)(2,1)S(1)} %shard_map.113.refs_0_.refs_9_), channel_id=1, source_target_pairs={{0,6},{1,7},{2,0},{3,1},{4,2},{5,3},{6,4},{7,5},{8,14},{9,15},{10,... | collective-permute-start | bytes 196616 | tf_op jit(solution)/shard_map/ppermute | solution.py:355
  33.5 4.0 %collective-permute-start.18 = (bf16[64,2048]{1,0:T(8,128)(2,1)S(1)}, bf16[64,2048]{1,0:T(8,128)(2,1)S(1)}, u32[]{:S(2)}, u32[]{:S(2)}) collective-permute-start(bf16[64,2048]{1,0:T(8,128)(2,1)S(1)} %shard_map.116._.own_ref), channel_id=1, source_target_pairs={{0,1},{1,0},{2,3},{3,2},{4,5},{5,4},{6,7},{7,6},{8,9},{9,8},{10,11... | collective-permute-start | bytes 786440 | tf_op jit(solution)/shard_map/ppermute | solution.py:358
  37.4 1.6 %collective-permute-start.17 = (bf16[64,2048]{1,0:T(8,128)(2,1)S(1)}, bf16[64,2048]{1,0:T(8,128)(2,1)S(1)}, u32[]{:S(2)}, u32[]{:S(2)}) collective-permute-start(bf16[64,2048]{1,0:T(8,128)(2,1)S(1)} %shard_map.118.own_ref), channel_id=1, source_target_pairs={{0,1},{1,0},{2,3},{3,2},{4,5},{5,4},{6,7},{7,6},{8,9},{9,8},{10,11... | collective-permute-start | bytes 786440 | tf_op jit(solution)/shard_map/ppermute | solution.py:358
  40.4 1.6 %collective-permute-start.23 = (bf16[64,2048]{1,0:T(8,128)(2,1)S(1)}, bf16[64,2048]{1,0:T(8,128)(2,1)S(1)}, u32[]{:S(2)}, u32[]{:S(2)}) collective-permute-start(bf16[64,2048]{1,0:T(8,128)(2,1)S(1)} %get-tuple-element.62), channel_id=1, source_target_pairs={{0,1},{1,0},{2,3},{3,2},{4,5},{5,4},{6,7},{7,6},{8,9},{9,8},{10,11... | collective-permute-start | bytes 786440 | tf_op jit(solution)/shard_map/ppermute | solution.py:358
  41.0 5.4 %collective-permute-start.19 = (bf16[64,2048]{1,0:T(8,128)(2,1)S(1)}, bf16[64,2048]{1,0:T(8,128)(2,1)S(1)}, u32[]{:S(2)}, u32[]{:S(2)}) collective-permute-start(bf16[64,2048]{1,0:T(8,128)(2,1)S(1)} %get-tuple-element.56), channel_id=1, source_target_pairs={{0,1},{1,0},{2,3},{3,2},{4,5},{5,4},{6,7},{7,6},{8,9},{9,8},{10,11... | collective-permute-start | bytes 786440 | tf_op jit(solution)/shard_map/ppermute | solution.py:358
  42.0 7.0 %collective-permute-start.24 = (bf16[16,2048]{1,0:T(8,128)(2,1)S(1)}, bf16[16,2048]{1,0:T(8,128)(2,1)S(1)}, u32[]{:S(2)}, u32[]{:S(2)}) collective-permute-start(bf16[16,2048]{1,0:T(8,128)(2,1)S(1)} %get-tuple-element.64), channel_id=1, source_target_pairs={{0,2},{1,3},{2,4},{3,5},{4,6},{5,7},{6,0},{7,1},{8,10},{9,11},{10,... | collective-permute-start | bytes 196616 | tf_op jit(solution)/shard_map/ppermute | solution.py:355
  43.9 8.8 %collective-permute-start.25 = (bf16[16,2048]{1,0:T(8,128)(2,1)S(1)}, bf16[16,2048]{1,0:T(8,128)(2,1)S(1)}, u32[]{:S(2)}, u32[]{:S(2)}) collective-permute-start(bf16[16,2048]{1,0:T(8,128)(2,1)S(1)} %get-tuple-element.65), channel_id=1, source_target_pairs={{0,4},{1,5},{2,6},{3,7},{4,0},{5,1},{6,2},{7,3},{8,12},{9,13},{10,... | collective-permute-start | bytes 196616 | tf_op jit(solution)/shard_map/ppermute | solution.py:355
  45.7 7.0 %collective-permute-start.26 = (bf16[16,2048]{1,0:T(8,128)(2,1)S(1)}, bf16[16,2048]{1,0:T(8,128)(2,1)S(1)}, u32[]{:S(2)}, u32[]{:S(2)}) collective-permute-start(bf16[16,2048]{1,0:T(8,128)(2,1)S(1)} %get-tuple-element.66), channel_id=1, source_target_pairs={{0,6},{1,7},{2,0},{3,1},{4,2},{5,3},{6,4},{7,5},{8,14},{9,15},{10,... | collective-permute-start | bytes 196616 | tf_op jit(solution)/shard_map/ppermute | solution.py:355
  46.5 6.9 %collective-permute-start.20 = (bf16[16,2048]{1,0:T(8,128)(2,1)S(1)}, bf16[16,2048]{1,0:T(8,128)(2,1)S(1)}, u32[]{:S(2)}, u32[]{:S(2)}) collective-permute-start(bf16[16,2048]{1,0:T(8,128)(2,1)S(1)} %get-tuple-element.58), channel_id=1, source_target_pairs={{0,2},{1,3},{2,4},{3,5},{4,6},{5,7},{6,0},{7,1},{8,10},{9,11},{10,... | collective-permute-start | bytes 196616 | tf_op jit(solution)/shard_map/ppermute | solution.py:355
  47.8 8.7 %collective-permute-start.21 = (bf16[16,2048]{1,0:T(8,128)(2,1)S(1)}, bf16[16,2048]{1,0:T(8,128)(2,1)S(1)}, u32[]{:S(2)}, u32[]{:S(2)}) collective-permute-start(bf16[16,2048]{1,0:T(8,128)(2,1)S(1)} %get-tuple-element.59), channel_id=1, source_target_pairs={{0,4},{1,5},{2,6},{3,7},{4,0},{5,1},{6,2},{7,3},{8,12},{9,13},{10,... | collective-permute-start | bytes 196616 | tf_op jit(solution)/shard_map/ppermute | solution.py:355
  49.0 7.5 %collective-permute-start.22 = (bf16[16,2048]{1,0:T(8,128)(2,1)S(1)}, bf16[16,2048]{1,0:T(8,128)(2,1)S(1)}, u32[]{:S(2)}, u32[]{:S(2)}) collective-permute-start(bf16[16,2048]{1,0:T(8,128)(2,1)S(1)} %get-tuple-element.60), channel_id=1, source_target_pairs={{0,6},{1,7},{2,0},{3,1},{4,2},{5,3},{6,4},{7,5},{8,14},{9,15},{10,... | collective-permute-start | bytes 196616 | tf_op jit(solution)/shard_map/ppermute | solution.py:355

commit v7 on v6

--- a/solution.py
+++ b/solution.py
@@ -376,7 +376,8 @@
         [block, block, decay_block, dma((3,))],
         far=3,
     )
-    moves = [lambda i, k=k: i ^ k for k in range(1, seq_count)]
+    order = [2, 1] + list(range(3, seq_count))
+    moves = [lambda i, k=k: i ^ k for k in order]
     states = [lax.ppermute(state, "seq", [(move(i), i) for i in range(seq_count)]) for move in moves]
     intra, grown, query_near, gain, w_out_near, w_in, member = call(
         functools.partial(within_kernel, n_pair),

time: 57.5 us -> 57.5 us (level)
  no operation moved by 1% of the time
where the time goes in v7:
time: 57.5 us; the launch traced here: 57.3 us
  starting transfers between devices  35.8 us (62%)
  waiting for transfers between devices  11 us (19%)
  Pallas kernels  10.2 us (18%)
    ppermute x18, starting transfers between devices, shift(): lax.ppermute(x, 'exp', [(e, (e + 2 * r) % exp_count) for e in range(exp_c...  30.4 us
    pallas_call x17, Pallas kernels, call(): pl.pallas_call(kernel, out_shape=outs, in_specs=[pl.BlockSpec(memory_spac...  10.2 us
    ppermute x18, waiting for transfers between devices, shift(): lax.ppermute(x, 'exp', [(e, (e + 2 * r) % exp_count) for e in range(exp_c...  7.71 us
    ppermute x3, starting transfers between devices, local(): lax.ppermute(state, 'seq', [(move(i), i) for i in range(seq_count)])  4.15 us
    ppermute x6, waiting for transfers between devices, across(): return lax.ppermute(x, 'exp', [(e, e ^ 1) for e in range(exp_count)])  2.4 us
    ppermute x6, starting transfers between devices, across(): return lax.ppermute(x, 'exp', [(e, e ^ 1) for e in range(exp_count)])  1.31 us
  transfers between devices with their start and end apart: 27, of which 9 were waited for; matrix products, arithmetic and copies ran while one was open for 0% of the time, Pallas kernels for 14%

profile of v7, /device:TPU:0, one launch (start us, length us, event | category | flops | bytes accessed | tf_op | source)
XLA Modules:
  0.0 57.3 jit_solution(6504805854941305027)
XLA Ops:
  0.0 0.5 collective-permute-start.4
  0.5 1.1 %shard_map.109._ = bf16[144,128]{1,0:T(8,128)(2,1)S(1)} custom-call(bf16[128,128]{1,0:T(8,128)(2,1)} %key_hbm.3, bf16[128,128]{1,0:T(8,128)(2,1)} %value_hbm.3, f32[1,128]{1,0:T(1,128)} %bitcast.15), custom_call_target="tpu_custom_call" | custom-call | tf_op jit(solution)/shard_map/pallas_call | solution.py:331
  1.6 3.5 %collective-permute-start.2 = (bf16[144,128]{1,0:T(8,128)(2,1)S(1)}, bf16[144,128]{1,0:T(8,128)(2,1)S(1)}, u32[]{:S(2)}, u32[]{:S(2)}) collective-permute-start(bf16[144,128]{1,0:T(8,128)(2,1)S(1)} %shard_map.109._), channel_id=1, source_target_pairs={{24,0},{16,8},{8,16},{0,24},{25,1},{17,9},{9,17},{1,25},{26,2},{18... | collective-permute-start | bytes 110600 | tf_op jit(solution)/shard_map/ppermute | solution.py:381
  5.1 0.5 collective-permute-start.1
  5.6 0.1 collective-permute-start
  5.7 2.9 %shard_map.110 = (f32[128,128]{1,0:T(8,128)S(1)}, f32[128,128]{1,0:T(8,128)S(1)}, bf16[128,128]{1,0:T(8,128)(2,1)S(1)}, f32[8,128]{1,0:T(8,128)S(1)}, bf16[128,4...) custom-call(bf16[128,128]{1,0:T(8,128)(2,1)} %query_hbm.1, bf16[128,128]{1,0:T(8,128)(2,1)} %key_hbm.3, ...), custom_call_target="tpu_custom_call" | custom-call | tf_op jit(solution)/shard_map/pallas_call | solution.py:331
  8.6 0.4 collective-permute-done.1.refs_1_
  9.0 0.5 collective-permute-done.refs_0_
  9.6 0.4 shard_map.111
  10.0 0.1 collective-permute-start.3
  10.1 1.2 %collective-permute-done.3.b_ref = bf16[64,128]{1,0:T(8,128)(2,1)S(1)} collective-permute-done((bf16[64,128]{1,0:T(8,128)(2,1)S(1)}, bf16[64,128]{1,0:T(8,128)(2,1)S(1)}, u32[]{:S(2)}, u32[]{:S(2)}) %collective-permute-start.3) | collective-permute-done | bytes 16416 | tf_op jit(solution)/shard_map/ppermute | solution.py:358
  11.2 0.3 shard_map.114
  11.5 1.6 %collective-permute-start.11 = (bf16[16,2048]{1,0:T(8,128)(2,1)S(1)}, bf16[16,2048]{1,0:T(8,128)(2,1)S(1)}, u32[]{:S(2)}, u32[]{:S(2)}) collective-permute-start(bf16[16,2048]{1,0:T(8,128)(2,1)S(1)} %get-tuple-element.49), channel_id=1, source_target_pairs={{0,2},{1,3},{2,4},{3,5},{4,6},{5,7},{6,0},{7,1},{8,10},{9,11},{10,... | collective-permute-start | bytes 196616 | tf_op jit(solution)/shard_map/ppermute | solution.py:355
  13.2 2.6 %collective-permute-start.12 = (bf16[16,2048]{1,0:T(8,128)(2,1)S(1)}, bf16[16,2048]{1,0:T(8,128)(2,1)S(1)}, u32[]{:S(2)}, u32[]{:S(2)}) collective-permute-start(bf16[16,2048]{1,0:T(8,128)(2,1)S(1)} %get-tuple-element.50), channel_id=1, source_target_pairs={{0,4},{1,5},{2,6},{3,7},{4,0},{5,1},{6,2},{7,3},{8,12},{9,13},{10,... | collective-permute-start | bytes 196616 | tf_op jit(solution)/shard_map/ppermute | solution.py:355
  15.8 1.3 %collective-permute-start.13 = (bf16[16,2048]{1,0:T(8,128)(2,1)S(1)}, bf16[16,2048]{1,0:T(8,128)(2,1)S(1)}, u32[]{:S(2)}, u32[]{:S(2)}) collective-permute-start(bf16[16,2048]{1,0:T(8,128)(2,1)S(1)} %get-tuple-element.51), channel_id=1, source_target_pairs={{0,6},{1,7},{2,0},{3,1},{4,2},{5,3},{6,4},{7,5},{8,14},{9,15},{10,... | collective-permute-start | bytes 196616 | tf_op jit(solution)/shard_map/ppermute | solution.py:355
  17.1 0.3 shard_map.112
  17.4 0.7 %collective-permute-start.5 = (bf16[16,2048]{1,0:T(8,128)(2,1)S(1)}, bf16[16,2048]{1,0:T(8,128)(2,1)S(1)}, u32[]{:S(2)}, u32[]{:S(2)}) collective-permute-start(bf16[16,2048]{1,0:T(8,128)(2,1)S(1)} %get-tuple-element.45), channel_id=1, source_target_pairs={{0,2},{1,3},{2,4},{3,5},{4,6},{5,7},{6,0},{7,1},{8,10},{9,11},{10,... | collective-permute-start | bytes 196616 | tf_op jit(solution)/shard_map/ppermute | solution.py:355
  18.1 0.3 collective-permute-start.6
  18.5 2.8 %collective-permute-start.7 = (bf16[16,2048]{1,0:T(8,128)(2,1)S(1)}, bf16[16,2048]{1,0:T(8,128)(2,1)S(1)}, u32[]{:S(2)}, u32[]{:S(2)}) collective-permute-start(bf16[16,2048]{1,0:T(8,128)(2,1)S(1)} %get-tuple-element.47), channel_id=1, source_target_pairs={{0,6},{1,7},{2,0},{3,1},{4,2},{5,3},{6,4},{7,5},{8,14},{9,15},{10,... | collective-permute-start | bytes 196616 | tf_op jit(solution)/shard_map/ppermute | solution.py:355
  21.3 4.1 %collective-permute-start.16 = (bf16[16,2048]{1,0:T(8,128)(2,1)S(1)}, bf16[16,2048]{1,0:T(8,128)(2,1)S(1)}, u32[]{:S(2)}, u32[]{:S(2)}) collective-permute-start(bf16[16,2048]{1,0:T(8,128)(2,1)S(1)} %shard_map.115.refs_0_.refs_4_), channel_id=1, source_target_pairs={{0,2},{1,3},{2,4},{3,5},{4,6},{5,7},{6,0},{7,1},{8,10},{9,11},{10,... | collective-permute-start | bytes 196616 | tf_op jit(solution)/shard_map/ppermute | solution.py:355
  25.4 2.4 %collective-permute-start.14 = (bf16[16,2048]{1,0:T(8,128)(2,1)S(1)}, bf16[16,2048]{1,0:T(8,128)(2,1)S(1)}, u32[]{:S(2)}, u32[]{:S(2)}) collective-permute-start(bf16[16,2048]{1,0:T(8,128)(2,1)S(1)} %shard_map.115.refs_0_.refs_4_), channel_id=1, source_target_pairs={{0,6},{1,7},{2,0},{3,1},{4,2},{5,3},{6,4},{7,5},{8,14},{9,15},{10,... | collective-permute-start | bytes 196616 | tf_op jit(solution)/shard_map/ppermute | solution.py:355
  27.9 3.1 %collective-permute-start.10 = (bf16[16,2048]{1,0:T(8,128)(2,1)S(1)}, bf16[16,2048]{1,0:T(8,128)(2,1)S(1)}, u32[]{:S(2)}, u32[]{:S(2)}) collective-permute-start(bf16[16,2048]{1,0:T(8,128)(2,1)S(1)} %shard_map.113.refs_0_.refs_9_), channel_id=1, source_target_pairs={{0,2},{1,3},{2,4},{3,5},{4,6},{5,7},{6,0},{7,1},{8,10},{9,11},{10,... | collective-permute-start | bytes 196616 | tf_op jit(solution)/shard_map/ppermute | solution.py:355
  31.0 0.0 collective-permute-start.9
  31.1 2.4 %collective-permute-start.8 = (bf16[16,2048]{1,0:T(8,128)(2,1)S(1)}, bf16[16,2048]{1,0:T(8,128)(2,1)S(1)}, u32[]{:S(2)}, u32[]{:S(2)}) collective-permute-start(bf16[16,2048]{1,0:T(8,128)(2,1)S(1)} %shard_map.113.refs_0_.refs_9_), channel_id=1, source_target_pairs={{0,6},{1,7},{2,0},{3,1},{4,2},{5,3},{6,4},{7,5},{8,14},{9,15},{10,... | collective-permute-start | bytes 196616 | tf_op jit(solution)/shard_map/ppermute | solution.py:355
  33.5 0.1 collective-permute-start.18
  33.6 1.7 %shard_map.117 = (bf16[288,4096]{1,0:T(8,128)(2,1)S(1)}, f32[8,128]{1,0:T(8,128)S(1)}) custom-call(bf16[288,4096]{1,0:T(8,128)(2,1)} %bitcast.13, bf16[64,2048]{1,0:T(8,128)(2,1)S(1)} %shard_map.116._.own_ref), custom_call_target="tpu_custom_call" | custom-call | tf_op jit(solution)/shard_map/pallas_call | solution.py:331
  35.3 2.1 %collective-permute-done.9.refs_2_ = bf16[16,2048]{1,0:T(8,128)(2,1)S(1)} collective-permute-done((bf16[16,2048]{1,0:T(8,128)(2,1)S(1)}, bf16[16,2048]{1,0:T(8,128)(2,1)S(1)}, u32[]{:S(2)}, u32[]{:S(2)}) %collective-permute-start.9) | collective-permute-done | bytes 65568 | tf_op jit(solution)/shard_map/ppermute | solution.py:355
  37.4 0.1 collective-permute-start.17
  37.5 0.8 %shard_map.119.before_ref = f32[592,128]{1,0:T(8,128)S(1)} custom-call(bf16[592,4096]{1,0:T(8,128)(2,1)S(1)} %get-tuple-element.36.in_ref, bf16[64,2048]{1,0:T(8,128)(2,1)S(1)} %shard_map.116._.own_ref, bf16[64,2048]{1,0:T(8,128)(2,1)S(1)} %collective-permute-done.18.other_ref), custom_call_target="tpu_custom_call" | custom-call | tf_op jit(solution)/shard_map/pallas_call | solution.py:331
  38.3 0.7 %collective-permute-done.17.other_ref = bf16[64,2048]{1,0:T(8,128)(2,1)S(1)} collective-permute-done((bf16[64,2048]{1,0:T(8,128)(2,1)S(1)}, bf16[64,2048]{1,0:T(8,128)(2,1)S(1)}, u32[]{:S(2)}, u32[]{:S(2)}) %collective-permute-start.17) | collective-permute-done | bytes 262176 | tf_op jit(solution)/shard_map/ppermute | solution.py:358
  39.0 0.9 %shard_map.120.x_ref = bf16[128,288]{1,0:T(8,128)(2,1)S(1)} custom-call(bf16[592,4096]{1,0:T(8,128)(2,1)S(1)} %get-tuple-element.36.in_ref, bf16[64,2048]{1,0:T(8,128)(2,1)S(1)} %shard_map.118.own_ref, bf16[64,2048]{1,0:T(8,128)(2,1)S(1)} %collective-permute-done.17.other_ref, f32[592,128]{1,0:T(8,128)S(1)} %shard_map.119.before_ref, ...), custom_call_target="tpu_custom_call" | custom-call | tf_op jit(solution)/shard_map/pallas_call | solution.py:331
  39.9 0.4 shard_map.123
  40.4 0.2 collective-permute-start.23
  40.6 0.4 shard_map.121
  41.0 0.4 collective-permute-start.19
  41.5 0.5 collective-permute-done.23.b_ref
  42.0 0.1 shard_map.124
  42.1 1.9 %collective-permute-start.24 = (bf16[16,2048]{1,0:T(8,128)(2,1)S(1)}, bf16[16,2048]{1,0:T(8,128)(2,1)S(1)}, u32[]{:S(2)}, u32[]{:S(2)}) collective-permute-start(bf16[16,2048]{1,0:T(8,128)(2,1)S(1)} %get-tuple-element.64), channel_id=1, source_target_pairs={{0,2},{1,3},{2,4},{3,5},{4,6},{5,7},{6,0},{7,1},{8,10},{9,11},{10,... | collective-permute-start | bytes 196616 | tf_op jit(solution)/shard_map/ppermute | solution.py:355
  44.0 1.7 %collective-permute-start.25 = (bf16[16,2048]{1,0:T(8,128)(2,1)S(1)}, bf16[16,2048]{1,0:T(8,128)(2,1)S(1)}, u32[]{:S(2)}, u32[]{:S(2)}) collective-permute-start(bf16[16,2048]{1,0:T(8,128)(2,1)S(1)} %get-tuple-element.65), channel_id=1, source_target_pairs={{0,4},{1,5},{2,6},{3,7},{4,0},{5,1},{6,2},{7,3},{8,12},{9,13},{10,... | collective-permute-start | bytes 196616 | tf_op jit(solution)/shard_map/ppermute | solution.py:355
  45.7 0.7 %collective-permute-start.26 = (bf16[16,2048]{1,0:T(8,128)(2,1)S(1)}, bf16[16,2048]{1,0:T(8,128)(2,1)S(1)}, u32[]{:S(2)}, u32[]{:S(2)}) collective-permute-start(bf16[16,2048]{1,0:T(8,128)(2,1)S(1)} %get-tuple-element.66), channel_id=1, source_target_pairs={{0,6},{1,7},{2,0},{3,1},{4,2},{5,3},{6,4},{7,5},{8,14},{9,15},{10,... | collective-permute-start | bytes 196616 | tf_op jit(solution)/shard_map/ppermute | solution.py:355
  46.4 0.1 shard_map.122
  46.5 1.4 %collective-permute-start.20 = (bf16[16,2048]{1,0:T(8,128)(2,1)S(1)}, bf16[16,2048]{1,0:T(8,128)(2,1)S(1)}, u32[]{:S(2)}, u32[]{:S(2)}) collective-permute-start(bf16[16,2048]{1,0:T(8,128)(2,1)S(1)} %get-tuple-element.58), channel_id=1, source_target_pairs={{0,2},{1,3},{2,4},{3,5},{4,6},{5,7},{6,0},{7,1},{8,10},{9,11},{10,... | collective-permute-start | bytes 196616 | tf_op jit(solution)/shard_map/ppermute | solution.py:355
  47.9 1.2 %collective-permute-start.21 = (bf16[16,2048]{1,0:T(8,128)(2,1)S(1)}, bf16[16,2048]{1,0:T(8,128)(2,1)S(1)}, u32[]{:S(2)}, u32[]{:S(2)}) collective-permute-start(bf16[16,2048]{1,0:T(8,128)(2,1)S(1)} %get-tuple-element.59), channel_id=1, source_target_pairs={{0,4},{1,5},{2,6},{3,7},{4,0},{5,1},{6,2},{7,3},{8,12},{9,13},{10,... | collective-permute-start | bytes 196616 | tf_op jit(solution)/shard_map/ppermute | solution.py:355
  49.1 1.9 %collective-permute-start.22 = (bf16[16,2048]{1,0:T(8,128)(2,1)S(1)}, bf16[16,2048]{1,0:T(8,128)(2,1)S(1)}, u32[]{:S(2)}, u32[]{:S(2)}) collective-permute-start(bf16[16,2048]{1,0:T(8,128)(2,1)S(1)} %get-tuple-element.60), channel_id=1, source_target_pairs={{0,6},{1,7},{2,0},{3,1},{4,2},{5,3},{6,4},{7,5},{8,14},{9,15},{10,... | collective-permute-start | bytes 196616 | tf_op jit(solution)/shard_map/ppermute | solution.py:355
  51.0 1.7 %collective-permute-done.25.refs_7_ = bf16[16,2048]{1,0:T(8,128)(2,1)S(1)} collective-permute-done((bf16[16,2048]{1,0:T(8,128)(2,1)S(1)}, bf16[16,2048]{1,0:T(8,128)(2,1)S(1)}, u32[]{:S(2)}, u32[]{:S(2)}) %collective-permute-start.25) | collective-permute-done | bytes 65568 | tf_op jit(solution)/shard_map/ppermute | solution.py:355
  52.7 0.6 %collective-permute-done.20.refs_1_ = bf16[16,2048]{1,0:T(8,128)(2,1)S(1)} collective-permute-done((bf16[16,2048]{1,0:T(8,128)(2,1)S(1)}, bf16[16,2048]{1,0:T(8,128)(2,1)S(1)}, u32[]{:S(2)}, u32[]{:S(2)}) %collective-permute-start.20) | collective-permute-done | bytes 65568 | tf_op jit(solution)/shard_map/ppermute | solution.py:355
  53.4 3.2 %collective-permute-done.21.refs_2_ = bf16[16,2048]{1,0:T(8,128)(2,1)S(1)} collective-permute-done((bf16[16,2048]{1,0:T(8,128)(2,1)S(1)}, bf16[16,2048]{1,0:T(8,128)(2,1)S(1)}, u32[]{:S(2)}, u32[]{:S(2)}) %collective-permute-start.21) | collective-permute-done | bytes 65568 | tf_op jit(solution)/shard_map/ppermute | solution.py:355
  56.6 0.7 %shard_map.125 = bf16[16,4096]{1,0:T(8,128)(2,1)} custom-call(bf16[16,2048]{1,0:T(8,128)(2,1)S(1)} %get-tuple-element.57.refs_0_, bf16[16,2048]{1,0:T(8,128)(2,1)S(1)} %collective-permute-done.20.refs_1_, bf16[16,2048]{1,0:T(8,128)(2,1)S(1)} %collective-permute-done.21.refs_2_, bf16[16,2048]{1,0:T(8,128)(2,1)S(1)} %collective-permute-done.22.refs_3_, ...), custom_call_target="tpu_custom_call" | custom-call | tf_op jit(solution)/shard_map/pallas_call | solution.py:331
  (23 shorter events, 0.2 us)
Async XLA Ops:
  0.0 11.2 %collective-permute-start.4 = (bf16[128,4096]{1,0:T(8,128)(2,1)}, bf16[128,4096]{1,0:T(8,128)(2,1)S(1)}, u32[]{:S(2)}, u32[]{:S(2)}) collective-permute-start(bf16[128,4096]{1,0:T(8,128)(2,1)} %w_out_hbm.1), channel_id=1, source_target_pairs={{0,1},{1,0},{2,3},{3,2},{4,5},{5,4},{6,7},{7,6},{8,9},{9,8},{10,11... | collective-permute-start | bytes 3145736 | tf_op jit(solution)/shard_map/ppermute | solution.py:358
  1.6 7.1 %collective-permute-start.2 = (bf16[144,128]{1,0:T(8,128)(2,1)S(1)}, bf16[144,128]{1,0:T(8,128)(2,1)S(1)}, u32[]{:S(2)}, u32[]{:S(2)}) collective-permute-start(bf16[144,128]{1,0:T(8,128)(2,1)S(1)} %shard_map.109._), channel_id=1, source_target_pairs={{24,0},{16,8},{8,16},{0,24},{25,1},{17,9},{9,17},{1,25},{26,2},{18... | collective-permute-start | bytes 110600 | tf_op jit(solution)/shard_map/ppermute | solution.py:381
  5.1 4.0 %collective-permute-start.1 = (bf16[144,128]{1,0:T(8,128)(2,1)S(1)}, bf16[144,128]{1,0:T(8,128)(2,1)S(1)}, u32[]{:S(2)}, u32[]{:S(2)}) collective-permute-start(bf16[144,128]{1,0:T(8,128)(2,1)S(1)} %shard_map.109._), channel_id=1, source_target_pairs={{8,0},{0,8},{24,16},{16,24},{9,1},{1,9},{25,17},{17,25},{10,2},{2,... | collective-permute-start | bytes 110600 | tf_op jit(solution)/shard_map/ppermute | solution.py:381
  5.6 4.0 %collective-permute-start = (bf16[144,128]{1,0:T(8,128)(2,1)S(1)}, bf16[144,128]{1,0:T(8,128)(2,1)S(1)}, u32[]{:S(2)}, u32[]{:S(2)}) collective-permute-start(bf16[144,128]{1,0:T(8,128)(2,1)S(1)} %shard_map.109._), channel_id=1, source_target_pairs={{16,0},{24,8},{0,16},{8,24},{17,1},{25,9},{1,17},{9,25},{18,2},{26... | collective-permute-start | bytes 110600 | tf_op jit(solution)/shard_map/ppermute | solution.py:381
  10.0 1.2 %collective-permute-start.3 = (bf16[64,128]{1,0:T(8,128)(2,1)S(1)}, bf16[64,128]{1,0:T(8,128)(2,1)S(1)}, u32[]{:S(2)}, u32[]{:S(2)}) collective-permute-start(bf16[64,128]{1,0:T(8,128)(2,1)S(1)} %get-tuple-element.42), channel_id=1, source_target_pairs={{0,1},{1,0},{2,3},{3,2},{4,5},{5,4},{6,7},{7,6},{8,9},{9,8},{10,11... | collective-permute-start | bytes 49160 | tf_op jit(solution)/shard_map/ppermute | solution.py:358
  11.5 6.9 %collective-permute-start.11 = (bf16[16,2048]{1,0:T(8,128)(2,1)S(1)}, bf16[16,2048]{1,0:T(8,128)(2,1)S(1)}, u32[]{:S(2)}, u32[]{:S(2)}) collective-permute-start(bf16[16,2048]{1,0:T(8,128)(2,1)S(1)} %get-tuple-element.49), channel_id=1, source_target_pairs={{0,2},{1,3},{2,4},{3,5},{4,6},{5,7},{6,0},{7,1},{8,10},{9,11},{10,... | collective-permute-start | bytes 196616 | tf_op jit(solution)/shard_map/ppermute | solution.py:355
  13.2 8.1 %collective-permute-start.12 = (bf16[16,2048]{1,0:T(8,128)(2,1)S(1)}, bf16[16,2048]{1,0:T(8,128)(2,1)S(1)}, u32[]{:S(2)}, u32[]{:S(2)}) collective-permute-start(bf16[16,2048]{1,0:T(8,128)(2,1)S(1)} %get-tuple-element.50), channel_id=1, source_target_pairs={{0,4},{1,5},{2,6},{3,7},{4,0},{5,1},{6,2},{7,3},{8,12},{9,13},{10,... | collective-permute-start | bytes 196616 | tf_op jit(solution)/shard_map/ppermute | solution.py:355
  15.8 5.5 %collective-permute-start.13 = (bf16[16,2048]{1,0:T(8,128)(2,1)S(1)}, bf16[16,2048]{1,0:T(8,128)(2,1)S(1)}, u32[]{:S(2)}, u32[]{:S(2)}) collective-permute-start(bf16[16,2048]{1,0:T(8,128)(2,1)S(1)} %get-tuple-element.51), channel_id=1, source_target_pairs={{0,6},{1,7},{2,0},{3,1},{4,2},{5,3},{6,4},{7,5},{8,14},{9,15},{10,... | collective-permute-start | bytes 196616 | tf_op jit(solution)/shard_map/ppermute | solution.py:355
  17.4 8.0 %collective-permute-start.5 = (bf16[16,2048]{1,0:T(8,128)(2,1)S(1)}, bf16[16,2048]{1,0:T(8,128)(2,1)S(1)}, u32[]{:S(2)}, u32[]{:S(2)}) collective-permute-start(bf16[16,2048]{1,0:T(8,128)(2,1)S(1)} %get-tuple-element.45), channel_id=1, source_target_pairs={{0,2},{1,3},{2,4},{3,5},{4,6},{5,7},{6,0},{7,1},{8,10},{9,11},{10,... | collective-permute-start | bytes 196616 | tf_op jit(solution)/shard_map/ppermute | solution.py:355
  18.1 9.7 %collective-permute-start.6 = (bf16[16,2048]{1,0:T(8,128)(2,1)S(1)}, bf16[16,2048]{1,0:T(8,128)(2,1)S(1)}, u32[]{:S(2)}, u32[]{:S(2)}) collective-permute-start(bf16[16,2048]{1,0:T(8,128)(2,1)S(1)} %get-tuple-element.46), channel_id=1, source_target_pairs={{0,4},{1,5},{2,6},{3,7},{4,0},{5,1},{6,2},{7,3},{8,12},{9,13},{10,... | collective-permute-start | bytes 196616 | tf_op jit(solution)/shard_map/ppermute | solution.py:355
  18.5 9.4 %collective-permute-start.7 = (bf16[16,2048]{1,0:T(8,128)(2,1)S(1)}, bf16[16,2048]{1,0:T(8,128)(2,1)S(1)}, u32[]{:S(2)}, u32[]{:S(2)}) collective-permute-start(bf16[16,2048]{1,0:T(8,128)(2,1)S(1)} %get-tuple-element.47), channel_id=1, source_target_pairs={{0,6},{1,7},{2,0},{3,1},{4,2},{5,3},{6,4},{7,5},{8,14},{9,15},{10,... | collective-permute-start | bytes 196616 | tf_op jit(solution)/shard_map/ppermute | solution.py:355
  21.3 9.7 %collective-permute-start.16 = (bf16[16,2048]{1,0:T(8,128)(2,1)S(1)}, bf16[16,2048]{1,0:T(8,128)(2,1)S(1)}, u32[]{:S(2)}, u32[]{:S(2)}) collective-permute-start(bf16[16,2048]{1,0:T(8,128)(2,1)S(1)} %shard_map.115.refs_0_.refs_4_), channel_id=1, source_target_pairs={{0,2},{1,3},{2,4},{3,5},{4,6},{5,7},{6,0},{7,1},{8,10},{9,11},{10,... | collective-permute-start | bytes 196616 | tf_op jit(solution)/shard_map/ppermute | solution.py:355
  25.4 8.1 %collective-permute-start.15 = (bf16[16,2048]{1,0:T(8,128)(2,1)S(1)}, bf16[16,2048]{1,0:T(8,128)(2,1)S(1)}, u32[]{:S(2)}, u32[]{:S(2)}) collective-permute-start(bf16[16,2048]{1,0:T(8,128)(2,1)S(1)} %shard_map.115.refs_0_.refs_4_), channel_id=1, source_target_pairs={{0,4},{1,5},{2,6},{3,7},{4,0},{5,1},{6,2},{7,3},{8,12},{9,13},{10,... | collective-permute-start | bytes 196616 | tf_op jit(solution)/shard_map/ppermute | solution.py:355
  25.4 8.1 %collective-permute-start.14 = (bf16[16,2048]{1,0:T(8,128)(2,1)S(1)}, bf16[16,2048]{1,0:T(8,128)(2,1)S(1)}, u32[]{:S(2)}, u32[]{:S(2)}) collective-permute-start(bf16[16,2048]{1,0:T(8,128)(2,1)S(1)} %shard_map.115.refs_0_.refs_4_), channel_id=1, source_target_pairs={{0,6},{1,7},{2,0},{3,1},{4,2},{5,3},{6,4},{7,5},{8,14},{9,15},{10,... | collective-permute-start | bytes 196616 | tf_op jit(solution)/shard_map/ppermute | solution.py:355
  27.9 7.4 %collective-permute-start.10 = (bf16[16,2048]{1,0:T(8,128)(2,1)S(1)}, bf16[16,2048]{1,0:T(8,128)(2,1)S(1)}, u32[]{:S(2)}, u32[]{:S(2)}) collective-permute-start(bf16[16,2048]{1,0:T(8,128)(2,1)S(1)} %shard_map.113.refs_0_.refs_9_), channel_id=1, source_target_pairs={{0,2},{1,3},{2,4},{3,5},{4,6},{5,7},{6,0},{7,1},{8,10},{9,11},{10,... | collective-permute-start | bytes 196616 | tf_op jit(solution)/shard_map/ppermute | solution.py:355
  31.0 6.4 %collective-permute-start.9 = (bf16[16,2048]{1,0:T(8,128)(2,1)S(1)}, bf16[16,2048]{1,0:T(8,128)(2,1)S(1)}, u32[]{:S(2)}, u32[]{:S(2)}) collective-permute-start(bf16[16,2048]{1,0:T(8,128)(2,1)S(1)} %shard_map.113.refs_0_.refs_9_), channel_id=1, source_target_pairs={{0,4},{1,5},{2,6},{3,7},{4,0},{5,1},{6,2},{7,3},{8,12},{9,13},{10,... | collective-permute-start | bytes 196616 | tf_op jit(solution)/shard_map/ppermute | solution.py:355
  31.1 6.3 %collective-permute-start.8 = (bf16[16,2048]{1,0:T(8,128)(2,1)S(1)}, bf16[16,2048]{1,0:T(8,128)(2,1)S(1)}, u32[]{:S(2)}, u32[]{:S(2)}) collective-permute-start(bf16[16,2048]{1,0:T(8,128)(2,1)S(1)} %shard_map.113.refs_0_.refs_9_), channel_id=1, source_target_pairs={{0,6},{1,7},{2,0},{3,1},{4,2},{5,3},{6,4},{7,5},{8,14},{9,15},{10,... | collective-permute-start | bytes 196616 | tf_op jit(solution)/shard_map/ppermute | solution.py:355
  33.5 4.0 %collective-permute-start.18 = (bf16[64,2048]{1,0:T(8,128)(2,1)S(1)}, bf16[64,2048]{1,0:T(8,128)(2,1)S(1)}, u32[]{:S(2)}, u32[]{:S(2)}) collective-permute-start(bf16[64,2048]{1,0:T(8,128)(2,1)S(1)} %shard_map.116._.own_ref), channel_id=1, source_target_pairs={{0,1},{1,0},{2,3},{3,2},{4,5},{5,4},{6,7},{7,6},{8,9},{9,8},{10,11... | collective-permute-start | bytes 786440 | tf_op jit(solution)/shard_map/ppermute | solution.py:358
  37.4 1.6 %collective-permute-start.17 = (bf16[64,2048]{1,0:T(8,128)(2,1)S(1)}, bf16[64,2048]{1,0:T(8,128)(2,1)S(1)}, u32[]{:S(2)}, u32[]{:S(2)}) collective-permute-start(bf16[64,2048]{1,0:T(8,128)(2,1)S(1)} %shard_map.118.own_ref), channel_id=1, source_target_pairs={{0,1},{1,0},{2,3},{3,2},{4,5},{5,4},{6,7},{7,6},{8,9},{9,8},{10,11... | collective-permute-start | bytes 786440 | tf_op jit(solution)/shard_map/ppermute | solution.py:358
  40.4 1.6 %collective-permute-start.23 = (bf16[64,2048]{1,0:T(8,128)(2,1)S(1)}, bf16[64,2048]{1,0:T(8,128)(2,1)S(1)}, u32[]{:S(2)}, u32[]{:S(2)}) collective-permute-start(bf16[64,2048]{1,0:T(8,128)(2,1)S(1)} %get-tuple-element.62), channel_id=1, source_target_pairs={{0,1},{1,0},{2,3},{3,2},{4,5},{5,4},{6,7},{7,6},{8,9},{9,8},{10,11... | collective-permute-start | bytes 786440 | tf_op jit(solution)/shard_map/ppermute | solution.py:358
  41.0 5.4 %collective-permute-start.19 = (bf16[64,2048]{1,0:T(8,128)(2,1)S(1)}, bf16[64,2048]{1,0:T(8,128)(2,1)S(1)}, u32[]{:S(2)}, u32[]{:S(2)}) collective-permute-start(bf16[64,2048]{1,0:T(8,128)(2,1)S(1)} %get-tuple-element.56), channel_id=1, source_target_pairs={{0,1},{1,0},{2,3},{3,2},{4,5},{5,4},{6,7},{7,6},{8,9},{9,8},{10,11... | collective-permute-start | bytes 786440 | tf_op jit(solution)/shard_map/ppermute | solution.py:358
  42.1 7.0 %collective-permute-start.24 = (bf16[16,2048]{1,0:T(8,128)(2,1)S(1)}, bf16[16,2048]{1,0:T(8,128)(2,1)S(1)}, u32[]{:S(2)}, u32[]{:S(2)}) collective-permute-start(bf16[16,2048]{1,0:T(8,128)(2,1)S(1)} %get-tuple-element.64), channel_id=1, source_target_pairs={{0,2},{1,3},{2,4},{3,5},{4,6},{5,7},{6,0},{7,1},{8,10},{9,11},{10,... | collective-permute-start | bytes 196616 | tf_op jit(solution)/shard_map/ppermute | solution.py:355
  44.0 8.8 %collective-permute-start.25 = (bf16[16,2048]{1,0:T(8,128)(2,1)S(1)}, bf16[16,2048]{1,0:T(8,128)(2,1)S(1)}, u32[]{:S(2)}, u32[]{:S(2)}) collective-permute-start(bf16[16,2048]{1,0:T(8,128)(2,1)S(1)} %get-tuple-element.65), channel_id=1, source_target_pairs={{0,4},{1,5},{2,6},{3,7},{4,0},{5,1},{6,2},{7,3},{8,12},{9,13},{10,... | collective-permute-start | bytes 196616 | tf_op jit(solution)/shard_map/ppermute | solution.py:355
  45.7 7.0 %collective-permute-start.26 = (bf16[16,2048]{1,0:T(8,128)(2,1)S(1)}, bf16[16,2048]{1,0:T(8,128)(2,1)S(1)}, u32[]{:S(2)}, u32[]{:S(2)}) collective-permute-start(bf16[16,2048]{1,0:T(8,128)(2,1)S(1)} %get-tuple-element.66), channel_id=1, source_target_pairs={{0,6},{1,7},{2,0},{3,1},{4,2},{5,3},{6,4},{7,5},{8,14},{9,15},{10,... | collective-permute-start | bytes 196616 | tf_op jit(solution)/shard_map/ppermute | solution.py:355
  46.5 6.9 %collective-permute-start.20 = (bf16[16,2048]{1,0:T(8,128)(2,1)S(1)}, bf16[16,2048]{1,0:T(8,128)(2,1)S(1)}, u32[]{:S(2)}, u32[]{:S(2)}) collective-permute-start(bf16[16,2048]{1,0:T(8,128)(2,1)S(1)} %get-tuple-element.58), channel_id=1, source_target_pairs={{0,2},{1,3},{2,4},{3,5},{4,6},{5,7},{6,0},{7,1},{8,10},{9,11},{10,... | collective-permute-start | bytes 196616 | tf_op jit(solution)/shard_map/ppermute | solution.py:355
  47.9 8.7 %collective-permute-start.21 = (bf16[16,2048]{1,0:T(8,128)(2,1)S(1)}, bf16[16,2048]{1,0:T(8,128)(2,1)S(1)}, u32[]{:S(2)}, u32[]{:S(2)}) collective-permute-start(bf16[16,2048]{1,0:T(8,128)(2,1)S(1)} %get-tuple-element.59), channel_id=1, source_target_pairs={{0,4},{1,5},{2,6},{3,7},{4,0},{5,1},{6,2},{7,3},{8,12},{9,13},{10,... | collective-permute-start | bytes 196616 | tf_op jit(solution)/shard_map/ppermute | solution.py:355
  49.1 7.5 %collective-permute-start.22 = (bf16[16,2048]{1,0:T(8,128)(2,1)S(1)}, bf16[16,2048]{1,0:T(8,128)(2,1)S(1)}, u32[]{:S(2)}, u32[]{:S(2)}) collective-permute-start(bf16[16,2048]{1,0:T(8,128)(2,1)S(1)} %get-tuple-element.60), channel_id=1, source_target_pairs={{0,6},{1,7},{2,0},{3,1},{4,2},{5,3},{6,4},{7,5},{8,14},{9,15},{10,... | collective-permute-start | bytes 196616 | tf_op jit(solution)/shard_map/ppermute | solution.py:355

commit v8 on v6

--- a/solution.py
+++ b/solution.py
@@ -364,7 +364,8 @@
         return out((count * rows, size), BF16)
 
     def send(terms):
-        return [[term[0]] + [shift(term[r], r) for r in range(1, n_pair)] for term in terms]
+        ways = [list(range(1, n_pair)), list(range(n_pair - 1, 0, -1))]
+        return [[term[0]] + [shift(term[r], r) for r in ways[i % 2]] for i, term in enumerate(terms)]
 
     decay_row = decay_log.T
     block = pltpu.VMEM((t, d), BF16)

time: 57.5 us -> 58.3 us (1.014)
  waiting for transfers between devices: 11 us -> 16.1 us
  starting transfers between devices: 35.8 us -> 31.6 us
    ppermute x18, waiting for transfers between devices: 7.71 us -> 12.8 us  [shift(): lax.ppermute(x, 'exp', [(e, (e + 2 * r) % exp_count) for e in range(exp_c...]
    ppermute x18, starting transfers between devices: 30.4 us -> 26.1 us  [shift(): lax.ppermute(x, 'exp', [(e, (e + 2 * r) % exp_count) for e in range(exp_c...]
  transfers between devices with their start and end apart: 27 -> 27, of which waited for: 9 -> 12; matrix products, arithmetic and copies ran while one was open for 0% -> 0% of each run, Pallas kernels for 14% -> 14%
where the time goes in v8:
time: 58.3 us; the launch traced here: 58.1 us
  starting transfers between devices  31.6 us (54%)
  waiting for transfers between devices  16.1 us (28%)
  Pallas kernels  10.3 us (18%)
    ppermute x18, starting transfers between devices, shift(): lax.ppermute(x, 'exp', [(e, (e + 2 * r) % exp_count) for e in range(exp_c...  26.1 us
    ppermute x18, waiting for transfers between devices, shift(): lax.ppermute(x, 'exp', [(e, (e + 2 * r) % exp_count) for e in range(exp_c...  12.8 us
    pallas_call x17, Pallas kernels, call(): pl.pallas_call(kernel, out_shape=outs, in_specs=[pl.BlockSpec(memory_spac...  10.3 us
    ppermute x3, starting transfers between devices, local(): lax.ppermute(state, 'seq', [(move(i), i) for i in range(seq_count)])  4.15 us
    ppermute x6, waiting for transfers between devices, across(): return lax.ppermute(x, 'exp', [(e, e ^ 1) for e in range(exp_count)])  2.4 us
    ppermute x6, starting transfers between devices, across(): return lax.ppermute(x, 'exp', [(e, e ^ 1) for e in range(exp_count)])  1.31 us
  transfers between devices with their start and end apart: 27, of which 12 were waited for; matrix products, arithmetic and copies ran while one was open for 0% of the time, Pallas kernels for 14%

profile of v8, /device:TPU:0, one launch (start us, length us, event | category | flops | bytes accessed | tf_op | source)
XLA Modules:
  0.0 58.1 jit_solution(10377208447041270499)
XLA Ops:
  0.0 0.5 collective-permute-start.4
  0.5 1.1 %shard_map.109._ = bf16[144,128]{1,0:T(8,128)(2,1)S(1)} custom-call(bf16[128,128]{1,0:T(8,128)(2,1)} %key_hbm.3, bf16[128,128]{1,0:T(8,128)(2,1)} %value_hbm.3, f32[1,128]{1,0:T(1,128)} %bitcast.15), custom_call_target="tpu_custom_call" | custom-call | tf_op jit(solution)/shard_map/pallas_call | solution.py:331
  1.6 3.5 %collective-permute-start.2 = (bf16[144,128]{1,0:T(8,128)(2,1)S(1)}, bf16[144,128]{1,0:T(8,128)(2,1)S(1)}, u32[]{:S(2)}, u32[]{:S(2)}) collective-permute-start(bf16[144,128]{1,0:T(8,128)(2,1)S(1)} %shard_map.109._), channel_id=1, source_target_pairs={{24,0},{16,8},{8,16},{0,24},{25,1},{17,9},{9,17},{1,25},{26,2},{18... | collective-permute-start | bytes 110600 | tf_op jit(solution)/shard_map/ppermute | solution.py:381
  5.1 0.5 collective-permute-start.1
  5.6 0.1 collective-permute-start
  5.7 2.9 %shard_map.110 = (f32[128,128]{1,0:T(8,128)S(1)}, f32[128,128]{1,0:T(8,128)S(1)}, bf16[128,128]{1,0:T(8,128)(2,1)S(1)}, f32[8,128]{1,0:T(8,128)S(1)}, bf16[128,4...) custom-call(bf16[128,128]{1,0:T(8,128)(2,1)} %query_hbm.1, bf16[128,128]{1,0:T(8,128)(2,1)} %key_hbm.3, ...), custom_call_target="tpu_custom_call" | custom-call | tf_op jit(solution)/shard_map/pallas_call | solution.py:331
  8.6 0.4 collective-permute-done.1.refs_1_
  9.0 0.5 collective-permute-done.refs_0_
  9.5 0.4 shard_map.111
  10.0 0.1 collective-permute-start.3
  10.0 1.2 %collective-permute-done.3.b_ref = bf16[64,128]{1,0:T(8,128)(2,1)S(1)} collective-permute-done((bf16[64,128]{1,0:T(8,128)(2,1)S(1)}, bf16[64,128]{1,0:T(8,128)(2,1)S(1)}, u32[]{:S(2)}, u32[]{:S(2)}) %collective-permute-start.3) | collective-permute-done | bytes 16416 | tf_op jit(solution)/shard_map/ppermute | solution.py:358
  11.2 0.3 shard_map.114
  11.5 1.6 %collective-permute-start.11 = (bf16[16,2048]{1,0:T(8,128)(2,1)S(1)}, bf16[16,2048]{1,0:T(8,128)(2,1)S(1)}, u32[]{:S(2)}, u32[]{:S(2)}) collective-permute-start(bf16[16,2048]{1,0:T(8,128)(2,1)S(1)} %get-tuple-element.49), channel_id=1, source_target_pairs={{0,2},{1,3},{2,4},{3,5},{4,6},{5,7},{6,0},{7,1},{8,10},{9,11},{10,... | collective-permute-start | bytes 196616 | tf_op jit(solution)/shard_map/ppermute | solution.py:355
  13.1 2.6 %collective-permute-start.12 = (bf16[16,2048]{1,0:T(8,128)(2,1)S(1)}, bf16[16,2048]{1,0:T(8,128)(2,1)S(1)}, u32[]{:S(2)}, u32[]{:S(2)}) collective-permute-start(bf16[16,2048]{1,0:T(8,128)(2,1)S(1)} %get-tuple-element.50), channel_id=1, source_target_pairs={{0,4},{1,5},{2,6},{3,7},{4,0},{5,1},{6,2},{7,3},{8,12},{9,13},{10,... | collective-permute-start | bytes 196616 | tf_op jit(solution)/shard_map/ppermute | solution.py:355
  15.7 1.3 %collective-permute-start.13 = (bf16[16,2048]{1,0:T(8,128)(2,1)S(1)}, bf16[16,2048]{1,0:T(8,128)(2,1)S(1)}, u32[]{:S(2)}, u32[]{:S(2)}) collective-permute-start(bf16[16,2048]{1,0:T(8,128)(2,1)S(1)} %get-tuple-element.51), channel_id=1, source_target_pairs={{0,6},{1,7},{2,0},{3,1},{4,2},{5,3},{6,4},{7,5},{8,14},{9,15},{10,... | collective-permute-start | bytes 196616 | tf_op jit(solution)/shard_map/ppermute | solution.py:355
  17.1 0.3 shard_map.112
  17.4 0.5 collective-permute-start.5
  17.9 1.7 %collective-permute-start.6 = (bf16[16,2048]{1,0:T(8,128)(2,1)S(1)}, bf16[16,2048]{1,0:T(8,128)(2,1)S(1)}, u32[]{:S(2)}, u32[]{:S(2)}) collective-permute-start(bf16[16,2048]{1,0:T(8,128)(2,1)S(1)} %get-tuple-element.46), channel_id=1, source_target_pairs={{0,4},{1,5},{2,6},{3,7},{4,0},{5,1},{6,2},{7,3},{8,12},{9,13},{10,... | collective-permute-start | bytes 196616 | tf_op jit(solution)/shard_map/ppermute | solution.py:355
  19.6 0.2 collective-permute-start.7
  19.8 0.7 %collective-permute-done.12.refs_2_ = bf16[16,2048]{1,0:T(8,128)(2,1)S(1)} collective-permute-done((bf16[16,2048]{1,0:T(8,128)(2,1)S(1)}, bf16[16,2048]{1,0:T(8,128)(2,1)S(1)}, u32[]{:S(2)}, u32[]{:S(2)}) %collective-permute-start.12) | collective-permute-done | bytes 65568 | tf_op jit(solution)/shard_map/ppermute | solution.py:355
  20.5 0.9 %collective-permute-done.13.refs_3_ = bf16[16,2048]{1,0:T(8,128)(2,1)S(1)} collective-permute-done((bf16[16,2048]{1,0:T(8,128)(2,1)S(1)}, bf16[16,2048]{1,0:T(8,128)(2,1)S(1)}, u32[]{:S(2)}, u32[]{:S(2)}) %collective-permute-start.13) | collective-permute-done | bytes 65568 | tf_op jit(solution)/shard_map/ppermute | solution.py:355
  21.4 1.9 %collective-permute-start.16 = (bf16[16,2048]{1,0:T(8,128)(2,1)S(1)}, bf16[16,2048]{1,0:T(8,128)(2,1)S(1)}, u32[]{:S(2)}, u32[]{:S(2)}) collective-permute-start(bf16[16,2048]{1,0:T(8,128)(2,1)S(1)} %shard_map.115.refs_0_.refs_4_), channel_id=1, source_target_pairs={{0,2},{1,3},{2,4},{3,5},{4,6},{5,7},{6,0},{7,1},{8,10},{9,11},{10,... | collective-permute-start | bytes 196616 | tf_op jit(solution)/shard_map/ppermute | solution.py:355
  23.3 3.9 %collective-permute-start.15 = (bf16[16,2048]{1,0:T(8,128)(2,1)S(1)}, bf16[16,2048]{1,0:T(8,128)(2,1)S(1)}, u32[]{:S(2)}, u32[]{:S(2)}) collective-permute-start(bf16[16,2048]{1,0:T(8,128)(2,1)S(1)} %shard_map.115.refs_0_.refs_4_), channel_id=1, source_target_pairs={{0,4},{1,5},{2,6},{3,7},{4,0},{5,1},{6,2},{7,3},{8,12},{9,13},{10,... | collective-permute-start | bytes 196616 | tf_op jit(solution)/shard_map/ppermute | solution.py:355
  27.2 3.1 %collective-permute-done.6.refs_2_ = bf16[16,2048]{1,0:T(8,128)(2,1)S(1)} collective-permute-done((bf16[16,2048]{1,0:T(8,128)(2,1)S(1)}, bf16[16,2048]{1,0:T(8,128)(2,1)S(1)}, u32[]{:S(2)}, u32[]{:S(2)}) %collective-permute-start.6) | collective-permute-done | bytes 65568 | tf_op jit(solution)/shard_map/ppermute | solution.py:355
  30.4 0.1 collective-permute-start.9
  30.5 3.7 %collective-permute-start.8 = (bf16[16,2048]{1,0:T(8,128)(2,1)S(1)}, bf16[16,2048]{1,0:T(8,128)(2,1)S(1)}, u32[]{:S(2)}, u32[]{:S(2)}) collective-permute-start(bf16[16,2048]{1,0:T(8,128)(2,1)S(1)} %shard_map.113.refs_0_.refs_9_), channel_id=1, source_target_pairs={{0,6},{1,7},{2,0},{3,1},{4,2},{5,3},{6,4},{7,5},{8,14},{9,15},{10,... | collective-permute-start | bytes 196616 | tf_op jit(solution)/shard_map/ppermute | solution.py:355
  34.3 0.1 collective-permute-start.18
  34.4 1.7 %shard_map.117 = (bf16[288,4096]{1,0:T(8,128)(2,1)S(1)}, f32[8,128]{1,0:T(8,128)S(1)}) custom-call(bf16[288,4096]{1,0:T(8,128)(2,1)} %bitcast.13, bf16[64,2048]{1,0:T(8,128)(2,1)S(1)} %shard_map.116._.own_ref), custom_call_target="tpu_custom_call" | custom-call | tf_op jit(solution)/shard_map/pallas_call | solution.py:331
  36.0 1.1 %collective-permute-done.10.refs_3_ = bf16[16,2048]{1,0:T(8,128)(2,1)S(1)} collective-permute-done((bf16[16,2048]{1,0:T(8,128)(2,1)S(1)}, bf16[16,2048]{1,0:T(8,128)(2,1)S(1)}, u32[]{:S(2)}, u32[]{:S(2)}) %collective-permute-start.10) | collective-permute-done | bytes 65568 | tf_op jit(solution)/shard_map/ppermute | solution.py:355
  37.2 1.7 %collective-permute-done.9.refs_2_ = bf16[16,2048]{1,0:T(8,128)(2,1)S(1)} collective-permute-done((bf16[16,2048]{1,0:T(8,128)(2,1)S(1)}, bf16[16,2048]{1,0:T(8,128)(2,1)S(1)}, u32[]{:S(2)}, u32[]{:S(2)}) %collective-permute-start.9) | collective-permute-done | bytes 65568 | tf_op jit(solution)/shard_map/ppermute | solution.py:355
  38.9 0.1 collective-permute-start.17
  39.0 0.8 %shard_map.119.before_ref = f32[592,128]{1,0:T(8,128)S(1)} custom-call(bf16[592,4096]{1,0:T(8,128)(2,1)S(1)} %get-tuple-element.36.in_ref, bf16[64,2048]{1,0:T(8,128)(2,1)S(1)} %shard_map.116._.own_ref, bf16[64,2048]{1,0:T(8,128)(2,1)S(1)} %collective-permute-done.18.other_ref), custom_call_target="tpu_custom_call" | custom-call | tf_op jit(solution)/shard_map/pallas_call | solution.py:331
  39.8 0.7 %collective-permute-done.17.other_ref = bf16[64,2048]{1,0:T(8,128)(2,1)S(1)} collective-permute-done((bf16[64,2048]{1,0:T(8,128)(2,1)S(1)}, bf16[64,2048]{1,0:T(8,128)(2,1)S(1)}, u32[]{:S(2)}, u32[]{:S(2)}) %collective-permute-start.17) | collective-permute-done | bytes 262176 | tf_op jit(solution)/shard_map/ppermute | solution.py:358
  40.5 0.9 %shard_map.120.x_ref = bf16[128,288]{1,0:T(8,128)(2,1)S(1)} custom-call(bf16[592,4096]{1,0:T(8,128)(2,1)S(1)} %get-tuple-element.36.in_ref, bf16[64,2048]{1,0:T(8,128)(2,1)S(1)} %shard_map.118.own_ref, bf16[64,2048]{1,0:T(8,128)(2,1)S(1)} %collective-permute-done.17.other_ref, f32[592,128]{1,0:T(8,128)S(1)} %shard_map.119.before_ref, ...), custom_call_target="tpu_custom_call" | custom-call | tf_op jit(solution)/shard_map/pallas_call | solution.py:331
  41.4 0.4 shard_map.123
  41.9 0.2 collective-permute-start.23
  42.0 0.4 shard_map.121
  42.5 0.5 collective-permute-start.19
  43.0 0.5 collective-permute-done.23.b_ref
  43.5 0.1 shard_map.124
  43.5 1.8 %collective-permute-start.24 = (bf16[16,2048]{1,0:T(8,128)(2,1)S(1)}, bf16[16,2048]{1,0:T(8,128)(2,1)S(1)}, u32[]{:S(2)}, u32[]{:S(2)}) collective-permute-start(bf16[16,2048]{1,0:T(8,128)(2,1)S(1)} %get-tuple-element.64), channel_id=1, source_target_pairs={{0,6},{1,7},{2,0},{3,1},{4,2},{5,3},{6,4},{7,5},{8,14},{9,15},{10,... | collective-permute-start | bytes 196616 | tf_op jit(solution)/shard_map/ppermute | solution.py:355
  45.4 1.0 %collective-permute-start.25 = (bf16[16,2048]{1,0:T(8,128)(2,1)S(1)}, bf16[16,2048]{1,0:T(8,128)(2,1)S(1)}, u32[]{:S(2)}, u32[]{:S(2)}) collective-permute-start(bf16[16,2048]{1,0:T(8,128)(2,1)S(1)} %get-tuple-element.65), channel_id=1, source_target_pairs={{0,4},{1,5},{2,6},{3,7},{4,0},{5,1},{6,2},{7,3},{8,12},{9,13},{10,... | collective-permute-start | bytes 196616 | tf_op jit(solution)/shard_map/ppermute | solution.py:355
  46.5 2.5 %collective-permute-start.20 = (bf16[16,2048]{1,0:T(8,128)(2,1)S(1)}, bf16[16,2048]{1,0:T(8,128)(2,1)S(1)}, u32[]{:S(2)}, u32[]{:S(2)}) collective-permute-start(bf16[16,2048]{1,0:T(8,128)(2,1)S(1)} %get-tuple-element.58), channel_id=1, source_target_pairs={{0,2},{1,3},{2,4},{3,5},{4,6},{5,7},{6,0},{7,1},{8,10},{9,11},{10,... | collective-permute-start | bytes 196616 | tf_op jit(solution)/shard_map/ppermute | solution.py:355
  49.0 1.9 %collective-permute-start.21 = (bf16[16,2048]{1,0:T(8,128)(2,1)S(1)}, bf16[16,2048]{1,0:T(8,128)(2,1)S(1)}, u32[]{:S(2)}, u32[]{:S(2)}) collective-permute-start(bf16[16,2048]{1,0:T(8,128)(2,1)S(1)} %get-tuple-element.59), channel_id=1, source_target_pairs={{0,4},{1,5},{2,6},{3,7},{4,0},{5,1},{6,2},{7,3},{8,12},{9,13},{10,... | collective-permute-start | bytes 196616 | tf_op jit(solution)/shard_map/ppermute | solution.py:355
  50.9 1.2 %collective-permute-start.22 = (bf16[16,2048]{1,0:T(8,128)(2,1)S(1)}, bf16[16,2048]{1,0:T(8,128)(2,1)S(1)}, u32[]{:S(2)}, u32[]{:S(2)}) collective-permute-start(bf16[16,2048]{1,0:T(8,128)(2,1)S(1)} %get-tuple-element.60), channel_id=1, source_target_pairs={{0,6},{1,7},{2,0},{3,1},{4,2},{5,3},{6,4},{7,5},{8,14},{9,15},{10,... | collective-permute-start | bytes 196616 | tf_op jit(solution)/shard_map/ppermute | solution.py:355
  52.1 3.8 %collective-permute-done.25.refs_7_ = bf16[16,2048]{1,0:T(8,128)(2,1)S(1)} collective-permute-done((bf16[16,2048]{1,0:T(8,128)(2,1)S(1)}, bf16[16,2048]{1,0:T(8,128)(2,1)S(1)}, u32[]{:S(2)}, u32[]{:S(2)}) %collective-permute-start.25) | collective-permute-done | bytes 65568 | tf_op jit(solution)/shard_map/ppermute | solution.py:355
  56.0 1.3 %collective-permute-done.21.refs_2_ = bf16[16,2048]{1,0:T(8,128)(2,1)S(1)} collective-permute-done((bf16[16,2048]{1,0:T(8,128)(2,1)S(1)}, bf16[16,2048]{1,0:T(8,128)(2,1)S(1)}, u32[]{:S(2)}, u32[]{:S(2)}) %collective-permute-start.21) | collective-permute-done | bytes 65568 | tf_op jit(solution)/shard_map/ppermute | solution.py:355
  57.3 0.7 %shard_map.125 = bf16[16,4096]{1,0:T(8,128)(2,1)} custom-call(bf16[16,2048]{1,0:T(8,128)(2,1)S(1)} %get-tuple-element.57.refs_0_, bf16[16,2048]{1,0:T(8,128)(2,1)S(1)} %collective-permute-done.20.refs_1_, bf16[16,2048]{1,0:T(8,128)(2,1)S(1)} %collective-permute-done.21.refs_2_, bf16[16,2048]{1,0:T(8,128)(2,1)S(1)} %collective-permute-done.22.refs_3_, ...), custom_call_target="tpu_custom_call" | custom-call | tf_op jit(solution)/shard_map/pallas_call | solution.py:331
  (23 shorter events, 0.3 us)
Async XLA Ops:
  0.0 11.2 %collective-permute-start.4 = (bf16[128,4096]{1,0:T(8,128)(2,1)}, bf16[128,4096]{1,0:T(8,128)(2,1)S(1)}, u32[]{:S(2)}, u32[]{:S(2)}) collective-permute-start(bf16[128,4096]{1,0:T(8,128)(2,1)} %w_out_hbm.1), channel_id=1, source_target_pairs={{0,1},{1,0},{2,3},{3,2},{4,5},{5,4},{6,7},{7,6},{8,9},{9,8},{10,11... | collective-permute-start | bytes 3145736 | tf_op jit(solution)/shard_map/ppermute | solution.py:358
  1.6 7.1 %collective-permute-start.2 = (bf16[144,128]{1,0:T(8,128)(2,1)S(1)}, bf16[144,128]{1,0:T(8,128)(2,1)S(1)}, u32[]{:S(2)}, u32[]{:S(2)}) collective-permute-start(bf16[144,128]{1,0:T(8,128)(2,1)S(1)} %shard_map.109._), channel_id=1, source_target_pairs={{24,0},{16,8},{8,16},{0,24},{25,1},{17,9},{9,17},{1,25},{26,2},{18... | collective-permute-start | bytes 110600 | tf_op jit(solution)/shard_map/ppermute | solution.py:381
  5.1 4.0 %collective-permute-start.1 = (bf16[144,128]{1,0:T(8,128)(2,1)S(1)}, bf16[144,128]{1,0:T(8,128)(2,1)S(1)}, u32[]{:S(2)}, u32[]{:S(2)}) collective-permute-start(bf16[144,128]{1,0:T(8,128)(2,1)S(1)} %shard_map.109._), channel_id=1, source_target_pairs={{16,0},{24,8},{0,16},{8,24},{17,1},{25,9},{1,17},{9,25},{18,2},{26... | collective-permute-start | bytes 110600 | tf_op jit(solution)/shard_map/ppermute | solution.py:381
  5.6 4.0 %collective-permute-start = (bf16[144,128]{1,0:T(8,128)(2,1)S(1)}, bf16[144,128]{1,0:T(8,128)(2,1)S(1)}, u32[]{:S(2)}, u32[]{:S(2)}) collective-permute-start(bf16[144,128]{1,0:T(8,128)(2,1)S(1)} %shard_map.109._), channel_id=1, source_target_pairs={{8,0},{0,8},{24,16},{16,24},{9,1},{1,9},{25,17},{17,25},{10,2},{2,... | collective-permute-start | bytes 110600 | tf_op jit(solution)/shard_map/ppermute | solution.py:381
  10.0 1.2 %collective-permute-start.3 = (bf16[64,128]{1,0:T(8,128)(2,1)S(1)}, bf16[64,128]{1,0:T(8,128)(2,1)S(1)}, u32[]{:S(2)}, u32[]{:S(2)}) collective-permute-start(bf16[64,128]{1,0:T(8,128)(2,1)S(1)} %get-tuple-element.42), channel_id=1, source_target_pairs={{0,1},{1,0},{2,3},{3,2},{4,5},{5,4},{6,7},{7,6},{8,9},{9,8},{10,11... | collective-permute-start | bytes 49160 | tf_op jit(solution)/shard_map/ppermute | solution.py:358
  11.5 8.1 %collective-permute-start.11 = (bf16[16,2048]{1,0:T(8,128)(2,1)S(1)}, bf16[16,2048]{1,0:T(8,128)(2,1)S(1)}, u32[]{:S(2)}, u32[]{:S(2)}) collective-permute-start(bf16[16,2048]{1,0:T(8,128)(2,1)S(1)} %get-tuple-element.49), channel_id=1, source_target_pairs={{0,2},{1,3},{2,4},{3,5},{4,6},{5,7},{6,0},{7,1},{8,10},{9,11},{10,... | collective-permute-start | bytes 196616 | tf_op jit(solution)/shard_map/ppermute | solution.py:355
  13.1 7.3 %collective-permute-start.12 = (bf16[16,2048]{1,0:T(8,128)(2,1)S(1)}, bf16[16,2048]{1,0:T(8,128)(2,1)S(1)}, u32[]{:S(2)}, u32[]{:S(2)}) collective-permute-start(bf16[16,2048]{1,0:T(8,128)(2,1)S(1)} %get-tuple-element.50), channel_id=1, source_target_pairs={{0,4},{1,5},{2,6},{3,7},{4,0},{5,1},{6,2},{7,3},{8,12},{9,13},{10,... | collective-permute-start | bytes 196616 | tf_op jit(solution)/shard_map/ppermute | solution.py:355
  15.7 5.7 %collective-permute-start.13 = (bf16[16,2048]{1,0:T(8,128)(2,1)S(1)}, bf16[16,2048]{1,0:T(8,128)(2,1)S(1)}, u32[]{:S(2)}, u32[]{:S(2)}) collective-permute-start(bf16[16,2048]{1,0:T(8,128)(2,1)S(1)} %get-tuple-element.51), channel_id=1, source_target_pairs={{0,6},{1,7},{2,0},{3,1},{4,2},{5,3},{6,4},{7,5},{8,14},{9,15},{10,... | collective-permute-start | bytes 196616 | tf_op jit(solution)/shard_map/ppermute | solution.py:355
  17.4 9.8 %collective-permute-start.5 = (bf16[16,2048]{1,0:T(8,128)(2,1)S(1)}, bf16[16,2048]{1,0:T(8,128)(2,1)S(1)}, u32[]{:S(2)}, u32[]{:S(2)}) collective-permute-start(bf16[16,2048]{1,0:T(8,128)(2,1)S(1)} %get-tuple-element.45), channel_id=1, source_target_pairs={{0,6},{1,7},{2,0},{3,1},{4,2},{5,3},{6,4},{7,5},{8,14},{9,15},{10,... | collective-permute-start | bytes 196616 | tf_op jit(solution)/shard_map/ppermute | solution.py:355
  17.9 12.4 %collective-permute-start.6 = (bf16[16,2048]{1,0:T(8,128)(2,1)S(1)}, bf16[16,2048]{1,0:T(8,128)(2,1)S(1)}, u32[]{:S(2)}, u32[]{:S(2)}) collective-permute-start(bf16[16,2048]{1,0:T(8,128)(2,1)S(1)} %get-tuple-element.46), channel_id=1, source_target_pairs={{0,4},{1,5},{2,6},{3,7},{4,0},{5,1},{6,2},{7,3},{8,12},{9,13},{10,... | collective-permute-start | bytes 196616 | tf_op jit(solution)/shard_map/ppermute | solution.py:355
  19.6 10.8 %collective-permute-start.7 = (bf16[16,2048]{1,0:T(8,128)(2,1)S(1)}, bf16[16,2048]{1,0:T(8,128)(2,1)S(1)}, u32[]{:S(2)}, u32[]{:S(2)}) collective-permute-start(bf16[16,2048]{1,0:T(8,128)(2,1)S(1)} %get-tuple-element.47), channel_id=1, source_target_pairs={{0,2},{1,3},{2,4},{3,5},{4,6},{5,7},{6,0},{7,1},{8,10},{9,11},{10,... | collective-permute-start | bytes 196616 | tf_op jit(solution)/shard_map/ppermute | solution.py:355
  21.4 9.1 %collective-permute-start.16 = (bf16[16,2048]{1,0:T(8,128)(2,1)S(1)}, bf16[16,2048]{1,0:T(8,128)(2,1)S(1)}, u32[]{:S(2)}, u32[]{:S(2)}) collective-permute-start(bf16[16,2048]{1,0:T(8,128)(2,1)S(1)} %shard_map.115.refs_0_.refs_4_), channel_id=1, source_target_pairs={{0,2},{1,3},{2,4},{3,5},{4,6},{5,7},{6,0},{7,1},{8,10},{9,11},{10,... | collective-permute-start | bytes 196616 | tf_op jit(solution)/shard_map/ppermute | solution.py:355
  23.3 10.9 %collective-permute-start.15 = (bf16[16,2048]{1,0:T(8,128)(2,1)S(1)}, bf16[16,2048]{1,0:T(8,128)(2,1)S(1)}, u32[]{:S(2)}, u32[]{:S(2)}) collective-permute-start(bf16[16,2048]{1,0:T(8,128)(2,1)S(1)} %shard_map.115.refs_0_.refs_4_), channel_id=1, source_target_pairs={{0,4},{1,5},{2,6},{3,7},{4,0},{5,1},{6,2},{7,3},{8,12},{9,13},{10,... | collective-permute-start | bytes 196616 | tf_op jit(solution)/shard_map/ppermute | solution.py:355
  27.2 7.1 %collective-permute-start.14 = (bf16[16,2048]{1,0:T(8,128)(2,1)S(1)}, bf16[16,2048]{1,0:T(8,128)(2,1)S(1)}, u32[]{:S(2)}, u32[]{:S(2)}) collective-permute-start(bf16[16,2048]{1,0:T(8,128)(2,1)S(1)} %shard_map.115.refs_0_.refs_4_), channel_id=1, source_target_pairs={{0,6},{1,7},{2,0},{3,1},{4,2},{5,3},{6,4},{7,5},{8,14},{9,15},{10,... | collective-permute-start | bytes 196616 | tf_op jit(solution)/shard_map/ppermute | solution.py:355
  30.4 6.8 %collective-permute-start.10 = (bf16[16,2048]{1,0:T(8,128)(2,1)S(1)}, bf16[16,2048]{1,0:T(8,128)(2,1)S(1)}, u32[]{:S(2)}, u32[]{:S(2)}) collective-permute-start(bf16[16,2048]{1,0:T(8,128)(2,1)S(1)} %shard_map.113.refs_0_.refs_9_), channel_id=1, source_target_pairs={{0,2},{1,3},{2,4},{3,5},{4,6},{5,7},{6,0},{7,1},{8,10},{9,11},{10,... | collective-permute-start | bytes 196616 | tf_op jit(solution)/shard_map/ppermute | solution.py:355
  30.4 8.4 %collective-permute-start.9 = (bf16[16,2048]{1,0:T(8,128)(2,1)S(1)}, bf16[16,2048]{1,0:T(8,128)(2,1)S(1)}, u32[]{:S(2)}, u32[]{:S(2)}) collective-permute-start(bf16[16,2048]{1,0:T(8,128)(2,1)S(1)} %shard_map.113.refs_0_.refs_9_), channel_id=1, source_target_pairs={{0,4},{1,5},{2,6},{3,7},{4,0},{5,1},{6,2},{7,3},{8,12},{9,13},{10,... | collective-permute-start | bytes 196616 | tf_op jit(solution)/shard_map/ppermute | solution.py:355
  30.5 8.3 %collective-permute-start.8 = (bf16[16,2048]{1,0:T(8,128)(2,1)S(1)}, bf16[16,2048]{1,0:T(8,128)(2,1)S(1)}, u32[]{:S(2)}, u32[]{:S(2)}) collective-permute-start(bf16[16,2048]{1,0:T(8,128)(2,1)S(1)} %shard_map.113.refs_0_.refs_9_), channel_id=1, source_target_pairs={{0,6},{1,7},{2,0},{3,1},{4,2},{5,3},{6,4},{7,5},{8,14},{9,15},{10,... | collective-permute-start | bytes 196616 | tf_op jit(solution)/shard_map/ppermute | solution.py:355
  34.3 4.7 %collective-permute-start.18 = (bf16[64,2048]{1,0:T(8,128)(2,1)S(1)}, bf16[64,2048]{1,0:T(8,128)(2,1)S(1)}, u32[]{:S(2)}, u32[]{:S(2)}) collective-permute-start(bf16[64,2048]{1,0:T(8,128)(2,1)S(1)} %shard_map.116._.own_ref), channel_id=1, source_target_pairs={{0,1},{1,0},{2,3},{3,2},{4,5},{5,4},{6,7},{7,6},{8,9},{9,8},{10,11... | collective-permute-start | bytes 786440 | tf_op jit(solution)/shard_map/ppermute | solution.py:358
  38.9 1.6 %collective-permute-start.17 = (bf16[64,2048]{1,0:T(8,128)(2,1)S(1)}, bf16[64,2048]{1,0:T(8,128)(2,1)S(1)}, u32[]{:S(2)}, u32[]{:S(2)}) collective-permute-start(bf16[64,2048]{1,0:T(8,128)(2,1)S(1)} %shard_map.118.own_ref), channel_id=1, source_target_pairs={{0,1},{1,0},{2,3},{3,2},{4,5},{5,4},{6,7},{7,6},{8,9},{9,8},{10,11... | collective-permute-start | bytes 786440 | tf_op jit(solution)/shard_map/ppermute | solution.py:358
  41.9 1.6 %collective-permute-start.23 = (bf16[64,2048]{1,0:T(8,128)(2,1)S(1)}, bf16[64,2048]{1,0:T(8,128)(2,1)S(1)}, u32[]{:S(2)}, u32[]{:S(2)}) collective-permute-start(bf16[64,2048]{1,0:T(8,128)(2,1)S(1)} %get-tuple-element.62), channel_id=1, source_target_pairs={{0,1},{1,0},{2,3},{3,2},{4,5},{5,4},{6,7},{7,6},{8,9},{9,8},{10,11... | collective-permute-start | bytes 786440 | tf_op jit(solution)/shard_map/ppermute | solution.py:358
  42.5 3.9 %collective-permute-start.19 = (bf16[64,2048]{1,0:T(8,128)(2,1)S(1)}, bf16[64,2048]{1,0:T(8,128)(2,1)S(1)}, u32[]{:S(2)}, u32[]{:S(2)}) collective-permute-start(bf16[64,2048]{1,0:T(8,128)(2,1)S(1)} %get-tuple-element.56), channel_id=1, source_target_pairs={{0,1},{1,0},{2,3},{3,2},{4,5},{5,4},{6,7},{7,6},{8,9},{9,8},{10,11... | collective-permute-start | bytes 786440 | tf_op jit(solution)/shard_map/ppermute | solution.py:358
  43.5 7.4 %collective-permute-start.24 = (bf16[16,2048]{1,0:T(8,128)(2,1)S(1)}, bf16[16,2048]{1,0:T(8,128)(2,1)S(1)}, u32[]{:S(2)}, u32[]{:S(2)}) collective-permute-start(bf16[16,2048]{1,0:T(8,128)(2,1)S(1)} %get-tuple-element.64), channel_id=1, source_target_pairs={{0,6},{1,7},{2,0},{3,1},{4,2},{5,3},{6,4},{7,5},{8,14},{9,15},{10,... | collective-permute-start | bytes 196616 | tf_op jit(solution)/shard_map/ppermute | solution.py:355
  45.4 10.6 %collective-permute-start.25 = (bf16[16,2048]{1,0:T(8,128)(2,1)S(1)}, bf16[16,2048]{1,0:T(8,128)(2,1)S(1)}, u32[]{:S(2)}, u32[]{:S(2)}) collective-permute-start(bf16[16,2048]{1,0:T(8,128)(2,1)S(1)} %get-tuple-element.65), channel_id=1, source_target_pairs={{0,4},{1,5},{2,6},{3,7},{4,0},{5,1},{6,2},{7,3},{8,12},{9,13},{10,... | collective-permute-start | bytes 196616 | tf_op jit(solution)/shard_map/ppermute | solution.py:355
  46.4 9.6 %collective-permute-start.26 = (bf16[16,2048]{1,0:T(8,128)(2,1)S(1)}, bf16[16,2048]{1,0:T(8,128)(2,1)S(1)}, u32[]{:S(2)}, u32[]{:S(2)}) collective-permute-start(bf16[16,2048]{1,0:T(8,128)(2,1)S(1)} %get-tuple-element.66), channel_id=1, source_target_pairs={{0,2},{1,3},{2,4},{3,5},{4,6},{5,7},{6,0},{7,1},{8,10},{9,11},{10,... | collective-permute-start | bytes 196616 | tf_op jit(solution)/shard_map/ppermute | solution.py:355
  46.5 9.5 %collective-permute-start.20 = (bf16[16,2048]{1,0:T(8,128)(2,1)S(1)}, bf16[16,2048]{1,0:T(8,128)(2,1)S(1)}, u32[]{:S(2)}, u32[]{:S(2)}) collective-permute-start(bf16[16,2048]{1,0:T(8,128)(2,1)S(1)} %get-tuple-element.58), channel_id=1, source_target_pairs={{0,2},{1,3},{2,4},{3,5},{4,6},{5,7},{6,0},{7,1},{8,10},{9,11},{10,... | collective-permute-start | bytes 196616 | tf_op jit(solution)/shard_map/ppermute | solution.py:355
  49.0 8.4 %collective-permute-start.21 = (bf16[16,2048]{1,0:T(8,128)(2,1)S(1)}, bf16[16,2048]{1,0:T(8,128)(2,1)S(1)}, u32[]{:S(2)}, u32[]{:S(2)}) collective-permute-start(bf16[16,2048]{1,0:T(8,128)(2,1)S(1)} %get-tuple-element.59), channel_id=1, source_target_pairs={{0,4},{1,5},{2,6},{3,7},{4,0},{5,1},{6,2},{7,3},{8,12},{9,13},{10,... | collective-permute-start | bytes 196616 | tf_op jit(solution)/shard_map/ppermute | solution.py:355
  50.9 6.4 %collective-permute-start.22 = (bf16[16,2048]{1,0:T(8,128)(2,1)S(1)}, bf16[16,2048]{1,0:T(8,128)(2,1)S(1)}, u32[]{:S(2)}, u32[]{:S(2)}) collective-permute-start(bf16[16,2048]{1,0:T(8,128)(2,1)S(1)} %get-tuple-element.60), channel_id=1, source_target_pairs={{0,6},{1,7},{2,0},{3,1},{4,2},{5,3},{6,4},{7,5},{8,14},{9,15},{10,... | collective-permute-start | bytes 196616 | tf_op jit(solution)/shard_map/ppermute | solution.py:355

commit v9 on v6

--- a/solution.py
+++ b/solution.py
@@ -10,7 +10,7 @@
 F32 = jnp.float32
 BF16 = jnp.bfloat16
 TILE_ROWS = 16
-COLUMNS = 1024
+COLUMNS = 2048
 VMEM_LIMIT = 16 * 1024 * 1024
 
 

time: 57.5 us -> 57.5 us (level)
  no operation moved by 1% of the time
where the time goes in v9:
time: 57.5 us; the launch traced here: 57.3 us
  starting transfers between devices  35.8 us (62%)
  waiting for transfers between devices  11 us (19%)
  Pallas kernels  10.3 us (18%)
    ppermute x18, starting transfers between devices, shift(): lax.ppermute(x, 'exp', [(e, (e + 2 * r) % exp_count) for e in range(exp_c...  30.4 us
    pallas_call x17, Pallas kernels, call(): pl.pallas_call(kernel, out_shape=outs, in_specs=[pl.BlockSpec(memory_spac...  10.3 us
    ppermute x18, waiting for transfers between devices, shift(): lax.ppermute(x, 'exp', [(e, (e + 2 * r) % exp_count) for e in range(exp_c...  7.71 us
    ppermute x3, starting transfers between devices, local(): lax.ppermute(state, 'seq', [(move(i), i) for i in range(seq_count)])  4.15 us
    ppermute x6, waiting for transfers between devices, across(): return lax.ppermute(x, 'exp', [(e, e ^ 1) for e in range(exp_count)])  2.4 us
    ppermute x6, starting transfers between devices, across(): return lax.ppermute(x, 'exp', [(e, e ^ 1) for e in range(exp_count)])  1.31 us
  transfers between devices with their start and end apart: 27, of which 9 were waited for; matrix products, arithmetic and copies ran while one was open for 0% of the time, Pallas kernels for 14%

profile of v9, /device:TPU:0, one launch (start us, length us, event | category | flops | bytes accessed | tf_op | source)
XLA Modules:
  0.0 57.3 jit_solution(13090042167349163008)
XLA Ops:
  0.0 0.5 collective-permute-start.4
  0.5 1.1 %shard_map.109._ = bf16[144,128]{1,0:T(8,128)(2,1)S(1)} custom-call(bf16[128,128]{1,0:T(8,128)(2,1)} %key_hbm.3, bf16[128,128]{1,0:T(8,128)(2,1)} %value_hbm.3, f32[1,128]{1,0:T(1,128)} %bitcast.15), custom_call_target="tpu_custom_call" | custom-call | tf_op jit(solution)/shard_map/pallas_call | solution.py:331
  1.6 3.5 %collective-permute-start.2 = (bf16[144,128]{1,0:T(8,128)(2,1)S(1)}, bf16[144,128]{1,0:T(8,128)(2,1)S(1)}, u32[]{:S(2)}, u32[]{:S(2)}) collective-permute-start(bf16[144,128]{1,0:T(8,128)(2,1)S(1)} %shard_map.109._), channel_id=1, source_target_pairs={{24,0},{16,8},{8,16},{0,24},{25,1},{17,9},{9,17},{1,25},{26,2},{18... | collective-permute-start | bytes 110600 | tf_op jit(solution)/shard_map/ppermute | solution.py:380
  5.1 0.5 collective-permute-start.1
  5.6 0.1 collective-permute-start
  5.7 2.9 %shard_map.110 = (f32[128,128]{1,0:T(8,128)S(1)}, f32[128,128]{1,0:T(8,128)S(1)}, bf16[128,128]{1,0:T(8,128)(2,1)S(1)}, f32[8,128]{1,0:T(8,128)S(1)}, bf16[128,4...) custom-call(bf16[128,128]{1,0:T(8,128)(2,1)} %query_hbm.1, bf16[128,128]{1,0:T(8,128)(2,1)} %key_hbm.3, ...), custom_call_target="tpu_custom_call" | custom-call | tf_op jit(solution)/shard_map/pallas_call | solution.py:331
  8.6 0.4 collective-permute-done.1.refs_1_
  9.0 0.5 collective-permute-done.refs_0_
  9.5 0.4 shard_map.111
  10.0 0.1 collective-permute-start.3
  10.0 1.2 %collective-permute-done.3.b_ref = bf16[64,128]{1,0:T(8,128)(2,1)S(1)} collective-permute-done((bf16[64,128]{1,0:T(8,128)(2,1)S(1)}, bf16[64,128]{1,0:T(8,128)(2,1)S(1)}, u32[]{:S(2)}, u32[]{:S(2)}) %collective-permute-start.3) | collective-permute-done | bytes 16416 | tf_op jit(solution)/shard_map/ppermute | solution.py:358
  11.2 0.3 shard_map.114
  11.5 1.6 %collective-permute-start.11 = (bf16[16,2048]{1,0:T(8,128)(2,1)S(1)}, bf16[16,2048]{1,0:T(8,128)(2,1)S(1)}, u32[]{:S(2)}, u32[]{:S(2)}) collective-permute-start(bf16[16,2048]{1,0:T(8,128)(2,1)S(1)} %get-tuple-element.49), channel_id=1, source_target_pairs={{0,2},{1,3},{2,4},{3,5},{4,6},{5,7},{6,0},{7,1},{8,10},{9,11},{10,... | collective-permute-start | bytes 196616 | tf_op jit(solution)/shard_map/ppermute | solution.py:355
  13.2 2.6 %collective-permute-start.12 = (bf16[16,2048]{1,0:T(8,128)(2,1)S(1)}, bf16[16,2048]{1,0:T(8,128)(2,1)S(1)}, u32[]{:S(2)}, u32[]{:S(2)}) collective-permute-start(bf16[16,2048]{1,0:T(8,128)(2,1)S(1)} %get-tuple-element.50), channel_id=1, source_target_pairs={{0,4},{1,5},{2,6},{3,7},{4,0},{5,1},{6,2},{7,3},{8,12},{9,13},{10,... | collective-permute-start | bytes 196616 | tf_op jit(solution)/shard_map/ppermute | solution.py:355
  15.7 1.3 %collective-permute-start.13 = (bf16[16,2048]{1,0:T(8,128)(2,1)S(1)}, bf16[16,2048]{1,0:T(8,128)(2,1)S(1)}, u32[]{:S(2)}, u32[]{:S(2)}) collective-permute-start(bf16[16,2048]{1,0:T(8,128)(2,1)S(1)} %get-tuple-element.51), channel_id=1, source_target_pairs={{0,6},{1,7},{2,0},{3,1},{4,2},{5,3},{6,4},{7,5},{8,14},{9,15},{10,... | collective-permute-start | bytes 196616 | tf_op jit(solution)/shard_map/ppermute | solution.py:355
  17.1 0.3 shard_map.112
  17.4 0.7 %collective-permute-start.5 = (bf16[16,2048]{1,0:T(8,128)(2,1)S(1)}, bf16[16,2048]{1,0:T(8,128)(2,1)S(1)}, u32[]{:S(2)}, u32[]{:S(2)}) collective-permute-start(bf16[16,2048]{1,0:T(8,128)(2,1)S(1)} %get-tuple-element.45), channel_id=1, source_target_pairs={{0,2},{1,3},{2,4},{3,5},{4,6},{5,7},{6,0},{7,1},{8,10},{9,11},{10,... | collective-permute-start | bytes 196616 | tf_op jit(solution)/shard_map/ppermute | solution.py:355
  18.1 0.3 collective-permute-start.6
  18.5 2.8 %collective-permute-start.7 = (bf16[16,2048]{1,0:T(8,128)(2,1)S(1)}, bf16[16,2048]{1,0:T(8,128)(2,1)S(1)}, u32[]{:S(2)}, u32[]{:S(2)}) collective-permute-start(bf16[16,2048]{1,0:T(8,128)(2,1)S(1)} %get-tuple-element.47), channel_id=1, source_target_pairs={{0,6},{1,7},{2,0},{3,1},{4,2},{5,3},{6,4},{7,5},{8,14},{9,15},{10,... | collective-permute-start | bytes 196616 | tf_op jit(solution)/shard_map/ppermute | solution.py:355
  21.3 3.1 %collective-permute-start.16 = (bf16[16,2048]{1,0:T(8,128)(2,1)S(1)}, bf16[16,2048]{1,0:T(8,128)(2,1)S(1)}, u32[]{:S(2)}, u32[]{:S(2)}) collective-permute-start(bf16[16,2048]{1,0:T(8,128)(2,1)S(1)} %shard_map.115.refs_0_.refs_4_), channel_id=1, source_target_pairs={{0,2},{1,3},{2,4},{3,5},{4,6},{5,7},{6,0},{7,1},{8,10},{9,11},{10,... | collective-permute-start | bytes 196616 | tf_op jit(solution)/shard_map/ppermute | solution.py:355
  24.4 0.5 collective-permute-start.15
  24.9 1.9 %collective-permute-start.14 = (bf16[16,2048]{1,0:T(8,128)(2,1)S(1)}, bf16[16,2048]{1,0:T(8,128)(2,1)S(1)}, u32[]{:S(2)}, u32[]{:S(2)}) collective-permute-start(bf16[16,2048]{1,0:T(8,128)(2,1)S(1)} %shard_map.115.refs_0_.refs_4_), channel_id=1, source_target_pairs={{0,6},{1,7},{2,0},{3,1},{4,2},{5,3},{6,4},{7,5},{8,14},{9,15},{10,... | collective-permute-start | bytes 196616 | tf_op jit(solution)/shard_map/ppermute | solution.py:355
  26.9 4.1 %collective-permute-start.10 = (bf16[16,2048]{1,0:T(8,128)(2,1)S(1)}, bf16[16,2048]{1,0:T(8,128)(2,1)S(1)}, u32[]{:S(2)}, u32[]{:S(2)}) collective-permute-start(bf16[16,2048]{1,0:T(8,128)(2,1)S(1)} %shard_map.113.refs_0_.refs_9_), channel_id=1, source_target_pairs={{0,2},{1,3},{2,4},{3,5},{4,6},{5,7},{6,0},{7,1},{8,10},{9,11},{10,... | collective-permute-start | bytes 196616 | tf_op jit(solution)/shard_map/ppermute | solution.py:355
  31.0 2.4 %collective-permute-start.8 = (bf16[16,2048]{1,0:T(8,128)(2,1)S(1)}, bf16[16,2048]{1,0:T(8,128)(2,1)S(1)}, u32[]{:S(2)}, u32[]{:S(2)}) collective-permute-start(bf16[16,2048]{1,0:T(8,128)(2,1)S(1)} %shard_map.113.refs_0_.refs_9_), channel_id=1, source_target_pairs={{0,6},{1,7},{2,0},{3,1},{4,2},{5,3},{6,4},{7,5},{8,14},{9,15},{10,... | collective-permute-start | bytes 196616 | tf_op jit(solution)/shard_map/ppermute | solution.py:355
  33.5 0.1 collective-permute-start.18
  33.5 1.7 %shard_map.117 = (bf16[288,4096]{1,0:T(8,128)(2,1)S(1)}, f32[8,128]{1,0:T(8,128)S(1)}) custom-call(bf16[288,4096]{1,0:T(8,128)(2,1)} %bitcast.13, bf16[64,2048]{1,0:T(8,128)(2,1)S(1)} %shard_map.116._.own_ref), custom_call_target="tpu_custom_call" | custom-call | tf_op jit(solution)/shard_map/pallas_call | solution.py:331
  35.2 2.1 %collective-permute-done.9.refs_2_ = bf16[16,2048]{1,0:T(8,128)(2,1)S(1)} collective-permute-done((bf16[16,2048]{1,0:T(8,128)(2,1)S(1)}, bf16[16,2048]{1,0:T(8,128)(2,1)S(1)}, u32[]{:S(2)}, u32[]{:S(2)}) %collective-permute-start.9) | collective-permute-done | bytes 65568 | tf_op jit(solution)/shard_map/ppermute | solution.py:355
  37.4 0.1 collective-permute-start.17
  37.5 0.8 %shard_map.119.before_ref = f32[592,128]{1,0:T(8,128)S(1)} custom-call(bf16[592,4096]{1,0:T(8,128)(2,1)S(1)} %get-tuple-element.36.in_ref, bf16[64,2048]{1,0:T(8,128)(2,1)S(1)} %shard_map.116._.own_ref, bf16[64,2048]{1,0:T(8,128)(2,1)S(1)} %collective-permute-done.18.other_ref), custom_call_target="tpu_custom_call" | custom-call | tf_op jit(solution)/shard_map/pallas_call | solution.py:331
  38.3 0.7 %collective-permute-done.17.other_ref = bf16[64,2048]{1,0:T(8,128)(2,1)S(1)} collective-permute-done((bf16[64,2048]{1,0:T(8,128)(2,1)S(1)}, bf16[64,2048]{1,0:T(8,128)(2,1)S(1)}, u32[]{:S(2)}, u32[]{:S(2)}) %collective-permute-start.17) | collective-permute-done | bytes 262176 | tf_op jit(solution)/shard_map/ppermute | solution.py:358
  39.0 0.9 %shard_map.120.x_ref = bf16[128,288]{1,0:T(8,128)(2,1)S(1)} custom-call(bf16[592,4096]{1,0:T(8,128)(2,1)S(1)} %get-tuple-element.36.in_ref, bf16[64,2048]{1,0:T(8,128)(2,1)S(1)} %shard_map.118.own_ref, bf16[64,2048]{1,0:T(8,128)(2,1)S(1)} %collective-permute-done.17.other_ref, f32[592,128]{1,0:T(8,128)S(1)} %shard_map.119.before_ref, ...), custom_call_target="tpu_custom_call" | custom-call | tf_op jit(solution)/shard_map/pallas_call | solution.py:331
  39.9 0.4 shard_map.123
  40.4 0.2 collective-permute-start.23
  40.6 0.4 shard_map.121
  41.0 0.4 collective-permute-start.19
  41.4 0.5 collective-permute-done.23.b_ref
  42.0 0.1 shard_map.124
  42.0 1.9 %collective-permute-start.24 = (bf16[16,2048]{1,0:T(8,128)(2,1)S(1)}, bf16[16,2048]{1,0:T(8,128)(2,1)S(1)}, u32[]{:S(2)}, u32[]{:S(2)}) collective-permute-start(bf16[16,2048]{1,0:T(8,128)(2,1)S(1)} %get-tuple-element.64), channel_id=1, source_target_pairs={{0,2},{1,3},{2,4},{3,5},{4,6},{5,7},{6,0},{7,1},{8,10},{9,11},{10,... | collective-permute-start | bytes 196616 | tf_op jit(solution)/shard_map/ppermute | solution.py:355
  44.0 1.7 %collective-permute-start.25 = (bf16[16,2048]{1,0:T(8,128)(2,1)S(1)}, bf16[16,2048]{1,0:T(8,128)(2,1)S(1)}, u32[]{:S(2)}, u32[]{:S(2)}) collective-permute-start(bf16[16,2048]{1,0:T(8,128)(2,1)S(1)} %get-tuple-element.65), channel_id=1, source_target_pairs={{0,4},{1,5},{2,6},{3,7},{4,0},{5,1},{6,2},{7,3},{8,12},{9,13},{10,... | collective-permute-start | bytes 196616 | tf_op jit(solution)/shard_map/ppermute | solution.py:355
  45.7 0.7 %collective-permute-start.26 = (bf16[16,2048]{1,0:T(8,128)(2,1)S(1)}, bf16[16,2048]{1,0:T(8,128)(2,1)S(1)}, u32[]{:S(2)}, u32[]{:S(2)}) collective-permute-start(bf16[16,2048]{1,0:T(8,128)(2,1)S(1)} %get-tuple-element.66), channel_id=1, source_target_pairs={{0,6},{1,7},{2,0},{3,1},{4,2},{5,3},{6,4},{7,5},{8,14},{9,15},{10,... | collective-permute-start | bytes 196616 | tf_op jit(solution)/shard_map/ppermute | solution.py:355
  46.4 0.1 shard_map.122
  46.5 1.4 %collective-permute-start.20 = (bf16[16,2048]{1,0:T(8,128)(2,1)S(1)}, bf16[16,2048]{1,0:T(8,128)(2,1)S(1)}, u32[]{:S(2)}, u32[]{:S(2)}) collective-permute-start(bf16[16,2048]{1,0:T(8,128)(2,1)S(1)} %get-tuple-element.58), channel_id=1, source_target_pairs={{0,2},{1,3},{2,4},{3,5},{4,6},{5,7},{6,0},{7,1},{8,10},{9,11},{10,... | collective-permute-start | bytes 196616 | tf_op jit(solution)/shard_map/ppermute | solution.py:355
  47.8 1.2 %collective-permute-start.21 = (bf16[16,2048]{1,0:T(8,128)(2,1)S(1)}, bf16[16,2048]{1,0:T(8,128)(2,1)S(1)}, u32[]{:S(2)}, u32[]{:S(2)}) collective-permute-start(bf16[16,2048]{1,0:T(8,128)(2,1)S(1)} %get-tuple-element.59), channel_id=1, source_target_pairs={{0,4},{1,5},{2,6},{3,7},{4,0},{5,1},{6,2},{7,3},{8,12},{9,13},{10,... | collective-permute-start | bytes 196616 | tf_op jit(solution)/shard_map/ppermute | solution.py:355
  49.0 2.0 %collective-permute-start.22 = (bf16[16,2048]{1,0:T(8,128)(2,1)S(1)}, bf16[16,2048]{1,0:T(8,128)(2,1)S(1)}, u32[]{:S(2)}, u32[]{:S(2)}) collective-permute-start(bf16[16,2048]{1,0:T(8,128)(2,1)S(1)} %get-tuple-element.60), channel_id=1, source_target_pairs={{0,6},{1,7},{2,0},{3,1},{4,2},{5,3},{6,4},{7,5},{8,14},{9,15},{10,... | collective-permute-start | bytes 196616 | tf_op jit(solution)/shard_map/ppermute | solution.py:355
  51.0 1.7 %collective-permute-done.25.refs_7_ = bf16[16,2048]{1,0:T(8,128)(2,1)S(1)} collective-permute-done((bf16[16,2048]{1,0:T(8,128)(2,1)S(1)}, bf16[16,2048]{1,0:T(8,128)(2,1)S(1)}, u32[]{:S(2)}, u32[]{:S(2)}) %collective-permute-start.25) | collective-permute-done | bytes 65568 | tf_op jit(solution)/shard_map/ppermute | solution.py:355
  52.7 0.6 %collective-permute-done.20.refs_1_ = bf16[16,2048]{1,0:T(8,128)(2,1)S(1)} collective-permute-done((bf16[16,2048]{1,0:T(8,128)(2,1)S(1)}, bf16[16,2048]{1,0:T(8,128)(2,1)S(1)}, u32[]{:S(2)}, u32[]{:S(2)}) %collective-permute-start.20) | collective-permute-done | bytes 65568 | tf_op jit(solution)/shard_map/ppermute | solution.py:355
  53.3 3.2 %collective-permute-done.21.refs_2_ = bf16[16,2048]{1,0:T(8,128)(2,1)S(1)} collective-permute-done((bf16[16,2048]{1,0:T(8,128)(2,1)S(1)}, bf16[16,2048]{1,0:T(8,128)(2,1)S(1)}, u32[]{:S(2)}, u32[]{:S(2)}) %collective-permute-start.21) | collective-permute-done | bytes 65568 | tf_op jit(solution)/shard_map/ppermute | solution.py:355
  56.5 0.7 %shard_map.125 = bf16[16,4096]{1,0:T(8,128)(2,1)} custom-call(bf16[16,2048]{1,0:T(8,128)(2,1)S(1)} %get-tuple-element.57.refs_0_, bf16[16,2048]{1,0:T(8,128)(2,1)S(1)} %collective-permute-done.20.refs_1_, bf16[16,2048]{1,0:T(8,128)(2,1)S(1)} %collective-permute-done.21.refs_2_, bf16[16,2048]{1,0:T(8,128)(2,1)S(1)} %collective-permute-done.22.refs_3_, ...), custom_call_target="tpu_custom_call" | custom-call | tf_op jit(solution)/shard_map/pallas_call | solution.py:331
  (23 shorter events, 0.2 us)
Async XLA Ops:
  0.0 11.2 %collective-permute-start.4 = (bf16[128,4096]{1,0:T(8,128)(2,1)}, bf16[128,4096]{1,0:T(8,128)(2,1)S(1)}, u32[]{:S(2)}, u32[]{:S(2)}) collective-permute-start(bf16[128,4096]{1,0:T(8,128)(2,1)} %w_out_hbm.1), channel_id=1, source_target_pairs={{0,1},{1,0},{2,3},{3,2},{4,5},{5,4},{6,7},{7,6},{8,9},{9,8},{10,11... | collective-permute-start | bytes 3145736 | tf_op jit(solution)/shard_map/ppermute | solution.py:358
  1.6 7.1 %collective-permute-start.2 = (bf16[144,128]{1,0:T(8,128)(2,1)S(1)}, bf16[144,128]{1,0:T(8,128)(2,1)S(1)}, u32[]{:S(2)}, u32[]{:S(2)}) collective-permute-start(bf16[144,128]{1,0:T(8,128)(2,1)S(1)} %shard_map.109._), channel_id=1, source_target_pairs={{24,0},{16,8},{8,16},{0,24},{25,1},{17,9},{9,17},{1,25},{26,2},{18... | collective-permute-start | bytes 110600 | tf_op jit(solution)/shard_map/ppermute | solution.py:380
  5.1 4.0 %collective-permute-start.1 = (bf16[144,128]{1,0:T(8,128)(2,1)S(1)}, bf16[144,128]{1,0:T(8,128)(2,1)S(1)}, u32[]{:S(2)}, u32[]{:S(2)}) collective-permute-start(bf16[144,128]{1,0:T(8,128)(2,1)S(1)} %shard_map.109._), channel_id=1, source_target_pairs={{16,0},{24,8},{0,16},{8,24},{17,1},{25,9},{1,17},{9,25},{18,2},{26... | collective-permute-start | bytes 110600 | tf_op jit(solution)/shard_map/ppermute | solution.py:380
  5.6 4.0 %collective-permute-start = (bf16[144,128]{1,0:T(8,128)(2,1)S(1)}, bf16[144,128]{1,0:T(8,128)(2,1)S(1)}, u32[]{:S(2)}, u32[]{:S(2)}) collective-permute-start(bf16[144,128]{1,0:T(8,128)(2,1)S(1)} %shard_map.109._), channel_id=1, source_target_pairs={{8,0},{0,8},{24,16},{16,24},{9,1},{1,9},{25,17},{17,25},{10,2},{2,... | collective-permute-start | bytes 110600 | tf_op jit(solution)/shard_map/ppermute | solution.py:380
  10.0 1.2 %collective-permute-start.3 = (bf16[64,128]{1,0:T(8,128)(2,1)S(1)}, bf16[64,128]{1,0:T(8,128)(2,1)S(1)}, u32[]{:S(2)}, u32[]{:S(2)}) collective-permute-start(bf16[64,128]{1,0:T(8,128)(2,1)S(1)} %get-tuple-element.42), channel_id=1, source_target_pairs={{0,1},{1,0},{2,3},{3,2},{4,5},{5,4},{6,7},{7,6},{8,9},{9,8},{10,11... | collective-permute-start | bytes 49160 | tf_op jit(solution)/shard_map/ppermute | solution.py:358
  11.5 6.9 %collective-permute-start.11 = (bf16[16,2048]{1,0:T(8,128)(2,1)S(1)}, bf16[16,2048]{1,0:T(8,128)(2,1)S(1)}, u32[]{:S(2)}, u32[]{:S(2)}) collective-permute-start(bf16[16,2048]{1,0:T(8,128)(2,1)S(1)} %get-tuple-element.49), channel_id=1, source_target_pairs={{0,2},{1,3},{2,4},{3,5},{4,6},{5,7},{6,0},{7,1},{8,10},{9,11},{10,... | collective-permute-start | bytes 196616 | tf_op jit(solution)/shard_map/ppermute | solution.py:355
  13.2 8.1 %collective-permute-start.12 = (bf16[16,2048]{1,0:T(8,128)(2,1)S(1)}, bf16[16,2048]{1,0:T(8,128)(2,1)S(1)}, u32[]{:S(2)}, u32[]{:S(2)}) collective-permute-start(bf16[16,2048]{1,0:T(8,128)(2,1)S(1)} %get-tuple-element.50), channel_id=1, source_target_pairs={{0,4},{1,5},{2,6},{3,7},{4,0},{5,1},{6,2},{7,3},{8,12},{9,13},{10,... | collective-permute-start | bytes 196616 | tf_op jit(solution)/shard_map/ppermute | solution.py:355
  15.7 5.5 %collective-permute-start.13 = (bf16[16,2048]{1,0:T(8,128)(2,1)S(1)}, bf16[16,2048]{1,0:T(8,128)(2,1)S(1)}, u32[]{:S(2)}, u32[]{:S(2)}) collective-permute-start(bf16[16,2048]{1,0:T(8,128)(2,1)S(1)} %get-tuple-element.51), channel_id=1, source_target_pairs={{0,6},{1,7},{2,0},{3,1},{4,2},{5,3},{6,4},{7,5},{8,14},{9,15},{10,... | collective-permute-start | bytes 196616 | tf_op jit(solution)/shard_map/ppermute | solution.py:355
  17.4 7.5 %collective-permute-start.5 = (bf16[16,2048]{1,0:T(8,128)(2,1)S(1)}, bf16[16,2048]{1,0:T(8,128)(2,1)S(1)}, u32[]{:S(2)}, u32[]{:S(2)}) collective-permute-start(bf16[16,2048]{1,0:T(8,128)(2,1)S(1)} %get-tuple-element.45), channel_id=1, source_target_pairs={{0,2},{1,3},{2,4},{3,5},{4,6},{5,7},{6,0},{7,1},{8,10},{9,11},{10,... | collective-permute-start | bytes 196616 | tf_op jit(solution)/shard_map/ppermute | solution.py:355
  18.1 8.7 %collective-permute-start.6 = (bf16[16,2048]{1,0:T(8,128)(2,1)S(1)}, bf16[16,2048]{1,0:T(8,128)(2,1)S(1)}, u32[]{:S(2)}, u32[]{:S(2)}) collective-permute-start(bf16[16,2048]{1,0:T(8,128)(2,1)S(1)} %get-tuple-element.46), channel_id=1, source_target_pairs={{0,4},{1,5},{2,6},{3,7},{4,0},{5,1},{6,2},{7,3},{8,12},{9,13},{10,... | collective-permute-start | bytes 196616 | tf_op jit(solution)/shard_map/ppermute | solution.py:355
  18.5 8.4 %collective-permute-start.7 = (bf16[16,2048]{1,0:T(8,128)(2,1)S(1)}, bf16[16,2048]{1,0:T(8,128)(2,1)S(1)}, u32[]{:S(2)}, u32[]{:S(2)}) collective-permute-start(bf16[16,2048]{1,0:T(8,128)(2,1)S(1)} %get-tuple-element.47), channel_id=1, source_target_pairs={{0,6},{1,7},{2,0},{3,1},{4,2},{5,3},{6,4},{7,5},{8,14},{9,15},{10,... | collective-permute-start | bytes 196616 | tf_op jit(solution)/shard_map/ppermute | solution.py:355
  21.3 9.7 %collective-permute-start.16 = (bf16[16,2048]{1,0:T(8,128)(2,1)S(1)}, bf16[16,2048]{1,0:T(8,128)(2,1)S(1)}, u32[]{:S(2)}, u32[]{:S(2)}) collective-permute-start(bf16[16,2048]{1,0:T(8,128)(2,1)S(1)} %shard_map.115.refs_0_.refs_4_), channel_id=1, source_target_pairs={{0,2},{1,3},{2,4},{3,5},{4,6},{5,7},{6,0},{7,1},{8,10},{9,11},{10,... | collective-permute-start | bytes 196616 | tf_op jit(solution)/shard_map/ppermute | solution.py:355
  24.4 9.0 %collective-permute-start.15 = (bf16[16,2048]{1,0:T(8,128)(2,1)S(1)}, bf16[16,2048]{1,0:T(8,128)(2,1)S(1)}, u32[]{:S(2)}, u32[]{:S(2)}) collective-permute-start(bf16[16,2048]{1,0:T(8,128)(2,1)S(1)} %shard_map.115.refs_0_.refs_4_), channel_id=1, source_target_pairs={{0,4},{1,5},{2,6},{3,7},{4,0},{5,1},{6,2},{7,3},{8,12},{9,13},{10,... | collective-permute-start | bytes 196616 | tf_op jit(solution)/shard_map/ppermute | solution.py:355
  24.9 8.5 %collective-permute-start.14 = (bf16[16,2048]{1,0:T(8,128)(2,1)S(1)}, bf16[16,2048]{1,0:T(8,128)(2,1)S(1)}, u32[]{:S(2)}, u32[]{:S(2)}) collective-permute-start(bf16[16,2048]{1,0:T(8,128)(2,1)S(1)} %shard_map.115.refs_0_.refs_4_), channel_id=1, source_target_pairs={{0,6},{1,7},{2,0},{3,1},{4,2},{5,3},{6,4},{7,5},{8,14},{9,15},{10,... | collective-permute-start | bytes 196616 | tf_op jit(solution)/shard_map/ppermute | solution.py:355
  26.9 8.3 %collective-permute-start.10 = (bf16[16,2048]{1,0:T(8,128)(2,1)S(1)}, bf16[16,2048]{1,0:T(8,128)(2,1)S(1)}, u32[]{:S(2)}, u32[]{:S(2)}) collective-permute-start(bf16[16,2048]{1,0:T(8,128)(2,1)S(1)} %shard_map.113.refs_0_.refs_9_), channel_id=1, source_target_pairs={{0,2},{1,3},{2,4},{3,5},{4,6},{5,7},{6,0},{7,1},{8,10},{9,11},{10,... | collective-permute-start | bytes 196616 | tf_op jit(solution)/shard_map/ppermute | solution.py:355
  31.0 6.4 %collective-permute-start.9 = (bf16[16,2048]{1,0:T(8,128)(2,1)S(1)}, bf16[16,2048]{1,0:T(8,128)(2,1)S(1)}, u32[]{:S(2)}, u32[]{:S(2)}) collective-permute-start(bf16[16,2048]{1,0:T(8,128)(2,1)S(1)} %shard_map.113.refs_0_.refs_9_), channel_id=1, source_target_pairs={{0,4},{1,5},{2,6},{3,7},{4,0},{5,1},{6,2},{7,3},{8,12},{9,13},{10,... | collective-permute-start | bytes 196616 | tf_op jit(solution)/shard_map/ppermute | solution.py:355
  31.0 6.3 %collective-permute-start.8 = (bf16[16,2048]{1,0:T(8,128)(2,1)S(1)}, bf16[16,2048]{1,0:T(8,128)(2,1)S(1)}, u32[]{:S(2)}, u32[]{:S(2)}) collective-permute-start(bf16[16,2048]{1,0:T(8,128)(2,1)S(1)} %shard_map.113.refs_0_.refs_9_), channel_id=1, source_target_pairs={{0,6},{1,7},{2,0},{3,1},{4,2},{5,3},{6,4},{7,5},{8,14},{9,15},{10,... | collective-permute-start | bytes 196616 | tf_op jit(solution)/shard_map/ppermute | solution.py:355
  33.5 4.0 %collective-permute-start.18 = (bf16[64,2048]{1,0:T(8,128)(2,1)S(1)}, bf16[64,2048]{1,0:T(8,128)(2,1)S(1)}, u32[]{:S(2)}, u32[]{:S(2)}) collective-permute-start(bf16[64,2048]{1,0:T(8,128)(2,1)S(1)} %shard_map.116._.own_ref), channel_id=1, source_target_pairs={{0,1},{1,0},{2,3},{3,2},{4,5},{5,4},{6,7},{7,6},{8,9},{9,8},{10,11... | collective-permute-start | bytes 786440 | tf_op jit(solution)/shard_map/ppermute | solution.py:358
  37.4 1.6 %collective-permute-start.17 = (bf16[64,2048]{1,0:T(8,128)(2,1)S(1)}, bf16[64,2048]{1,0:T(8,128)(2,1)S(1)}, u32[]{:S(2)}, u32[]{:S(2)}) collective-permute-start(bf16[64,2048]{1,0:T(8,128)(2,1)S(1)} %shard_map.118.own_ref), channel_id=1, source_target_pairs={{0,1},{1,0},{2,3},{3,2},{4,5},{5,4},{6,7},{7,6},{8,9},{9,8},{10,11... | collective-permute-start | bytes 786440 | tf_op jit(solution)/shard_map/ppermute | solution.py:358
  40.4 1.6 %collective-permute-start.23 = (bf16[64,2048]{1,0:T(8,128)(2,1)S(1)}, bf16[64,2048]{1,0:T(8,128)(2,1)S(1)}, u32[]{:S(2)}, u32[]{:S(2)}) collective-permute-start(bf16[64,2048]{1,0:T(8,128)(2,1)S(1)} %get-tuple-element.62), channel_id=1, source_target_pairs={{0,1},{1,0},{2,3},{3,2},{4,5},{5,4},{6,7},{7,6},{8,9},{9,8},{10,11... | collective-permute-start | bytes 786440 | tf_op jit(solution)/shard_map/ppermute | solution.py:358
  41.0 5.4 %collective-permute-start.19 = (bf16[64,2048]{1,0:T(8,128)(2,1)S(1)}, bf16[64,2048]{1,0:T(8,128)(2,1)S(1)}, u32[]{:S(2)}, u32[]{:S(2)}) collective-permute-start(bf16[64,2048]{1,0:T(8,128)(2,1)S(1)} %get-tuple-element.56), channel_id=1, source_target_pairs={{0,1},{1,0},{2,3},{3,2},{4,5},{5,4},{6,7},{7,6},{8,9},{9,8},{10,11... | collective-permute-start | bytes 786440 | tf_op jit(solution)/shard_map/ppermute | solution.py:358
  42.0 7.0 %collective-permute-start.24 = (bf16[16,2048]{1,0:T(8,128)(2,1)S(1)}, bf16[16,2048]{1,0:T(8,128)(2,1)S(1)}, u32[]{:S(2)}, u32[]{:S(2)}) collective-permute-start(bf16[16,2048]{1,0:T(8,128)(2,1)S(1)} %get-tuple-element.64), channel_id=1, source_target_pairs={{0,2},{1,3},{2,4},{3,5},{4,6},{5,7},{6,0},{7,1},{8,10},{9,11},{10,... | collective-permute-start | bytes 196616 | tf_op jit(solution)/shard_map/ppermute | solution.py:355
  44.0 8.8 %collective-permute-start.25 = (bf16[16,2048]{1,0:T(8,128)(2,1)S(1)}, bf16[16,2048]{1,0:T(8,128)(2,1)S(1)}, u32[]{:S(2)}, u32[]{:S(2)}) collective-permute-start(bf16[16,2048]{1,0:T(8,128)(2,1)S(1)} %get-tuple-element.65), channel_id=1, source_target_pairs={{0,4},{1,5},{2,6},{3,7},{4,0},{5,1},{6,2},{7,3},{8,12},{9,13},{10,... | collective-permute-start | bytes 196616 | tf_op jit(solution)/shard_map/ppermute | solution.py:355
  45.7 7.0 %collective-permute-start.26 = (bf16[16,2048]{1,0:T(8,128)(2,1)S(1)}, bf16[16,2048]{1,0:T(8,128)(2,1)S(1)}, u32[]{:S(2)}, u32[]{:S(2)}) collective-permute-start(bf16[16,2048]{1,0:T(8,128)(2,1)S(1)} %get-tuple-element.66), channel_id=1, source_target_pairs={{0,6},{1,7},{2,0},{3,1},{4,2},{5,3},{6,4},{7,5},{8,14},{9,15},{10,... | collective-permute-start | bytes 196616 | tf_op jit(solution)/shard_map/ppermute | solution.py:355
  46.5 6.9 %collective-permute-start.20 = (bf16[16,2048]{1,0:T(8,128)(2,1)S(1)}, bf16[16,2048]{1,0:T(8,128)(2,1)S(1)}, u32[]{:S(2)}, u32[]{:S(2)}) collective-permute-start(bf16[16,2048]{1,0:T(8,128)(2,1)S(1)} %get-tuple-element.58), channel_id=1, source_target_pairs={{0,2},{1,3},{2,4},{3,5},{4,6},{5,7},{6,0},{7,1},{8,10},{9,11},{10,... | collective-permute-start | bytes 196616 | tf_op jit(solution)/shard_map/ppermute | solution.py:355
  47.8 8.7 %collective-permute-start.21 = (bf16[16,2048]{1,0:T(8,128)(2,1)S(1)}, bf16[16,2048]{1,0:T(8,128)(2,1)S(1)}, u32[]{:S(2)}, u32[]{:S(2)}) collective-permute-start(bf16[16,2048]{1,0:T(8,128)(2,1)S(1)} %get-tuple-element.59), channel_id=1, source_target_pairs={{0,4},{1,5},{2,6},{3,7},{4,0},{5,1},{6,2},{7,3},{8,12},{9,13},{10,... | collective-permute-start | bytes 196616 | tf_op jit(solution)/shard_map/ppermute | solution.py:355
  49.0 7.5 %collective-permute-start.22 = (bf16[16,2048]{1,0:T(8,128)(2,1)S(1)}, bf16[16,2048]{1,0:T(8,128)(2,1)S(1)}, u32[]{:S(2)}, u32[]{:S(2)}) collective-permute-start(bf16[16,2048]{1,0:T(8,128)(2,1)S(1)} %get-tuple-element.60), channel_id=1, source_target_pairs={{0,6},{1,7},{2,0},{3,1},{4,2},{5,3},{6,4},{7,5},{8,14},{9,15},{10,... | collective-permute-start | bytes 196616 | tf_op jit(solution)/shard_map/ppermute | solution.py:355
